TPU v7x, 512 devices: a whole 4x4x16 slice. The times are simulated.
512 devices in a mesh: pair: 8 (over z_hi, x), row: 8 (over y, core), col: 8 (over z_lo).
Axes of the slice: x: 4, y: 4, z: 16 (z_hi: 2, z_lo: 8; z = z_hi * 8 + z_lo), core: 2. Of those that a mesh axis runs over, the one named last changes fastest.
Arguments:
- pair_elements: bfloat16 [16384, 8192], P('pair', ('row', 'col')), may hold values from -0.25 to 0.25
- valence_of: int32 [16384], P('pair'), may hold values from 0 to 1999
- conduction_of: int32 [16384], P('pair'), may hold values from 0 to 4095
- valence_depth: float32 [2000], replicated, may hold values from 0.2 to 12
- conduction_height: float32 [4096], replicated, may hold values from 0.2 to 12
Outputs:
- chi_zero: float32 [8, 1024, 8, 1024], P('row', 'pair', None, 'col')
All inputs are finite; a program needn't handle non-finite values.
Results may differ from a plain program's by a relative error of at most 0.0021.
Values may be sent and summed in bfloat16 or wider, within the bound.
No kernel may reach another device: no remote copies, remote signals or barrier semaphores. Data moves between devices by JAX's collectives and lax.ppermute only.
A program may use at most 64 MiB of HBM per device.

v0:
```python
import jax
import jax.numpy as jnp
from jax import lax
from jax.sharding import PartitionSpec as P


def lookup(indices, table):
    hits = indices[:, None] == jnp.arange(table.shape[0], dtype=jnp.int32)[None, :]
    return jnp.sum(jnp.where(hits, table[None, :], jnp.float32(0.0)), axis=1)


def body(pair_elements, valence_of, conduction_of, valence_depth, conduction_height):
    pair_gap = lookup(valence_of, valence_depth) + lookup(conduction_of, conduction_height)
    factor = -4.0 / pair_gap
    weighted = (pair_elements.astype(jnp.float32) * factor[:, None]).astype(jnp.bfloat16)
    row_panel = lax.all_gather(weighted, "col", axis=1, tiled=True)
    col_panel = lax.all_gather(pair_elements, "row", axis=1, tiled=True)
    row_count = row_panel.shape[1] // lax.axis_size("pair")
    partial_value = lax.dot_general(
        row_panel, col_panel, (((0,), (0,)), ((), ())), preferred_element_type=jnp.float32
    )
    result = lax.psum_scatter(partial_value, "pair", scatter_dimension=0, tiled=True)
    return result.reshape(1, row_count, lax.axis_size("row"), -1)


def solution(mesh):
    placed = (P("pair", ("row", "col")), P("pair"), P("pair"), P(), P())
    return jax.shard_map(
        body, mesh=mesh, in_specs=placed, out_specs=P("row", "pair", None, "col"), check_vma=False
    )
```

profile of v0, /device:TPU:8, one launch (start us, length us, event | category | flops | bytes accessed | tf_op | source)
XLA Modules:
  0.0 399.2 jit_solution(11744925309499042128)
XLA Ops:
  6.5 0.0 all-gather.5.cloned.1.call-start
  6.5 0.7 all-gather.5.cloned.1.call-update
  7.3 0.0 all-gather.3.cloned.1.call-start
  7.3 2.7 select_reduce_fusion.1
  10.0 5.2 %select_reduce_fusion = f32[2048]{0:T(1024)S(1)} fusion(f32[4096]{0:T(1024)} %param.9, s32[2048]{0:T(1024)} %param.7), kind=kLoop, calls=%fused_computation | loop fusion | flops 25163776 | bytes 32768 | tf_op jit(solution)/shard_map/reduce_sum | solution.py:9
  15.2 2.2 multiply_convert_fusion
  17.3 0.0 all-gather.3.cloned.1.call-update
  17.4 0.0 reduce-scatter.2.cloned.1.call-start
  17.4 39.9 %all-gather.5.cloned.1.call-done = bf16[2048,1024]{1,0:T(8,128)(2,1)} async-done(((bf16[2048,128]{1,0:T(8,128)(2,1)}), bf16[2048,1024]{1,0:T(8,128)(2,1)}) %all-gather.5.cloned.1.call-update) | async-done | bytes 4194320 | tf_op jit(solution)/shard_map/all_gather | solution.py:17
  57.3 110.7 %all-gather.3.cloned.1.call-done = bf16[2048,1024]{1,0:T(8,128)(2,1)} async-done(((bf16[2048,128]{1,0:T(8,128)(2,1)}), bf16[2048,1024]{1,0:T(8,128)(2,1)}) %all-gather.3.cloned.1.call-update) | async-done | bytes 4194320 | tf_op jit(solution)/shard_map/all_gather | solution.py:16
  168.0 10.0 %fusion = f32[1024,1024]{1,0:T(8,128)} fusion(bf16[2048,1024]{1,0:T(8,128)(2,1)} %all-gather.3.cloned.1.call-done, bf16[2048,1024]{1,0:T(8,128)(2,1)} %all-gather.5.cloned.1.call-done), kind=kOutput, calls=%fused_computation.6 | convolution fusion | flops 4294967296 | bytes 12582912 | tf_op jit(solution)/shard_map/dot_general | solution.py:19
  178.0 0.0 reduce-scatter.2.cloned.1.call-update
  178.0 212.7 %reduce-scatter.2.cloned.1.call-done = f32[128,1024]{1,0:T(8,128)} async-done(((f32[1024,1024]{1,0:T(8,128)}), f32[128,1024]{1,0:T(8,128)}) %reduce-scatter.2.cloned.1.call-update) | async-done | bytes 524304 | tf_op jit(solution)/shard_map/reduce_scatter | solution.py:22
  390.7 1.9 copy.6
  (1 shorter events, 0.0 us)
Async XLA Ops:
  6.5 50.8 %all-gather.5.cloned.1.call-start = ((), (), s32[]{:S(2)}) async-start(), calls=%async_computation.2 | async-start | bytes 4718592 | tf_op jit(solution)/shard_map/all_gather | solution.py:17
  7.3 160.8 %all-gather.3.cloned.1.call-start = ((), (), s32[]{:S(2)}) async-start(), calls=%async_computation.1 | async-start | bytes 4718592 | tf_op jit(solution)/shard_map/all_gather | solution.py:16
  17.4 373.3 %reduce-scatter.2.cloned.1.call-start = ((), (), s32[]{:S(2)}) async-start(), calls=%async_computation.3 | async-start | bytes 4718592 | tf_op jit(solution)/shard_map/reduce_scatter | solution.py:22
Sparse Core Ops, SparseCore 0:
  9.5 47.7 all-gather.4
  59.3 108.6 all-gather.2
  178.2 212.4 reduce-scatter.1
where the time goes:
time: 400 us; the launch traced here: 399 us
  waiting for transfers between devices  364 us (91%)
  between operations  13.1 us (3%)
  other arithmetic  10 us (2%)
  matrix products  9.97 us (2%)
    reduce_scatter x1, waiting for transfers between devices, body(): lax.psum_scatter(partial_value, 'pair', scatter_dimension=0, tiled=True)  213 us
    all_gather x1, waiting for transfers between devices, body(): row_panel = lax.all_gather(weighted, 'col', axis=1, tiled=True)  111 us
    all_gather x1, waiting for transfers between devices, body(): col_panel = lax.all_gather(pair_elements, 'row', axis=1, tiled=True)  39.9 us
    dot_general x1, matrix products, body(): lax.dot_general(row_panel, col_panel, (((0,), (0,)), ((), ())), preferred...  9.97 us
  transfers between devices with their start and end apart: 3, of which 3 were waited for; matrix products, arithmetic and copies ran while one was open for 3% of the time, Pallas kernels for 0%

commit v1 on v0

v1 whole, which is shorter than its diff:
```python
import jax
import jax.numpy as jnp
from jax import lax
from jax.sharding import Mesh, PartitionSpec as P

NAMES = ("zh", "x", "y", "core", "zl")
SHAPE = (2, 4, 4, 2, 8)


def shift(n, s):
    return [(i, (i + s) % n) for i in range(n)]


SWAP = shift(2, 1)


def lookup(indices, table):
    hits = indices[:, None] == jnp.arange(table.shape[0], dtype=jnp.int32)[None, :]
    return jnp.sum(jnp.where(hits, table[None, :], jnp.float32(0.0)), axis=1)


def body(pair_elements, valence_of, conduction_of, valence_depth, conduction_height):
    n_pair, n_g = pair_elements.shape
    n_y, n_x, n_z = (lax.axis_size(name) for name in ("y", "x", "zl"))
    rows = lax.all_gather(pair_elements.T, "zl", axis=0, tiled=True)

    near = [pair_elements] + [
        lax.ppermute(pair_elements, "y", shift(n_y, -s)) for s in range(1, n_y)
    ]
    panels = []
    for piece in near:
        panels += [piece, lax.ppermute(piece, "core", SWAP)]
    columns = jnp.concatenate(panels, axis=1)

    pair_gap = lookup(valence_of, valence_depth) + lookup(conduction_of, conduction_height)
    factor = -4.0 / pair_gap
    weighted = (rows.astype(jnp.float32) * factor[None, :]).astype(jnp.bfloat16)
    partial = lax.dot_general(
        weighted, columns, (((1,), (0,)), ((), ())), preferred_element_type=jnp.float32
    ).astype(jnp.bfloat16)

    partial = partial.reshape(2, n_x, n_g, -1).swapaxes(0, 1)
    taken = lax.all_to_all(partial, "x", 0, 0, tiled=True)
    taken = jnp.sum(taken.astype(jnp.float32), axis=0)
    half = lax.axis_index("zh")
    kept = lax.dynamic_index_in_dim(taken, half, 0, keepdims=False)
    given = lax.dynamic_index_in_dim(taken, 1 - half, 0, keepdims=False)
    got = lax.ppermute(given.astype(jnp.bfloat16), "zh", SWAP)
    total = kept + got.astype(jnp.float32)

    total = total.reshape(n_g, n_y, 2, n_g)
    total = jnp.where(lax.axis_index("core") == 0, total, total[:, :, ::-1])
    total = jnp.concatenate([total, total], axis=1)
    total = lax.dynamic_slice_in_dim(total, lax.rem(n_y - lax.axis_index("y"), n_y), n_y, 1)
    return total.reshape(1, n_g, 2 * n_y, n_g)


def solution(mesh):
    fine = Mesh(mesh.devices.reshape(SHAPE), NAMES)
    pair, row = ("zh", "x"), ("y", "core")
    placed = (P(pair, row + ("zl",)), P(pair), P(pair), P(), P())
    return jax.shard_map(
        body, mesh=fine, in_specs=placed, out_specs=P(row, pair, None, "zl"), check_vma=False
    )
```

time: 400 us -> 203 us (0.51)
  the two profiles are of different devices: /device:TPU:8 before, /device:TPU:73 now
where the time goes in v1:
time: 203 us; the launch traced here: 202 us
  waiting for transfers between devices  127 us (63%)
  starting transfers between devices  32.3 us (16%)
  between operations  13.6 us (7%)
  local copies, waits for them, and re-layouts  11.5 us (6%)
  other arithmetic  9.52 us (5%)
  matrix products  8.19 us (4%)
    all_gather x1, waiting for transfers between devices, body(): rows = lax.all_gather(pair_elements.T, 'zl', axis=0, tiled=True)  67.7 us
    ppermute x1, waiting for transfers between devices, body(): got = lax.ppermute(given.astype(jnp.bfloat16), 'zh', SWAP)  27.7 us
    all_to_all x1, waiting for transfers between devices, body(): taken = lax.all_to_all(partial, 'x', 0, 0, tiled=True)  25.7 us
    ppermute x4, starting transfers between devices, body(): panels += [piece, lax.ppermute(piece, 'core', SWAP)]  10.1 us
    ppermute x3, starting transfers between devices, body(): lax.ppermute(pair_elements, 'y', shift(n_y, -s))  9.82 us
    dot_general x1, matrix products, body(): lax.dot_general(weighted, columns, (((1,), (0,)), ((), ())), preferred_el...  8.19 us
    reduce_sum x2, other arithmetic, lookup(): return jnp.sum(jnp.where(hits, table[None, :], jnp.float32(0.0)), axis=1)  7.85 us
    ppermute x1, starting transfers between devices, body(): got = lax.ppermute(given.astype(jnp.bfloat16), 'zh', SWAP)  7.63 us
  transfers between devices with their start and end apart: 10, of which 4 were waited for; matrix products, arithmetic and copies ran while one was open for 8% of the time, Pallas kernels for 0%

profile of v1, /device:TPU:73, one launch (start us, length us, event | category | flops | bytes accessed | tf_op | source)
XLA Modules:
  0.0 202.4 jit_solution(16664938473662315605)
XLA Ops:
  6.5 0.7 all-gather.2.cloned.1.call-update
  7.3 2.6 %collective-permute-start = (bf16[2048,128]{1,0:T(8,128)(2,1)}, bf16[2048,128]{1,0:T(8,128)(2,1)S(1)}, u32[]{:S(2)}, u32[]{:S(2)}) collective-permute-start(bf16[2048,128]{1,0:T(8,128)(2,1)} %param.5), channel_id=1, source_target_pairs={{0,8},{8,0},{1,9},{9,1},{2,10},{10,2},{3,11},{11,3},{4,12},{12,4},... | collective-permute-start | bytes 1572872 | tf_op jit(solution)/shard_map/ppermute | solution.py:32
  9.8 2.1 %collective-permute-start.1 = (bf16[2048,128]{1,0:T(8,128)(2,1)}, bf16[2048,128]{1,0:T(8,128)(2,1)S(1)}, u32[]{:S(2)}, u32[]{:S(2)}) collective-permute-start(bf16[2048,128]{1,0:T(8,128)(2,1)} %param.5), channel_id=1, source_target_pairs={{0,48},{16,0},{32,16},{48,32},{1,49},{17,1},{33,17},{49,33},{2,50}... | collective-permute-start | bytes 1572872 | tf_op jit(solution)/shard_map/ppermute | solution.py:28
  11.9 4.2 %collective-permute-start.3 = (bf16[2048,128]{1,0:T(8,128)(2,1)}, bf16[2048,128]{1,0:T(8,128)(2,1)S(1)}, u32[]{:S(2)}, u32[]{:S(2)}) collective-permute-start(bf16[2048,128]{1,0:T(8,128)(2,1)} %param.5), channel_id=1, source_target_pairs={{0,32},{16,48},{32,0},{48,16},{1,33},{17,49},{33,1},{49,17},{2,34}... | collective-permute-start | bytes 1572872 | tf_op jit(solution)/shard_map/ppermute | solution.py:28
  16.2 3.5 %collective-permute-start.5 = (bf16[2048,128]{1,0:T(8,128)(2,1)}, bf16[2048,128]{1,0:T(8,128)(2,1)S(1)}, u32[]{:S(2)}, u32[]{:S(2)}) collective-permute-start(bf16[2048,128]{1,0:T(8,128)(2,1)} %param.5), channel_id=1, source_target_pairs={{0,16},{16,32},{32,48},{48,0},{1,17},{17,33},{33,49},{49,1},{2,18}... | collective-permute-start | bytes 1572872 | tf_op jit(solution)/shard_map/ppermute | solution.py:28
  19.7 5.2 %select_reduce_fusion = f32[2048]{0:T(1024)S(1)} fusion(f32[4096]{0:T(1024)} %param.9, s32[2048]{0:T(1024)} %param.7), kind=kLoop, calls=%fused_computation | loop fusion | flops 25163776 | bytes 32768 | tf_op jit(solution)/shard_map/reduce_sum | solution.py:19
  24.8 2.7 %select_reduce_fusion.1 = f32[2048]{0:T(1024)S(1)} fusion(f32[2000]{0:T(1024)} %param.8, s32[2048]{0:T(1024)} %param.6), kind=kLoop, calls=%fused_computation.2 | loop fusion | flops 12285952 | bytes 24384 | tf_op jit(solution)/shard_map/reduce_sum | solution.py:19
  27.5 1.9 constant_dynamic-update-slice_fusion.7
  29.5 2.7 %collective-permute-start.2 = (bf16[2048,128]{1,0:T(8,128)(2,1)S(1)}, bf16[2048,128]{1,0:T(8,128)(2,1)S(1)}, u32[]{:S(2)}, u32[]{:S(2)}) collective-permute-start(bf16[2048,128]{1,0:T(8,128)(2,1)S(1)} %collective-permute-done.1), channel_id=1, source_target_pairs={{0,8},{8,0},{1,9},{9,1},{2,10},{10,2},{3,11},{11,3},{4,12},{12,4},... | collective-permute-start | bytes 1572872 | tf_op jit(solution)/shard_map/ppermute | solution.py:32
  32.3 5.5 %collective-permute-done.3 = bf16[2048,128]{1,0:T(8,128)(2,1)S(1)} collective-permute-done((bf16[2048,128]{1,0:T(8,128)(2,1)}, bf16[2048,128]{1,0:T(8,128)(2,1)S(1)}, u32[]{:S(2)}, u32[]{:S(2)}) %collective-permute-start.3) | collective-permute-done | bytes 524320 | tf_op jit(solution)/shard_map/ppermute | solution.py:28
  37.7 2.7 %collective-permute-start.4 = (bf16[2048,128]{1,0:T(8,128)(2,1)S(1)}, bf16[2048,128]{1,0:T(8,128)(2,1)S(1)}, u32[]{:S(2)}, u32[]{:S(2)}) collective-permute-start(bf16[2048,128]{1,0:T(8,128)(2,1)S(1)} %collective-permute-done.3), channel_id=1, source_target_pairs={{0,8},{8,0},{1,9},{9,1},{2,10},{10,2},{3,11},{11,3},{4,12},{12,4},... | collective-permute-start | bytes 1572872 | tf_op jit(solution)/shard_map/ppermute | solution.py:32
  40.5 0.9 constant_dynamic-update-slice_fusion.6
  41.4 0.9 constant_dynamic-update-slice_fusion.5
  42.3 2.1 %collective-permute-start.6 = (bf16[2048,128]{1,0:T(8,128)(2,1)S(1)}, bf16[2048,128]{1,0:T(8,128)(2,1)S(1)}, u32[]{:S(2)}, u32[]{:S(2)}) collective-permute-start(bf16[2048,128]{1,0:T(8,128)(2,1)S(1)} %collective-permute-done.5), channel_id=1, source_target_pairs={{0,8},{8,0},{1,9},{9,1},{2,10},{10,2},{3,11},{11,3},{4,12},{12,4},... | collective-permute-start | bytes 1572872 | tf_op jit(solution)/shard_map/ppermute | solution.py:32
  44.4 0.9 constant_dynamic-update-slice_fusion.4
  45.3 0.9 constant_dynamic-update-slice_fusion.3
  46.1 0.9 constant_dynamic-update-slice_fusion.2
  47.0 0.9 constant_dynamic-update-slice_fusion.1
  47.9 0.9 constant_dynamic-update-slice_fusion
  48.8 67.7 %all-gather.2.cloned.1.call-done = bf16[1024,2048]{0,1:T(8,128)(2,1)} async-done(((bf16[128,2048]{0,1:T(8,128)(2,1)}), bf16[1024,2048]{0,1:T(8,128)(2,1)}) %all-gather.2.cloned.1.call-update) | async-done | bytes 4194320 | tf_op jit(solution)/shard_map/all_gather | solution.py:25
  116.5 8.2 %fusion.2 = bf16[1024,1024]{1,0:T(8,128)(2,1)S(1)} fusion(bf16[2048,1024]{1,0:T(8,128)(2,1)} %constant_dynamic-update-slice_fusion, bf16[1024,2048]{0,1:T(8,128)(2,1)} %all-gather.2.cloned.1.call-done, f32[2048]{0:T(1024)S(1)} %add_divide_fusion), kind=kOutput, calls=%fused_computation.9 | convolution fusion | flops 4302307328 | bytes 10493952 | tf_op jit(solution)/shard_map/dot_general | solution.py:38
  124.7 1.5 copy.9
  126.2 4.8 %all-to-all-start = ((bf16[4,2,128,1024]{3,2,1,0:T(8,128)(2,1)}), bf16[4,2,128,1024]{3,2,1,0:T(8,128)(2,1)S(1)}, u32[]{:S(2)}, u32[]{:S(2)}) async-start(bf16[4,2,128,1024]{3,2,1,0:T(8,128)(2,1)} %bitcast.14), calls=%async_computation | async-start | bytes 4194304 | tf_op jit(solution)/shard_map/all_to_all | solution.py:43
  131.0 25.7 %all-to-all-done = bf16[4,2,128,1024]{3,2,1,0:T(8,128)(2,1)S(1)} async-done(((bf16[4,2,128,1024]{3,2,1,0:T(8,128)(2,1)}), bf16[4,2,128,1024]{3,2,1,0:T(8,128)(2,1)S(1)}, u32[]{:S(2)}, u32[]{:S(2)}) %all-to-all-start) | async-done | bytes 2097184 | tf_op jit(solution)/shard_map/all_to_all | solution.py:43
  156.6 0.4 convert_reduce_fusion
  157.1 7.6 %collective-permute-start.7 = (bf16[128,1024]{1,0:T(8,128)(2,1)S(1)}, bf16[128,1024]{1,0:T(8,128)(2,1)S(1)}, u32[]{:S(2)}, u32[]{:S(2)}) collective-permute-start(bf16[128,1024]{1,0:T(8,128)(2,1)S(1)} %fusion.4), channel_id=1, source_target_pairs={{0,256},{256,0},{1,257},{257,1},{2,258},{258,2},{3,259},{259,3},{4... | collective-permute-start | bytes 786440 | tf_op jit(solution)/shard_map/ppermute | solution.py:48
  164.7 27.7 %collective-permute-done.7 = bf16[128,1024]{1,0:T(8,128)(2,1)S(1)} collective-permute-done((bf16[128,1024]{1,0:T(8,128)(2,1)S(1)}, bf16[128,1024]{1,0:T(8,128)(2,1)S(1)}, u32[]{:S(2)}, u32[]{:S(2)}) %collective-permute-start.7) | collective-permute-done | bytes 262176 | tf_op jit(solution)/shard_map/ppermute | solution.py:48
  192.4 0.1 bitcast_add_fusion
  192.4 0.4 reshape.21
  192.9 1.4 rev.3
  194.3 0.1 broadcast_select_fusion
  194.4 1.2 fusion.3
  (9 shorter events, 0.1 us)
Async XLA Ops:
  6.5 110.0 %all-gather.2.cloned.1.call-start = ((), (), s32[]{:S(2)}) async-start(), calls=%async_computation.1 | async-start | bytes 4718592 | tf_op jit(solution)/shard_map/all_gather | solution.py:25
  7.3 33.2 %collective-permute-start = (bf16[2048,128]{1,0:T(8,128)(2,1)}, bf16[2048,128]{1,0:T(8,128)(2,1)S(1)}, u32[]{:S(2)}, u32[]{:S(2)}) collective-permute-start(bf16[2048,128]{1,0:T(8,128)(2,1)} %param.5), channel_id=1, source_target_pairs={{0,8},{8,0},{1,9},{9,1},{2,10},{10,2},{3,11},{11,3},{4,12},{12,4},... | collective-permute-start | bytes 1572872 | tf_op jit(solution)/shard_map/ppermute | solution.py:32
  9.8 19.6 %collective-permute-start.1 = (bf16[2048,128]{1,0:T(8,128)(2,1)}, bf16[2048,128]{1,0:T(8,128)(2,1)S(1)}, u32[]{:S(2)}, u32[]{:S(2)}) collective-permute-start(bf16[2048,128]{1,0:T(8,128)(2,1)} %param.5), channel_id=1, source_target_pairs={{0,48},{16,0},{32,16},{48,32},{1,49},{17,1},{33,17},{49,33},{2,50}... | collective-permute-start | bytes 1572872 | tf_op jit(solution)/shard_map/ppermute | solution.py:28
  11.9 25.8 %collective-permute-start.3 = (bf16[2048,128]{1,0:T(8,128)(2,1)}, bf16[2048,128]{1,0:T(8,128)(2,1)S(1)}, u32[]{:S(2)}, u32[]{:S(2)}) collective-permute-start(bf16[2048,128]{1,0:T(8,128)(2,1)} %param.5), channel_id=1, source_target_pairs={{0,32},{16,48},{32,0},{48,16},{1,33},{17,49},{33,1},{49,17},{2,34}... | collective-permute-start | bytes 1572872 | tf_op jit(solution)/shard_map/ppermute | solution.py:28
  16.2 26.1 %collective-permute-start.5 = (bf16[2048,128]{1,0:T(8,128)(2,1)}, bf16[2048,128]{1,0:T(8,128)(2,1)S(1)}, u32[]{:S(2)}, u32[]{:S(2)}) collective-permute-start(bf16[2048,128]{1,0:T(8,128)(2,1)} %param.5), channel_id=1, source_target_pairs={{0,16},{16,32},{32,48},{48,0},{1,17},{17,33},{33,49},{49,1},{2,18}... | collective-permute-start | bytes 1572872 | tf_op jit(solution)/shard_map/ppermute | solution.py:28
  29.5 14.9 %collective-permute-start.2 = (bf16[2048,128]{1,0:T(8,128)(2,1)S(1)}, bf16[2048,128]{1,0:T(8,128)(2,1)S(1)}, u32[]{:S(2)}, u32[]{:S(2)}) collective-permute-start(bf16[2048,128]{1,0:T(8,128)(2,1)S(1)} %collective-permute-done.1), channel_id=1, source_target_pairs={{0,8},{8,0},{1,9},{9,1},{2,10},{10,2},{3,11},{11,3},{4,12},{12,4},... | collective-permute-start | bytes 1572872 | tf_op jit(solution)/shard_map/ppermute | solution.py:32
  37.7 8.4 %collective-permute-start.4 = (bf16[2048,128]{1,0:T(8,128)(2,1)S(1)}, bf16[2048,128]{1,0:T(8,128)(2,1)S(1)}, u32[]{:S(2)}, u32[]{:S(2)}) collective-permute-start(bf16[2048,128]{1,0:T(8,128)(2,1)S(1)} %collective-permute-done.3), channel_id=1, source_target_pairs={{0,8},{8,0},{1,9},{9,1},{2,10},{10,2},{3,11},{11,3},{4,12},{12,4},... | collective-permute-start | bytes 1572872 | tf_op jit(solution)/shard_map/ppermute | solution.py:32
  42.3 5.6 %collective-permute-start.6 = (bf16[2048,128]{1,0:T(8,128)(2,1)S(1)}, bf16[2048,128]{1,0:T(8,128)(2,1)S(1)}, u32[]{:S(2)}, u32[]{:S(2)}) collective-permute-start(bf16[2048,128]{1,0:T(8,128)(2,1)S(1)} %collective-permute-done.5), channel_id=1, source_target_pairs={{0,8},{8,0},{1,9},{9,1},{2,10},{10,2},{3,11},{11,3},{4,12},{12,4},... | collective-permute-start | bytes 1572872 | tf_op jit(solution)/shard_map/ppermute | solution.py:32
  126.2 30.4 %all-to-all-start = ((bf16[4,2,128,1024]{3,2,1,0:T(8,128)(2,1)}), bf16[4,2,128,1024]{3,2,1,0:T(8,128)(2,1)S(1)}, u32[]{:S(2)}, u32[]{:S(2)}) async-start(bf16[4,2,128,1024]{3,2,1,0:T(8,128)(2,1)} %bitcast.14), calls=%async_computation | async-start | bytes 4194304 | tf_op jit(solution)/shard_map/all_to_all | solution.py:43
  157.1 35.3 %collective-permute-start.7 = (bf16[128,1024]{1,0:T(8,128)(2,1)S(1)}, bf16[128,1024]{1,0:T(8,128)(2,1)S(1)}, u32[]{:S(2)}, u32[]{:S(2)}) collective-permute-start(bf16[128,1024]{1,0:T(8,128)(2,1)S(1)} %fusion.4), channel_id=1, source_target_pairs={{0,256},{256,0},{1,257},{257,1},{2,258},{258,2},{3,259},{259,3},{4... | collective-permute-start | bytes 786440 | tf_op jit(solution)/shard_map/ppermute | solution.py:48
Sparse Core Ops, SparseCore 0:
  9.4 107.0 all-gather.1

commit v2 on v0

v2 whole, which is shorter than its diff:
```python
import jax
import jax.numpy as jnp
from jax import lax
from jax.sharding import Mesh, PartitionSpec as P

NAMES = ("zh", "x", "y", "core", "zq", "zr")
SHAPE = (2, 4, 4, 2, 2, 4)


def shift(n, s):
    return [(i, (i + s) % n) for i in range(n)]


SWAP = shift(2, 1)


def lookup(indices, table):
    hits = indices[:, None] == jnp.arange(table.shape[0], dtype=jnp.int32)[None, :]
    return jnp.sum(jnp.where(hits, table[None, :], jnp.float32(0.0)), axis=1)


def panel(piece):
    n_y = lax.axis_size("y")
    near = [piece] + [lax.ppermute(piece, "y", shift(n_y, -s)) for s in range(1, n_y)]
    pieces = []
    for one in near:
        pieces += [one, lax.ppermute(one, "core", SWAP)]
    return jnp.concatenate(pieces, axis=1)


def body(pair_elements, valence_of, conduction_of, valence_depth, conduction_height):
    n_g = pair_elements.shape[1]
    n_x, n_y = lax.axis_size("x"), lax.axis_size("y")
    my_x = lax.axis_index("x")
    rows = lax.all_gather(pair_elements.T, "zr", axis=0, tiled=True)
    across = lax.ppermute(pair_elements, "zq", SWAP)
    own_columns = panel(pair_elements)
    cross_columns = panel(across)

    pair_gap = lookup(valence_of, valence_depth) + lookup(conduction_of, conduction_height)
    factor = -4.0 / pair_gap
    weighted = (rows.astype(jnp.float32) * factor[None, :]).astype(jnp.bfloat16)

    def summed_over_x(columns, earlier=None):
        partial = lax.dot_general(
            weighted, columns, (((1,), (0,)), ((), ())), preferred_element_type=jnp.float32
        ).reshape(n_x, n_g, -1)
        taken = lax.all_to_all(partial.astype(jnp.bfloat16), "x", 0, 0, tiled=True)
        if earlier is not None:
            taken, earlier = lax.optimization_barrier((taken, earlier))
        mine = jnp.arange(n_x)[:, None, None] == my_x
        others = jnp.sum(jnp.where(mine, 0.0, taken.astype(jnp.float32)), axis=0)
        return lax.dynamic_index_in_dim(partial, my_x, 0, keepdims=False) + others, earlier

    half = ("zh", "zq")
    own, _ = summed_over_x(own_columns)
    own_got = lax.ppermute(own.astype(jnp.bfloat16), half, [(2, 0), (1, 3)])
    cross, own_got = summed_over_x(cross_columns, own_got)
    cross = cross.astype(jnp.bfloat16)
    near_got = lax.ppermute(cross, half, [(0, 1), (3, 2)])
    next_got = lax.ppermute(cross, half, [(2, 1), (1, 2)])
    stays = lax.axis_index("zh") == lax.axis_index("zq")
    total = jnp.where(
        stays,
        own + own_got.astype(jnp.float32),
        near_got.astype(jnp.float32) + next_got.astype(jnp.float32),
    )

    total = total.reshape(n_g, n_y, 2, n_g)
    total = jnp.where(lax.axis_index("core") == 0, total, total[:, :, ::-1])
    total = jnp.concatenate([total, total], axis=1)
    total = lax.dynamic_slice_in_dim(total, lax.rem(n_y - lax.axis_index("y"), n_y), n_y, 1)
    return total.reshape(1, n_g, 2 * n_y, n_g)


def solution(mesh):
    fine = Mesh(mesh.devices.reshape(SHAPE), NAMES)
    pair, row, col = ("zh", "x"), ("y", "core"), ("zq", "zr")
    placed = (P(pair, row + col), P(pair), P(pair), P(), P())
    return jax.shard_map(
        body, mesh=fine, in_specs=placed, out_specs=P(row, pair, None, col), check_vma=False
    )
```

time: 400 us -> 212 us (0.53)
  the two profiles are of different devices: /device:TPU:8 before, /device:TPU:99 now
where the time goes in v2:
time: 212 us; the launch traced here: 211 us
  starting transfers between devices  78.1 us (37%)
  waiting for transfers between devices  70.5 us (33%)
  local copies, waits for them, and re-layouts  21.3 us (10%)
  other arithmetic  16.9 us (8%)
  between operations  13.7 us (6%)
  matrix products  10.5 us (5%)
    ppermute x1, waiting for transfers between devices, body(): across = lax.ppermute(pair_elements, 'zq', SWAP)  21.9 us
    ppermute x1, starting transfers between devices, body(): near_got = lax.ppermute(cross, half, [(0, 1), (3, 2)])  19.5 us
    ppermute x8, starting transfers between devices, panel(): pieces += [one, lax.ppermute(one, 'core', SWAP)]  19.2 us
    ppermute x6, starting transfers between devices, panel(): lax.ppermute(piece, 'y', shift(n_y, -s))  19 us
    ppermute x1, waiting for transfers between devices, body(): near_got = lax.ppermute(cross, half, [(0, 1), (3, 2)])  18.2 us
    unnamed x20, local copies, waits for them, and re-layouts  16.6 us
    all_to_all x2, waiting for transfers between devices, summed_over_x(): taken = lax.all_to_all(partial.astype(jnp.bfloat16), 'x', 0, 0, tiled=True)  13 us
    ppermute x6, waiting for transfers between devices, panel(): lax.ppermute(piece, 'y', shift(n_y, -s))  11.5 us
  transfers between devices with their start and end apart: 21, of which 7 were waited for; matrix products, arithmetic and copies ran while one was open for 19% of the time, Pallas kernels for 0%

profile of v2, /device:TPU:99, one launch (start us, length us, event | category | flops | bytes accessed | tf_op | source)
XLA Modules:
  0.0 210.9 jit_solution(8498943674743367346)
XLA Ops:
  6.5 8.8 %collective-permute-start.7 = (bf16[2048,128]{1,0:T(8,128)(2,1)}, bf16[2048,128]{1,0:T(8,128)(2,1)S(1)}, u32[]{:S(2)}, u32[]{:S(2)}) collective-permute-start(bf16[2048,128]{1,0:T(8,128)(2,1)} %param.5), channel_id=1, source_target_pairs={{0,4},{4,0},{1,5},{5,1},{2,6},{6,2},{3,7},{7,3},{8,12},{12,8},{9,1... | collective-permute-start | bytes 1572872 | tf_op jit(solution)/shard_map/ppermute | solution.py:36
  15.4 2.9 %collective-permute-start = (bf16[2048,128]{1,0:T(8,128)(2,1)}, bf16[2048,128]{1,0:T(8,128)(2,1)S(1)}, u32[]{:S(2)}, u32[]{:S(2)}) collective-permute-start(bf16[2048,128]{1,0:T(8,128)(2,1)} %param.5), channel_id=1, source_target_pairs={{0,8},{8,0},{1,9},{9,1},{2,10},{10,2},{3,11},{11,3},{4,12},{12,4},... | collective-permute-start | bytes 1572872 | tf_op jit(solution)/shard_map/ppermute | solution.py:27
  18.2 4.6 %collective-permute-start.1 = (bf16[2048,128]{1,0:T(8,128)(2,1)}, bf16[2048,128]{1,0:T(8,128)(2,1)S(1)}, u32[]{:S(2)}, u32[]{:S(2)}) collective-permute-start(bf16[2048,128]{1,0:T(8,128)(2,1)} %param.5), channel_id=1, source_target_pairs={{0,48},{16,0},{32,16},{48,32},{1,49},{17,1},{33,17},{49,33},{2,50}... | collective-permute-start | bytes 1572872 | tf_op jit(solution)/shard_map/ppermute | solution.py:24
  22.9 2.3 %collective-permute-start.3 = (bf16[2048,128]{1,0:T(8,128)(2,1)}, bf16[2048,128]{1,0:T(8,128)(2,1)S(1)}, u32[]{:S(2)}, u32[]{:S(2)}) collective-permute-start(bf16[2048,128]{1,0:T(8,128)(2,1)} %param.5), channel_id=1, source_target_pairs={{0,32},{16,48},{32,0},{48,16},{1,33},{17,49},{33,1},{49,17},{2,34}... | collective-permute-start | bytes 1572872 | tf_op jit(solution)/shard_map/ppermute | solution.py:24
  25.1 2.6 %collective-permute-start.5 = (bf16[2048,128]{1,0:T(8,128)(2,1)}, bf16[2048,128]{1,0:T(8,128)(2,1)S(1)}, u32[]{:S(2)}, u32[]{:S(2)}) collective-permute-start(bf16[2048,128]{1,0:T(8,128)(2,1)} %param.5), channel_id=1, source_target_pairs={{0,16},{16,32},{32,48},{48,0},{1,17},{17,33},{33,49},{49,1},{2,18}... | collective-permute-start | bytes 1572872 | tf_op jit(solution)/shard_map/ppermute | solution.py:24
  27.8 5.2 %select_reduce_fusion = f32[2048]{0:T(1024)S(1)} fusion(f32[4096]{0:T(1024)} %param.9, s32[2048]{0:T(1024)} %param.7), kind=kLoop, calls=%fused_computation | loop fusion | flops 25163776 | bytes 32768 | tf_op jit(solution)/shard_map/reduce_sum | solution.py:19
  32.9 2.7 %select_reduce_fusion.1 = f32[2048]{0:T(1024)S(1)} fusion(f32[2000]{0:T(1024)} %param.8, s32[2048]{0:T(1024)} %param.6), kind=kLoop, calls=%fused_computation.2 | loop fusion | flops 12285952 | bytes 24384 | tf_op jit(solution)/shard_map/reduce_sum | solution.py:19
  35.6 1.9 constant_dynamic-update-slice_fusion.7
  37.6 21.9 %collective-permute-done.7 = bf16[2048,128]{1,0:T(8,128)(2,1)S(1)} collective-permute-done((bf16[2048,128]{1,0:T(8,128)(2,1)}, bf16[2048,128]{1,0:T(8,128)(2,1)S(1)}, u32[]{:S(2)}, u32[]{:S(2)}) %collective-permute-start.7) | collective-permute-done | bytes 524320 | tf_op jit(solution)/shard_map/ppermute | solution.py:36
  59.5 2.6 %collective-permute-start.8 = (bf16[2048,128]{1,0:T(8,128)(2,1)S(1)}, bf16[2048,128]{1,0:T(8,128)(2,1)S(1)}, u32[]{:S(2)}, u32[]{:S(2)}) collective-permute-start(bf16[2048,128]{1,0:T(8,128)(2,1)S(1)} %collective-permute-done.7), channel_id=1, source_target_pairs={{0,8},{8,0},{1,9},{9,1},{2,10},{10,2},{3,11},{11,3},{4,12},{12,4},... | collective-permute-start | bytes 1572872 | tf_op jit(solution)/shard_map/ppermute | solution.py:27
  63.0 4.6 %collective-permute-start.9 = (bf16[2048,128]{1,0:T(8,128)(2,1)S(1)}, bf16[2048,128]{1,0:T(8,128)(2,1)S(1)}, u32[]{:S(2)}, u32[]{:S(2)}) collective-permute-start(bf16[2048,128]{1,0:T(8,128)(2,1)S(1)} %collective-permute-done.7), channel_id=1, source_target_pairs={{0,48},{16,0},{32,16},{48,32},{1,49},{17,1},{33,17},{49,33},{2,50}... | collective-permute-start | bytes 1572872 | tf_op jit(solution)/shard_map/ppermute | solution.py:24
  68.5 2.2 %collective-permute-start.11 = (bf16[2048,128]{1,0:T(8,128)(2,1)S(1)}, bf16[2048,128]{1,0:T(8,128)(2,1)S(1)}, u32[]{:S(2)}, u32[]{:S(2)}) collective-permute-start(bf16[2048,128]{1,0:T(8,128)(2,1)S(1)} %collective-permute-done.7), channel_id=1, source_target_pairs={{0,32},{16,48},{32,0},{48,16},{1,33},{17,49},{33,1},{49,17},{2,34}... | collective-permute-start | bytes 1572872 | tf_op jit(solution)/shard_map/ppermute | solution.py:24
  70.8 2.6 %collective-permute-start.13 = (bf16[2048,128]{1,0:T(8,128)(2,1)S(1)}, bf16[2048,128]{1,0:T(8,128)(2,1)}, u32[]{:S(2)}, u32[]{:S(2)}) collective-permute-start(bf16[2048,128]{1,0:T(8,128)(2,1)S(1)} %collective-permute-done.7), channel_id=1, source_target_pairs={{0,16},{16,32},{32,48},{48,0},{1,17},{17,33},{33,49},{49,1},{2,18}... | collective-permute-start | bytes 1572872 | tf_op jit(solution)/shard_map/ppermute | solution.py:24
  73.4 2.8 %collective-permute-start.2 = (bf16[2048,128]{1,0:T(8,128)(2,1)S(1)}, bf16[2048,128]{1,0:T(8,128)(2,1)S(1)}, u32[]{:S(2)}, u32[]{:S(2)}) collective-permute-start(bf16[2048,128]{1,0:T(8,128)(2,1)S(1)} %collective-permute-done.1), channel_id=1, source_target_pairs={{0,8},{8,0},{1,9},{9,1},{2,10},{10,2},{3,11},{11,3},{4,12},{12,4},... | collective-permute-start | bytes 1572872 | tf_op jit(solution)/shard_map/ppermute | solution.py:27
  78.0 1.9 collective-permute-start.4
  79.9 10.1 %collective-permute-done.9 = bf16[2048,128]{1,0:T(8,128)(2,1)S(1)} collective-permute-done((bf16[2048,128]{1,0:T(8,128)(2,1)S(1)}, bf16[2048,128]{1,0:T(8,128)(2,1)S(1)}, u32[]{:S(2)}, u32[]{:S(2)}) %collective-permute-start.9) | collective-permute-done | bytes 524320 | tf_op jit(solution)/shard_map/ppermute | solution.py:24
  90.1 2.8 %collective-permute-start.6 = (bf16[2048,128]{1,0:T(8,128)(2,1)S(1)}, bf16[2048,128]{1,0:T(8,128)(2,1)S(1)}, u32[]{:S(2)}, u32[]{:S(2)}) collective-permute-start(bf16[2048,128]{1,0:T(8,128)(2,1)S(1)} %collective-permute-done.5), channel_id=1, source_target_pairs={{0,8},{8,0},{1,9},{9,1},{2,10},{10,2},{3,11},{11,3},{4,12},{12,4},... | collective-permute-start | bytes 1572872 | tf_op jit(solution)/shard_map/ppermute | solution.py:27
  93.8 1.9 collective-permute-start.10
  97.1 2.4 %collective-permute-start.12 = (bf16[2048,128]{1,0:T(8,128)(2,1)S(1)}, bf16[2048,128]{1,0:T(8,128)(2,1)S(1)}, u32[]{:S(2)}, u32[]{:S(2)}) collective-permute-start(bf16[2048,128]{1,0:T(8,128)(2,1)S(1)} %collective-permute-done.11), channel_id=1, source_target_pairs={{0,8},{8,0},{1,9},{9,1},{2,10},{10,2},{3,11},{11,3},{4,12},{12,4},... | collective-permute-start | bytes 1572872 | tf_op jit(solution)/shard_map/ppermute | solution.py:27
  99.5 1.9 collective-permute-start.14
  108.6 1.9 constant_dynamic-update-slice_fusion.9
  110.5 5.3 %fusion.1 = f32[512,1024]{1,0:T(8,128)S(1)} fusion(bf16[2048,1024]{1,0:T(8,128)(2,1)} %constant_dynamic-update-slice_fusion, bf16[512,2048]{0,1:T(8,128)(2,1)} %all-gather.2.cloned.1.call-done, f32[2048]{0:T(1024)S(1)} %add_divide_fusion), kind=kOutput, calls=%fused_computation.10 | convolution fusion | flops 2150629376 | bytes 8396800 | tf_op jit(solution)/shard_map/dot_general | solution.py:45
  116.9 4.3 %all-to-all-start = ((bf16[4,128,1024]{2,1,0:T(8,128)(2,1)}), bf16[4,128,1024]{2,1,0:T(8,128)(2,1)S(1)}, u32[]{:S(2)}, u32[]{:S(2)}) async-start(bf16[4,128,1024]{2,1,0:T(8,128)(2,1)} %convert_element_type.35), calls=%async_computation | async-start | bytes 2097152 | tf_op jit(solution)/shard_map/all_to_all | solution.py:48
  121.2 1.9 constant_dynamic-update-slice_fusion.8
  123.1 5.3 %fusion = f32[512,1024]{1,0:T(8,128)S(1)} fusion(bf16[2048,1024]{1,0:T(8,128)(2,1)} %constant_dynamic-update-slice_fusion.8, bf16[512,2048]{0,1:T(8,128)(2,1)} %all-gather.2.cloned.1.call-done, f32[2048]{0:T(1024)S(1)} %add_divide_fusion), kind=kOutput, calls=%fused_computation.9 | convolution fusion | flops 2150629376 | bytes 8396800 | tf_op jit(solution)/shard_map/dot_general | solution.py:45
  130.8 3.6 %all-to-all-done = bf16[4,128,1024]{2,1,0:T(8,128)(2,1)S(1)} async-done(((bf16[4,128,1024]{2,1,0:T(8,128)(2,1)}), bf16[4,128,1024]{2,1,0:T(8,128)(2,1)S(1)}, u32[]{:S(2)}, u32[]{:S(2)}) %all-to-all-start) | async-done | bytes 1048608 | tf_op jit(solution)/shard_map/all_to_all | solution.py:48
  134.4 5.4 %all-to-all-start.1 = ((bf16[4,128,1024]{2,1,0:T(8,128)(2,1)}), bf16[4,128,1024]{2,1,0:T(8,128)(2,1)}, u32[]{:S(2)}, u32[]{:S(2)}) async-start(bf16[4,128,1024]{2,1,0:T(8,128)(2,1)} %convert_element_type.37), calls=%async_computation.1 | async-start | bytes 2097152 | tf_op jit(solution)/shard_map/all_to_all | solution.py:48
  139.8 1.6 select_reduce_fusion.3
  142.7 9.5 %all-to-all-done.1 = bf16[4,128,1024]{2,1,0:T(8,128)(2,1)} async-done(((bf16[4,128,1024]{2,1,0:T(8,128)(2,1)}), bf16[4,128,1024]{2,1,0:T(8,128)(2,1)}, u32[]{:S(2)}, u32[]{:S(2)}) %all-to-all-start.1) | async-done | bytes 1048608 | tf_op jit(solution)/shard_map/all_to_all | solution.py:48
  152.2 5.7 %collective-permute-done.15 = bf16[128,1024]{1,0:T(8,128)(2,1)S(1)} collective-permute-done((bf16[128,1024]{1,0:T(8,128)(2,1)S(1)}, bf16[128,1024]{1,0:T(8,128)(2,1)S(1)}, u32[]{:S(2)}, u32[]{:S(2)}) %collective-permute-start.15) | collective-permute-done | bytes 262176 | tf_op jit(solution)/shard_map/ppermute | solution.py:57
  161.3 19.5 %collective-permute-start.16 = (bf16[128,1024]{1,0:T(8,128)(2,1)S(1)}, bf16[128,1024]{1,0:T(8,128)(2,1)}, u32[]{:S(2)}, u32[]{:S(2)}) collective-permute-start(bf16[128,1024]{1,0:T(8,128)(2,1)S(1)} %fusion.3), channel_id=1, source_target_pairs={{0,4},{260,256},{1,5},{261,257},{2,6},{262,258},{3,7},{263,259},{8... | collective-permute-start | bytes 786440 | tf_op jit(solution)/shard_map/ppermute | solution.py:60
  181.5 18.2 %collective-permute-done.16 = bf16[128,1024]{1,0:T(8,128)(2,1)} collective-permute-done((bf16[128,1024]{1,0:T(8,128)(2,1)S(1)}, bf16[128,1024]{1,0:T(8,128)(2,1)}, u32[]{:S(2)}, u32[]{:S(2)}) %collective-permute-start.16) | collective-permute-done | bytes 262176 | tf_op jit(solution)/shard_map/ppermute | solution.py:60
  (50 shorter events, 26.3 us)
Async XLA Ops:
  6.5 104.0 %all-gather.2.cloned.1.call-start = ((), (), s32[]{:S(2)}) async-start(), calls=%async_computation.2 | async-start | bytes 2621440 | tf_op jit(solution)/shard_map/all_gather | solution.py:35
  6.5 53.0 %collective-permute-start.7 = (bf16[2048,128]{1,0:T(8,128)(2,1)}, bf16[2048,128]{1,0:T(8,128)(2,1)S(1)}, u32[]{:S(2)}, u32[]{:S(2)}) collective-permute-start(bf16[2048,128]{1,0:T(8,128)(2,1)} %param.5), channel_id=1, source_target_pairs={{0,4},{4,0},{1,5},{5,1},{2,6},{6,2},{3,7},{7,3},{8,12},{12,8},{9,1... | collective-permute-start | bytes 1572872 | tf_op jit(solution)/shard_map/ppermute | solution.py:36
  15.4 47.7 %collective-permute-start = (bf16[2048,128]{1,0:T(8,128)(2,1)}, bf16[2048,128]{1,0:T(8,128)(2,1)S(1)}, u32[]{:S(2)}, u32[]{:S(2)}) collective-permute-start(bf16[2048,128]{1,0:T(8,128)(2,1)} %param.5), channel_id=1, source_target_pairs={{0,8},{8,0},{1,9},{9,1},{2,10},{10,2},{3,11},{11,3},{4,12},{12,4},... | collective-permute-start | bytes 1572872 | tf_op jit(solution)/shard_map/ppermute | solution.py:27
  18.2 50.3 %collective-permute-start.1 = (bf16[2048,128]{1,0:T(8,128)(2,1)}, bf16[2048,128]{1,0:T(8,128)(2,1)S(1)}, u32[]{:S(2)}, u32[]{:S(2)}) collective-permute-start(bf16[2048,128]{1,0:T(8,128)(2,1)} %param.5), channel_id=1, source_target_pairs={{0,48},{16,0},{32,16},{48,32},{1,49},{17,1},{33,17},{49,33},{2,50}... | collective-permute-start | bytes 1572872 | tf_op jit(solution)/shard_map/ppermute | solution.py:24
  22.9 47.9 %collective-permute-start.3 = (bf16[2048,128]{1,0:T(8,128)(2,1)}, bf16[2048,128]{1,0:T(8,128)(2,1)S(1)}, u32[]{:S(2)}, u32[]{:S(2)}) collective-permute-start(bf16[2048,128]{1,0:T(8,128)(2,1)} %param.5), channel_id=1, source_target_pairs={{0,32},{16,48},{32,0},{48,16},{1,33},{17,49},{33,1},{49,17},{2,34}... | collective-permute-start | bytes 1572872 | tf_op jit(solution)/shard_map/ppermute | solution.py:24
  25.1 52.9 %collective-permute-start.5 = (bf16[2048,128]{1,0:T(8,128)(2,1)}, bf16[2048,128]{1,0:T(8,128)(2,1)S(1)}, u32[]{:S(2)}, u32[]{:S(2)}) collective-permute-start(bf16[2048,128]{1,0:T(8,128)(2,1)} %param.5), channel_id=1, source_target_pairs={{0,16},{16,32},{32,48},{48,0},{1,17},{17,33},{33,49},{49,1},{2,18}... | collective-permute-start | bytes 1572872 | tf_op jit(solution)/shard_map/ppermute | solution.py:24
  59.5 13.9 %collective-permute-start.8 = (bf16[2048,128]{1,0:T(8,128)(2,1)S(1)}, bf16[2048,128]{1,0:T(8,128)(2,1)S(1)}, u32[]{:S(2)}, u32[]{:S(2)}) collective-permute-start(bf16[2048,128]{1,0:T(8,128)(2,1)S(1)} %collective-permute-done.7), channel_id=1, source_target_pairs={{0,8},{8,0},{1,9},{9,1},{2,10},{10,2},{3,11},{11,3},{4,12},{12,4},... | collective-permute-start | bytes 1572872 | tf_op jit(solution)/shard_map/ppermute | solution.py:27
  63.0 27.1 %collective-permute-start.9 = (bf16[2048,128]{1,0:T(8,128)(2,1)S(1)}, bf16[2048,128]{1,0:T(8,128)(2,1)S(1)}, u32[]{:S(2)}, u32[]{:S(2)}) collective-permute-start(bf16[2048,128]{1,0:T(8,128)(2,1)S(1)} %collective-permute-done.7), channel_id=1, source_target_pairs={{0,48},{16,0},{32,16},{48,32},{1,49},{17,1},{33,17},{49,33},{2,50}... | collective-permute-start | bytes 1572872 | tf_op jit(solution)/shard_map/ppermute | solution.py:24
  68.5 25.3 %collective-permute-start.11 = (bf16[2048,128]{1,0:T(8,128)(2,1)S(1)}, bf16[2048,128]{1,0:T(8,128)(2,1)S(1)}, u32[]{:S(2)}, u32[]{:S(2)}) collective-permute-start(bf16[2048,128]{1,0:T(8,128)(2,1)S(1)} %collective-permute-done.7), channel_id=1, source_target_pairs={{0,32},{16,48},{32,0},{48,16},{1,33},{17,49},{33,1},{49,17},{2,34}... | collective-permute-start | bytes 1572872 | tf_op jit(solution)/shard_map/ppermute | solution.py:24
  70.8 26.3 %collective-permute-start.13 = (bf16[2048,128]{1,0:T(8,128)(2,1)S(1)}, bf16[2048,128]{1,0:T(8,128)(2,1)}, u32[]{:S(2)}, u32[]{:S(2)}) collective-permute-start(bf16[2048,128]{1,0:T(8,128)(2,1)S(1)} %collective-permute-done.7), channel_id=1, source_target_pairs={{0,16},{16,32},{32,48},{48,0},{1,17},{17,33},{33,49},{49,1},{2,18}... | collective-permute-start | bytes 1572872 | tf_op jit(solution)/shard_map/ppermute | solution.py:24
  73.4 26.1 %collective-permute-start.2 = (bf16[2048,128]{1,0:T(8,128)(2,1)S(1)}, bf16[2048,128]{1,0:T(8,128)(2,1)S(1)}, u32[]{:S(2)}, u32[]{:S(2)}) collective-permute-start(bf16[2048,128]{1,0:T(8,128)(2,1)S(1)} %collective-permute-done.1), channel_id=1, source_target_pairs={{0,8},{8,0},{1,9},{9,1},{2,10},{10,2},{3,11},{11,3},{4,12},{12,4},... | collective-permute-start | bytes 1572872 | tf_op jit(solution)/shard_map/ppermute | solution.py:27
  78.0 25.2 %collective-permute-start.4 = (bf16[2048,128]{1,0:T(8,128)(2,1)S(1)}, bf16[2048,128]{1,0:T(8,128)(2,1)S(1)}, u32[]{:S(2)}, u32[]{:S(2)}) collective-permute-start(bf16[2048,128]{1,0:T(8,128)(2,1)S(1)} %collective-permute-done.3), channel_id=1, source_target_pairs={{0,8},{8,0},{1,9},{9,1},{2,10},{10,2},{3,11},{11,3},{4,12},{12,4},... | collective-permute-start | bytes 1572872 | tf_op jit(solution)/shard_map/ppermute | solution.py:27
  90.1 15.0 %collective-permute-start.6 = (bf16[2048,128]{1,0:T(8,128)(2,1)S(1)}, bf16[2048,128]{1,0:T(8,128)(2,1)S(1)}, u32[]{:S(2)}, u32[]{:S(2)}) collective-permute-start(bf16[2048,128]{1,0:T(8,128)(2,1)S(1)} %collective-permute-done.5), channel_id=1, source_target_pairs={{0,8},{8,0},{1,9},{9,1},{2,10},{10,2},{3,11},{11,3},{4,12},{12,4},... | collective-permute-start | bytes 1572872 | tf_op jit(solution)/shard_map/ppermute | solution.py:27
  93.8 12.1 %collective-permute-start.10 = (bf16[2048,128]{1,0:T(8,128)(2,1)S(1)}, bf16[2048,128]{1,0:T(8,128)(2,1)S(1)}, u32[]{:S(2)}, u32[]{:S(2)}) collective-permute-start(bf16[2048,128]{1,0:T(8,128)(2,1)S(1)} %collective-permute-done.9), channel_id=1, source_target_pairs={{0,8},{8,0},{1,9},{9,1},{2,10},{10,2},{3,11},{11,3},{4,12},{12,4},... | collective-permute-start | bytes 1572872 | tf_op jit(solution)/shard_map/ppermute | solution.py:27
  97.1 10.6 %collective-permute-start.12 = (bf16[2048,128]{1,0:T(8,128)(2,1)S(1)}, bf16[2048,128]{1,0:T(8,128)(2,1)S(1)}, u32[]{:S(2)}, u32[]{:S(2)}) collective-permute-start(bf16[2048,128]{1,0:T(8,128)(2,1)S(1)} %collective-permute-done.11), channel_id=1, source_target_pairs={{0,8},{8,0},{1,9},{9,1},{2,10},{10,2},{3,11},{11,3},{4,12},{12,4},... | collective-permute-start | bytes 1572872 | tf_op jit(solution)/shard_map/ppermute | solution.py:27
  99.5 21.7 %collective-permute-start.14 = (bf16[2048,128]{1,0:T(8,128)(2,1)}, bf16[2048,128]{1,0:T(8,128)(2,1)}, u32[]{:S(2)}, u32[]{:S(2)}) collective-permute-start(bf16[2048,128]{1,0:T(8,128)(2,1)} %collective-permute-done.13), channel_id=1, source_target_pairs={{0,8},{8,0},{1,9},{9,1},{2,10},{10,2},{3,11},{11,3},{4,12},{12,4},... | collective-permute-start | bytes 1572872 | tf_op jit(solution)/shard_map/ppermute | solution.py:27
  116.9 17.5 %all-to-all-start = ((bf16[4,128,1024]{2,1,0:T(8,128)(2,1)}), bf16[4,128,1024]{2,1,0:T(8,128)(2,1)S(1)}, u32[]{:S(2)}, u32[]{:S(2)}) async-start(bf16[4,128,1024]{2,1,0:T(8,128)(2,1)} %convert_element_type.35), calls=%async_computation | async-start | bytes 2097152 | tf_op jit(solution)/shard_map/all_to_all | solution.py:48
  128.4 1.3 copy-start.1
  134.4 5.4 %copy-start = (bf16[4,128,1024]{2,1,0:T(8,128)(2,1)}, bf16[4,128,1024]{2,1,0:T(8,128)(2,1)S(1)}, u32[]{:S(2)}) copy-start(bf16[4,128,1024]{2,1,0:T(8,128)(2,1)S(1)} %all-to-all-done) | copy-start | bytes 3145732
  134.4 17.8 %all-to-all-start.1 = ((bf16[4,128,1024]{2,1,0:T(8,128)(2,1)}), bf16[4,128,1024]{2,1,0:T(8,128)(2,1)}, u32[]{:S(2)}, u32[]{:S(2)}) async-start(bf16[4,128,1024]{2,1,0:T(8,128)(2,1)} %convert_element_type.37), calls=%async_computation.1 | async-start | bytes 2097152 | tf_op jit(solution)/shard_map/all_to_all | solution.py:48
  141.4 16.5 %collective-permute-start.15 = (bf16[128,1024]{1,0:T(8,128)(2,1)S(1)}, bf16[128,1024]{1,0:T(8,128)(2,1)S(1)}, u32[]{:S(2)}, u32[]{:S(2)}) collective-permute-start(bf16[128,1024]{1,0:T(8,128)(2,1)S(1)} %fusion.4), channel_id=1, source_target_pairs={{256,0},{4,260},{257,1},{5,261},{258,2},{6,262},{259,3},{7,263},{2... | collective-permute-start | bytes 786440 | tf_op jit(solution)/shard_map/ppermute | solution.py:57
  160.6 20.2 %collective-permute-start.17 = (bf16[128,1024]{1,0:T(8,128)(2,1)S(1)}, bf16[128,1024]{1,0:T(8,128)(2,1)S(1)}, u32[]{:S(2)}, u32[]{:S(2)}) collective-permute-start(bf16[128,1024]{1,0:T(8,128)(2,1)S(1)} %fusion.3), channel_id=1, source_target_pairs={{256,4},{4,256},{257,5},{5,257},{258,6},{6,258},{259,7},{7,259},{2... | collective-permute-start | bytes 786440 | tf_op jit(solution)/shard_map/ppermute | solution.py:61
  161.3 38.5 %collective-permute-start.16 = (bf16[128,1024]{1,0:T(8,128)(2,1)S(1)}, bf16[128,1024]{1,0:T(8,128)(2,1)}, u32[]{:S(2)}, u32[]{:S(2)}) collective-permute-start(bf16[128,1024]{1,0:T(8,128)(2,1)S(1)} %fusion.3), channel_id=1, source_target_pairs={{0,4},{260,256},{1,5},{261,257},{2,6},{262,258},{3,7},{263,259},{8... | collective-permute-start | bytes 786440 | tf_op jit(solution)/shard_map/ppermute | solution.py:60
  180.8 0.7 copy-start.2
Sparse Core Ops, SparseCore 0:
  27.9 62.6 all-gather.1

commit v3 on v0

v3 whole, which is shorter than its diff:
```python
import jax
import jax.numpy as jnp
from jax import lax
from jax.sharding import Mesh, PartitionSpec as P

NAMES = ("zh", "x", "y", "core", "zl")
SHAPE = (2, 4, 4, 2, 8)


def shift(n, s):
    return [(i, (i + s) % n) for i in range(n)]


def circle(n):
    return list(range(0, n, 2)) + list(range(n - 1, 0, -2))


def lookup(indices, table):
    hits = indices[:, None] == jnp.arange(table.shape[0], dtype=jnp.int32)[None, :]
    return jnp.sum(jnp.where(hits, table[None, :], jnp.float32(0.0)), axis=1)


def place(col, n):
    return jnp.where(col % 2 == 0, col // 2, (2 * n - 1 - col) // 2)


def body(pair_elements, valence_of, conduction_of, valence_depth, conduction_height):
    n_pair, n_g = pair_elements.shape
    n_x, n_z = lax.axis_size("x"), lax.axis_size("zl")
    columns = lax.all_gather(pair_elements, ("y", "core"), axis=1, tiled=True)

    order = circle(n_z)
    step = [(order[i], order[(i + 1) % n_z]) for i in range(n_z)]
    chunks = [pair_elements[: n_pair // 2], pair_elements[n_pair // 2 :]]
    arrived = [[chunk] for chunk in chunks]
    for _ in range(n_z - 1):
        for i in range(2):
            chunks[i] = lax.ppermute(chunks[i], "zl", step)
            arrived[i].append(chunks[i])
    rows = jnp.concatenate([jnp.concatenate(one, axis=1) for one in arrived], axis=0)

    pair_gap = lookup(valence_of, valence_depth) + lookup(conduction_of, conduction_height)
    factor = -4.0 / pair_gap
    weighted = (rows.astype(jnp.float32) * factor[:, None]).astype(jnp.bfloat16)

    my_half, my_x = lax.axis_index("zh"), lax.axis_index("x")
    mine_at = place(lax.axis_index("zl"), n_z)

    def summed_over_x(part, *earlier):
        partial = lax.dot_general(
            weighted, part, (((0,), (0,)), ((), ())), preferred_element_type=jnp.float32
        ).reshape(n_z, n_g, -1)

        def blocks(x):
            picked = []
            for half in (my_half, 1 - my_half):
                turn = lax.rem(mine_at - place(half * n_x + x, n_z) + n_z, n_z)
                picked.append(lax.dynamic_slice_in_dim(partial, turn, 1, 0))
            return jnp.concatenate(picked, axis=0)

        sent = [blocks(lax.rem(my_x + s, n_x)).astype(jnp.bfloat16) for s in range(1, n_x)]
        mine, *sent = lax.optimization_barrier((blocks(my_x), *sent))
        got = [lax.ppermute(one, "x", shift(n_x, s)) for s, one in enumerate(sent, 1)]
        got, earlier = lax.optimization_barrier((got, earlier))
        total = mine
        for one in got:
            total = total + one.astype(jnp.float32)
        return total[0], total[1].astype(jnp.bfloat16), *earlier

    def swapped(given):
        return lax.ppermute(given, "zh", shift(2, 1))

    width = columns.shape[1] // 2
    kept_a, given = summed_over_x(columns[:, :width])
    got_a = swapped(given)
    kept_b, given, got_a = summed_over_x(columns[:, width:], got_a)
    got_b = swapped(given)
    total_a = kept_a + got_a.astype(jnp.float32)
    total_b = kept_b + got_b.astype(jnp.float32)
    total = jnp.concatenate([total_a, total_b], axis=1)
    return total.reshape(1, n_g, -1, n_g)


def solution(mesh):
    fine = Mesh(mesh.devices.reshape(SHAPE), NAMES)
    pair, row = ("zh", "x"), ("y", "core")
    placed = (P(pair, row + ("zl",)), P(pair), P(pair), P(), P())
    return jax.shard_map(
        body, mesh=fine, in_specs=placed, out_specs=P(row, pair, None, "zl"), check_vma=False
    )
```

time: 400 us -> 180 us (0.45)
  the two profiles are of different devices: /device:TPU:8 before, /device:TPU:132 now
where the time goes in v3:
time: 180 us; the launch traced here: 179 us
  waiting for transfers between devices  71.4 us (40%)
  starting transfers between devices  70.1 us (39%)
  between operations  14.3 us (8%)
  local copies, waits for them, and re-layouts  9.1 us (5%)
  matrix products  7.3 us (4%)
  other arithmetic  7.02 us (4%)
    ppermute x14, waiting for transfers between devices, body(): chunks[i] = lax.ppermute(chunks[i], 'zl', step)  42.8 us
    ppermute x14, starting transfers between devices, body(): chunks[i] = lax.ppermute(chunks[i], 'zl', step)  37.7 us
    ppermute x2, waiting for transfers between devices, swapped(): return lax.ppermute(given, 'zh', shift(2, 1))  27.9 us
    ppermute x6, starting transfers between devices, summed_over_x(): lax.ppermute(one, 'x', shift(n_x, s))  20.2 us
    ppermute x2, starting transfers between devices, swapped(): return lax.ppermute(given, 'zh', shift(2, 1))  12.1 us
    dot_general x2, matrix products, summed_over_x(): lax.dot_general(weighted, part, (((0,), (0,)), ((), ())), preferred_eleme...  7.3 us
    reduce_sum x2, other arithmetic, lookup(): return jnp.sum(jnp.where(hits, table[None, :], jnp.float32(0.0)), axis=1)  6.41 us
    unnamed x25, local copies, waits for them, and re-layouts  5.99 us
  transfers between devices with their start and end apart: 23, of which 14 were waited for; matrix products, arithmetic and copies ran while one was open for 8% of the time, Pallas kernels for 0%

profile of v3, /device:TPU:132, one launch (start us, length us, event | category | flops | bytes accessed | tf_op | source)
XLA Modules:
  0.0 179.2 jit_solution(8379202201956738968)
XLA Ops:
  9.2 5.2 %collective-permute-start.7 = (bf16[1024,128]{1,0:T(8,128)(2,1)S(1)}, bf16[1024,128]{1,0:T(8,128)(2,1)S(1)}, u32[]{:S(2)}, u32[]{:S(2)}) collective-permute-start(bf16[1024,128]{1,0:T(8,128)(2,1)S(1)} %get-tuple-element.54), channel_id=1, source_target_pairs={{0,2},{2,4},{4,6},{6,7},{7,5},{5,3},{3,1},{1,0},{8,10},{10,12},{12... | collective-permute-start | bytes 786440 | tf_op jit(solution)/shard_map/ppermute | solution.py:38
  14.4 3.8 %collective-permute-start = (bf16[1024,128]{1,0:T(8,128)(2,1)S(1)}, bf16[1024,128]{1,0:T(8,128)(2,1)S(1)}, u32[]{:S(2)}, u32[]{:S(2)}) collective-permute-start(bf16[1024,128]{1,0:T(8,128)(2,1)S(1)} %get-tuple-element.51), channel_id=1, source_target_pairs={{0,2},{2,4},{4,6},{6,7},{7,5},{5,3},{3,1},{1,0},{8,10},{10,12},{12... | collective-permute-start | bytes 786440 | tf_op jit(solution)/shard_map/ppermute | solution.py:38
  18.2 3.7 %collective-permute-done.7 = bf16[1024,128]{1,0:T(8,128)(2,1)S(1)} collective-permute-done((bf16[1024,128]{1,0:T(8,128)(2,1)S(1)}, bf16[1024,128]{1,0:T(8,128)(2,1)S(1)}, u32[]{:S(2)}, u32[]{:S(2)}) %collective-permute-start.7) | collective-permute-done | bytes 262176 | tf_op jit(solution)/shard_map/ppermute | solution.py:38
  21.9 4.5 %collective-permute-start.8 = (bf16[1024,128]{1,0:T(8,128)(2,1)S(1)}, bf16[1024,128]{1,0:T(8,128)(2,1)S(1)}, u32[]{:S(2)}, u32[]{:S(2)}) collective-permute-start(bf16[1024,128]{1,0:T(8,128)(2,1)S(1)} %collective-permute-done.7), channel_id=1, source_target_pairs={{0,2},{2,4},{4,6},{6,7},{7,5},{5,3},{3,1},{1,0},{8,10},{10,12},{12... | collective-permute-start | bytes 786440 | tf_op jit(solution)/shard_map/ppermute | solution.py:38
  26.3 4.4 %select_reduce_fusion = f32[2048]{0:T(1024)S(1)} fusion(f32[4096]{0:T(1024)S(1)} %copy-done.2, s32[2048]{0:T(1024)S(1)} %copy-done.3), kind=kLoop, calls=%fused_computation | loop fusion | flops 25163776 | bytes 32768 | tf_op jit(solution)/shard_map/reduce_sum | solution.py:20
  30.8 2.9 %collective-permute-start.1 = (bf16[1024,128]{1,0:T(8,128)(2,1)S(1)}, bf16[1024,128]{1,0:T(8,128)(2,1)S(1)}, u32[]{:S(2)}, u32[]{:S(2)}) collective-permute-start(bf16[1024,128]{1,0:T(8,128)(2,1)S(1)} %collective-permute-done), channel_id=1, source_target_pairs={{0,2},{2,4},{4,6},{6,7},{7,5},{5,3},{3,1},{1,0},{8,10},{10,12},{12... | collective-permute-start | bytes 786440 | tf_op jit(solution)/shard_map/ppermute | solution.py:38
  33.7 2.8 %collective-permute-start.9 = (bf16[1024,128]{1,0:T(8,128)(2,1)S(1)}, bf16[1024,128]{1,0:T(8,128)(2,1)S(1)}, u32[]{:S(2)}, u32[]{:S(2)}) collective-permute-start(bf16[1024,128]{1,0:T(8,128)(2,1)S(1)} %collective-permute-done.8), channel_id=1, source_target_pairs={{0,2},{2,4},{4,6},{6,7},{7,5},{5,3},{3,1},{1,0},{8,10},{10,12},{12... | collective-permute-start | bytes 786440 | tf_op jit(solution)/shard_map/ppermute | solution.py:38
  38.9 4.5 %collective-permute-done.1 = bf16[1024,128]{1,0:T(8,128)(2,1)S(1)} collective-permute-done((bf16[1024,128]{1,0:T(8,128)(2,1)S(1)}, bf16[1024,128]{1,0:T(8,128)(2,1)S(1)}, u32[]{:S(2)}, u32[]{:S(2)}) %collective-permute-start.1) | collective-permute-done | bytes 262176 | tf_op jit(solution)/shard_map/ppermute | solution.py:38
  43.4 2.2 %collective-permute-start.2 = (bf16[1024,128]{1,0:T(8,128)(2,1)S(1)}, bf16[1024,128]{1,0:T(8,128)(2,1)S(1)}, u32[]{:S(2)}, u32[]{:S(2)}) collective-permute-start(bf16[1024,128]{1,0:T(8,128)(2,1)S(1)} %collective-permute-done.1), channel_id=1, source_target_pairs={{0,2},{2,4},{4,6},{6,7},{7,5},{5,3},{3,1},{1,0},{8,10},{10,12},{12... | collective-permute-start | bytes 786440 | tf_op jit(solution)/shard_map/ppermute | solution.py:38
  45.6 2.5 %collective-permute-done.9 = bf16[1024,128]{1,0:T(8,128)(2,1)S(1)} collective-permute-done((bf16[1024,128]{1,0:T(8,128)(2,1)S(1)}, bf16[1024,128]{1,0:T(8,128)(2,1)S(1)}, u32[]{:S(2)}, u32[]{:S(2)}) %collective-permute-start.9) | collective-permute-done | bytes 262176 | tf_op jit(solution)/shard_map/ppermute | solution.py:38
  48.1 2.8 %collective-permute-start.10 = (bf16[1024,128]{1,0:T(8,128)(2,1)S(1)}, bf16[1024,128]{1,0:T(8,128)(2,1)S(1)}, u32[]{:S(2)}, u32[]{:S(2)}) collective-permute-start(bf16[1024,128]{1,0:T(8,128)(2,1)S(1)} %collective-permute-done.9), channel_id=1, source_target_pairs={{0,2},{2,4},{4,6},{6,7},{7,5},{5,3},{3,1},{1,0},{8,10},{10,12},{12... | collective-permute-start | bytes 786440 | tf_op jit(solution)/shard_map/ppermute | solution.py:38
  51.7 3.3 %collective-permute-done.2 = bf16[1024,128]{1,0:T(8,128)(2,1)S(1)} collective-permute-done((bf16[1024,128]{1,0:T(8,128)(2,1)S(1)}, bf16[1024,128]{1,0:T(8,128)(2,1)S(1)}, u32[]{:S(2)}, u32[]{:S(2)}) %collective-permute-start.2) | collective-permute-done | bytes 262176 | tf_op jit(solution)/shard_map/ppermute | solution.py:38
  57.7 3.5 %collective-permute-done.10 = bf16[1024,128]{1,0:T(8,128)(2,1)S(1)} collective-permute-done((bf16[1024,128]{1,0:T(8,128)(2,1)S(1)}, bf16[1024,128]{1,0:T(8,128)(2,1)S(1)}, u32[]{:S(2)}, u32[]{:S(2)}) %collective-permute-start.10) | collective-permute-done | bytes 262176 | tf_op jit(solution)/shard_map/ppermute | solution.py:38
  63.3 3.3 %collective-permute-done.3 = bf16[1024,128]{1,0:T(8,128)(2,1)S(1)} collective-permute-done((bf16[1024,128]{1,0:T(8,128)(2,1)S(1)}, bf16[1024,128]{1,0:T(8,128)(2,1)S(1)}, u32[]{:S(2)}, u32[]{:S(2)}) %collective-permute-start.3) | collective-permute-done | bytes 262176 | tf_op jit(solution)/shard_map/ppermute | solution.py:38
  69.4 4.9 %collective-permute-done.11 = bf16[1024,128]{1,0:T(8,128)(2,1)S(1)} collective-permute-done((bf16[1024,128]{1,0:T(8,128)(2,1)S(1)}, bf16[1024,128]{1,0:T(8,128)(2,1)S(1)}, u32[]{:S(2)}, u32[]{:S(2)}) %collective-permute-start.11) | collective-permute-done | bytes 262176 | tf_op jit(solution)/shard_map/ppermute | solution.py:38
  76.9 2.0 %collective-permute-done.4 = bf16[1024,128]{1,0:T(8,128)(2,1)S(1)} collective-permute-done((bf16[1024,128]{1,0:T(8,128)(2,1)S(1)}, bf16[1024,128]{1,0:T(8,128)(2,1)S(1)}, u32[]{:S(2)}, u32[]{:S(2)}) %collective-permute-start.4) | collective-permute-done | bytes 262176 | tf_op jit(solution)/shard_map/ppermute | solution.py:38
  81.8 3.4 %collective-permute-done.12 = bf16[1024,128]{1,0:T(8,128)(2,1)S(1)} collective-permute-done((bf16[1024,128]{1,0:T(8,128)(2,1)S(1)}, bf16[1024,128]{1,0:T(8,128)(2,1)S(1)}, u32[]{:S(2)}, u32[]{:S(2)}) %collective-permute-start.12) | collective-permute-done | bytes 262176 | tf_op jit(solution)/shard_map/ppermute | solution.py:38
  87.1 5.1 %collective-permute-done.5 = bf16[1024,128]{1,0:T(8,128)(2,1)S(1)} collective-permute-done((bf16[1024,128]{1,0:T(8,128)(2,1)S(1)}, bf16[1024,128]{1,0:T(8,128)(2,1)S(1)}, u32[]{:S(2)}, u32[]{:S(2)}) %collective-permute-start.5) | collective-permute-done | bytes 262176 | tf_op jit(solution)/shard_map/ppermute | solution.py:38
  92.2 2.1 %collective-permute-start.6 = (bf16[1024,128]{1,0:T(8,128)(2,1)S(1)}, bf16[1024,128]{1,0:T(8,128)(2,1)S(1)}, u32[]{:S(2)}, u32[]{:S(2)}) collective-permute-start(bf16[1024,128]{1,0:T(8,128)(2,1)S(1)} %collective-permute-done.5), channel_id=1, source_target_pairs={{0,2},{2,4},{4,6},{6,7},{7,5},{5,3},{3,1},{1,0},{8,10},{10,12},{12... | collective-permute-start | bytes 786440 | tf_op jit(solution)/shard_map/ppermute | solution.py:38
  96.6 5.9 %collective-permute-done.6 = bf16[1024,128]{1,0:T(8,128)(2,1)S(1)} collective-permute-done((bf16[1024,128]{1,0:T(8,128)(2,1)S(1)}, bf16[1024,128]{1,0:T(8,128)(2,1)S(1)}, u32[]{:S(2)}, u32[]{:S(2)}) %collective-permute-start.6) | collective-permute-done | bytes 262176 | tf_op jit(solution)/shard_map/ppermute | solution.py:38
  102.7 4.8 %fusion = f32[1024,512]{1,0:T(8,128)S(1)} fusion(bf16[2048,1024]{1,0:T(8,128)(2,1)} %all-gather.2.cloned.1.call-done, bf16[1024,1024]{1,0:T(8,128)(2,1)} %constant_dynamic-update-slice_fusion.8, bf16[1024,1024]{1,0:T(8,128)(2,1)S(1)} %constant_dynamic-update-slice_fusion, f32[2048]{0:T(1024)S(1)} %add_divide_fusion), kind=kOutput, calls=%fused_computation.5 | convolution fusion | flops 2160066560 | bytes 8396800 | tf_op jit(solution)/shard_map/dot_general | solution.py:50
  107.6 2.5 %fusion.2 = f32[1024,512]{1,0:T(8,128)S(1)} fusion(bf16[2048,1024]{1,0:T(8,128)(2,1)S(1)} %copy-done.1, bf16[1024,1024]{1,0:T(8,128)(2,1)S(1)} %copy-done, bf16[1024,1024]{1,0:T(8,128)(2,1)S(1)} %constant_dynamic-update-slice_fusion, f32[2048]{0:T(1024)S(1)} %add_divide_fusion), kind=kOutput, calls=%fused_computation.7 | convolution fusion | flops 2160066560 | bytes 8396800 | tf_op jit(solution)/shard_map/dot_general | solution.py:50
  110.5 3.1 %collective-permute-start.14 = (bf16[2,128,512]{2,1,0:T(8,128)(2,1)S(1)}, bf16[2,128,512]{2,1,0:T(8,128)(2,1)S(1)}, u32[]{:S(2)}, u32[]{:S(2)}) collective-permute-start(bf16[2,128,512]{2,1,0:T(8,128)(2,1)S(1)} %pad_maximum_fusion.2), channel_id=1, source_target_pairs={{0,64},{64,128},{128,192},{192,0},{1,65},{65,129},{129,193},{193,1... | collective-permute-start | bytes 786440 | tf_op jit(solution)/shard_map/ppermute | solution.py:63
  113.6 2.7 %collective-permute-start.15 = (bf16[2,128,512]{2,1,0:T(8,128)(2,1)S(1)}, bf16[2,128,512]{2,1,0:T(8,128)(2,1)S(1)}, u32[]{:S(2)}, u32[]{:S(2)}) collective-permute-start(bf16[2,128,512]{2,1,0:T(8,128)(2,1)S(1)} %pad_maximum_fusion.3), channel_id=1, source_target_pairs={{0,128},{64,192},{128,0},{192,64},{1,129},{65,193},{129,1},{193,65... | collective-permute-start | bytes 786440 | tf_op jit(solution)/shard_map/ppermute | solution.py:63
  116.4 3.0 %collective-permute-start.16 = (bf16[2,128,512]{2,1,0:T(8,128)(2,1)S(1)}, bf16[2,128,512]{2,1,0:T(8,128)(2,1)S(1)}, u32[]{:S(2)}, u32[]{:S(2)}) collective-permute-start(bf16[2,128,512]{2,1,0:T(8,128)(2,1)S(1)} %pad_maximum_fusion.4), channel_id=1, source_target_pairs={{0,192},{64,0},{128,64},{192,128},{1,193},{65,1},{129,65},{193,129... | collective-permute-start | bytes 786440 | tf_op jit(solution)/shard_map/ppermute | solution.py:63
  119.6 2.9 %collective-permute-start.17 = (bf16[2,128,512]{2,1,0:T(8,128)(2,1)S(1)}, bf16[2,128,512]{2,1,0:T(8,128)(2,1)S(1)}, u32[]{:S(2)}, u32[]{:S(2)}) collective-permute-start(bf16[2,128,512]{2,1,0:T(8,128)(2,1)S(1)} %pad_maximum_fusion.5), channel_id=1, source_target_pairs={{0,64},{64,128},{128,192},{192,0},{1,65},{65,129},{129,193},{193,1... | collective-permute-start | bytes 786440 | tf_op jit(solution)/shard_map/ppermute | solution.py:63
  122.5 4.6 %collective-permute-start.18 = (bf16[2,128,512]{2,1,0:T(8,128)(2,1)S(1)}, bf16[2,128,512]{2,1,0:T(8,128)(2,1)S(1)}, u32[]{:S(2)}, u32[]{:S(2)}) collective-permute-start(bf16[2,128,512]{2,1,0:T(8,128)(2,1)S(1)} %pad_maximum_fusion.6), channel_id=1, source_target_pairs={{0,128},{64,192},{128,0},{192,64},{1,129},{65,193},{129,1},{193,65... | collective-permute-start | bytes 786440 | tf_op jit(solution)/shard_map/ppermute | solution.py:63
  127.0 3.9 %collective-permute-start.19 = (bf16[2,128,512]{2,1,0:T(8,128)(2,1)S(1)}, bf16[2,128,512]{2,1,0:T(8,128)(2,1)S(1)}, u32[]{:S(2)}, u32[]{:S(2)}) collective-permute-start(bf16[2,128,512]{2,1,0:T(8,128)(2,1)S(1)} %pad_maximum_fusion.7), channel_id=1, source_target_pairs={{0,192},{64,0},{128,64},{192,128},{1,193},{65,1},{129,65},{193,129... | collective-permute-start | bytes 786440 | tf_op jit(solution)/shard_map/ppermute | solution.py:63
  131.2 9.2 %collective-permute-start.20 = (bf16[128,512]{1,0:T(8,128)(2,1)S(1)}, bf16[128,512]{1,0:T(8,128)(2,1)S(1)}, u32[]{:S(2)}, u32[]{:S(2)}) collective-permute-start(bf16[128,512]{1,0:T(8,128)(2,1)S(1)} %fusion.6), channel_id=1, source_target_pairs={{0,256},{256,0},{1,257},{257,1},{2,258},{258,2},{3,259},{259,3},{4... | collective-permute-start | bytes 393224 | tf_op jit(solution)/shard_map/ppermute | solution.py:71
  140.4 15.2 %collective-permute-done.20 = bf16[128,512]{1,0:T(8,128)(2,1)S(1)} collective-permute-done((bf16[128,512]{1,0:T(8,128)(2,1)S(1)}, bf16[128,512]{1,0:T(8,128)(2,1)S(1)}, u32[]{:S(2)}, u32[]{:S(2)}) %collective-permute-start.20) | collective-permute-done | bytes 131104 | tf_op jit(solution)/shard_map/ppermute | solution.py:71
  155.8 2.9 %collective-permute-start.21 = (bf16[128,512]{1,0:T(8,128)(2,1)S(1)}, bf16[128,512]{1,0:T(8,128)(2,1)S(1)}, u32[]{:S(2)}, u32[]{:S(2)}) collective-permute-start(bf16[128,512]{1,0:T(8,128)(2,1)S(1)} %fusion.7), channel_id=1, source_target_pairs={{0,256},{256,0},{1,257},{257,1},{2,258},{258,2},{3,259},{259,3},{4... | collective-permute-start | bytes 393224 | tf_op jit(solution)/shard_map/ppermute | solution.py:71
  158.7 12.7 %collective-permute-done.21 = bf16[128,512]{1,0:T(8,128)(2,1)S(1)} collective-permute-done((bf16[128,512]{1,0:T(8,128)(2,1)S(1)}, bf16[128,512]{1,0:T(8,128)(2,1)S(1)}, u32[]{:S(2)}, u32[]{:S(2)}) %collective-permute-start.21) | collective-permute-done | bytes 131104 | tf_op jit(solution)/shard_map/ppermute | solution.py:71
  (65 shorter events, 24.6 us)
Async XLA Ops:
  6.5 19.8 %copy-start.2 = (f32[4096]{0:T(1024)S(1)}, f32[4096]{0:T(1024)}, u32[]{:S(2)}) copy-start(f32[4096]{0:T(1024)} %param.9) | copy-start | bytes 49156
  6.5 19.8 %copy-start.3 = (s32[2048]{0:T(1024)S(1)}, s32[2048]{0:T(1024)}, u32[]{:S(2)}) copy-start(s32[2048]{0:T(1024)} %param.7) | copy-start | bytes 24580
  6.5 30.0 %copy-start.4 = (f32[2000]{0:T(1024)S(1)}, f32[2000]{0:T(1024)}, u32[]{:S(2)}) copy-start(f32[2000]{0:T(1024)} %param.8) | copy-start | bytes 24004
  6.5 30.0 %copy-start.5 = (s32[2048]{0:T(1024)S(1)}, s32[2048]{0:T(1024)}, u32[]{:S(2)}) copy-start(s32[2048]{0:T(1024)} %param.6) | copy-start | bytes 24580
  6.5 96.2 %all-gather.2.cloned.1.call-start = ((), (), s32[]{:S(2)}) async-start(), calls=%async_computation | async-start | bytes 4718592 | tf_op jit(solution)/shard_map/all_gather | solution.py:30
  9.2 12.7 %collective-permute-start.7 = (bf16[1024,128]{1,0:T(8,128)(2,1)S(1)}, bf16[1024,128]{1,0:T(8,128)(2,1)S(1)}, u32[]{:S(2)}, u32[]{:S(2)}) collective-permute-start(bf16[1024,128]{1,0:T(8,128)(2,1)S(1)} %get-tuple-element.54), channel_id=1, source_target_pairs={{0,2},{2,4},{4,6},{6,7},{7,5},{5,3},{3,1},{1,0},{8,10},{10,12},{12... | collective-permute-start | bytes 786440 | tf_op jit(solution)/shard_map/ppermute | solution.py:38
  14.4 16.4 %collective-permute-start = (bf16[1024,128]{1,0:T(8,128)(2,1)S(1)}, bf16[1024,128]{1,0:T(8,128)(2,1)S(1)}, u32[]{:S(2)}, u32[]{:S(2)}) collective-permute-start(bf16[1024,128]{1,0:T(8,128)(2,1)S(1)} %get-tuple-element.51), channel_id=1, source_target_pairs={{0,2},{2,4},{4,6},{6,7},{7,5},{5,3},{3,1},{1,0},{8,10},{10,12},{12... | collective-permute-start | bytes 786440 | tf_op jit(solution)/shard_map/ppermute | solution.py:38
  21.9 11.9 %collective-permute-start.8 = (bf16[1024,128]{1,0:T(8,128)(2,1)S(1)}, bf16[1024,128]{1,0:T(8,128)(2,1)S(1)}, u32[]{:S(2)}, u32[]{:S(2)}) collective-permute-start(bf16[1024,128]{1,0:T(8,128)(2,1)S(1)} %collective-permute-done.7), channel_id=1, source_target_pairs={{0,2},{2,4},{4,6},{6,7},{7,5},{5,3},{3,1},{1,0},{8,10},{10,12},{12... | collective-permute-start | bytes 786440 | tf_op jit(solution)/shard_map/ppermute | solution.py:38
  30.8 12.6 %collective-permute-start.1 = (bf16[1024,128]{1,0:T(8,128)(2,1)S(1)}, bf16[1024,128]{1,0:T(8,128)(2,1)S(1)}, u32[]{:S(2)}, u32[]{:S(2)}) collective-permute-start(bf16[1024,128]{1,0:T(8,128)(2,1)S(1)} %collective-permute-done), channel_id=1, source_target_pairs={{0,2},{2,4},{4,6},{6,7},{7,5},{5,3},{3,1},{1,0},{8,10},{10,12},{12... | collective-permute-start | bytes 786440 | tf_op jit(solution)/shard_map/ppermute | solution.py:38
  33.7 14.4 %collective-permute-start.9 = (bf16[1024,128]{1,0:T(8,128)(2,1)S(1)}, bf16[1024,128]{1,0:T(8,128)(2,1)S(1)}, u32[]{:S(2)}, u32[]{:S(2)}) collective-permute-start(bf16[1024,128]{1,0:T(8,128)(2,1)S(1)} %collective-permute-done.8), channel_id=1, source_target_pairs={{0,2},{2,4},{4,6},{6,7},{7,5},{5,3},{3,1},{1,0},{8,10},{10,12},{12... | collective-permute-start | bytes 786440 | tf_op jit(solution)/shard_map/ppermute | solution.py:38
  43.4 11.6 %collective-permute-start.2 = (bf16[1024,128]{1,0:T(8,128)(2,1)S(1)}, bf16[1024,128]{1,0:T(8,128)(2,1)S(1)}, u32[]{:S(2)}, u32[]{:S(2)}) collective-permute-start(bf16[1024,128]{1,0:T(8,128)(2,1)S(1)} %collective-permute-done.1), channel_id=1, source_target_pairs={{0,2},{2,4},{4,6},{6,7},{7,5},{5,3},{3,1},{1,0},{8,10},{10,12},{12... | collective-permute-start | bytes 786440 | tf_op jit(solution)/shard_map/ppermute | solution.py:38
  48.1 13.2 %collective-permute-start.10 = (bf16[1024,128]{1,0:T(8,128)(2,1)S(1)}, bf16[1024,128]{1,0:T(8,128)(2,1)S(1)}, u32[]{:S(2)}, u32[]{:S(2)}) collective-permute-start(bf16[1024,128]{1,0:T(8,128)(2,1)S(1)} %collective-permute-done.9), channel_id=1, source_target_pairs={{0,2},{2,4},{4,6},{6,7},{7,5},{5,3},{3,1},{1,0},{8,10},{10,12},{12... | collective-permute-start | bytes 786440 | tf_op jit(solution)/shard_map/ppermute | solution.py:38
  55.0 11.6 %collective-permute-start.3 = (bf16[1024,128]{1,0:T(8,128)(2,1)S(1)}, bf16[1024,128]{1,0:T(8,128)(2,1)S(1)}, u32[]{:S(2)}, u32[]{:S(2)}) collective-permute-start(bf16[1024,128]{1,0:T(8,128)(2,1)S(1)} %collective-permute-done.2), channel_id=1, source_target_pairs={{0,2},{2,4},{4,6},{6,7},{7,5},{5,3},{3,1},{1,0},{8,10},{10,12},{12... | collective-permute-start | bytes 786440 | tf_op jit(solution)/shard_map/ppermute | solution.py:38
  61.3 13.0 %collective-permute-start.11 = (bf16[1024,128]{1,0:T(8,128)(2,1)S(1)}, bf16[1024,128]{1,0:T(8,128)(2,1)S(1)}, u32[]{:S(2)}, u32[]{:S(2)}) collective-permute-start(bf16[1024,128]{1,0:T(8,128)(2,1)S(1)} %collective-permute-done.10), channel_id=1, source_target_pairs={{0,2},{2,4},{4,6},{6,7},{7,5},{5,3},{3,1},{1,0},{8,10},{10,12},{12... | collective-permute-start | bytes 786440 | tf_op jit(solution)/shard_map/ppermute | solution.py:38
  66.6 12.4 %collective-permute-start.4 = (bf16[1024,128]{1,0:T(8,128)(2,1)S(1)}, bf16[1024,128]{1,0:T(8,128)(2,1)S(1)}, u32[]{:S(2)}, u32[]{:S(2)}) collective-permute-start(bf16[1024,128]{1,0:T(8,128)(2,1)S(1)} %collective-permute-done.3), channel_id=1, source_target_pairs={{0,2},{2,4},{4,6},{6,7},{7,5},{5,3},{3,1},{1,0},{8,10},{10,12},{12... | collective-permute-start | bytes 786440 | tf_op jit(solution)/shard_map/ppermute | solution.py:38
  74.3 10.8 %collective-permute-start.12 = (bf16[1024,128]{1,0:T(8,128)(2,1)S(1)}, bf16[1024,128]{1,0:T(8,128)(2,1)S(1)}, u32[]{:S(2)}, u32[]{:S(2)}) collective-permute-start(bf16[1024,128]{1,0:T(8,128)(2,1)S(1)} %collective-permute-done.11), channel_id=1, source_target_pairs={{0,2},{2,4},{4,6},{6,7},{7,5},{5,3},{3,1},{1,0},{8,10},{10,12},{12... | collective-permute-start | bytes 786440 | tf_op jit(solution)/shard_map/ppermute | solution.py:38
  79.0 13.2 %collective-permute-start.5 = (bf16[1024,128]{1,0:T(8,128)(2,1)S(1)}, bf16[1024,128]{1,0:T(8,128)(2,1)S(1)}, u32[]{:S(2)}, u32[]{:S(2)}) collective-permute-start(bf16[1024,128]{1,0:T(8,128)(2,1)S(1)} %collective-permute-done.4), channel_id=1, source_target_pairs={{0,2},{2,4},{4,6},{6,7},{7,5},{5,3},{3,1},{1,0},{8,10},{10,12},{12... | collective-permute-start | bytes 786440 | tf_op jit(solution)/shard_map/ppermute | solution.py:38
  85.1 10.8 %collective-permute-start.13 = (bf16[1024,128]{1,0:T(8,128)(2,1)S(1)}, bf16[1024,128]{1,0:T(8,128)(2,1)S(1)}, u32[]{:S(2)}, u32[]{:S(2)}) collective-permute-start(bf16[1024,128]{1,0:T(8,128)(2,1)S(1)} %collective-permute-done.12), channel_id=1, source_target_pairs={{0,2},{2,4},{4,6},{6,7},{7,5},{5,3},{3,1},{1,0},{8,10},{10,12},{12... | collective-permute-start | bytes 786440 | tf_op jit(solution)/shard_map/ppermute | solution.py:38
  92.2 10.4 %collective-permute-start.6 = (bf16[1024,128]{1,0:T(8,128)(2,1)S(1)}, bf16[1024,128]{1,0:T(8,128)(2,1)S(1)}, u32[]{:S(2)}, u32[]{:S(2)}) collective-permute-start(bf16[1024,128]{1,0:T(8,128)(2,1)S(1)} %collective-permute-done.5), channel_id=1, source_target_pairs={{0,2},{2,4},{4,6},{6,7},{7,5},{5,3},{3,1},{1,0},{8,10},{10,12},{12... | collective-permute-start | bytes 786440 | tf_op jit(solution)/shard_map/ppermute | solution.py:38
  102.7 4.9 %copy-start = (bf16[1024,1024]{1,0:T(8,128)(2,1)S(1)}, bf16[1024,1024]{1,0:T(8,128)(2,1)}, u32[]{:S(2)}) copy-start(bf16[1024,1024]{1,0:T(8,128)(2,1)} %constant_dynamic-update-slice_fusion.8) | copy-start | bytes 6291460
  102.7 4.9 %copy-start.1 = (bf16[2048,1024]{1,0:T(8,128)(2,1)S(1)}, bf16[2048,1024]{1,0:T(8,128)(2,1)}, u32[]{:S(2)}) copy-start(bf16[2048,1024]{1,0:T(8,128)(2,1)} %all-gather.2.cloned.1.call-done) | copy-start | bytes 12582916
  110.5 16.5 %collective-permute-start.14 = (bf16[2,128,512]{2,1,0:T(8,128)(2,1)S(1)}, bf16[2,128,512]{2,1,0:T(8,128)(2,1)S(1)}, u32[]{:S(2)}, u32[]{:S(2)}) collective-permute-start(bf16[2,128,512]{2,1,0:T(8,128)(2,1)S(1)} %pad_maximum_fusion.2), channel_id=1, source_target_pairs={{0,64},{64,128},{128,192},{192,0},{1,65},{65,129},{129,193},{193,1... | collective-permute-start | bytes 786440 | tf_op jit(solution)/shard_map/ppermute | solution.py:63
  113.6 17.3 %collective-permute-start.15 = (bf16[2,128,512]{2,1,0:T(8,128)(2,1)S(1)}, bf16[2,128,512]{2,1,0:T(8,128)(2,1)S(1)}, u32[]{:S(2)}, u32[]{:S(2)}) collective-permute-start(bf16[2,128,512]{2,1,0:T(8,128)(2,1)S(1)} %pad_maximum_fusion.3), channel_id=1, source_target_pairs={{0,128},{64,192},{128,0},{192,64},{1,129},{65,193},{129,1},{193,65... | collective-permute-start | bytes 786440 | tf_op jit(solution)/shard_map/ppermute | solution.py:63
  116.4 14.6 %collective-permute-start.16 = (bf16[2,128,512]{2,1,0:T(8,128)(2,1)S(1)}, bf16[2,128,512]{2,1,0:T(8,128)(2,1)S(1)}, u32[]{:S(2)}, u32[]{:S(2)}) collective-permute-start(bf16[2,128,512]{2,1,0:T(8,128)(2,1)S(1)} %pad_maximum_fusion.4), channel_id=1, source_target_pairs={{0,192},{64,0},{128,64},{192,128},{1,193},{65,1},{129,65},{193,129... | collective-permute-start | bytes 786440 | tf_op jit(solution)/shard_map/ppermute | solution.py:63
  119.6 20.8 %collective-permute-start.17 = (bf16[2,128,512]{2,1,0:T(8,128)(2,1)S(1)}, bf16[2,128,512]{2,1,0:T(8,128)(2,1)S(1)}, u32[]{:S(2)}, u32[]{:S(2)}) collective-permute-start(bf16[2,128,512]{2,1,0:T(8,128)(2,1)S(1)} %pad_maximum_fusion.5), channel_id=1, source_target_pairs={{0,64},{64,128},{128,192},{192,0},{1,65},{65,129},{129,193},{193,1... | collective-permute-start | bytes 786440 | tf_op jit(solution)/shard_map/ppermute | solution.py:63
  122.5 17.9 %collective-permute-start.18 = (bf16[2,128,512]{2,1,0:T(8,128)(2,1)S(1)}, bf16[2,128,512]{2,1,0:T(8,128)(2,1)S(1)}, u32[]{:S(2)}, u32[]{:S(2)}) collective-permute-start(bf16[2,128,512]{2,1,0:T(8,128)(2,1)S(1)} %pad_maximum_fusion.6), channel_id=1, source_target_pairs={{0,128},{64,192},{128,0},{192,64},{1,129},{65,193},{129,1},{193,65... | collective-permute-start | bytes 786440 | tf_op jit(solution)/shard_map/ppermute | solution.py:63
  127.0 13.4 %collective-permute-start.19 = (bf16[2,128,512]{2,1,0:T(8,128)(2,1)S(1)}, bf16[2,128,512]{2,1,0:T(8,128)(2,1)S(1)}, u32[]{:S(2)}, u32[]{:S(2)}) collective-permute-start(bf16[2,128,512]{2,1,0:T(8,128)(2,1)S(1)} %pad_maximum_fusion.7), channel_id=1, source_target_pairs={{0,192},{64,0},{128,64},{192,128},{1,193},{65,1},{129,65},{193,129... | collective-permute-start | bytes 786440 | tf_op jit(solution)/shard_map/ppermute | solution.py:63
  131.2 24.4 %collective-permute-start.20 = (bf16[128,512]{1,0:T(8,128)(2,1)S(1)}, bf16[128,512]{1,0:T(8,128)(2,1)S(1)}, u32[]{:S(2)}, u32[]{:S(2)}) collective-permute-start(bf16[128,512]{1,0:T(8,128)(2,1)S(1)} %fusion.6), channel_id=1, source_target_pairs={{0,256},{256,0},{1,257},{257,1},{2,258},{258,2},{3,259},{259,3},{4... | collective-permute-start | bytes 393224 | tf_op jit(solution)/shard_map/ppermute | solution.py:71
  155.8 15.6 %collective-permute-start.21 = (bf16[128,512]{1,0:T(8,128)(2,1)S(1)}, bf16[128,512]{1,0:T(8,128)(2,1)S(1)}, u32[]{:S(2)}, u32[]{:S(2)}) collective-permute-start(bf16[128,512]{1,0:T(8,128)(2,1)S(1)} %fusion.7), channel_id=1, source_target_pairs={{0,256},{256,0},{1,257},{257,1},{2,258},{258,2},{3,259},{259,3},{4... | collective-permute-start | bytes 393224 | tf_op jit(solution)/shard_map/ppermute | solution.py:71
Sparse Core Ops, SparseCore 0:
  9.5 46.7 all-gather.1

commit v4 on v0

v4 whole, which is shorter than its diff:
```python
import jax
import jax.numpy as jnp
from jax import lax
from jax.sharding import Mesh, PartitionSpec as P

NAMES = ("zh", "x", "y", "core", "zq", "zr")
SHAPE = (2, 4, 4, 2, 2, 4)


def shift(n, s):
    return [(i, (i + s) % n) for i in range(n)]


def circle(n):
    return list(range(0, n, 2)) + list(range(n - 1, 0, -2))


def place(col, n):
    return jnp.where(col % 2 == 0, col // 2, (2 * n - 1 - col) // 2)


def lookup(indices, table):
    hits = indices[:, None] == jnp.arange(table.shape[0], dtype=jnp.int32)[None, :]
    return jnp.sum(jnp.where(hits, table[None, :], jnp.float32(0.0)), axis=1)


def body(pair_elements, valence_of, conduction_of, valence_depth, conduction_height):
    n_g = pair_elements.shape[1]
    n_x, n_r = lax.axis_size("x"), lax.axis_size("zr")
    my_x = lax.axis_index("x")

    def row_panel(elements):
        return lax.all_gather(elements, ("y", "core"), axis=1, tiled=True)

    across = lax.ppermute(pair_elements, "zq", shift(2, 1))
    own_columns = row_panel(pair_elements)
    order = circle(n_r)
    step = [(order[i], order[(i + 1) % n_r]) for i in range(n_r)]
    pair_gap = lookup(valence_of, valence_depth) + lookup(conduction_of, conduction_height)
    factor = -4.0 / pair_gap
    arrived = [pair_elements]
    for _ in range(n_r - 1):
        last, factor = lax.optimization_barrier((arrived[-1], factor)) if arrived[1:] else (pair_elements, factor)
        arrived.append(lax.ppermute(last, "zr", step))
    across, _ = lax.optimization_barrier((across, arrived[n_r - 2]))
    cross_columns = row_panel(across)
    rows = lax.optimization_barrier(jnp.concatenate(arrived, axis=1))
    weighted = (rows.astype(jnp.float32) * factor[:, None]).astype(jnp.bfloat16)
    mine_at = place(lax.axis_index("zr"), n_r)

    def summed_over_x(columns, *earlier):
        partial = lax.dot_general(
            weighted, columns, (((0,), (0,)), ((), ())), preferred_element_type=jnp.float32
        ).reshape(n_r, n_g, -1)

        def block(x):
            turn = lax.rem(mine_at - place(x, n_r) + n_r, n_r)
            return lax.dynamic_index_in_dim(partial, turn, 0, keepdims=False)

        sent = [block(lax.rem(my_x + s, n_x)).astype(jnp.bfloat16) for s in range(1, n_x)]
        mine, *sent = lax.optimization_barrier((block(my_x), *sent))
        got = [lax.ppermute(one, "x", shift(n_x, s)) for s, one in enumerate(sent, 1)]
        got, earlier = lax.optimization_barrier((got, earlier))
        total = mine
        for one in got:
            total = total + one.astype(jnp.float32)
        return total, sent[0], *earlier

    half = ("zh", "zq")
    own, sent = summed_over_x(own_columns)
    cross_columns, _ = lax.optimization_barrier((cross_columns, sent))
    own_got = lax.ppermute(own.astype(jnp.bfloat16), half, [(2, 0), (1, 3)])
    cross, _, own_got = summed_over_x(cross_columns, own_got)
    cross = cross.astype(jnp.bfloat16)
    near = lax.ppermute(cross, half, [(0, 1), (3, 2)])
    far = lax.ppermute(cross, half, [(2, 1), (1, 2)])
    total = jnp.where(
        lax.axis_index("zh") == lax.axis_index("zq"),
        own + own_got.astype(jnp.float32),
        near.astype(jnp.float32) + far.astype(jnp.float32),
    )
    return total.reshape(1, n_g, -1, n_g)


def solution(mesh):
    fine = Mesh(mesh.devices.reshape(SHAPE), NAMES)
    pair, row, col = ("zh", "x"), ("y", "core"), ("zq", "zr")
    placed = (P(pair, row + col), P(pair), P(pair), P(), P())
    return jax.shard_map(
        body, mesh=fine, in_specs=placed, out_specs=P(row, pair, None, col), check_vma=False
    )
```

time: 400 us -> 188 us (0.47)
  the two profiles are of different devices: /device:TPU:8 before, /device:TPU:218 now
where the time goes in v4:
time: 188 us; the launch traced here: 187 us
  waiting for transfers between devices  108 us (57%)
  starting transfers between devices  43.3 us (23%)
  between operations  13.8 us (7%)
  other arithmetic  11.5 us (6%)
  matrix products  9.5 us (5%)
    ppermute x3, waiting for transfers between devices, body(): arrived.append(lax.ppermute(last, 'zr', step))  37.4 us
    ppermute x1, waiting for transfers between devices, body(): across = lax.ppermute(pair_elements, 'zq', shift(2, 1))  26.4 us
    ppermute x6, starting transfers between devices, summed_over_x(): lax.ppermute(one, 'x', shift(n_x, s))  20.2 us
    ppermute x1, waiting for transfers between devices, body(): near = lax.ppermute(cross, half, [(0, 1), (3, 2)])  17.4 us
    ppermute x6, waiting for transfers between devices, summed_over_x(): lax.ppermute(one, 'x', shift(n_x, s))  15.9 us
    ppermute x1, starting transfers between devices, body(): own_got = lax.ppermute(own.astype(jnp.bfloat16), half, [(2, 0), (1, 3)])  10.2 us
    ppermute x1, waiting for transfers between devices, body(): far = lax.ppermute(cross, half, [(2, 1), (1, 2)])  9.71 us
    dot_general x2, matrix products, summed_over_x(): lax.dot_general(weighted, columns, (((0,), (0,)), ((), ())), preferred_el...  9.5 us
  transfers between devices with their start and end apart: 15, of which 11 were waited for; matrix products, arithmetic and copies ran while one was open for 11% of the time, Pallas kernels for 0%

profile of v4, /device:TPU:218, one launch (start us, length us, event | category | flops | bytes accessed | tf_op | source)
XLA Modules:
  0.0 186.9 jit_solution(12741133945961871149)
XLA Ops:
  7.3 3.8 %collective-permute-start = (bf16[2048,128]{1,0:T(8,128)(2,1)}, bf16[2048,128]{1,0:T(8,128)(2,1)S(1)}, u32[]{:S(2)}, u32[]{:S(2)}) collective-permute-start(bf16[2048,128]{1,0:T(8,128)(2,1)} %param.5), channel_id=1, source_target_pairs={{0,2},{2,3},{3,1},{1,0},{4,6},{6,7},{7,5},{5,4},{8,10},{10,11},{11... | collective-permute-start | bytes 1572872 | tf_op jit(solution)/shard_map/ppermute | solution.py:44
  11.1 1.9 %collective-permute-start.6 = (bf16[2048,128]{1,0:T(8,128)(2,1)}, bf16[2048,128]{1,0:T(8,128)(2,1)S(1)}, u32[]{:S(2)}, u32[]{:S(2)}) collective-permute-start(bf16[2048,128]{1,0:T(8,128)(2,1)} %param.5), channel_id=1, source_target_pairs={{0,4},{4,0},{1,5},{5,1},{2,6},{6,2},{3,7},{7,3},{8,12},{12,8},{9,1... | collective-permute-start | bytes 1572872 | tf_op jit(solution)/shard_map/ppermute | solution.py:35
  13.1 5.2 %select_reduce_fusion = f32[2048]{0:T(1024)S(1)} fusion(f32[4096]{0:T(1024)} %param.9, s32[2048]{0:T(1024)} %param.7), kind=kLoop, calls=%fused_computation | loop fusion | flops 25163776 | bytes 32768 | tf_op jit(solution)/shard_map/reduce_sum | solution.py:24
  18.2 2.7 %select_reduce_fusion.1 = f32[2048]{0:T(1024)S(1)} fusion(f32[2000]{0:T(1024)} %param.8, s32[2048]{0:T(1024)} %param.6), kind=kLoop, calls=%fused_computation.2 | loop fusion | flops 12285952 | bytes 24384 | tf_op jit(solution)/shard_map/reduce_sum | solution.py:24
  20.9 7.3 %collective-permute-done = bf16[2048,128]{1,0:T(8,128)(2,1)S(1)} collective-permute-done((bf16[2048,128]{1,0:T(8,128)(2,1)}, bf16[2048,128]{1,0:T(8,128)(2,1)S(1)}, u32[]{:S(2)}, u32[]{:S(2)}) %collective-permute-start) | collective-permute-done | bytes 524320 | tf_op jit(solution)/shard_map/ppermute | solution.py:44
  28.2 2.0 %collective-permute-start.1 = (bf16[2048,128]{1,0:T(8,128)(2,1)S(1)}, bf16[2048,128]{1,0:T(8,128)(2,1)S(1)}, u32[]{:S(2)}, u32[]{:S(2)}) collective-permute-start(bf16[2048,128]{1,0:T(8,128)(2,1)S(1)} %collective-permute-done), channel_id=1, source_target_pairs={{0,2},{2,3},{3,1},{1,0},{4,6},{6,7},{7,5},{5,4},{8,10},{10,11},{11... | collective-permute-start | bytes 1572872 | tf_op jit(solution)/shard_map/ppermute | solution.py:44
  30.2 26.4 %collective-permute-done.6 = bf16[2048,128]{1,0:T(8,128)(2,1)S(1)} collective-permute-done((bf16[2048,128]{1,0:T(8,128)(2,1)}, bf16[2048,128]{1,0:T(8,128)(2,1)S(1)}, u32[]{:S(2)}, u32[]{:S(2)}) %collective-permute-start.6) | collective-permute-done | bytes 524320 | tf_op jit(solution)/shard_map/ppermute | solution.py:35
  56.6 16.6 %collective-permute-done.1 = bf16[2048,128]{1,0:T(8,128)(2,1)S(1)} collective-permute-done((bf16[2048,128]{1,0:T(8,128)(2,1)S(1)}, bf16[2048,128]{1,0:T(8,128)(2,1)S(1)}, u32[]{:S(2)}, u32[]{:S(2)}) %collective-permute-start.1) | collective-permute-done | bytes 524320 | tf_op jit(solution)/shard_map/ppermute | solution.py:44
  73.2 1.9 %collective-permute-start.2 = (bf16[2048,128]{1,0:T(8,128)(2,1)S(1)}, bf16[2048,128]{1,0:T(8,128)(2,1)S(1)}, u32[]{:S(2)}, u32[]{:S(2)}) collective-permute-start(bf16[2048,128]{1,0:T(8,128)(2,1)S(1)} %collective-permute-done.1), channel_id=1, source_target_pairs={{0,2},{2,3},{3,1},{1,0},{4,6},{6,7},{7,5},{5,4},{8,10},{10,11},{11... | collective-permute-start | bytes 1572872 | tf_op jit(solution)/shard_map/ppermute | solution.py:44
  75.4 13.5 %collective-permute-done.2 = bf16[2048,128]{1,0:T(8,128)(2,1)S(1)} collective-permute-done((bf16[2048,128]{1,0:T(8,128)(2,1)S(1)}, bf16[2048,128]{1,0:T(8,128)(2,1)S(1)}, u32[]{:S(2)}, u32[]{:S(2)}) %collective-permute-start.2) | collective-permute-done | bytes 524320 | tf_op jit(solution)/shard_map/ppermute | solution.py:44
  88.9 1.4 pad_maximum_fusion
  90.4 4.9 %fusion.1 = f32[512,1024]{1,0:T(8,128)S(1)} fusion(bf16[2048,1024]{1,0:T(8,128)(2,1)} %all-gather.3.cloned.1.call-done, bf16[2048,512]{1,0:T(8,128)(2,1)S(1)} %pad_maximum_fusion, f32[2048]{0:T(1024)S(1)} %add_divide_fusion), kind=kOutput, calls=%fused_computation.7 | convolution fusion | flops 2150629376 | bytes 8396800 | tf_op jit(solution)/shard_map/dot_general | solution.py:52
  95.4 3.4 %collective-permute-start.3 = (bf16[128,1024]{1,0:T(8,128)(2,1)S(1)}, bf16[128,1024]{1,0:T(8,128)(2,1)S(1)}, u32[]{:S(2)}, u32[]{:S(2)}) collective-permute-start(bf16[128,1024]{1,0:T(8,128)(2,1)S(1)} %get-tuple-element.31), channel_id=1, source_target_pairs={{0,64},{64,128},{128,192},{192,0},{1,65},{65,129},{129,193},{193,1... | collective-permute-start | bytes 786440 | tf_op jit(solution)/shard_map/ppermute | solution.py:62
  98.8 3.0 %collective-permute-start.4 = (bf16[128,1024]{1,0:T(8,128)(2,1)S(1)}, bf16[128,1024]{1,0:T(8,128)(2,1)S(1)}, u32[]{:S(2)}, u32[]{:S(2)}) collective-permute-start(bf16[128,1024]{1,0:T(8,128)(2,1)S(1)} %get-tuple-element.32), channel_id=1, source_target_pairs={{0,128},{64,192},{128,0},{192,64},{1,129},{65,193},{129,1},{193,65... | collective-permute-start | bytes 786440 | tf_op jit(solution)/shard_map/ppermute | solution.py:62
  101.9 4.1 %collective-permute-start.5 = (bf16[128,1024]{1,0:T(8,128)(2,1)S(1)}, bf16[128,1024]{1,0:T(8,128)(2,1)S(1)}, u32[]{:S(2)}, u32[]{:S(2)}) collective-permute-start(bf16[128,1024]{1,0:T(8,128)(2,1)S(1)} %get-tuple-element.33), channel_id=1, source_target_pairs={{0,192},{64,0},{128,64},{192,128},{1,193},{65,1},{129,65},{193,129... | collective-permute-start | bytes 786440 | tf_op jit(solution)/shard_map/ppermute | solution.py:62
  105.9 5.0 %collective-permute-done.4 = bf16[128,1024]{1,0:T(8,128)(2,1)S(1)} collective-permute-done((bf16[128,1024]{1,0:T(8,128)(2,1)S(1)}, bf16[128,1024]{1,0:T(8,128)(2,1)S(1)}, u32[]{:S(2)}, u32[]{:S(2)}) %collective-permute-start.4) | collective-permute-done | bytes 262176 | tf_op jit(solution)/shard_map/ppermute | solution.py:62
  111.0 2.7 %collective-permute-done.5 = bf16[128,1024]{1,0:T(8,128)(2,1)S(1)} collective-permute-done((bf16[128,1024]{1,0:T(8,128)(2,1)S(1)}, bf16[128,1024]{1,0:T(8,128)(2,1)S(1)}, u32[]{:S(2)}, u32[]{:S(2)}) %collective-permute-start.5) | collective-permute-done | bytes 262176 | tf_op jit(solution)/shard_map/ppermute | solution.py:62
  113.7 0.8 fusion.8
  114.5 10.2 %collective-permute-start.10 = (bf16[128,1024]{1,0:T(8,128)(2,1)}, bf16[128,1024]{1,0:T(8,128)(2,1)}, u32[]{:S(2)}, u32[]{:S(2)}) collective-permute-start(bf16[128,1024]{1,0:T(8,128)(2,1)} %fusion.8), channel_id=1, source_target_pairs={{256,0},{4,260},{257,1},{5,261},{258,2},{6,262},{259,3},{7,263},{2... | collective-permute-start | bytes 786440 | tf_op jit(solution)/shard_map/ppermute | solution.py:72
  124.7 4.6 %fusion = f32[512,1024]{1,0:T(8,128)S(1)} fusion(bf16[2048,1024]{1,0:T(8,128)(2,1)} %all-gather.5.cloned.1.call-done, bf16[2048,512]{1,0:T(8,128)(2,1)S(1)} %pad_maximum_fusion, f32[2048]{0:T(1024)S(1)} %add_divide_fusion), kind=kOutput, calls=%fused_computation.6 | convolution fusion | flops 2150629376 | bytes 8396800 | tf_op jit(solution)/shard_map/dot_general | solution.py:52
  129.5 2.5 %collective-permute-start.7 = (bf16[128,1024]{1,0:T(8,128)(2,1)S(1)}, bf16[128,1024]{1,0:T(8,128)(2,1)S(1)}, u32[]{:S(2)}, u32[]{:S(2)}) collective-permute-start(bf16[128,1024]{1,0:T(8,128)(2,1)S(1)} %get-tuple-element.39), channel_id=1, source_target_pairs={{0,64},{64,128},{128,192},{192,0},{1,65},{65,129},{129,193},{193,1... | collective-permute-start | bytes 786440 | tf_op jit(solution)/shard_map/ppermute | solution.py:62
  132.0 3.3 %collective-permute-start.8 = (bf16[128,1024]{1,0:T(8,128)(2,1)S(1)}, bf16[128,1024]{1,0:T(8,128)(2,1)S(1)}, u32[]{:S(2)}, u32[]{:S(2)}) collective-permute-start(bf16[128,1024]{1,0:T(8,128)(2,1)S(1)} %get-tuple-element.40), channel_id=1, source_target_pairs={{0,128},{64,192},{128,0},{192,64},{1,129},{65,193},{129,1},{193,65... | collective-permute-start | bytes 786440 | tf_op jit(solution)/shard_map/ppermute | solution.py:62
  135.2 4.0 %collective-permute-start.9 = (bf16[128,1024]{1,0:T(8,128)(2,1)S(1)}, bf16[128,1024]{1,0:T(8,128)(2,1)S(1)}, u32[]{:S(2)}, u32[]{:S(2)}) collective-permute-start(bf16[128,1024]{1,0:T(8,128)(2,1)S(1)} %get-tuple-element.41), channel_id=1, source_target_pairs={{0,192},{64,0},{128,64},{192,128},{1,193},{65,1},{129,65},{193,129... | collective-permute-start | bytes 786440 | tf_op jit(solution)/shard_map/ppermute | solution.py:62
  139.2 1.4 collective-permute-done.7
  140.6 4.0 %collective-permute-done.8 = bf16[128,1024]{1,0:T(8,128)(2,1)S(1)} collective-permute-done((bf16[128,1024]{1,0:T(8,128)(2,1)S(1)}, bf16[128,1024]{1,0:T(8,128)(2,1)S(1)}, u32[]{:S(2)}, u32[]{:S(2)}) %collective-permute-start.8) | collective-permute-done | bytes 262176 | tf_op jit(solution)/shard_map/ppermute | solution.py:62
  144.6 2.9 %collective-permute-done.9 = bf16[128,1024]{1,0:T(8,128)(2,1)S(1)} collective-permute-done((bf16[128,1024]{1,0:T(8,128)(2,1)S(1)}, bf16[128,1024]{1,0:T(8,128)(2,1)S(1)}, u32[]{:S(2)}, u32[]{:S(2)}) %collective-permute-start.9) | collective-permute-done | bytes 262176 | tf_op jit(solution)/shard_map/ppermute | solution.py:62
  147.6 1.3 collective-permute-start.11
  148.9 1.9 %collective-permute-start.12 = (bf16[128,1024]{1,0:T(8,128)(2,1)S(1)}, bf16[128,1024]{1,0:T(8,128)(2,1)S(1)}, u32[]{:S(2)}, u32[]{:S(2)}) collective-permute-start(bf16[128,1024]{1,0:T(8,128)(2,1)S(1)} %add_convert_fusion), channel_id=1, source_target_pairs={{256,4},{4,256},{257,5},{5,257},{258,6},{6,258},{259,7},{7,259},{2... | collective-permute-start | bytes 786440 | tf_op jit(solution)/shard_map/ppermute | solution.py:76
  150.8 17.4 %collective-permute-done.11 = bf16[128,1024]{1,0:T(8,128)(2,1)S(1)} collective-permute-done((bf16[128,1024]{1,0:T(8,128)(2,1)S(1)}, bf16[128,1024]{1,0:T(8,128)(2,1)S(1)}, u32[]{:S(2)}, u32[]{:S(2)}) %collective-permute-start.11) | collective-permute-done | bytes 262176 | tf_op jit(solution)/shard_map/ppermute | solution.py:75
  168.2 9.7 %collective-permute-done.12 = bf16[128,1024]{1,0:T(8,128)(2,1)S(1)} collective-permute-done((bf16[128,1024]{1,0:T(8,128)(2,1)S(1)}, bf16[128,1024]{1,0:T(8,128)(2,1)S(1)}, u32[]{:S(2)}, u32[]{:S(2)}) %collective-permute-start.12) | collective-permute-done | bytes 262176 | tf_op jit(solution)/shard_map/ppermute | solution.py:76
  178.0 1.2 select_bitcast_fusion
  179.2 0.9 copy.6
  (18 shorter events, 1.3 us)
Async XLA Ops:
  6.5 83.8 %all-gather.3.cloned.1.call-start = ((), (), s32[]{:S(2)}) async-start(), calls=%async_computation | async-start | bytes 4718592 | tf_op jit(solution)/shard_map/all_gather | solution.py:33
  7.3 117.4 %all-gather.5.cloned.1.call-start = ((), (), s32[]{:S(2)}) async-start(), calls=%async_computation.1 | async-start | bytes 4718592 | tf_op jit(solution)/shard_map/all_gather | solution.py:33
  7.3 20.9 %collective-permute-start = (bf16[2048,128]{1,0:T(8,128)(2,1)}, bf16[2048,128]{1,0:T(8,128)(2,1)S(1)}, u32[]{:S(2)}, u32[]{:S(2)}) collective-permute-start(bf16[2048,128]{1,0:T(8,128)(2,1)} %param.5), channel_id=1, source_target_pairs={{0,2},{2,3},{3,1},{1,0},{4,6},{6,7},{7,5},{5,4},{8,10},{10,11},{11... | collective-permute-start | bytes 1572872 | tf_op jit(solution)/shard_map/ppermute | solution.py:44
  11.1 45.5 %collective-permute-start.6 = (bf16[2048,128]{1,0:T(8,128)(2,1)}, bf16[2048,128]{1,0:T(8,128)(2,1)S(1)}, u32[]{:S(2)}, u32[]{:S(2)}) collective-permute-start(bf16[2048,128]{1,0:T(8,128)(2,1)} %param.5), channel_id=1, source_target_pairs={{0,4},{4,0},{1,5},{5,1},{2,6},{6,2},{3,7},{7,3},{8,12},{12,8},{9,1... | collective-permute-start | bytes 1572872 | tf_op jit(solution)/shard_map/ppermute | solution.py:35
  28.2 45.0 %collective-permute-start.1 = (bf16[2048,128]{1,0:T(8,128)(2,1)S(1)}, bf16[2048,128]{1,0:T(8,128)(2,1)S(1)}, u32[]{:S(2)}, u32[]{:S(2)}) collective-permute-start(bf16[2048,128]{1,0:T(8,128)(2,1)S(1)} %collective-permute-done), channel_id=1, source_target_pairs={{0,2},{2,3},{3,1},{1,0},{4,6},{6,7},{7,5},{5,4},{8,10},{10,11},{11... | collective-permute-start | bytes 1572872 | tf_op jit(solution)/shard_map/ppermute | solution.py:44
  56.6 16.6 %copy-start = (bf16[2048,128]{1,0:T(8,128)(2,1)}, bf16[2048,128]{1,0:T(8,128)(2,1)S(1)}, u32[]{:S(2)}) copy-start(bf16[2048,128]{1,0:T(8,128)(2,1)S(1)} %collective-permute-done.6) | copy-start | bytes 1572868
  73.2 2.2 %copy-start.1 = (bf16[2048,128]{1,0:T(8,128)(2,1)}, bf16[2048,128]{1,0:T(8,128)(2,1)S(1)}, u32[]{:S(2)}) copy-start(bf16[2048,128]{1,0:T(8,128)(2,1)S(1)} %collective-permute-done.1) | copy-start | bytes 1572868
  73.2 15.7 %collective-permute-start.2 = (bf16[2048,128]{1,0:T(8,128)(2,1)S(1)}, bf16[2048,128]{1,0:T(8,128)(2,1)S(1)}, u32[]{:S(2)}, u32[]{:S(2)}) collective-permute-start(bf16[2048,128]{1,0:T(8,128)(2,1)S(1)} %collective-permute-done.1), channel_id=1, source_target_pairs={{0,2},{2,3},{3,1},{1,0},{4,6},{6,7},{7,5},{5,4},{8,10},{10,11},{11... | collective-permute-start | bytes 1572872 | tf_op jit(solution)/shard_map/ppermute | solution.py:44
  95.4 10.5 %collective-permute-start.3 = (bf16[128,1024]{1,0:T(8,128)(2,1)S(1)}, bf16[128,1024]{1,0:T(8,128)(2,1)S(1)}, u32[]{:S(2)}, u32[]{:S(2)}) collective-permute-start(bf16[128,1024]{1,0:T(8,128)(2,1)S(1)} %get-tuple-element.31), channel_id=1, source_target_pairs={{0,64},{64,128},{128,192},{192,0},{1,65},{65,129},{129,193},{193,1... | collective-permute-start | bytes 786440 | tf_op jit(solution)/shard_map/ppermute | solution.py:62
  98.8 12.1 %collective-permute-start.4 = (bf16[128,1024]{1,0:T(8,128)(2,1)S(1)}, bf16[128,1024]{1,0:T(8,128)(2,1)S(1)}, u32[]{:S(2)}, u32[]{:S(2)}) collective-permute-start(bf16[128,1024]{1,0:T(8,128)(2,1)S(1)} %get-tuple-element.32), channel_id=1, source_target_pairs={{0,128},{64,192},{128,0},{192,64},{1,129},{65,193},{129,1},{193,65... | collective-permute-start | bytes 786440 | tf_op jit(solution)/shard_map/ppermute | solution.py:62
  101.9 11.8 %collective-permute-start.5 = (bf16[128,1024]{1,0:T(8,128)(2,1)S(1)}, bf16[128,1024]{1,0:T(8,128)(2,1)S(1)}, u32[]{:S(2)}, u32[]{:S(2)}) collective-permute-start(bf16[128,1024]{1,0:T(8,128)(2,1)S(1)} %get-tuple-element.33), channel_id=1, source_target_pairs={{0,192},{64,0},{128,64},{192,128},{1,193},{65,1},{129,65},{193,129... | collective-permute-start | bytes 786440 | tf_op jit(solution)/shard_map/ppermute | solution.py:62
  114.5 24.7 %collective-permute-start.10 = (bf16[128,1024]{1,0:T(8,128)(2,1)}, bf16[128,1024]{1,0:T(8,128)(2,1)}, u32[]{:S(2)}, u32[]{:S(2)}) collective-permute-start(bf16[128,1024]{1,0:T(8,128)(2,1)} %fusion.8), channel_id=1, source_target_pairs={{256,0},{4,260},{257,1},{5,261},{258,2},{6,262},{259,3},{7,263},{2... | collective-permute-start | bytes 786440 | tf_op jit(solution)/shard_map/ppermute | solution.py:72
  129.5 11.1 %collective-permute-start.7 = (bf16[128,1024]{1,0:T(8,128)(2,1)S(1)}, bf16[128,1024]{1,0:T(8,128)(2,1)S(1)}, u32[]{:S(2)}, u32[]{:S(2)}) collective-permute-start(bf16[128,1024]{1,0:T(8,128)(2,1)S(1)} %get-tuple-element.39), channel_id=1, source_target_pairs={{0,64},{64,128},{128,192},{192,0},{1,65},{65,129},{129,193},{193,1... | collective-permute-start | bytes 786440 | tf_op jit(solution)/shard_map/ppermute | solution.py:62
  132.0 12.6 %collective-permute-start.8 = (bf16[128,1024]{1,0:T(8,128)(2,1)S(1)}, bf16[128,1024]{1,0:T(8,128)(2,1)S(1)}, u32[]{:S(2)}, u32[]{:S(2)}) collective-permute-start(bf16[128,1024]{1,0:T(8,128)(2,1)S(1)} %get-tuple-element.40), channel_id=1, source_target_pairs={{0,128},{64,192},{128,0},{192,64},{1,129},{65,193},{129,1},{193,65... | collective-permute-start | bytes 786440 | tf_op jit(solution)/shard_map/ppermute | solution.py:62
  135.2 12.2 %collective-permute-start.9 = (bf16[128,1024]{1,0:T(8,128)(2,1)S(1)}, bf16[128,1024]{1,0:T(8,128)(2,1)S(1)}, u32[]{:S(2)}, u32[]{:S(2)}) collective-permute-start(bf16[128,1024]{1,0:T(8,128)(2,1)S(1)} %get-tuple-element.41), channel_id=1, source_target_pairs={{0,192},{64,0},{128,64},{192,128},{1,193},{65,1},{129,65},{193,129... | collective-permute-start | bytes 786440 | tf_op jit(solution)/shard_map/ppermute | solution.py:62
  147.6 20.6 %collective-permute-start.11 = (bf16[128,1024]{1,0:T(8,128)(2,1)S(1)}, bf16[128,1024]{1,0:T(8,128)(2,1)S(1)}, u32[]{:S(2)}, u32[]{:S(2)}) collective-permute-start(bf16[128,1024]{1,0:T(8,128)(2,1)S(1)} %add_convert_fusion), channel_id=1, source_target_pairs={{0,4},{260,256},{1,5},{261,257},{2,6},{262,258},{3,7},{263,259},{8... | collective-permute-start | bytes 786440 | tf_op jit(solution)/shard_map/ppermute | solution.py:75
  148.9 29.0 %collective-permute-start.12 = (bf16[128,1024]{1,0:T(8,128)(2,1)S(1)}, bf16[128,1024]{1,0:T(8,128)(2,1)S(1)}, u32[]{:S(2)}, u32[]{:S(2)}) collective-permute-start(bf16[128,1024]{1,0:T(8,128)(2,1)S(1)} %add_convert_fusion), channel_id=1, source_target_pairs={{256,4},{4,256},{257,5},{5,257},{258,6},{6,258},{259,7},{7,259},{2... | collective-permute-start | bytes 786440 | tf_op jit(solution)/shard_map/ppermute | solution.py:76
Sparse Core Ops, SparseCore 0:
  9.5 45.0 all-gather.2
  73.4 44.6 all-gather.4

commit v5 on v3

v5 whole, which is shorter than its diff:
```python
import jax
import jax.numpy as jnp
from jax import lax
from jax.sharding import Mesh, PartitionSpec as P

NAMES = ("zh", "x", "y", "core", "zl")
SHAPE = (2, 4, 4, 2, 8)


def shift(n, s):
    return [(i, (i + s) % n) for i in range(n)]


def circle(n):
    return list(range(0, n, 2)) + list(range(n - 1, 0, -2))


def cut(array, parts):
    tiles = array.shape[0] // 16
    ends = [16 * (tiles * i // parts) for i in range(parts + 1)]
    return [array[a:b] for a, b in zip(ends, ends[1:])]


def lookup(indices, table):
    hits = indices[:, None] == jnp.arange(table.shape[0], dtype=jnp.int32)[None, :]
    return jnp.sum(jnp.where(hits, table[None, :], jnp.float32(0.0)), axis=1)


def place(col, n):
    return jnp.where(col % 2 == 0, col // 2, (2 * n - 1 - col) // 2)


def body(pair_elements, valence_of, conduction_of, valence_depth, conduction_height):
    n_pair, n_g = pair_elements.shape
    n_x, n_z = lax.axis_size("x"), lax.axis_size("zl")
    columns = lax.all_gather(pair_elements, ("y", "core"), axis=1, tiled=True)

    order = circle(n_z)
    step = [(order[i], order[(i + 1) % n_z]) for i in range(n_z)]
    chunks = cut(pair_elements, 3)
    arrived = [[chunk] for chunk in chunks]
    for _ in range(n_z - 1):
        for i in range(len(chunks)):
            chunks[i] = lax.ppermute(chunks[i], "zl", step)
            arrived[i].append(chunks[i])
    rows = jnp.concatenate([jnp.concatenate(one, axis=1) for one in arrived], axis=0)

    pair_gap = lookup(valence_of, valence_depth) + lookup(conduction_of, conduction_height)
    factor = -4.0 / pair_gap
    weighted = (rows.astype(jnp.float32) * factor[:, None]).astype(jnp.bfloat16)

    my_half, my_x = lax.axis_index("zh"), lax.axis_index("x")
    mine_at = place(lax.axis_index("zl"), n_z)

    partial = lax.dot_general(
        weighted, columns, (((0,), (0,)), ((), ())), preferred_element_type=jnp.float32
    ).reshape(n_z, n_g, -1)

    def blocks(half):
        own, *others = [
            lax.dynamic_index_in_dim(partial, turn, 0, keepdims=False)
            for turn in (
                lax.rem(mine_at - place(half * n_x + lax.rem(my_x + s, n_x), n_z) + n_z, n_z)
                for s in range(n_x)
            )
        ]
        return own, [one.astype(jnp.bfloat16) for one in others]

    def over_x(sent):
        return [lax.ppermute(one, "x", shift(n_x, s)) for s, one in enumerate(sent, 1)]

    def added(own, got):
        for one in got:
            own = own + one.astype(jnp.float32)
        return own

    given, given_sent = blocks(1 - my_half)
    kept, kept_sent = blocks(my_half)
    given, given_sent, kept, kept_sent = lax.optimization_barrier(
        (given, given_sent, kept, kept_sent)
    )
    given = added(given, over_x(given_sent)).astype(jnp.bfloat16)
    given, kept_sent = lax.optimization_barrier((given, kept_sent))
    got = lax.ppermute(given, "zh", shift(2, 1))
    total = added(kept, over_x(kept_sent)) + got.astype(jnp.float32)
    return total.reshape(1, n_g, -1, n_g)


def solution(mesh):
    fine = Mesh(mesh.devices.reshape(SHAPE), NAMES)
    pair, row = ("zh", "x"), ("y", "core")
    placed = (P(pair, row + ("zl",)), P(pair), P(pair), P(), P())
    return jax.shard_map(
        body, mesh=fine, in_specs=placed, out_specs=P(row, pair, None, "zl"), check_vma=False
    )
```

time: 180 us -> 171 us (0.950)
  the two profiles are of different devices: /device:TPU:132 before, /device:TPU:120 now
where the time goes in v5:
time: 171 us; the launch traced here: 170 us
  starting transfers between devices  96.8 us (57%)
  waiting for transfers between devices  29.4 us (17%)
  local copies, waits for them, and re-layouts  15 us (9%)
  between operations  14.2 us (8%)
  matrix products  7.72 us (5%)
  other arithmetic  6.76 us (4%)
    ppermute x21, starting transfers between devices, body(): chunks[i] = lax.ppermute(chunks[i], 'zl', step)  68.5 us
    ppermute x6, starting transfers between devices, over_x(): lax.ppermute(one, 'x', shift(n_x, s))  18.4 us
    ppermute x1, waiting for transfers between devices, body(): got = lax.ppermute(given, 'zh', shift(2, 1))  11 us
    ppermute x21, waiting for transfers between devices, body(): chunks[i] = lax.ppermute(chunks[i], 'zl', step)  10.6 us
    ppermute x1, starting transfers between devices, body(): got = lax.ppermute(given, 'zh', shift(2, 1))  9.76 us
    unnamed x27, local copies, waits for them, and re-layouts  9.71 us
    dot_general x1, matrix products, body(): lax.dot_general(weighted, columns, (((0,), (0,)), ((), ())), preferred_el...  7.72 us
    ppermute x6, waiting for transfers between devices, over_x(): lax.ppermute(one, 'x', shift(n_x, s))  7.06 us
  transfers between devices with their start and end apart: 29, of which 13 were waited for; matrix products, arithmetic and copies ran while one was open for 12% of the time, Pallas kernels for 0%

profile of v5, /device:TPU:120, one launch (start us, length us, event | category | flops | bytes accessed | tf_op | source)
XLA Modules:
  0.0 169.8 jit_solution(17091915522979833970)
XLA Ops:
  14.6 4.9 %collective-permute-start = (bf16[672,128]{1,0:T(8,128)(2,1)S(1)}, bf16[672,128]{1,0:T(8,128)(2,1)S(1)}, u32[]{:S(2)}, u32[]{:S(2)}) collective-permute-start(bf16[672,128]{1,0:T(8,128)(2,1)S(1)} %get-tuple-element.37), channel_id=1, source_target_pairs={{0,2},{2,4},{4,6},{6,7},{7,5},{5,3},{3,1},{1,0},{8,10},{10,12},{12... | collective-permute-start | bytes 516104 | tf_op jit(solution)/shard_map/ppermute | solution.py:44
  19.5 2.0 %select_reduce_fusion.1 = f32[2048]{0:T(1024)S(1)} fusion(f32[2000]{0:T(1024)S(1)} %copy-done.1, s32[2048]{0:T(1024)S(1)} %copy-done.2), kind=kLoop, calls=%fused_computation.2 | loop fusion | flops 12285952 | bytes 24384 | tf_op jit(solution)/shard_map/reduce_sum | solution.py:26
  21.5 4.4 %select_reduce_fusion = f32[2048]{0:T(1024)S(1)} fusion(f32[4096]{0:T(1024)S(1)} %copy-done, s32[2048]{0:T(1024)S(1)} %copy-done.3), kind=kLoop, calls=%fused_computation | loop fusion | flops 25163776 | bytes 32768 | tf_op jit(solution)/shard_map/reduce_sum | solution.py:26
  27.4 5.4 %collective-permute-start.1 = (bf16[672,128]{1,0:T(8,128)(2,1)S(1)}, bf16[672,128]{1,0:T(8,128)(2,1)S(1)}, u32[]{:S(2)}, u32[]{:S(2)}) collective-permute-start(bf16[672,128]{1,0:T(8,128)(2,1)S(1)} %collective-permute-done), channel_id=1, source_target_pairs={{0,2},{2,4},{4,6},{6,7},{7,5},{5,3},{3,1},{1,0},{8,10},{10,12},{12... | collective-permute-start | bytes 516104 | tf_op jit(solution)/shard_map/ppermute | solution.py:44
  33.5 5.2 %collective-permute-start.15 = (bf16[688,128]{1,0:T(8,128)(2,1)S(1)}, bf16[688,128]{1,0:T(8,128)(2,1)S(1)}, u32[]{:S(2)}, u32[]{:S(2)}) collective-permute-start(bf16[688,128]{1,0:T(8,128)(2,1)S(1)} %collective-permute-done.14), channel_id=1, source_target_pairs={{0,2},{2,4},{4,6},{6,7},{7,5},{5,3},{3,1},{1,0},{8,10},{10,12},{12... | collective-permute-start | bytes 528392 | tf_op jit(solution)/shard_map/ppermute | solution.py:44
  39.4 3.8 %collective-permute-start.8 = (bf16[688,128]{1,0:T(8,128)(2,1)S(1)}, bf16[688,128]{1,0:T(8,128)(2,1)S(1)}, u32[]{:S(2)}, u32[]{:S(2)}) collective-permute-start(bf16[688,128]{1,0:T(8,128)(2,1)S(1)} %collective-permute-done.7), channel_id=1, source_target_pairs={{0,2},{2,4},{4,6},{6,7},{7,5},{5,3},{3,1},{1,0},{8,10},{10,12},{12... | collective-permute-start | bytes 528392 | tf_op jit(solution)/shard_map/ppermute | solution.py:44
  43.3 2.7 %collective-permute-start.2 = (bf16[672,128]{1,0:T(8,128)(2,1)S(1)}, bf16[672,128]{1,0:T(8,128)(2,1)S(1)}, u32[]{:S(2)}, u32[]{:S(2)}) collective-permute-start(bf16[672,128]{1,0:T(8,128)(2,1)S(1)} %collective-permute-done.1), channel_id=1, source_target_pairs={{0,2},{2,4},{4,6},{6,7},{7,5},{5,3},{3,1},{1,0},{8,10},{10,12},{12... | collective-permute-start | bytes 516104 | tf_op jit(solution)/shard_map/ppermute | solution.py:44
  49.6 3.6 %collective-permute-start.9 = (bf16[688,128]{1,0:T(8,128)(2,1)S(1)}, bf16[688,128]{1,0:T(8,128)(2,1)S(1)}, u32[]{:S(2)}, u32[]{:S(2)}) collective-permute-start(bf16[688,128]{1,0:T(8,128)(2,1)S(1)} %collective-permute-done.8), channel_id=1, source_target_pairs={{0,2},{2,4},{4,6},{6,7},{7,5},{5,3},{3,1},{1,0},{8,10},{10,12},{12... | collective-permute-start | bytes 528392 | tf_op jit(solution)/shard_map/ppermute | solution.py:44
  54.6 2.3 %collective-permute-start.3 = (bf16[672,128]{1,0:T(8,128)(2,1)S(1)}, bf16[672,128]{1,0:T(8,128)(2,1)S(1)}, u32[]{:S(2)}, u32[]{:S(2)}) collective-permute-start(bf16[672,128]{1,0:T(8,128)(2,1)S(1)} %collective-permute-done.2), channel_id=1, source_target_pairs={{0,2},{2,4},{4,6},{6,7},{7,5},{5,3},{3,1},{1,0},{8,10},{10,12},{12... | collective-permute-start | bytes 516104 | tf_op jit(solution)/shard_map/ppermute | solution.py:44
  58.4 2.3 %collective-permute-start.17 = (bf16[688,128]{1,0:T(8,128)(2,1)S(1)}, bf16[688,128]{1,0:T(8,128)(2,1)S(1)}, u32[]{:S(2)}, u32[]{:S(2)}) collective-permute-start(bf16[688,128]{1,0:T(8,128)(2,1)S(1)} %collective-permute-done.16), channel_id=1, source_target_pairs={{0,2},{2,4},{4,6},{6,7},{7,5},{5,3},{3,1},{1,0},{8,10},{10,12},{12... | collective-permute-start | bytes 528392 | tf_op jit(solution)/shard_map/ppermute | solution.py:44
  62.2 2.4 %collective-permute-start.10 = (bf16[688,128]{1,0:T(8,128)(2,1)S(1)}, bf16[688,128]{1,0:T(8,128)(2,1)S(1)}, u32[]{:S(2)}, u32[]{:S(2)}) collective-permute-start(bf16[688,128]{1,0:T(8,128)(2,1)S(1)} %collective-permute-done.9), channel_id=1, source_target_pairs={{0,2},{2,4},{4,6},{6,7},{7,5},{5,3},{3,1},{1,0},{8,10},{10,12},{12... | collective-permute-start | bytes 528392 | tf_op jit(solution)/shard_map/ppermute | solution.py:44
  65.9 3.8 %collective-permute-start.4 = (bf16[672,128]{1,0:T(8,128)(2,1)S(1)}, bf16[672,128]{1,0:T(8,128)(2,1)S(1)}, u32[]{:S(2)}, u32[]{:S(2)}) collective-permute-start(bf16[672,128]{1,0:T(8,128)(2,1)S(1)} %collective-permute-done.3), channel_id=1, source_target_pairs={{0,2},{2,4},{4,6},{6,7},{7,5},{5,3},{3,1},{1,0},{8,10},{10,12},{12... | collective-permute-start | bytes 516104 | tf_op jit(solution)/shard_map/ppermute | solution.py:44
  70.5 3.8 %collective-permute-start.18 = (bf16[688,128]{1,0:T(8,128)(2,1)S(1)}, bf16[688,128]{1,0:T(8,128)(2,1)S(1)}, u32[]{:S(2)}, u32[]{:S(2)}) collective-permute-start(bf16[688,128]{1,0:T(8,128)(2,1)S(1)} %collective-permute-done.17), channel_id=1, source_target_pairs={{0,2},{2,4},{4,6},{6,7},{7,5},{5,3},{3,1},{1,0},{8,10},{10,12},{12... | collective-permute-start | bytes 528392 | tf_op jit(solution)/shard_map/ppermute | solution.py:44
  75.0 2.7 %collective-permute-start.11 = (bf16[688,128]{1,0:T(8,128)(2,1)S(1)}, bf16[688,128]{1,0:T(8,128)(2,1)S(1)}, u32[]{:S(2)}, u32[]{:S(2)}) collective-permute-start(bf16[688,128]{1,0:T(8,128)(2,1)S(1)} %collective-permute-done.10), channel_id=1, source_target_pairs={{0,2},{2,4},{4,6},{6,7},{7,5},{5,3},{3,1},{1,0},{8,10},{10,12},{12... | collective-permute-start | bytes 528392 | tf_op jit(solution)/shard_map/ppermute | solution.py:44
  77.7 2.7 %collective-permute-start.5 = (bf16[672,128]{1,0:T(8,128)(2,1)S(1)}, bf16[672,128]{1,0:T(8,128)(2,1)S(1)}, u32[]{:S(2)}, u32[]{:S(2)}) collective-permute-start(bf16[672,128]{1,0:T(8,128)(2,1)S(1)} %collective-permute-done.4), channel_id=1, source_target_pairs={{0,2},{2,4},{4,6},{6,7},{7,5},{5,3},{3,1},{1,0},{8,10},{10,12},{12... | collective-permute-start | bytes 516104 | tf_op jit(solution)/shard_map/ppermute | solution.py:44
  81.7 3.9 %collective-permute-start.19 = (bf16[688,128]{1,0:T(8,128)(2,1)S(1)}, bf16[688,128]{1,0:T(8,128)(2,1)S(1)}, u32[]{:S(2)}, u32[]{:S(2)}) collective-permute-start(bf16[688,128]{1,0:T(8,128)(2,1)S(1)} %collective-permute-done.18), channel_id=1, source_target_pairs={{0,2},{2,4},{4,6},{6,7},{7,5},{5,3},{3,1},{1,0},{8,10},{10,12},{12... | collective-permute-start | bytes 528392 | tf_op jit(solution)/shard_map/ppermute | solution.py:44
  86.4 3.0 %collective-permute-start.12 = (bf16[688,128]{1,0:T(8,128)(2,1)S(1)}, bf16[688,128]{1,0:T(8,128)(2,1)S(1)}, u32[]{:S(2)}, u32[]{:S(2)}) collective-permute-start(bf16[688,128]{1,0:T(8,128)(2,1)S(1)} %collective-permute-done.11), channel_id=1, source_target_pairs={{0,2},{2,4},{4,6},{6,7},{7,5},{5,3},{3,1},{1,0},{8,10},{10,12},{12... | collective-permute-start | bytes 528392 | tf_op jit(solution)/shard_map/ppermute | solution.py:44
  89.9 3.2 %collective-permute-start.6 = (bf16[672,128]{1,0:T(8,128)(2,1)S(1)}, bf16[672,128]{1,0:T(8,128)(2,1)S(1)}, u32[]{:S(2)}, u32[]{:S(2)}) collective-permute-start(bf16[672,128]{1,0:T(8,128)(2,1)S(1)} %collective-permute-done.5), channel_id=1, source_target_pairs={{0,2},{2,4},{4,6},{6,7},{7,5},{5,3},{3,1},{1,0},{8,10},{10,12},{12... | collective-permute-start | bytes 516104 | tf_op jit(solution)/shard_map/ppermute | solution.py:44
  93.8 3.2 %collective-permute-start.20 = (bf16[688,128]{1,0:T(8,128)(2,1)S(1)}, bf16[688,128]{1,0:T(8,128)(2,1)S(1)}, u32[]{:S(2)}, u32[]{:S(2)}) collective-permute-start(bf16[688,128]{1,0:T(8,128)(2,1)S(1)} %collective-permute-done.19), channel_id=1, source_target_pairs={{0,2},{2,4},{4,6},{6,7},{7,5},{5,3},{3,1},{1,0},{8,10},{10,12},{12... | collective-permute-start | bytes 528392 | tf_op jit(solution)/shard_map/ppermute | solution.py:44
  97.8 3.8 %collective-permute-start.13 = (bf16[688,128]{1,0:T(8,128)(2,1)S(1)}, bf16[688,128]{1,0:T(8,128)(2,1)S(1)}, u32[]{:S(2)}, u32[]{:S(2)}) collective-permute-start(bf16[688,128]{1,0:T(8,128)(2,1)S(1)} %collective-permute-done.12), channel_id=1, source_target_pairs={{0,2},{2,4},{4,6},{6,7},{7,5},{5,3},{3,1},{1,0},{8,10},{10,12},{12... | collective-permute-start | bytes 528392 | tf_op jit(solution)/shard_map/ppermute | solution.py:44
  104.4 2.8 %collective-permute-done.13 = bf16[688,128]{1,0:T(8,128)(2,1)S(1)} collective-permute-done((bf16[688,128]{1,0:T(8,128)(2,1)S(1)}, bf16[688,128]{1,0:T(8,128)(2,1)S(1)}, u32[]{:S(2)}, u32[]{:S(2)}) %collective-permute-start.13) | collective-permute-done | bytes 176160 | tf_op jit(solution)/shard_map/ppermute | solution.py:44
  107.3 7.7 %fusion = f32[1024,1024]{1,0:T(8,128)S(1)} fusion(bf16[2048,1024]{1,0:T(8,128)(2,1)} %all-gather.2.cloned.1.call-done, bf16[688,1024]{1,0:T(8,128)(2,1)} %constant_dynamic-update-slice_fusion.16, bf16[688,1024]{1,0:T(8,128)(2,1)S(1)} %constant_dynamic-update-slice_fusion.8, bf16[672,1024]{1,0:T(8,128)(2,1)} %constant_dynamic-update-slice_fusion, ...), kind=kOutput, calls=%fused_computation.5 | convolution fusion | flops 4311744512 | bytes 12591104 | tf_op jit(solution)/shard_map/dot_general | solution.py:55
  115.4 4.7 %collective-permute-start.23 = (bf16[128,1024]{1,0:T(8,128)(2,1)S(1)}, bf16[128,1024]{1,0:T(8,128)(2,1)S(1)}, u32[]{:S(2)}, u32[]{:S(2)}) collective-permute-start(bf16[128,1024]{1,0:T(8,128)(2,1)S(1)} %get-tuple-element.21), channel_id=1, source_target_pairs={{0,192},{64,0},{128,64},{192,128},{1,193},{65,1},{129,65},{193,129... | collective-permute-start | bytes 786440 | tf_op jit(solution)/shard_map/ppermute | solution.py:70
  120.1 2.7 %collective-permute-start.22 = (bf16[128,1024]{1,0:T(8,128)(2,1)S(1)}, bf16[128,1024]{1,0:T(8,128)(2,1)S(1)}, u32[]{:S(2)}, u32[]{:S(2)}) collective-permute-start(bf16[128,1024]{1,0:T(8,128)(2,1)S(1)} %get-tuple-element.20), channel_id=1, source_target_pairs={{0,128},{64,192},{128,0},{192,64},{1,129},{65,193},{129,1},{193,65... | collective-permute-start | bytes 786440 | tf_op jit(solution)/shard_map/ppermute | solution.py:70
  122.8 2.8 %collective-permute-start.21 = (bf16[128,1024]{1,0:T(8,128)(2,1)S(1)}, bf16[128,1024]{1,0:T(8,128)(2,1)S(1)}, u32[]{:S(2)}, u32[]{:S(2)}) collective-permute-start(bf16[128,1024]{1,0:T(8,128)(2,1)S(1)} %get-tuple-element.19), channel_id=1, source_target_pairs={{0,64},{64,128},{128,192},{192,0},{1,65},{65,129},{129,193},{193,1... | collective-permute-start | bytes 786440 | tf_op jit(solution)/shard_map/ppermute | solution.py:70
  125.6 4.3 %collective-permute-done.22 = bf16[128,1024]{1,0:T(8,128)(2,1)S(1)} collective-permute-done((bf16[128,1024]{1,0:T(8,128)(2,1)S(1)}, bf16[128,1024]{1,0:T(8,128)(2,1)S(1)}, u32[]{:S(2)}, u32[]{:S(2)}) %collective-permute-start.22) | collective-permute-done | bytes 262176 | tf_op jit(solution)/shard_map/ppermute | solution.py:70
  129.9 2.8 %collective-permute-done.21 = bf16[128,1024]{1,0:T(8,128)(2,1)S(1)} collective-permute-done((bf16[128,1024]{1,0:T(8,128)(2,1)S(1)}, bf16[128,1024]{1,0:T(8,128)(2,1)S(1)}, u32[]{:S(2)}, u32[]{:S(2)}) %collective-permute-start.21) | collective-permute-done | bytes 262176 | tf_op jit(solution)/shard_map/ppermute | solution.py:70
  132.8 9.8 %collective-permute-start.27 = (bf16[128,1024]{1,0:T(8,128)(2,1)S(1)}, bf16[128,1024]{1,0:T(8,128)(2,1)S(1)}, u32[]{:S(2)}, u32[]{:S(2)}) collective-permute-start(bf16[128,1024]{1,0:T(8,128)(2,1)S(1)} %add_convert_fusion), channel_id=1, source_target_pairs={{0,256},{256,0},{1,257},{257,1},{2,258},{258,2},{3,259},{259,3},{4... | collective-permute-start | bytes 786440 | tf_op jit(solution)/shard_map/ppermute | solution.py:84
  142.6 2.5 %collective-permute-start.26 = (bf16[128,1024]{1,0:T(8,128)(2,1)S(1)}, bf16[128,1024]{1,0:T(8,128)(2,1)S(1)}, u32[]{:S(2)}, u32[]{:S(2)}) collective-permute-start(bf16[128,1024]{1,0:T(8,128)(2,1)S(1)} %get-tuple-element.27), channel_id=1, source_target_pairs={{0,192},{64,0},{128,64},{192,128},{1,193},{65,1},{129,65},{193,129... | collective-permute-start | bytes 786440 | tf_op jit(solution)/shard_map/ppermute | solution.py:70
  145.0 2.7 %collective-permute-start.25 = (bf16[128,1024]{1,0:T(8,128)(2,1)S(1)}, bf16[128,1024]{1,0:T(8,128)(2,1)S(1)}, u32[]{:S(2)}, u32[]{:S(2)}) collective-permute-start(bf16[128,1024]{1,0:T(8,128)(2,1)S(1)} %get-tuple-element.26), channel_id=1, source_target_pairs={{0,128},{64,192},{128,0},{192,64},{1,129},{65,193},{129,1},{193,65... | collective-permute-start | bytes 786440 | tf_op jit(solution)/shard_map/ppermute | solution.py:70
  147.8 3.1 %collective-permute-start.24 = (bf16[128,1024]{1,0:T(8,128)(2,1)S(1)}, bf16[128,1024]{1,0:T(8,128)(2,1)S(1)}, u32[]{:S(2)}, u32[]{:S(2)}) collective-permute-start(bf16[128,1024]{1,0:T(8,128)(2,1)S(1)} %get-tuple-element.25), channel_id=1, source_target_pairs={{0,64},{64,128},{128,192},{192,0},{1,65},{65,129},{129,193},{193,1... | collective-permute-start | bytes 786440 | tf_op jit(solution)/shard_map/ppermute | solution.py:70
  150.9 11.0 %collective-permute-done.27 = bf16[128,1024]{1,0:T(8,128)(2,1)S(1)} collective-permute-done((bf16[128,1024]{1,0:T(8,128)(2,1)S(1)}, bf16[128,1024]{1,0:T(8,128)(2,1)S(1)}, u32[]{:S(2)}, u32[]{:S(2)}) %collective-permute-start.27) | collective-permute-done | bytes 262176 | tf_op jit(solution)/shard_map/ppermute | solution.py:84
  (67 shorter events, 29.7 us)
Async XLA Ops:
  6.5 13.0 %copy-start.2 = (s32[2048]{0:T(1024)S(1)}, s32[2048]{0:T(1024)}, u32[]{:S(2)}) copy-start(s32[2048]{0:T(1024)} %param.6) | copy-start | bytes 24580
  6.5 15.0 %copy-start = (f32[4096]{0:T(1024)S(1)}, f32[4096]{0:T(1024)}, u32[]{:S(2)}) copy-start(f32[4096]{0:T(1024)} %param.9) | copy-start | bytes 49156
  6.5 15.0 %copy-start.3 = (s32[2048]{0:T(1024)S(1)}, s32[2048]{0:T(1024)}, u32[]{:S(2)}) copy-start(s32[2048]{0:T(1024)} %param.7) | copy-start | bytes 24580
  6.5 100.8 %all-gather.2.cloned.1.call-start = ((), (), s32[]{:S(2)}) async-start(), calls=%async_computation | async-start | bytes 4718592 | tf_op jit(solution)/shard_map/all_gather | solution.py:36
  9.1 24.4 %collective-permute-start.14 = (bf16[688,128]{1,0:T(8,128)(2,1)S(1)}, bf16[688,128]{1,0:T(8,128)(2,1)S(1)}, u32[]{:S(2)}, u32[]{:S(2)}) collective-permute-start(bf16[688,128]{1,0:T(8,128)(2,1)S(1)} %get-tuple-element.42), channel_id=1, source_target_pairs={{0,2},{2,4},{4,6},{6,7},{7,5},{5,3},{3,1},{1,0},{8,10},{10,12},{12... | collective-permute-start | bytes 528392 | tf_op jit(solution)/shard_map/ppermute | solution.py:44
  11.0 28.4 %collective-permute-start.7 = (bf16[688,128]{1,0:T(8,128)(2,1)S(1)}, bf16[688,128]{1,0:T(8,128)(2,1)S(1)}, u32[]{:S(2)}, u32[]{:S(2)}) collective-permute-start(bf16[688,128]{1,0:T(8,128)(2,1)S(1)} %get-tuple-element.39), channel_id=1, source_target_pairs={{0,2},{2,4},{4,6},{6,7},{7,5},{5,3},{3,1},{1,0},{8,10},{10,12},{12... | collective-permute-start | bytes 528392 | tf_op jit(solution)/shard_map/ppermute | solution.py:44
  14.6 12.8 %collective-permute-start = (bf16[672,128]{1,0:T(8,128)(2,1)S(1)}, bf16[672,128]{1,0:T(8,128)(2,1)S(1)}, u32[]{:S(2)}, u32[]{:S(2)}) collective-permute-start(bf16[672,128]{1,0:T(8,128)(2,1)S(1)} %get-tuple-element.37), channel_id=1, source_target_pairs={{0,2},{2,4},{4,6},{6,7},{7,5},{5,3},{3,1},{1,0},{8,10},{10,12},{12... | collective-permute-start | bytes 516104 | tf_op jit(solution)/shard_map/ppermute | solution.py:44
  27.4 15.9 %collective-permute-start.1 = (bf16[672,128]{1,0:T(8,128)(2,1)S(1)}, bf16[672,128]{1,0:T(8,128)(2,1)S(1)}, u32[]{:S(2)}, u32[]{:S(2)}) collective-permute-start(bf16[672,128]{1,0:T(8,128)(2,1)S(1)} %collective-permute-done), channel_id=1, source_target_pairs={{0,2},{2,4},{4,6},{6,7},{7,5},{5,3},{3,1},{1,0},{8,10},{10,12},{12... | collective-permute-start | bytes 516104 | tf_op jit(solution)/shard_map/ppermute | solution.py:44
  33.5 13.1 %collective-permute-start.15 = (bf16[688,128]{1,0:T(8,128)(2,1)S(1)}, bf16[688,128]{1,0:T(8,128)(2,1)S(1)}, u32[]{:S(2)}, u32[]{:S(2)}) collective-permute-start(bf16[688,128]{1,0:T(8,128)(2,1)S(1)} %collective-permute-done.14), channel_id=1, source_target_pairs={{0,2},{2,4},{4,6},{6,7},{7,5},{5,3},{3,1},{1,0},{8,10},{10,12},{12... | collective-permute-start | bytes 528392 | tf_op jit(solution)/shard_map/ppermute | solution.py:44
  39.4 10.2 %collective-permute-start.8 = (bf16[688,128]{1,0:T(8,128)(2,1)S(1)}, bf16[688,128]{1,0:T(8,128)(2,1)S(1)}, u32[]{:S(2)}, u32[]{:S(2)}) collective-permute-start(bf16[688,128]{1,0:T(8,128)(2,1)S(1)} %collective-permute-done.7), channel_id=1, source_target_pairs={{0,2},{2,4},{4,6},{6,7},{7,5},{5,3},{3,1},{1,0},{8,10},{10,12},{12... | collective-permute-start | bytes 528392 | tf_op jit(solution)/shard_map/ppermute | solution.py:44
  43.3 11.3 %collective-permute-start.2 = (bf16[672,128]{1,0:T(8,128)(2,1)S(1)}, bf16[672,128]{1,0:T(8,128)(2,1)S(1)}, u32[]{:S(2)}, u32[]{:S(2)}) collective-permute-start(bf16[672,128]{1,0:T(8,128)(2,1)S(1)} %collective-permute-done.1), channel_id=1, source_target_pairs={{0,2},{2,4},{4,6},{6,7},{7,5},{5,3},{3,1},{1,0},{8,10},{10,12},{12... | collective-permute-start | bytes 516104 | tf_op jit(solution)/shard_map/ppermute | solution.py:44
  46.7 11.7 %collective-permute-start.16 = (bf16[688,128]{1,0:T(8,128)(2,1)S(1)}, bf16[688,128]{1,0:T(8,128)(2,1)S(1)}, u32[]{:S(2)}, u32[]{:S(2)}) collective-permute-start(bf16[688,128]{1,0:T(8,128)(2,1)S(1)} %collective-permute-done.15), channel_id=1, source_target_pairs={{0,2},{2,4},{4,6},{6,7},{7,5},{5,3},{3,1},{1,0},{8,10},{10,12},{12... | collective-permute-start | bytes 528392 | tf_op jit(solution)/shard_map/ppermute | solution.py:44
  49.6 12.5 %collective-permute-start.9 = (bf16[688,128]{1,0:T(8,128)(2,1)S(1)}, bf16[688,128]{1,0:T(8,128)(2,1)S(1)}, u32[]{:S(2)}, u32[]{:S(2)}) collective-permute-start(bf16[688,128]{1,0:T(8,128)(2,1)S(1)} %collective-permute-done.8), channel_id=1, source_target_pairs={{0,2},{2,4},{4,6},{6,7},{7,5},{5,3},{3,1},{1,0},{8,10},{10,12},{12... | collective-permute-start | bytes 528392 | tf_op jit(solution)/shard_map/ppermute | solution.py:44
  54.6 11.3 %collective-permute-start.3 = (bf16[672,128]{1,0:T(8,128)(2,1)S(1)}, bf16[672,128]{1,0:T(8,128)(2,1)S(1)}, u32[]{:S(2)}, u32[]{:S(2)}) collective-permute-start(bf16[672,128]{1,0:T(8,128)(2,1)S(1)} %collective-permute-done.2), channel_id=1, source_target_pairs={{0,2},{2,4},{4,6},{6,7},{7,5},{5,3},{3,1},{1,0},{8,10},{10,12},{12... | collective-permute-start | bytes 516104 | tf_op jit(solution)/shard_map/ppermute | solution.py:44
  58.4 12.1 %collective-permute-start.17 = (bf16[688,128]{1,0:T(8,128)(2,1)S(1)}, bf16[688,128]{1,0:T(8,128)(2,1)S(1)}, u32[]{:S(2)}, u32[]{:S(2)}) collective-permute-start(bf16[688,128]{1,0:T(8,128)(2,1)S(1)} %collective-permute-done.16), channel_id=1, source_target_pairs={{0,2},{2,4},{4,6},{6,7},{7,5},{5,3},{3,1},{1,0},{8,10},{10,12},{12... | collective-permute-start | bytes 528392 | tf_op jit(solution)/shard_map/ppermute | solution.py:44
  62.2 12.8 %collective-permute-start.10 = (bf16[688,128]{1,0:T(8,128)(2,1)S(1)}, bf16[688,128]{1,0:T(8,128)(2,1)S(1)}, u32[]{:S(2)}, u32[]{:S(2)}) collective-permute-start(bf16[688,128]{1,0:T(8,128)(2,1)S(1)} %collective-permute-done.9), channel_id=1, source_target_pairs={{0,2},{2,4},{4,6},{6,7},{7,5},{5,3},{3,1},{1,0},{8,10},{10,12},{12... | collective-permute-start | bytes 528392 | tf_op jit(solution)/shard_map/ppermute | solution.py:44
  65.9 11.8 %collective-permute-start.4 = (bf16[672,128]{1,0:T(8,128)(2,1)S(1)}, bf16[672,128]{1,0:T(8,128)(2,1)S(1)}, u32[]{:S(2)}, u32[]{:S(2)}) collective-permute-start(bf16[672,128]{1,0:T(8,128)(2,1)S(1)} %collective-permute-done.3), channel_id=1, source_target_pairs={{0,2},{2,4},{4,6},{6,7},{7,5},{5,3},{3,1},{1,0},{8,10},{10,12},{12... | collective-permute-start | bytes 516104 | tf_op jit(solution)/shard_map/ppermute | solution.py:44
  70.5 11.3 %collective-permute-start.18 = (bf16[688,128]{1,0:T(8,128)(2,1)S(1)}, bf16[688,128]{1,0:T(8,128)(2,1)S(1)}, u32[]{:S(2)}, u32[]{:S(2)}) collective-permute-start(bf16[688,128]{1,0:T(8,128)(2,1)S(1)} %collective-permute-done.17), channel_id=1, source_target_pairs={{0,2},{2,4},{4,6},{6,7},{7,5},{5,3},{3,1},{1,0},{8,10},{10,12},{12... | collective-permute-start | bytes 528392 | tf_op jit(solution)/shard_map/ppermute | solution.py:44
  75.0 11.4 %collective-permute-start.11 = (bf16[688,128]{1,0:T(8,128)(2,1)S(1)}, bf16[688,128]{1,0:T(8,128)(2,1)S(1)}, u32[]{:S(2)}, u32[]{:S(2)}) collective-permute-start(bf16[688,128]{1,0:T(8,128)(2,1)S(1)} %collective-permute-done.10), channel_id=1, source_target_pairs={{0,2},{2,4},{4,6},{6,7},{7,5},{5,3},{3,1},{1,0},{8,10},{10,12},{12... | collective-permute-start | bytes 528392 | tf_op jit(solution)/shard_map/ppermute | solution.py:44
  77.7 12.2 %collective-permute-start.5 = (bf16[672,128]{1,0:T(8,128)(2,1)S(1)}, bf16[672,128]{1,0:T(8,128)(2,1)S(1)}, u32[]{:S(2)}, u32[]{:S(2)}) collective-permute-start(bf16[672,128]{1,0:T(8,128)(2,1)S(1)} %collective-permute-done.4), channel_id=1, source_target_pairs={{0,2},{2,4},{4,6},{6,7},{7,5},{5,3},{3,1},{1,0},{8,10},{10,12},{12... | collective-permute-start | bytes 516104 | tf_op jit(solution)/shard_map/ppermute | solution.py:44
  81.7 12.1 %collective-permute-start.19 = (bf16[688,128]{1,0:T(8,128)(2,1)S(1)}, bf16[688,128]{1,0:T(8,128)(2,1)S(1)}, u32[]{:S(2)}, u32[]{:S(2)}) collective-permute-start(bf16[688,128]{1,0:T(8,128)(2,1)S(1)} %collective-permute-done.18), channel_id=1, source_target_pairs={{0,2},{2,4},{4,6},{6,7},{7,5},{5,3},{3,1},{1,0},{8,10},{10,12},{12... | collective-permute-start | bytes 528392 | tf_op jit(solution)/shard_map/ppermute | solution.py:44
  86.4 11.4 %collective-permute-start.12 = (bf16[688,128]{1,0:T(8,128)(2,1)S(1)}, bf16[688,128]{1,0:T(8,128)(2,1)S(1)}, u32[]{:S(2)}, u32[]{:S(2)}) collective-permute-start(bf16[688,128]{1,0:T(8,128)(2,1)S(1)} %collective-permute-done.11), channel_id=1, source_target_pairs={{0,2},{2,4},{4,6},{6,7},{7,5},{5,3},{3,1},{1,0},{8,10},{10,12},{12... | collective-permute-start | bytes 528392 | tf_op jit(solution)/shard_map/ppermute | solution.py:44
  89.9 11.8 %collective-permute-start.6 = (bf16[672,128]{1,0:T(8,128)(2,1)S(1)}, bf16[672,128]{1,0:T(8,128)(2,1)S(1)}, u32[]{:S(2)}, u32[]{:S(2)}) collective-permute-start(bf16[672,128]{1,0:T(8,128)(2,1)S(1)} %collective-permute-done.5), channel_id=1, source_target_pairs={{0,2},{2,4},{4,6},{6,7},{7,5},{5,3},{3,1},{1,0},{8,10},{10,12},{12... | collective-permute-start | bytes 516104 | tf_op jit(solution)/shard_map/ppermute | solution.py:44
  93.8 9.9 %collective-permute-start.20 = (bf16[688,128]{1,0:T(8,128)(2,1)S(1)}, bf16[688,128]{1,0:T(8,128)(2,1)S(1)}, u32[]{:S(2)}, u32[]{:S(2)}) collective-permute-start(bf16[688,128]{1,0:T(8,128)(2,1)S(1)} %collective-permute-done.19), channel_id=1, source_target_pairs={{0,2},{2,4},{4,6},{6,7},{7,5},{5,3},{3,1},{1,0},{8,10},{10,12},{12... | collective-permute-start | bytes 528392 | tf_op jit(solution)/shard_map/ppermute | solution.py:44
  97.8 9.4 %collective-permute-start.13 = (bf16[688,128]{1,0:T(8,128)(2,1)S(1)}, bf16[688,128]{1,0:T(8,128)(2,1)S(1)}, u32[]{:S(2)}, u32[]{:S(2)}) collective-permute-start(bf16[688,128]{1,0:T(8,128)(2,1)S(1)} %collective-permute-done.12), channel_id=1, source_target_pairs={{0,2},{2,4},{4,6},{6,7},{7,5},{5,3},{3,1},{1,0},{8,10},{10,12},{12... | collective-permute-start | bytes 528392 | tf_op jit(solution)/shard_map/ppermute | solution.py:44
  115.4 10.2 %collective-permute-start.23 = (bf16[128,1024]{1,0:T(8,128)(2,1)S(1)}, bf16[128,1024]{1,0:T(8,128)(2,1)S(1)}, u32[]{:S(2)}, u32[]{:S(2)}) collective-permute-start(bf16[128,1024]{1,0:T(8,128)(2,1)S(1)} %get-tuple-element.21), channel_id=1, source_target_pairs={{0,192},{64,0},{128,64},{192,128},{1,193},{65,1},{129,65},{193,129... | collective-permute-start | bytes 786440 | tf_op jit(solution)/shard_map/ppermute | solution.py:70
  120.1 9.8 %collective-permute-start.22 = (bf16[128,1024]{1,0:T(8,128)(2,1)S(1)}, bf16[128,1024]{1,0:T(8,128)(2,1)S(1)}, u32[]{:S(2)}, u32[]{:S(2)}) collective-permute-start(bf16[128,1024]{1,0:T(8,128)(2,1)S(1)} %get-tuple-element.20), channel_id=1, source_target_pairs={{0,128},{64,192},{128,0},{192,64},{1,129},{65,193},{129,1},{193,65... | collective-permute-start | bytes 786440 | tf_op jit(solution)/shard_map/ppermute | solution.py:70
  122.8 9.9 %collective-permute-start.21 = (bf16[128,1024]{1,0:T(8,128)(2,1)S(1)}, bf16[128,1024]{1,0:T(8,128)(2,1)S(1)}, u32[]{:S(2)}, u32[]{:S(2)}) collective-permute-start(bf16[128,1024]{1,0:T(8,128)(2,1)S(1)} %get-tuple-element.19), channel_id=1, source_target_pairs={{0,64},{64,128},{128,192},{192,0},{1,65},{65,129},{129,193},{193,1... | collective-permute-start | bytes 786440 | tf_op jit(solution)/shard_map/ppermute | solution.py:70
  132.8 29.1 %collective-permute-start.27 = (bf16[128,1024]{1,0:T(8,128)(2,1)S(1)}, bf16[128,1024]{1,0:T(8,128)(2,1)S(1)}, u32[]{:S(2)}, u32[]{:S(2)}) collective-permute-start(bf16[128,1024]{1,0:T(8,128)(2,1)S(1)} %add_convert_fusion), channel_id=1, source_target_pairs={{0,256},{256,0},{1,257},{257,1},{2,258},{258,2},{3,259},{259,3},{4... | collective-permute-start | bytes 786440 | tf_op jit(solution)/shard_map/ppermute | solution.py:84
  142.6 19.3 %collective-permute-start.26 = (bf16[128,1024]{1,0:T(8,128)(2,1)S(1)}, bf16[128,1024]{1,0:T(8,128)(2,1)S(1)}, u32[]{:S(2)}, u32[]{:S(2)}) collective-permute-start(bf16[128,1024]{1,0:T(8,128)(2,1)S(1)} %get-tuple-element.27), channel_id=1, source_target_pairs={{0,192},{64,0},{128,64},{192,128},{1,193},{65,1},{129,65},{193,129... | collective-permute-start | bytes 786440 | tf_op jit(solution)/shard_map/ppermute | solution.py:70
  145.0 16.8 %collective-permute-start.25 = (bf16[128,1024]{1,0:T(8,128)(2,1)S(1)}, bf16[128,1024]{1,0:T(8,128)(2,1)S(1)}, u32[]{:S(2)}, u32[]{:S(2)}) collective-permute-start(bf16[128,1024]{1,0:T(8,128)(2,1)S(1)} %get-tuple-element.26), channel_id=1, source_target_pairs={{0,128},{64,192},{128,0},{192,64},{1,129},{65,193},{129,1},{193,65... | collective-permute-start | bytes 786440 | tf_op jit(solution)/shard_map/ppermute | solution.py:70
  147.8 14.1 %collective-permute-start.24 = (bf16[128,1024]{1,0:T(8,128)(2,1)S(1)}, bf16[128,1024]{1,0:T(8,128)(2,1)S(1)}, u32[]{:S(2)}, u32[]{:S(2)}) collective-permute-start(bf16[128,1024]{1,0:T(8,128)(2,1)S(1)} %get-tuple-element.25), channel_id=1, source_target_pairs={{0,64},{64,128},{128,192},{192,0},{1,65},{65,129},{129,193},{193,1... | collective-permute-start | bytes 786440 | tf_op jit(solution)/shard_map/ppermute | solution.py:70
  (1 other events, 13.0 us)
Sparse Core Ops, SparseCore 0:
  9.5 46.1 all-gather.1

commit v6 on v5

--- a/solution.py
+++ b/solution.py
@@ -22,8 +22,17 @@
 
 
 def lookup(indices, table):
-    hits = indices[:, None] == jnp.arange(table.shape[0], dtype=jnp.int32)[None, :]
-    return jnp.sum(jnp.where(hits, table[None, :], jnp.float32(0.0)), axis=1)
+    width = 64
+    lines = -(-table.shape[0] // width)
+    grid = jnp.pad(table, (0, lines * width - table.shape[0])).reshape(lines, width)
+    high = lax.reduce_precision(grid, 8, 7)
+    middle = lax.reduce_precision(grid - high, 8, 7)
+    parts = jnp.concatenate([high, middle, grid - high - middle], axis=1).astype(jnp.bfloat16)
+    column = indices[:, None]
+    line_hits = (column // width == jnp.arange(lines, dtype=jnp.int32)).astype(jnp.bfloat16)
+    picked = jnp.dot(line_hits, parts, preferred_element_type=jnp.float32)
+    hits = column % width == jnp.arange(3 * width, dtype=jnp.int32) % width
+    return jnp.sum(jnp.where(hits, picked, 0.0), axis=1, keepdims=True)
 
 
 def place(col, n):
@@ -37,23 +46,32 @@
 
     order = circle(n_z)
     step = [(order[i], order[(i + 1) % n_z]) for i in range(n_z)]
-    chunks = cut(pair_elements, 3)
+    chunks = list(lax.optimization_barrier(cut(pair_elements, 3)))
     arrived = [[chunk] for chunk in chunks]
     for _ in range(n_z - 1):
         for i in range(len(chunks)):
             chunks[i] = lax.ppermute(chunks[i], "zl", step)
             arrived[i].append(chunks[i])
-    rows = jnp.concatenate([jnp.concatenate(one, axis=1) for one in arrived], axis=0)
+    pair_gap = lookup(valence_of, valence_depth) + lookup(conduction_of, conduction_height)
+    factors = cut(lax.optimization_barrier(-4.0 / pair_gap), len(chunks))
 
-    pair_gap = lookup(valence_of, valence_depth) + lookup(conduction_of, conduction_height)
-    factor = -4.0 / pair_gap
-    weighted = (rows.astype(jnp.float32) * factor[:, None]).astype(jnp.bfloat16)
+    def weighted(one, factor):
+        return (one.astype(jnp.float32) * factor).astype(jnp.bfloat16)
+
+    rows = jnp.zeros((n_pair, n_z * n_g), jnp.bfloat16)
+    for turn in range(n_z):
+        first = 0
+        for pieces, factor in zip(arrived, factors):
+            piece = weighted(pieces[turn], factor)
+            rows = lax.dynamic_update_slice(rows, piece, (first, turn * n_g))
+            first += piece.shape[0]
+    rows = lax.optimization_barrier(rows)
 
     my_half, my_x = lax.axis_index("zh"), lax.axis_index("x")
     mine_at = place(lax.axis_index("zl"), n_z)
 
     partial = lax.dot_general(
-        weighted, columns, (((0,), (0,)), ((), ())), preferred_element_type=jnp.float32
+        rows, columns, (((0,), (0,)), ((), ())), preferred_element_type=jnp.float32
     ).reshape(n_z, n_g, -1)
 
     def blocks(half):
@@ -81,8 +99,8 @@
     )
     given = added(given, over_x(given_sent)).astype(jnp.bfloat16)
     given, kept_sent = lax.optimization_barrier((given, kept_sent))
-    got = lax.ppermute(given, "zh", shift(2, 1))
-    total = added(kept, over_x(kept_sent)) + got.astype(jnp.float32)
+    got = lax.ppermute(given, "zh", shift(2, 1)).astype(jnp.float32)
+    total = added(kept + got, over_x(kept_sent))
     return total.reshape(1, n_g, -1, n_g)
 
 

time: 171 us -> 174 us (1.018)
  the two profiles are of different devices: /device:TPU:120 before, /device:TPU:112 now
where the time goes in v6:
time: 174 us; the launch traced here: 173 us
  starting transfers between devices  102 us (59%)
  other arithmetic  20.9 us (12%)
  waiting for transfers between devices  19.5 us (11%)
  between operations  14.2 us (8%)
  matrix products  9.2 us (5%)
  local copies, waits for them, and re-layouts  7.37 us (4%)
    ppermute x21, starting transfers between devices, body(): chunks[i] = lax.ppermute(chunks[i], 'zl', step)  69.9 us
    ppermute x6, starting transfers between devices, over_x(): lax.ppermute(one, 'x', shift(n_x, s))  21.5 us
    dynamic_update_slice x23, other arithmetic, body(): rows = lax.dynamic_update_slice(rows, piece, (first, turn * n_g))  19.6 us
    ppermute x1, starting transfers between devices, body(): got = lax.ppermute(given, 'zh', shift(2, 1)).astype(jnp.float32)  10.9 us
    ppermute x1, waiting for transfers between devices, body(): got = lax.ppermute(given, 'zh', shift(2, 1)).astype(jnp.float32)  8.12 us
    dot_general x1, matrix products, body(): lax.dot_general(rows, columns, (((0,), (0,)), ((), ())), preferred_elemen...  7.58 us
    ppermute x21, waiting for transfers between devices, body(): chunks[i] = lax.ppermute(chunks[i], 'zl', step)  5.76 us
    ppermute x6, waiting for transfers between devices, over_x(): lax.ppermute(one, 'x', shift(n_x, s))  4.91 us
  transfers between devices with their start and end apart: 29, of which 7 were waited for; matrix products, arithmetic and copies ran while one was open for 16% of the time, Pallas kernels for 0%

profile of v6, /device:TPU:112, one launch (start us, length us, event | category | flops | bytes accessed | tf_op | source)
XLA Modules:
  0.0 173.5 jit_solution(9283747837863506364)
XLA Ops:
  9.2 1.9 %collective-permute-start = (bf16[672,128]{1,0:T(8,128)(2,1)S(1)}, bf16[672,128]{1,0:T(8,128)(2,1)S(1)}, u32[]{:S(2)}, u32[]{:S(2)}) collective-permute-start(bf16[672,128]{1,0:T(8,128)(2,1)S(1)} %slice.18), channel_id=1, source_target_pairs={{0,2},{2,4},{4,6},{6,7},{7,5},{5,3},{3,1},{1,0},{8,10},{10,12},{12... | collective-permute-start | bytes 516104 | tf_op jit(solution)/shard_map/ppermute | solution.py:53
  11.2 1.9 %collective-permute-start.1 = (bf16[688,128]{1,0:T(8,128)(2,1)S(1)}, bf16[688,128]{1,0:T(8,128)(2,1)S(1)}, u32[]{:S(2)}, u32[]{:S(2)}) collective-permute-start(bf16[688,128]{1,0:T(8,128)(2,1)S(1)} %get-tuple-element.21), channel_id=1, source_target_pairs={{0,2},{2,4},{4,6},{6,7},{7,5},{5,3},{3,1},{1,0},{8,10},{10,12},{12... | collective-permute-start | bytes 528392 | tf_op jit(solution)/shard_map/ppermute | solution.py:53
  13.1 4.9 %collective-permute-start.2 = (bf16[688,128]{1,0:T(8,128)(2,1)S(1)}, bf16[688,128]{1,0:T(8,128)(2,1)S(1)}, u32[]{:S(2)}, u32[]{:S(2)}) collective-permute-start(bf16[688,128]{1,0:T(8,128)(2,1)S(1)} %get-tuple-element.22), channel_id=1, source_target_pairs={{0,2},{2,4},{4,6},{6,7},{7,5},{5,3},{3,1},{1,0},{8,10},{10,12},{12... | collective-permute-start | bytes 528392 | tf_op jit(solution)/shard_map/ppermute | solution.py:53
  22.6 2.5 %dynamic_update_slice.72 = bf16[2048,1024]{1,0:T(8,128)(2,1)} pad(bf16[672,128]{1,0:T(8,128)(2,1)S(1)} %multiply_convert_fusion.23, bf16[]{:T(256)} %constant.297.clone.1), padding=0_1376x0_896 | pad | bytes 4366338 | tf_op jit(solution)/shard_map/dynamic_update_slice | solution.py:66
  26.9 6.4 %collective-permute-start.3 = (bf16[672,128]{1,0:T(8,128)(2,1)S(1)}, bf16[672,128]{1,0:T(8,128)(2,1)S(1)}, u32[]{:S(2)}, u32[]{:S(2)}) collective-permute-start(bf16[672,128]{1,0:T(8,128)(2,1)S(1)} %collective-permute-done), channel_id=1, source_target_pairs={{0,2},{2,4},{4,6},{6,7},{7,5},{5,3},{3,1},{1,0},{8,10},{10,12},{12... | collective-permute-start | bytes 516104 | tf_op jit(solution)/shard_map/ppermute | solution.py:53
  34.2 5.2 %collective-permute-start.4 = (bf16[688,128]{1,0:T(8,128)(2,1)S(1)}, bf16[688,128]{1,0:T(8,128)(2,1)S(1)}, u32[]{:S(2)}, u32[]{:S(2)}) collective-permute-start(bf16[688,128]{1,0:T(8,128)(2,1)S(1)} %collective-permute-done.1), channel_id=1, source_target_pairs={{0,2},{2,4},{4,6},{6,7},{7,5},{5,3},{3,1},{1,0},{8,10},{10,12},{12... | collective-permute-start | bytes 528392 | tf_op jit(solution)/shard_map/ppermute | solution.py:53
  39.3 3.8 %collective-permute-start.5 = (bf16[688,128]{1,0:T(8,128)(2,1)S(1)}, bf16[688,128]{1,0:T(8,128)(2,1)S(1)}, u32[]{:S(2)}, u32[]{:S(2)}) collective-permute-start(bf16[688,128]{1,0:T(8,128)(2,1)S(1)} %collective-permute-done.2), channel_id=1, source_target_pairs={{0,2},{2,4},{4,6},{6,7},{7,5},{5,3},{3,1},{1,0},{8,10},{10,12},{12... | collective-permute-start | bytes 528392 | tf_op jit(solution)/shard_map/ppermute | solution.py:53
  44.9 1.9 %collective-permute-start.6 = (bf16[672,128]{1,0:T(8,128)(2,1)S(1)}, bf16[672,128]{1,0:T(8,128)(2,1)S(1)}, u32[]{:S(2)}, u32[]{:S(2)}) collective-permute-start(bf16[672,128]{1,0:T(8,128)(2,1)S(1)} %collective-permute-done.3), channel_id=1, source_target_pairs={{0,2},{2,4},{4,6},{6,7},{7,5},{5,3},{3,1},{1,0},{8,10},{10,12},{12... | collective-permute-start | bytes 516104 | tf_op jit(solution)/shard_map/ppermute | solution.py:53
  47.7 1.9 %collective-permute-start.7 = (bf16[688,128]{1,0:T(8,128)(2,1)S(1)}, bf16[688,128]{1,0:T(8,128)(2,1)S(1)}, u32[]{:S(2)}, u32[]{:S(2)}) collective-permute-start(bf16[688,128]{1,0:T(8,128)(2,1)S(1)} %collective-permute-done.4), channel_id=1, source_target_pairs={{0,2},{2,4},{4,6},{6,7},{7,5},{5,3},{3,1},{1,0},{8,10},{10,12},{12... | collective-permute-start | bytes 528392 | tf_op jit(solution)/shard_map/ppermute | solution.py:53
  49.6 2.8 %collective-permute-start.8 = (bf16[688,128]{1,0:T(8,128)(2,1)S(1)}, bf16[688,128]{1,0:T(8,128)(2,1)S(1)}, u32[]{:S(2)}, u32[]{:S(2)}) collective-permute-start(bf16[688,128]{1,0:T(8,128)(2,1)S(1)} %collective-permute-done.5), channel_id=1, source_target_pairs={{0,2},{2,4},{4,6},{6,7},{7,5},{5,3},{3,1},{1,0},{8,10},{10,12},{12... | collective-permute-start | bytes 528392 | tf_op jit(solution)/shard_map/ppermute | solution.py:53
  54.1 2.0 %collective-permute-done.6 = bf16[672,128]{1,0:T(8,128)(2,1)S(1)} collective-permute-done((bf16[672,128]{1,0:T(8,128)(2,1)S(1)}, bf16[672,128]{1,0:T(8,128)(2,1)S(1)}, u32[]{:S(2)}, u32[]{:S(2)}) %collective-permute-start.6) | collective-permute-done | bytes 172064 | tf_op jit(solution)/shard_map/ppermute | solution.py:53
  56.1 1.9 %collective-permute-start.9 = (bf16[672,128]{1,0:T(8,128)(2,1)S(1)}, bf16[672,128]{1,0:T(8,128)(2,1)S(1)}, u32[]{:S(2)}, u32[]{:S(2)}) collective-permute-start(bf16[672,128]{1,0:T(8,128)(2,1)S(1)} %collective-permute-done.6), channel_id=1, source_target_pairs={{0,2},{2,4},{4,6},{6,7},{7,5},{5,3},{3,1},{1,0},{8,10},{10,12},{12... | collective-permute-start | bytes 516104 | tf_op jit(solution)/shard_map/ppermute | solution.py:53
  63.7 2.9 %collective-permute-start.11 = (bf16[688,128]{1,0:T(8,128)(2,1)S(1)}, bf16[688,128]{1,0:T(8,128)(2,1)S(1)}, u32[]{:S(2)}, u32[]{:S(2)}) collective-permute-start(bf16[688,128]{1,0:T(8,128)(2,1)S(1)} %collective-permute-done.8), channel_id=1, source_target_pairs={{0,2},{2,4},{4,6},{6,7},{7,5},{5,3},{3,1},{1,0},{8,10},{10,12},{12... | collective-permute-start | bytes 528392 | tf_op jit(solution)/shard_map/ppermute | solution.py:53
  68.3 5.2 %collective-permute-start.12 = (bf16[672,128]{1,0:T(8,128)(2,1)S(1)}, bf16[672,128]{1,0:T(8,128)(2,1)S(1)}, u32[]{:S(2)}, u32[]{:S(2)}) collective-permute-start(bf16[672,128]{1,0:T(8,128)(2,1)S(1)} %collective-permute-done.9), channel_id=1, source_target_pairs={{0,2},{2,4},{4,6},{6,7},{7,5},{5,3},{3,1},{1,0},{8,10},{10,12},{12... | collective-permute-start | bytes 516104 | tf_op jit(solution)/shard_map/ppermute | solution.py:53
  74.3 3.8 %collective-permute-start.13 = (bf16[688,128]{1,0:T(8,128)(2,1)S(1)}, bf16[688,128]{1,0:T(8,128)(2,1)S(1)}, u32[]{:S(2)}, u32[]{:S(2)}) collective-permute-start(bf16[688,128]{1,0:T(8,128)(2,1)S(1)} %collective-permute-done.10), channel_id=1, source_target_pairs={{0,2},{2,4},{4,6},{6,7},{7,5},{5,3},{3,1},{1,0},{8,10},{10,12},{12... | collective-permute-start | bytes 528392 | tf_op jit(solution)/shard_map/ppermute | solution.py:53
  78.2 1.9 %collective-permute-start.14 = (bf16[688,128]{1,0:T(8,128)(2,1)S(1)}, bf16[688,128]{1,0:T(8,128)(2,1)S(1)}, u32[]{:S(2)}, u32[]{:S(2)}) collective-permute-start(bf16[688,128]{1,0:T(8,128)(2,1)S(1)} %collective-permute-done.11), channel_id=1, source_target_pairs={{0,2},{2,4},{4,6},{6,7},{7,5},{5,3},{3,1},{1,0},{8,10},{10,12},{12... | collective-permute-start | bytes 528392 | tf_op jit(solution)/shard_map/ppermute | solution.py:53
  81.8 2.2 %collective-permute-start.15 = (bf16[672,128]{1,0:T(8,128)(2,1)S(1)}, bf16[672,128]{1,0:T(8,128)(2,1)S(1)}, u32[]{:S(2)}, u32[]{:S(2)}) collective-permute-start(bf16[672,128]{1,0:T(8,128)(2,1)S(1)} %collective-permute-done.12), channel_id=1, source_target_pairs={{0,2},{2,4},{4,6},{6,7},{7,5},{5,3},{3,1},{1,0},{8,10},{10,12},{12... | collective-permute-start | bytes 516104 | tf_op jit(solution)/shard_map/ppermute | solution.py:53
  84.9 4.7 %collective-permute-start.16 = (bf16[688,128]{1,0:T(8,128)(2,1)S(1)}, bf16[688,128]{1,0:T(8,128)(2,1)S(1)}, u32[]{:S(2)}, u32[]{:S(2)}) collective-permute-start(bf16[688,128]{1,0:T(8,128)(2,1)S(1)} %collective-permute-done.13), channel_id=1, source_target_pairs={{0,2},{2,4},{4,6},{6,7},{7,5},{5,3},{3,1},{1,0},{8,10},{10,12},{12... | collective-permute-start | bytes 528392 | tf_op jit(solution)/shard_map/ppermute | solution.py:53
  89.6 3.8 %collective-permute-start.17 = (bf16[688,128]{1,0:T(8,128)(2,1)S(1)}, bf16[688,128]{1,0:T(8,128)(2,1)S(1)}, u32[]{:S(2)}, u32[]{:S(2)}) collective-permute-start(bf16[688,128]{1,0:T(8,128)(2,1)S(1)} %collective-permute-done.14), channel_id=1, source_target_pairs={{0,2},{2,4},{4,6},{6,7},{7,5},{5,3},{3,1},{1,0},{8,10},{10,12},{12... | collective-permute-start | bytes 528392 | tf_op jit(solution)/shard_map/ppermute | solution.py:53
  95.1 2.7 %collective-permute-start.18 = (bf16[672,128]{1,0:T(8,128)(2,1)S(1)}, bf16[672,128]{1,0:T(8,128)(2,1)S(1)}, u32[]{:S(2)}, u32[]{:S(2)}) collective-permute-start(bf16[672,128]{1,0:T(8,128)(2,1)S(1)} %collective-permute-done.15), channel_id=1, source_target_pairs={{0,2},{2,4},{4,6},{6,7},{7,5},{5,3},{3,1},{1,0},{8,10},{10,12},{12... | collective-permute-start | bytes 516104 | tf_op jit(solution)/shard_map/ppermute | solution.py:53
  98.7 2.9 %collective-permute-start.19 = (bf16[688,128]{1,0:T(8,128)(2,1)S(1)}, bf16[688,128]{1,0:T(8,128)(2,1)S(1)}, u32[]{:S(2)}, u32[]{:S(2)}) collective-permute-start(bf16[688,128]{1,0:T(8,128)(2,1)S(1)} %collective-permute-done.16), channel_id=1, source_target_pairs={{0,2},{2,4},{4,6},{6,7},{7,5},{5,3},{3,1},{1,0},{8,10},{10,12},{12... | collective-permute-start | bytes 528392 | tf_op jit(solution)/shard_map/ppermute | solution.py:53
  101.6 5.2 %collective-permute-start.20 = (bf16[688,128]{1,0:T(8,128)(2,1)S(1)}, bf16[688,128]{1,0:T(8,128)(2,1)S(1)}, u32[]{:S(2)}, u32[]{:S(2)}) collective-permute-start(bf16[688,128]{1,0:T(8,128)(2,1)S(1)} %collective-permute-done.17), channel_id=1, source_target_pairs={{0,2},{2,4},{4,6},{6,7},{7,5},{5,3},{3,1},{1,0},{8,10},{10,12},{12... | collective-permute-start | bytes 528392 | tf_op jit(solution)/shard_map/ppermute | solution.py:53
  111.9 7.6 %fusion.52 = f32[1024,1024]{1,0:T(8,128)S(1)} fusion(bf16[2048,1024]{1,0:T(8,128)(2,1)} %fusion.25, bf16[2048,1024]{1,0:T(8,128)(2,1)} %all-gather.2.cloned.1.call-done), kind=kOutput, calls=%fused_computation.115 | convolution fusion | flops 4294967296 | bytes 12582912 | tf_op jit(solution)/shard_map/dot_general | solution.py:73
  119.8 3.4 %collective-permute-start.21 = (bf16[128,1024]{1,0:T(8,128)(2,1)S(1)}, bf16[128,1024]{1,0:T(8,128)(2,1)S(1)}, u32[]{:S(2)}, u32[]{:S(2)}) collective-permute-start(bf16[128,1024]{1,0:T(8,128)(2,1)S(1)} %get-tuple-element.25), channel_id=1, source_target_pairs={{0,64},{64,128},{128,192},{192,0},{1,65},{65,129},{129,193},{193,1... | collective-permute-start | bytes 786440 | tf_op jit(solution)/shard_map/ppermute | solution.py:88
  123.3 4.6 %collective-permute-start.22 = (bf16[128,1024]{1,0:T(8,128)(2,1)S(1)}, bf16[128,1024]{1,0:T(8,128)(2,1)S(1)}, u32[]{:S(2)}, u32[]{:S(2)}) collective-permute-start(bf16[128,1024]{1,0:T(8,128)(2,1)S(1)} %get-tuple-element.26), channel_id=1, source_target_pairs={{0,128},{64,192},{128,0},{192,64},{1,129},{65,193},{129,1},{193,65... | collective-permute-start | bytes 786440 | tf_op jit(solution)/shard_map/ppermute | solution.py:88
  127.9 3.3 %collective-permute-start.23 = (bf16[128,1024]{1,0:T(8,128)(2,1)S(1)}, bf16[128,1024]{1,0:T(8,128)(2,1)S(1)}, u32[]{:S(2)}, u32[]{:S(2)}) collective-permute-start(bf16[128,1024]{1,0:T(8,128)(2,1)S(1)} %get-tuple-element.27), channel_id=1, source_target_pairs={{0,192},{64,0},{128,64},{192,128},{1,193},{65,1},{129,65},{193,129... | collective-permute-start | bytes 786440 | tf_op jit(solution)/shard_map/ppermute | solution.py:88
  133.1 3.0 %collective-permute-done.23 = bf16[128,1024]{1,0:T(8,128)(2,1)S(1)} collective-permute-done((bf16[128,1024]{1,0:T(8,128)(2,1)S(1)}, bf16[128,1024]{1,0:T(8,128)(2,1)S(1)}, u32[]{:S(2)}, u32[]{:S(2)}) %collective-permute-start.23) | collective-permute-done | bytes 262176 | tf_op jit(solution)/shard_map/ppermute | solution.py:88
  136.3 10.9 %collective-permute-start.24 = (bf16[128,1024]{1,0:T(8,128)(2,1)S(1)}, bf16[128,1024]{1,0:T(8,128)(2,1)S(1)}, u32[]{:S(2)}, u32[]{:S(2)}) collective-permute-start(bf16[128,1024]{1,0:T(8,128)(2,1)S(1)} %add_convert_fusion), channel_id=1, source_target_pairs={{0,256},{256,0},{1,257},{257,1},{2,258},{258,2},{3,259},{259,3},{4... | collective-permute-start | bytes 786440 | tf_op jit(solution)/shard_map/ppermute | solution.py:102
  147.2 3.1 %collective-permute-start.25 = (bf16[128,1024]{1,0:T(8,128)(2,1)S(1)}, bf16[128,1024]{1,0:T(8,128)(2,1)S(1)}, u32[]{:S(2)}, u32[]{:S(2)}) collective-permute-start(bf16[128,1024]{1,0:T(8,128)(2,1)S(1)} %get-tuple-element.32), channel_id=1, source_target_pairs={{0,64},{64,128},{128,192},{192,0},{1,65},{65,129},{129,193},{193,1... | collective-permute-start | bytes 786440 | tf_op jit(solution)/shard_map/ppermute | solution.py:88
  150.3 4.9 %collective-permute-start.26 = (bf16[128,1024]{1,0:T(8,128)(2,1)S(1)}, bf16[128,1024]{1,0:T(8,128)(2,1)S(1)}, u32[]{:S(2)}, u32[]{:S(2)}) collective-permute-start(bf16[128,1024]{1,0:T(8,128)(2,1)S(1)} %get-tuple-element.33), channel_id=1, source_target_pairs={{0,128},{64,192},{128,0},{192,64},{1,129},{65,193},{129,1},{193,65... | collective-permute-start | bytes 786440 | tf_op jit(solution)/shard_map/ppermute | solution.py:88
  155.2 2.2 %collective-permute-start.27 = (bf16[128,1024]{1,0:T(8,128)(2,1)S(1)}, bf16[128,1024]{1,0:T(8,128)(2,1)S(1)}, u32[]{:S(2)}, u32[]{:S(2)}) collective-permute-start(bf16[128,1024]{1,0:T(8,128)(2,1)S(1)} %get-tuple-element.34), channel_id=1, source_target_pairs={{0,192},{64,0},{128,64},{192,128},{1,193},{65,1},{129,65},{193,129... | collective-permute-start | bytes 786440 | tf_op jit(solution)/shard_map/ppermute | solution.py:88
  157.4 8.1 %collective-permute-done.24 = bf16[128,1024]{1,0:T(8,128)(2,1)S(1)} collective-permute-done((bf16[128,1024]{1,0:T(8,128)(2,1)S(1)}, bf16[128,1024]{1,0:T(8,128)(2,1)S(1)}, u32[]{:S(2)}, u32[]{:S(2)}) %collective-permute-start.24) | collective-permute-done | bytes 262176 | tf_op jit(solution)/shard_map/ppermute | solution.py:102
  (72 shorter events, 35.6 us)
Async XLA Ops:
  6.5 105.4 %all-gather.2.cloned.1.call-start = ((), (), s32[]{:S(2)}) async-start(), calls=%async_computation | async-start | bytes 4718592 | tf_op jit(solution)/shard_map/all_gather | solution.py:45
  9.2 17.7 %collective-permute-start = (bf16[672,128]{1,0:T(8,128)(2,1)S(1)}, bf16[672,128]{1,0:T(8,128)(2,1)S(1)}, u32[]{:S(2)}, u32[]{:S(2)}) collective-permute-start(bf16[672,128]{1,0:T(8,128)(2,1)S(1)} %slice.18), channel_id=1, source_target_pairs={{0,2},{2,4},{4,6},{6,7},{7,5},{5,3},{3,1},{1,0},{8,10},{10,12},{12... | collective-permute-start | bytes 516104 | tf_op jit(solution)/shard_map/ppermute | solution.py:53
  11.2 23.0 %collective-permute-start.1 = (bf16[688,128]{1,0:T(8,128)(2,1)S(1)}, bf16[688,128]{1,0:T(8,128)(2,1)S(1)}, u32[]{:S(2)}, u32[]{:S(2)}) collective-permute-start(bf16[688,128]{1,0:T(8,128)(2,1)S(1)} %get-tuple-element.21), channel_id=1, source_target_pairs={{0,2},{2,4},{4,6},{6,7},{7,5},{5,3},{3,1},{1,0},{8,10},{10,12},{12... | collective-permute-start | bytes 528392 | tf_op jit(solution)/shard_map/ppermute | solution.py:53
  13.1 26.3 %collective-permute-start.2 = (bf16[688,128]{1,0:T(8,128)(2,1)S(1)}, bf16[688,128]{1,0:T(8,128)(2,1)S(1)}, u32[]{:S(2)}, u32[]{:S(2)}) collective-permute-start(bf16[688,128]{1,0:T(8,128)(2,1)S(1)} %get-tuple-element.22), channel_id=1, source_target_pairs={{0,2},{2,4},{4,6},{6,7},{7,5},{5,3},{3,1},{1,0},{8,10},{10,12},{12... | collective-permute-start | bytes 528392 | tf_op jit(solution)/shard_map/ppermute | solution.py:53
  26.9 18.0 %collective-permute-start.3 = (bf16[672,128]{1,0:T(8,128)(2,1)S(1)}, bf16[672,128]{1,0:T(8,128)(2,1)S(1)}, u32[]{:S(2)}, u32[]{:S(2)}) collective-permute-start(bf16[672,128]{1,0:T(8,128)(2,1)S(1)} %collective-permute-done), channel_id=1, source_target_pairs={{0,2},{2,4},{4,6},{6,7},{7,5},{5,3},{3,1},{1,0},{8,10},{10,12},{12... | collective-permute-start | bytes 516104 | tf_op jit(solution)/shard_map/ppermute | solution.py:53
  34.2 13.5 %collective-permute-start.4 = (bf16[688,128]{1,0:T(8,128)(2,1)S(1)}, bf16[688,128]{1,0:T(8,128)(2,1)S(1)}, u32[]{:S(2)}, u32[]{:S(2)}) collective-permute-start(bf16[688,128]{1,0:T(8,128)(2,1)S(1)} %collective-permute-done.1), channel_id=1, source_target_pairs={{0,2},{2,4},{4,6},{6,7},{7,5},{5,3},{3,1},{1,0},{8,10},{10,12},{12... | collective-permute-start | bytes 528392 | tf_op jit(solution)/shard_map/ppermute | solution.py:53
  39.3 10.3 %collective-permute-start.5 = (bf16[688,128]{1,0:T(8,128)(2,1)S(1)}, bf16[688,128]{1,0:T(8,128)(2,1)S(1)}, u32[]{:S(2)}, u32[]{:S(2)}) collective-permute-start(bf16[688,128]{1,0:T(8,128)(2,1)S(1)} %collective-permute-done.2), channel_id=1, source_target_pairs={{0,2},{2,4},{4,6},{6,7},{7,5},{5,3},{3,1},{1,0},{8,10},{10,12},{12... | collective-permute-start | bytes 528392 | tf_op jit(solution)/shard_map/ppermute | solution.py:53
  44.9 11.2 %collective-permute-start.6 = (bf16[672,128]{1,0:T(8,128)(2,1)S(1)}, bf16[672,128]{1,0:T(8,128)(2,1)S(1)}, u32[]{:S(2)}, u32[]{:S(2)}) collective-permute-start(bf16[672,128]{1,0:T(8,128)(2,1)S(1)} %collective-permute-done.3), channel_id=1, source_target_pairs={{0,2},{2,4},{4,6},{6,7},{7,5},{5,3},{3,1},{1,0},{8,10},{10,12},{12... | collective-permute-start | bytes 516104 | tf_op jit(solution)/shard_map/ppermute | solution.py:53
  47.7 12.2 %collective-permute-start.7 = (bf16[688,128]{1,0:T(8,128)(2,1)S(1)}, bf16[688,128]{1,0:T(8,128)(2,1)S(1)}, u32[]{:S(2)}, u32[]{:S(2)}) collective-permute-start(bf16[688,128]{1,0:T(8,128)(2,1)S(1)} %collective-permute-done.4), channel_id=1, source_target_pairs={{0,2},{2,4},{4,6},{6,7},{7,5},{5,3},{3,1},{1,0},{8,10},{10,12},{12... | collective-permute-start | bytes 528392 | tf_op jit(solution)/shard_map/ppermute | solution.py:53
  49.6 14.1 %collective-permute-start.8 = (bf16[688,128]{1,0:T(8,128)(2,1)S(1)}, bf16[688,128]{1,0:T(8,128)(2,1)S(1)}, u32[]{:S(2)}, u32[]{:S(2)}) collective-permute-start(bf16[688,128]{1,0:T(8,128)(2,1)S(1)} %collective-permute-done.5), channel_id=1, source_target_pairs={{0,2},{2,4},{4,6},{6,7},{7,5},{5,3},{3,1},{1,0},{8,10},{10,12},{12... | collective-permute-start | bytes 528392 | tf_op jit(solution)/shard_map/ppermute | solution.py:53
  56.1 12.2 %collective-permute-start.9 = (bf16[672,128]{1,0:T(8,128)(2,1)S(1)}, bf16[672,128]{1,0:T(8,128)(2,1)S(1)}, u32[]{:S(2)}, u32[]{:S(2)}) collective-permute-start(bf16[672,128]{1,0:T(8,128)(2,1)S(1)} %collective-permute-done.6), channel_id=1, source_target_pairs={{0,2},{2,4},{4,6},{6,7},{7,5},{5,3},{3,1},{1,0},{8,10},{10,12},{12... | collective-permute-start | bytes 516104 | tf_op jit(solution)/shard_map/ppermute | solution.py:53
  59.9 14.4 %collective-permute-start.10 = (bf16[688,128]{1,0:T(8,128)(2,1)S(1)}, bf16[688,128]{1,0:T(8,128)(2,1)S(1)}, u32[]{:S(2)}, u32[]{:S(2)}) collective-permute-start(bf16[688,128]{1,0:T(8,128)(2,1)S(1)} %collective-permute-done.7), channel_id=1, source_target_pairs={{0,2},{2,4},{4,6},{6,7},{7,5},{5,3},{3,1},{1,0},{8,10},{10,12},{12... | collective-permute-start | bytes 528392 | tf_op jit(solution)/shard_map/ppermute | solution.py:53
  63.7 14.5 %collective-permute-start.11 = (bf16[688,128]{1,0:T(8,128)(2,1)S(1)}, bf16[688,128]{1,0:T(8,128)(2,1)S(1)}, u32[]{:S(2)}, u32[]{:S(2)}) collective-permute-start(bf16[688,128]{1,0:T(8,128)(2,1)S(1)} %collective-permute-done.8), channel_id=1, source_target_pairs={{0,2},{2,4},{4,6},{6,7},{7,5},{5,3},{3,1},{1,0},{8,10},{10,12},{12... | collective-permute-start | bytes 528392 | tf_op jit(solution)/shard_map/ppermute | solution.py:53
  68.3 13.5 %collective-permute-start.12 = (bf16[672,128]{1,0:T(8,128)(2,1)S(1)}, bf16[672,128]{1,0:T(8,128)(2,1)S(1)}, u32[]{:S(2)}, u32[]{:S(2)}) collective-permute-start(bf16[672,128]{1,0:T(8,128)(2,1)S(1)} %collective-permute-done.9), channel_id=1, source_target_pairs={{0,2},{2,4},{4,6},{6,7},{7,5},{5,3},{3,1},{1,0},{8,10},{10,12},{12... | collective-permute-start | bytes 516104 | tf_op jit(solution)/shard_map/ppermute | solution.py:53
  74.3 10.6 %collective-permute-start.13 = (bf16[688,128]{1,0:T(8,128)(2,1)S(1)}, bf16[688,128]{1,0:T(8,128)(2,1)S(1)}, u32[]{:S(2)}, u32[]{:S(2)}) collective-permute-start(bf16[688,128]{1,0:T(8,128)(2,1)S(1)} %collective-permute-done.10), channel_id=1, source_target_pairs={{0,2},{2,4},{4,6},{6,7},{7,5},{5,3},{3,1},{1,0},{8,10},{10,12},{12... | collective-permute-start | bytes 528392 | tf_op jit(solution)/shard_map/ppermute | solution.py:53
  78.2 11.4 %collective-permute-start.14 = (bf16[688,128]{1,0:T(8,128)(2,1)S(1)}, bf16[688,128]{1,0:T(8,128)(2,1)S(1)}, u32[]{:S(2)}, u32[]{:S(2)}) collective-permute-start(bf16[688,128]{1,0:T(8,128)(2,1)S(1)} %collective-permute-done.11), channel_id=1, source_target_pairs={{0,2},{2,4},{4,6},{6,7},{7,5},{5,3},{3,1},{1,0},{8,10},{10,12},{12... | collective-permute-start | bytes 528392 | tf_op jit(solution)/shard_map/ppermute | solution.py:53
  81.8 13.2 %collective-permute-start.15 = (bf16[672,128]{1,0:T(8,128)(2,1)S(1)}, bf16[672,128]{1,0:T(8,128)(2,1)S(1)}, u32[]{:S(2)}, u32[]{:S(2)}) collective-permute-start(bf16[672,128]{1,0:T(8,128)(2,1)S(1)} %collective-permute-done.12), channel_id=1, source_target_pairs={{0,2},{2,4},{4,6},{6,7},{7,5},{5,3},{3,1},{1,0},{8,10},{10,12},{12... | collective-permute-start | bytes 516104 | tf_op jit(solution)/shard_map/ppermute | solution.py:53
  84.9 13.8 %collective-permute-start.16 = (bf16[688,128]{1,0:T(8,128)(2,1)S(1)}, bf16[688,128]{1,0:T(8,128)(2,1)S(1)}, u32[]{:S(2)}, u32[]{:S(2)}) collective-permute-start(bf16[688,128]{1,0:T(8,128)(2,1)S(1)} %collective-permute-done.13), channel_id=1, source_target_pairs={{0,2},{2,4},{4,6},{6,7},{7,5},{5,3},{3,1},{1,0},{8,10},{10,12},{12... | collective-permute-start | bytes 528392 | tf_op jit(solution)/shard_map/ppermute | solution.py:53
  89.6 12.0 %collective-permute-start.17 = (bf16[688,128]{1,0:T(8,128)(2,1)S(1)}, bf16[688,128]{1,0:T(8,128)(2,1)S(1)}, u32[]{:S(2)}, u32[]{:S(2)}) collective-permute-start(bf16[688,128]{1,0:T(8,128)(2,1)S(1)} %collective-permute-done.14), channel_id=1, source_target_pairs={{0,2},{2,4},{4,6},{6,7},{7,5},{5,3},{3,1},{1,0},{8,10},{10,12},{12... | collective-permute-start | bytes 528392 | tf_op jit(solution)/shard_map/ppermute | solution.py:53
  95.1 13.4 %collective-permute-start.18 = (bf16[672,128]{1,0:T(8,128)(2,1)S(1)}, bf16[672,128]{1,0:T(8,128)(2,1)S(1)}, u32[]{:S(2)}, u32[]{:S(2)}) collective-permute-start(bf16[672,128]{1,0:T(8,128)(2,1)S(1)} %collective-permute-done.15), channel_id=1, source_target_pairs={{0,2},{2,4},{4,6},{6,7},{7,5},{5,3},{3,1},{1,0},{8,10},{10,12},{12... | collective-permute-start | bytes 516104 | tf_op jit(solution)/shard_map/ppermute | solution.py:53
  98.7 10.7 %collective-permute-start.19 = (bf16[688,128]{1,0:T(8,128)(2,1)S(1)}, bf16[688,128]{1,0:T(8,128)(2,1)S(1)}, u32[]{:S(2)}, u32[]{:S(2)}) collective-permute-start(bf16[688,128]{1,0:T(8,128)(2,1)S(1)} %collective-permute-done.16), channel_id=1, source_target_pairs={{0,2},{2,4},{4,6},{6,7},{7,5},{5,3},{3,1},{1,0},{8,10},{10,12},{12... | collective-permute-start | bytes 528392 | tf_op jit(solution)/shard_map/ppermute | solution.py:53
  101.6 9.5 %collective-permute-start.20 = (bf16[688,128]{1,0:T(8,128)(2,1)S(1)}, bf16[688,128]{1,0:T(8,128)(2,1)S(1)}, u32[]{:S(2)}, u32[]{:S(2)}) collective-permute-start(bf16[688,128]{1,0:T(8,128)(2,1)S(1)} %collective-permute-done.17), channel_id=1, source_target_pairs={{0,2},{2,4},{4,6},{6,7},{7,5},{5,3},{3,1},{1,0},{8,10},{10,12},{12... | collective-permute-start | bytes 528392 | tf_op jit(solution)/shard_map/ppermute | solution.py:53
  119.8 11.4 %collective-permute-start.21 = (bf16[128,1024]{1,0:T(8,128)(2,1)S(1)}, bf16[128,1024]{1,0:T(8,128)(2,1)S(1)}, u32[]{:S(2)}, u32[]{:S(2)}) collective-permute-start(bf16[128,1024]{1,0:T(8,128)(2,1)S(1)} %get-tuple-element.25), channel_id=1, source_target_pairs={{0,64},{64,128},{128,192},{192,0},{1,65},{65,129},{129,193},{193,1... | collective-permute-start | bytes 786440 | tf_op jit(solution)/shard_map/ppermute | solution.py:88
  123.3 9.9 %collective-permute-start.22 = (bf16[128,1024]{1,0:T(8,128)(2,1)S(1)}, bf16[128,1024]{1,0:T(8,128)(2,1)S(1)}, u32[]{:S(2)}, u32[]{:S(2)}) collective-permute-start(bf16[128,1024]{1,0:T(8,128)(2,1)S(1)} %get-tuple-element.26), channel_id=1, source_target_pairs={{0,128},{64,192},{128,0},{192,64},{1,129},{65,193},{129,1},{193,65... | collective-permute-start | bytes 786440 | tf_op jit(solution)/shard_map/ppermute | solution.py:88
  127.9 8.3 %collective-permute-start.23 = (bf16[128,1024]{1,0:T(8,128)(2,1)S(1)}, bf16[128,1024]{1,0:T(8,128)(2,1)S(1)}, u32[]{:S(2)}, u32[]{:S(2)}) collective-permute-start(bf16[128,1024]{1,0:T(8,128)(2,1)S(1)} %get-tuple-element.27), channel_id=1, source_target_pairs={{0,192},{64,0},{128,64},{192,128},{1,193},{65,1},{129,65},{193,129... | collective-permute-start | bytes 786440 | tf_op jit(solution)/shard_map/ppermute | solution.py:88
  136.3 29.2 %collective-permute-start.24 = (bf16[128,1024]{1,0:T(8,128)(2,1)S(1)}, bf16[128,1024]{1,0:T(8,128)(2,1)S(1)}, u32[]{:S(2)}, u32[]{:S(2)}) collective-permute-start(bf16[128,1024]{1,0:T(8,128)(2,1)S(1)} %add_convert_fusion), channel_id=1, source_target_pairs={{0,256},{256,0},{1,257},{257,1},{2,258},{258,2},{3,259},{259,3},{4... | collective-permute-start | bytes 786440 | tf_op jit(solution)/shard_map/ppermute | solution.py:102
  147.2 18.3 %collective-permute-start.25 = (bf16[128,1024]{1,0:T(8,128)(2,1)S(1)}, bf16[128,1024]{1,0:T(8,128)(2,1)S(1)}, u32[]{:S(2)}, u32[]{:S(2)}) collective-permute-start(bf16[128,1024]{1,0:T(8,128)(2,1)S(1)} %get-tuple-element.32), channel_id=1, source_target_pairs={{0,64},{64,128},{128,192},{192,0},{1,65},{65,129},{129,193},{193,1... | collective-permute-start | bytes 786440 | tf_op jit(solution)/shard_map/ppermute | solution.py:88
  150.3 15.2 %collective-permute-start.26 = (bf16[128,1024]{1,0:T(8,128)(2,1)S(1)}, bf16[128,1024]{1,0:T(8,128)(2,1)S(1)}, u32[]{:S(2)}, u32[]{:S(2)}) collective-permute-start(bf16[128,1024]{1,0:T(8,128)(2,1)S(1)} %get-tuple-element.33), channel_id=1, source_target_pairs={{0,128},{64,192},{128,0},{192,64},{1,129},{65,193},{129,1},{193,65... | collective-permute-start | bytes 786440 | tf_op jit(solution)/shard_map/ppermute | solution.py:88
  155.2 10.3 %collective-permute-start.27 = (bf16[128,1024]{1,0:T(8,128)(2,1)S(1)}, bf16[128,1024]{1,0:T(8,128)(2,1)S(1)}, u32[]{:S(2)}, u32[]{:S(2)}) collective-permute-start(bf16[128,1024]{1,0:T(8,128)(2,1)S(1)} %get-tuple-element.34), channel_id=1, source_target_pairs={{0,192},{64,0},{128,64},{192,128},{1,193},{65,1},{129,65},{193,129... | collective-permute-start | bytes 786440 | tf_op jit(solution)/shard_map/ppermute | solution.py:88
Sparse Core Ops, SparseCore 0:
  9.5 46.6 all-gather.1

commit v7 on v0

v7 whole, which is shorter than its diff:
```python
import functools

import jax
import jax.numpy as jnp
from jax import lax
from jax.experimental import pallas as pl
from jax.experimental.pallas import tpu as pltpu
from jax.sharding import Mesh, PartitionSpec as P

NAMES = ("zh", "x", "y", "core", "zl")
SHAPE = (2, 4, 4, 2, 8)
WHOLE = pl.BlockSpec(memory_space=pltpu.VMEM)


def shift(n, s):
    return [(i, (i + s) % n) for i in range(n)]


def circle(n):
    return list(range(0, n, 2)) + list(range(n - 1, 0, -2))


def place(col, n):
    return jnp.where(col % 2 == 0, col // 2, (2 * n - 1 - col) // 2)


def cuts(rows, parts):
    tiles = rows // 16
    sizes = [16 * (tiles // parts + (i < tiles % parts)) for i in range(parts)]
    return [(sum(sizes[:i]), sum(sizes[: i + 1])) for i in range(parts)]


def lookup(indices, table):
    width = 64
    lines = -(-table.shape[0] // width)
    grid = jnp.pad(table, (0, lines * width - table.shape[0])).reshape(lines, width)
    high = lax.reduce_precision(grid, 8, 7)
    middle = lax.reduce_precision(grid - high, 8, 7)
    parts = jnp.concatenate([high, middle, grid - high - middle], axis=1).astype(jnp.bfloat16)
    line = jnp.arange(lines, dtype=jnp.int32)[:, None]
    line_hits = (indices[None, :] // width == line).astype(jnp.bfloat16)
    picked = lax.dot_general(
        parts, line_hits, (((0,), (0,)), ((), ())), preferred_element_type=jnp.float32
    )
    within = jnp.arange(3 * width, dtype=jnp.int32)[:, None] % width
    return jnp.sum(jnp.where(indices[None, :] % width == within, picked, 0.0), axis=0)


def turned_kernel(elements, *chunks):
    turned = elements[...].astype(jnp.float32).T.astype(jnp.bfloat16)
    first = 0
    for chunk in chunks:
        chunk[...] = turned[first : first + chunk.shape[0]]
        first += chunk.shape[0]


def turned(elements, parts):
    n_pair, n_g = elements.shape
    return pl.pallas_call(
        turned_kernel,
        out_shape=[
            jax.ShapeDtypeStruct((b - a, n_pair), elements.dtype) for a, b in cuts(n_g, parts)
        ],
        in_specs=[WHOLE],
        out_specs=[WHOLE] * parts,
    )(elements)


def product_kernel(n_turns, parts, slots, factor, columns, *refs):
    pieces = refs[: n_turns * parts]
    own, *others, rows = refs[n_turns * parts :]
    n_g = own.shape[0]
    for turn in range(n_turns):
        slot = slots[turn]

        @pl.when(slot < 1 + len(others))
        def _():
            base = slot * n_g
            offset = 0
            for piece in pieces[turn * parts : (turn + 1) * parts]:
                size = piece.shape[0]
                at = pl.multiple_of(base + offset, 16)
                value = piece[...].astype(jnp.float32) * factor[...]
                rows[pl.ds(at, size), :] = value.astype(jnp.bfloat16)
                offset += size

    for i in range(0, 1 + len(others), 2):
        both = jnp.dot(
            rows[i * n_g : (i + 2) * n_g, :], columns[...], preferred_element_type=jnp.float32
        )
        for out, value in zip((own, *others)[i : i + 2], (both[:n_g], both[n_g:])):
            out[...] = value.astype(out.dtype)


def product(slots, factor, columns, pieces, parts, n_slots):
    n_pair, width = columns.shape
    n_turns = len(pieces) // parts
    n_g = sum(piece.shape[0] for piece in pieces[:parts])
    kinds = [jnp.float32] + [jnp.bfloat16] * (n_slots - 1)
    return pl.pallas_call(
        functools.partial(product_kernel, n_turns, parts),
        out_shape=[jax.ShapeDtypeStruct((n_g, width), kind) for kind in kinds],
        in_specs=[pl.BlockSpec(memory_space=pltpu.SMEM)] + [WHOLE] * (2 + len(pieces)),
        out_specs=[WHOLE] * n_slots,
        scratch_shapes=[pltpu.VMEM((n_slots * n_g, n_pair), jnp.bfloat16)],
        compiler_params=pltpu.CompilerParams(vmem_limit_bytes=40 * 1024 * 1024),
        cost_estimate=pl.CostEstimate(
            flops=2 * n_slots * n_g * n_pair * width,
            bytes_accessed=8 * 1024 * 1024,
            transcendentals=0,
        ),
    )(slots, factor, columns, *pieces)


def body(pair_elements, valence_of, conduction_of, valence_depth, conduction_height):
    n_pair, n_g = pair_elements.shape
    n_x, n_z = lax.axis_size("x"), lax.axis_size("zl")
    columns = lax.all_gather(pair_elements, ("y", "core"), axis=1, tiled=True)

    order = circle(n_z)
    step = [(order[i], order[(i + 1) % n_z]) for i in range(n_z)]
    parts = 2
    chunks = turned(pair_elements, parts)
    pieces = list(chunks)
    for turn in range(1, n_z):
        chunks = [lax.ppermute(chunk, "zl", step) for chunk in chunks]
        pieces += chunks
        if turn == n_z // 2 - 1:
            valence_of, conduction_of, _ = lax.optimization_barrier(
                (valence_of, conduction_of, chunks[0])
            )
            pair_gap = lookup(valence_of, valence_depth)
            pair_gap = pair_gap + lookup(conduction_of, conduction_height)
            factor = (-4.0 / pair_gap)[None, :]
        if turn == n_z - 3:
            chunks[0], factor = lax.optimization_barrier((chunks[0], factor))

    my_half, my_x = lax.axis_index("zh"), lax.axis_index("x")
    turns = jnp.arange(n_z, dtype=jnp.int32)
    origin = lax.rem(place(lax.axis_index("zl"), n_z) - turns + n_z, n_z)
    col = jnp.where(origin < n_z // 2, 2 * origin, 2 * n_z - 1 - 2 * origin)
    slot = lax.rem(col % n_x - my_x + n_x, n_x)
    stays = col // n_x == my_half

    def summed_over_x(own, others):
        got = [lax.ppermute(one, "x", shift(n_x, s)) for s, one in enumerate(others, 1)]
        for one in got:
            own = own + one.astype(jnp.float32)
        return own

    given, *given_sent = product(
        jnp.where(stays, n_x, slot), factor, columns, pieces, parts, n_x
    )
    last = jnp.where(stays, slot, n_x)
    last, given, *given_sent = lax.optimization_barrier((last, given, *given_sent))
    kept, *kept_sent = product(last, factor, columns, pieces, parts, n_x)
    given = summed_over_x(given, given_sent).astype(jnp.bfloat16)
    given, *kept_sent = lax.optimization_barrier((given, *kept_sent))
    got = lax.ppermute(given, "zh", shift(2, 1)).astype(jnp.float32)
    total = summed_over_x(kept, kept_sent) + got
    return total.reshape(1, n_g, -1, n_g)


def solution(mesh):
    fine = Mesh(mesh.devices.reshape(SHAPE), NAMES)
    pair, row = ("zh", "x"), ("y", "core")
    placed = (P(pair, row + ("zl",)), P(pair), P(pair), P(), P())
    return jax.shard_map(
        body, mesh=fine, in_specs=placed, out_specs=P(row, pair, None, "zl"), check_vma=False
    )
```

time: 400 us -> 161 us (0.40)
  the two profiles are of different devices: /device:TPU:8 before, /device:TPU:120 now
where the time goes in v7:
time: 161 us; the launch traced here: 160 us
  waiting for transfers between devices  71.7 us (45%)
  starting transfers between devices  58.2 us (36%)
  between operations  13.7 us (9%)
  Pallas kernels  9.98 us (6%)
  local copies, waits for them, and re-layouts  4.66 us (3%)
    ppermute x14, waiting for transfers between devices, body(): chunks = [lax.ppermute(chunk, 'zl', step) for chunk in chunks]  61.1 us
    ppermute x14, starting transfers between devices, body(): chunks = [lax.ppermute(chunk, 'zl', step) for chunk in chunks]  26.7 us
    ppermute x6, starting transfers between devices, summed_over_x(): lax.ppermute(one, 'x', shift(n_x, s))  18.4 us
    ppermute x1, starting transfers between devices, body(): got = lax.ppermute(given, 'zh', shift(2, 1)).astype(jnp.float32)  13 us
    pallas_call x2, Pallas kernels, product(): pl.pallas_call(functools.partial(product_kernel, n_turns, parts), out_sha...  7.94 us
    ppermute x1, waiting for transfers between devices, body(): got = lax.ppermute(given, 'zh', shift(2, 1)).astype(jnp.float32)  6.65 us
    ppermute x6, waiting for transfers between devices, summed_over_x(): lax.ppermute(one, 'x', shift(n_x, s))  3.24 us
  transfers between devices with their start and end apart: 22, of which 18 were waited for; matrix products, arithmetic and copies ran while one was open for 2% of the time, Pallas kernels for 4%

profile of v7, /device:TPU:120, one launch (start us, length us, event | category | flops | bytes accessed | tf_op | source)
XLA Modules:
  0.0 160.3 jit_solution(14683690141673010665)
XLA Ops:
  7.3 2.0 %shard_map.55 = (bf16[64,2048]{1,0:T(8,128)(2,1)}, bf16[64,2048]{1,0:T(8,128)(2,1)}) custom-call(bf16[2048,128]{1,0:T(8,128)(2,1)} %elements.1), custom_call_target="tpu_custom_call" | custom-call | tf_op jit(solution)/shard_map/pallas_call | solution.py:59
  11.2 1.9 %collective-permute-start.5 = (bf16[64,2048]{1,0:T(8,128)(2,1)}, bf16[64,2048]{1,0:T(8,128)(2,1)S(1)}, u32[]{:S(2)}, u32[]{:S(2)}) collective-permute-start(bf16[64,2048]{1,0:T(8,128)(2,1)} %get-tuple-element.32.refs_1_), channel_id=1, source_target_pairs={{0,2},{2,4},{4,6},{6,7},{7,5},{5,3},{3,1},{1,0},{8,10},{10,12},{12... | collective-permute-start | bytes 786440 | tf_op jit(solution)/shard_map/ppermute | solution.py:126
  13.1 9.9 %collective-permute-done.refs_2_ = bf16[64,2048]{1,0:T(8,128)(2,1)S(1)} collective-permute-done((bf16[64,2048]{1,0:T(8,128)(2,1)}, bf16[64,2048]{1,0:T(8,128)(2,1)S(1)}, u32[]{:S(2)}, u32[]{:S(2)}) %collective-permute-start) | collective-permute-done | bytes 262176 | tf_op jit(solution)/shard_map/ppermute | solution.py:126
  23.0 1.9 %collective-permute-start.1 = (bf16[64,2048]{1,0:T(8,128)(2,1)S(1)}, bf16[64,2048]{1,0:T(8,128)(2,1)S(1)}, u32[]{:S(2)}, u32[]{:S(2)}) collective-permute-start(bf16[64,2048]{1,0:T(8,128)(2,1)S(1)} %collective-permute-done.refs_2_), channel_id=1, source_target_pairs={{0,2},{2,4},{4,6},{6,7},{7,5},{5,3},{3,1},{1,0},{8,10},{10,12},{12... | collective-permute-start | bytes 786440 | tf_op jit(solution)/shard_map/ppermute | solution.py:126
  24.9 2.9 %collective-permute-done.5.refs_3_ = bf16[64,2048]{1,0:T(8,128)(2,1)S(1)} collective-permute-done((bf16[64,2048]{1,0:T(8,128)(2,1)}, bf16[64,2048]{1,0:T(8,128)(2,1)S(1)}, u32[]{:S(2)}, u32[]{:S(2)}) %collective-permute-start.5) | collective-permute-done | bytes 262176 | tf_op jit(solution)/shard_map/ppermute | solution.py:126
  30.5 3.2 %collective-permute-done.1.refs_4_ = bf16[64,2048]{1,0:T(8,128)(2,1)S(1)} collective-permute-done((bf16[64,2048]{1,0:T(8,128)(2,1)S(1)}, bf16[64,2048]{1,0:T(8,128)(2,1)S(1)}, u32[]{:S(2)}, u32[]{:S(2)}) %collective-permute-start.1) | collective-permute-done | bytes 262176 | tf_op jit(solution)/shard_map/ppermute | solution.py:126
  35.6 5.0 %collective-permute-done.6.refs_5_ = bf16[64,2048]{1,0:T(8,128)(2,1)S(1)} collective-permute-done((bf16[64,2048]{1,0:T(8,128)(2,1)S(1)}, bf16[64,2048]{1,0:T(8,128)(2,1)S(1)}, u32[]{:S(2)}, u32[]{:S(2)}) %collective-permute-start.6) | collective-permute-done | bytes 262176 | tf_op jit(solution)/shard_map/ppermute | solution.py:126
  43.3 2.2 %collective-permute-done.2.refs_6_ = bf16[64,2048]{1,0:T(8,128)(2,1)S(1)} collective-permute-done((bf16[64,2048]{1,0:T(8,128)(2,1)S(1)}, bf16[64,2048]{1,0:T(8,128)(2,1)S(1)}, u32[]{:S(2)}, u32[]{:S(2)}) %collective-permute-start.2) | collective-permute-done | bytes 262176 | tf_op jit(solution)/shard_map/ppermute | solution.py:126
  47.4 4.8 %collective-permute-done.7.refs_7_ = bf16[64,2048]{1,0:T(8,128)(2,1)S(1)} collective-permute-done((bf16[64,2048]{1,0:T(8,128)(2,1)S(1)}, bf16[64,2048]{1,0:T(8,128)(2,1)S(1)}, u32[]{:S(2)}, u32[]{:S(2)}) %collective-permute-start.7) | collective-permute-done | bytes 262176 | tf_op jit(solution)/shard_map/ppermute | solution.py:126
  55.4 3.4 %collective-permute-done.3.refs_8_ = bf16[64,2048]{1,0:T(8,128)(2,1)S(1)} collective-permute-done((bf16[64,2048]{1,0:T(8,128)(2,1)S(1)}, bf16[64,2048]{1,0:T(8,128)(2,1)S(1)}, u32[]{:S(2)}, u32[]{:S(2)}) %collective-permute-start.3) | collective-permute-done | bytes 262176 | tf_op jit(solution)/shard_map/ppermute | solution.py:126
  60.6 3.4 %collective-permute-done.8.refs_9_ = bf16[64,2048]{1,0:T(8,128)(2,1)S(1)} collective-permute-done((bf16[64,2048]{1,0:T(8,128)(2,1)S(1)}, bf16[64,2048]{1,0:T(8,128)(2,1)S(1)}, u32[]{:S(2)}, u32[]{:S(2)}) %collective-permute-start.8) | collective-permute-done | bytes 262176 | tf_op jit(solution)/shard_map/ppermute | solution.py:126
  66.5 4.9 %collective-permute-done.4.refs_10_ = bf16[64,2048]{1,0:T(8,128)(2,1)S(1)} collective-permute-done((bf16[64,2048]{1,0:T(8,128)(2,1)S(1)}, bf16[64,2048]{1,0:T(8,128)(2,1)S(1)}, u32[]{:S(2)}, u32[]{:S(2)}) %collective-permute-start.4) | collective-permute-done | bytes 262176 | tf_op jit(solution)/shard_map/ppermute | solution.py:126
  73.3 3.7 %collective-permute-done.9.refs_11_ = bf16[64,2048]{1,0:T(8,128)(2,1)S(1)} collective-permute-done((bf16[64,2048]{1,0:T(8,128)(2,1)S(1)}, bf16[64,2048]{1,0:T(8,128)(2,1)S(1)}, u32[]{:S(2)}, u32[]{:S(2)}) %collective-permute-start.9) | collective-permute-done | bytes 262176 | tf_op jit(solution)/shard_map/ppermute | solution.py:126
  77.0 1.9 %collective-permute-start.11 = (bf16[64,2048]{1,0:T(8,128)(2,1)S(1)}, bf16[64,2048]{1,0:T(8,128)(2,1)}, u32[]{:S(2)}, u32[]{:S(2)}) collective-permute-start(bf16[64,2048]{1,0:T(8,128)(2,1)S(1)} %collective-permute-done.9.refs_11_), channel_id=1, source_target_pairs={{0,2},{2,4},{4,6},{6,7},{7,5},{5,3},{3,1},{1,0},{8,10},{10,12},{12... | collective-permute-start | bytes 786440 | tf_op jit(solution)/shard_map/ppermute | solution.py:126
  79.0 4.3 %collective-permute-done.10.refs_12_ = bf16[64,2048]{1,0:T(8,128)(2,1)S(1)} collective-permute-done((bf16[64,2048]{1,0:T(8,128)(2,1)S(1)}, bf16[64,2048]{1,0:T(8,128)(2,1)S(1)}, u32[]{:S(2)}, u32[]{:S(2)}) %collective-permute-start.10) | collective-permute-done | bytes 262176 | tf_op jit(solution)/shard_map/ppermute | solution.py:126
  83.3 1.9 %collective-permute-start.12 = (bf16[64,2048]{1,0:T(8,128)(2,1)S(1)}, bf16[64,2048]{1,0:T(8,128)(2,1)}, u32[]{:S(2)}, u32[]{:S(2)}) collective-permute-start(bf16[64,2048]{1,0:T(8,128)(2,1)S(1)} %collective-permute-done.10.refs_12_), channel_id=1, source_target_pairs={{0,2},{2,4},{4,6},{6,7},{7,5},{5,3},{3,1},{1,0},{8,10},{10,12},{12... | collective-permute-start | bytes 786440 | tf_op jit(solution)/shard_map/ppermute | solution.py:126
  85.2 4.7 %collective-permute-done.11.refs_13_ = bf16[64,2048]{1,0:T(8,128)(2,1)} collective-permute-done((bf16[64,2048]{1,0:T(8,128)(2,1)S(1)}, bf16[64,2048]{1,0:T(8,128)(2,1)}, u32[]{:S(2)}, u32[]{:S(2)}) %collective-permute-start.11) | collective-permute-done | bytes 262176 | tf_op jit(solution)/shard_map/ppermute | solution.py:126
  89.9 1.9 %collective-permute-start.13 = (bf16[64,2048]{1,0:T(8,128)(2,1)}, bf16[64,2048]{1,0:T(8,128)(2,1)}, u32[]{:S(2)}, u32[]{:S(2)}) collective-permute-start(bf16[64,2048]{1,0:T(8,128)(2,1)} %collective-permute-done.11.refs_13_), channel_id=1, source_target_pairs={{0,2},{2,4},{4,6},{6,7},{7,5},{5,3},{3,1},{1,0},{8,10},{10,12},{12... | collective-permute-start | bytes 786440 | tf_op jit(solution)/shard_map/ppermute | solution.py:126
  91.9 3.2 %collective-permute-done.12.refs_14_ = bf16[64,2048]{1,0:T(8,128)(2,1)} collective-permute-done((bf16[64,2048]{1,0:T(8,128)(2,1)S(1)}, bf16[64,2048]{1,0:T(8,128)(2,1)}, u32[]{:S(2)}, u32[]{:S(2)}) %collective-permute-start.12) | collective-permute-done | bytes 262176 | tf_op jit(solution)/shard_map/ppermute | solution.py:126
  95.1 5.5 %collective-permute-done.13.refs_15_ = bf16[64,2048]{1,0:T(8,128)(2,1)} collective-permute-done((bf16[64,2048]{1,0:T(8,128)(2,1)}, bf16[64,2048]{1,0:T(8,128)(2,1)}, u32[]{:S(2)}, u32[]{:S(2)}) %collective-permute-start.13) | collective-permute-done | bytes 262176 | tf_op jit(solution)/shard_map/ppermute | solution.py:126
  100.6 2.2 %copy-done = bf16[2048,1024]{1,0:T(8,128)(2,1)S(1)} copy-done((bf16[2048,1024]{1,0:T(8,128)(2,1)S(1)}, bf16[2048,1024]{1,0:T(8,128)(2,1)}, u32[]{:S(2)}) %copy-start) | copy-done | bytes 4194328
  102.8 4.0 %shard_map.56 = (f32[128,1024]{1,0:T(8,128)S(1)}, bf16[128,1024]{1,0:T(8,128)(2,1)S(1)}, bf16[128,1024]{1,0:T(8,128)(2,1)S(1)}, bf16[128,1024]{1,0:T(8,128)(2,1)S(1)}) custom-call(s32[8]{0:T(128)S(1)} %get-tuple-element.61.slots, f32[1,2048]{1,0:T(1,128)S(1)} %bitcast.5, bf16[2048,1024]{1,0:T(8,128)(2,1)S(1)} %copy-done, bf16[64,2048]{1,0:T(8,128)(2,1)S(1)} %copy-done.2, ...), custom_call_target="tpu_custom_call" | custom-call | flops 2147483648 | bytes 8388608 | tf_op jit(solution)/shard_map/pallas_call | solution.py:100
  106.9 4.7 %collective-permute-start.16 = (bf16[128,1024]{1,0:T(8,128)(2,1)S(1)}, bf16[128,1024]{1,0:T(8,128)(2,1)S(1)}, u32[]{:S(2)}, u32[]{:S(2)}) collective-permute-start(bf16[128,1024]{1,0:T(8,128)(2,1)S(1)} %get-tuple-element.43), channel_id=1, source_target_pairs={{0,192},{64,0},{128,64},{192,128},{1,193},{65,1},{129,65},{193,129... | collective-permute-start | bytes 786440 | tf_op jit(solution)/shard_map/ppermute | solution.py:146
  111.5 2.7 %collective-permute-start.15 = (bf16[128,1024]{1,0:T(8,128)(2,1)S(1)}, bf16[128,1024]{1,0:T(8,128)(2,1)S(1)}, u32[]{:S(2)}, u32[]{:S(2)}) collective-permute-start(bf16[128,1024]{1,0:T(8,128)(2,1)S(1)} %get-tuple-element.42), channel_id=1, source_target_pairs={{0,128},{64,192},{128,0},{192,64},{1,129},{65,193},{129,1},{193,65... | collective-permute-start | bytes 786440 | tf_op jit(solution)/shard_map/ppermute | solution.py:146
  114.2 2.8 %collective-permute-start.14 = (bf16[128,1024]{1,0:T(8,128)(2,1)S(1)}, bf16[128,1024]{1,0:T(8,128)(2,1)S(1)}, u32[]{:S(2)}, u32[]{:S(2)}) collective-permute-start(bf16[128,1024]{1,0:T(8,128)(2,1)S(1)} %get-tuple-element.41), channel_id=1, source_target_pairs={{0,64},{64,128},{128,192},{192,0},{1,65},{65,129},{129,193},{193,1... | collective-permute-start | bytes 786440 | tf_op jit(solution)/shard_map/ppermute | solution.py:146
  117.1 3.9 %shard_map.57 = (f32[128,1024]{1,0:T(8,128)S(1)}, bf16[128,1024]{1,0:T(8,128)(2,1)S(1)}, bf16[128,1024]{1,0:T(8,128)(2,1)S(1)}, bf16[128,1024]{1,0:T(8,128)(2,1)S(1)}) custom-call(s32[8]{0:T(128)S(1)} %get-tuple-element.38.slots, f32[1,2048]{1,0:T(1,128)S(1)} %bitcast.6, bf16[2048,1024]{1,0:T(8,128)(2,1)S(1)} %copy-done.1, bf16[64,2048]{1,0:T(8,128)(2,1)S(1)} %copy-done.2, ...), custom_call_target="tpu_custom_call" | custom-call | flops 2147483648 | bytes 8388608 | tf_op jit(solution)/shard_map/pallas_call | solution.py:100
  121.3 2.8 %collective-permute-done.14 = bf16[128,1024]{1,0:T(8,128)(2,1)S(1)} collective-permute-done((bf16[128,1024]{1,0:T(8,128)(2,1)S(1)}, bf16[128,1024]{1,0:T(8,128)(2,1)S(1)}, u32[]{:S(2)}, u32[]{:S(2)}) %collective-permute-start.14) | collective-permute-done | bytes 262176 | tf_op jit(solution)/shard_map/ppermute | solution.py:146
  124.3 13.0 %collective-permute-start.20 = (bf16[128,1024]{1,0:T(8,128)(2,1)S(1)}, bf16[128,1024]{1,0:T(8,128)(2,1)S(1)}, u32[]{:S(2)}, u32[]{:S(2)}) collective-permute-start(bf16[128,1024]{1,0:T(8,128)(2,1)S(1)} %add_convert_fusion), channel_id=1, source_target_pairs={{0,256},{256,0},{1,257},{257,1},{2,258},{258,2},{3,259},{259,3},{4... | collective-permute-start | bytes 786440 | tf_op jit(solution)/shard_map/ppermute | solution.py:159
  137.3 2.5 %collective-permute-start.19 = (bf16[128,1024]{1,0:T(8,128)(2,1)S(1)}, bf16[128,1024]{1,0:T(8,128)(2,1)S(1)}, u32[]{:S(2)}, u32[]{:S(2)}) collective-permute-start(bf16[128,1024]{1,0:T(8,128)(2,1)S(1)} %get-tuple-element.49), channel_id=1, source_target_pairs={{0,192},{64,0},{128,64},{192,128},{1,193},{65,1},{129,65},{193,129... | collective-permute-start | bytes 786440 | tf_op jit(solution)/shard_map/ppermute | solution.py:146
  139.8 2.7 %collective-permute-start.18 = (bf16[128,1024]{1,0:T(8,128)(2,1)S(1)}, bf16[128,1024]{1,0:T(8,128)(2,1)S(1)}, u32[]{:S(2)}, u32[]{:S(2)}) collective-permute-start(bf16[128,1024]{1,0:T(8,128)(2,1)S(1)} %get-tuple-element.48), channel_id=1, source_target_pairs={{0,128},{64,192},{128,0},{192,64},{1,129},{65,193},{129,1},{193,65... | collective-permute-start | bytes 786440 | tf_op jit(solution)/shard_map/ppermute | solution.py:146
  142.5 3.1 %collective-permute-start.17 = (bf16[128,1024]{1,0:T(8,128)(2,1)S(1)}, bf16[128,1024]{1,0:T(8,128)(2,1)S(1)}, u32[]{:S(2)}, u32[]{:S(2)}) collective-permute-start(bf16[128,1024]{1,0:T(8,128)(2,1)S(1)} %get-tuple-element.47), channel_id=1, source_target_pairs={{0,64},{64,128},{128,192},{192,0},{1,65},{65,129},{129,193},{193,1... | collective-permute-start | bytes 786440 | tf_op jit(solution)/shard_map/ppermute | solution.py:146
  145.6 6.6 %collective-permute-done.20 = bf16[128,1024]{1,0:T(8,128)(2,1)S(1)} collective-permute-done((bf16[128,1024]{1,0:T(8,128)(2,1)S(1)}, bf16[128,1024]{1,0:T(8,128)(2,1)S(1)}, u32[]{:S(2)}, u32[]{:S(2)}) %collective-permute-start.20) | collective-permute-done | bytes 262176 | tf_op jit(solution)/shard_map/ppermute | solution.py:159
  (38 shorter events, 22.9 us)
Async XLA Ops:
  6.5 94.1 %all-gather.2.cloned.1.call-start = ((), (), s32[]{:S(2)}) async-start(), calls=%async_computation | async-start | bytes 4718592 | tf_op jit(solution)/shard_map/all_gather | solution.py:118
  9.3 13.7 %collective-permute-start = (bf16[64,2048]{1,0:T(8,128)(2,1)}, bf16[64,2048]{1,0:T(8,128)(2,1)S(1)}, u32[]{:S(2)}, u32[]{:S(2)}) collective-permute-start(bf16[64,2048]{1,0:T(8,128)(2,1)} %get-tuple-element.28.refs_0_), channel_id=1, source_target_pairs={{0,2},{2,4},{4,6},{6,7},{7,5},{5,3},{3,1},{1,0},{8,10},{10,12},{12... | collective-permute-start | bytes 786440 | tf_op jit(solution)/shard_map/ppermute | solution.py:126
  11.2 16.6 %collective-permute-start.5 = (bf16[64,2048]{1,0:T(8,128)(2,1)}, bf16[64,2048]{1,0:T(8,128)(2,1)S(1)}, u32[]{:S(2)}, u32[]{:S(2)}) collective-permute-start(bf16[64,2048]{1,0:T(8,128)(2,1)} %get-tuple-element.32.refs_1_), channel_id=1, source_target_pairs={{0,2},{2,4},{4,6},{6,7},{7,5},{5,3},{3,1},{1,0},{8,10},{10,12},{12... | collective-permute-start | bytes 786440 | tf_op jit(solution)/shard_map/ppermute | solution.py:126
  23.0 10.7 %collective-permute-start.1 = (bf16[64,2048]{1,0:T(8,128)(2,1)S(1)}, bf16[64,2048]{1,0:T(8,128)(2,1)S(1)}, u32[]{:S(2)}, u32[]{:S(2)}) collective-permute-start(bf16[64,2048]{1,0:T(8,128)(2,1)S(1)} %collective-permute-done.refs_2_), channel_id=1, source_target_pairs={{0,2},{2,4},{4,6},{6,7},{7,5},{5,3},{3,1},{1,0},{8,10},{10,12},{12... | collective-permute-start | bytes 786440 | tf_op jit(solution)/shard_map/ppermute | solution.py:126
  27.8 12.8 %collective-permute-start.6 = (bf16[64,2048]{1,0:T(8,128)(2,1)S(1)}, bf16[64,2048]{1,0:T(8,128)(2,1)S(1)}, u32[]{:S(2)}, u32[]{:S(2)}) collective-permute-start(bf16[64,2048]{1,0:T(8,128)(2,1)S(1)} %collective-permute-done.5.refs_3_), channel_id=1, source_target_pairs={{0,2},{2,4},{4,6},{6,7},{7,5},{5,3},{3,1},{1,0},{8,10},{10,12},{12... | collective-permute-start | bytes 786440 | tf_op jit(solution)/shard_map/ppermute | solution.py:126
  33.7 11.8 %collective-permute-start.2 = (bf16[64,2048]{1,0:T(8,128)(2,1)S(1)}, bf16[64,2048]{1,0:T(8,128)(2,1)S(1)}, u32[]{:S(2)}, u32[]{:S(2)}) collective-permute-start(bf16[64,2048]{1,0:T(8,128)(2,1)S(1)} %collective-permute-done.1.refs_4_), channel_id=1, source_target_pairs={{0,2},{2,4},{4,6},{6,7},{7,5},{5,3},{3,1},{1,0},{8,10},{10,12},{12... | collective-permute-start | bytes 786440 | tf_op jit(solution)/shard_map/ppermute | solution.py:126
  40.6 11.6 %collective-permute-start.7 = (bf16[64,2048]{1,0:T(8,128)(2,1)S(1)}, bf16[64,2048]{1,0:T(8,128)(2,1)S(1)}, u32[]{:S(2)}, u32[]{:S(2)}) collective-permute-start(bf16[64,2048]{1,0:T(8,128)(2,1)S(1)} %collective-permute-done.6.refs_5_), channel_id=1, source_target_pairs={{0,2},{2,4},{4,6},{6,7},{7,5},{5,3},{3,1},{1,0},{8,10},{10,12},{12... | collective-permute-start | bytes 786440 | tf_op jit(solution)/shard_map/ppermute | solution.py:126
  45.5 13.2 %collective-permute-start.3 = (bf16[64,2048]{1,0:T(8,128)(2,1)S(1)}, bf16[64,2048]{1,0:T(8,128)(2,1)S(1)}, u32[]{:S(2)}, u32[]{:S(2)}) collective-permute-start(bf16[64,2048]{1,0:T(8,128)(2,1)S(1)} %collective-permute-done.2.refs_6_), channel_id=1, source_target_pairs={{0,2},{2,4},{4,6},{6,7},{7,5},{5,3},{3,1},{1,0},{8,10},{10,12},{12... | collective-permute-start | bytes 786440 | tf_op jit(solution)/shard_map/ppermute | solution.py:126
  52.2 11.8 %collective-permute-start.8 = (bf16[64,2048]{1,0:T(8,128)(2,1)S(1)}, bf16[64,2048]{1,0:T(8,128)(2,1)S(1)}, u32[]{:S(2)}, u32[]{:S(2)}) collective-permute-start(bf16[64,2048]{1,0:T(8,128)(2,1)S(1)} %collective-permute-done.7.refs_7_), channel_id=1, source_target_pairs={{0,2},{2,4},{4,6},{6,7},{7,5},{5,3},{3,1},{1,0},{8,10},{10,12},{12... | collective-permute-start | bytes 786440 | tf_op jit(solution)/shard_map/ppermute | solution.py:126
  54.9 45.7 %copy-start.2 = (bf16[64,2048]{1,0:T(8,128)(2,1)S(1)}, bf16[64,2048]{1,0:T(8,128)(2,1)}, u32[]{:S(2)}) copy-start(bf16[64,2048]{1,0:T(8,128)(2,1)} %get-tuple-element.28.refs_0_) | copy-start | bytes 786436
  54.9 45.7 %copy-start.3 = (bf16[64,2048]{1,0:T(8,128)(2,1)S(1)}, bf16[64,2048]{1,0:T(8,128)(2,1)}, u32[]{:S(2)}) copy-start(bf16[64,2048]{1,0:T(8,128)(2,1)} %get-tuple-element.32.refs_1_) | copy-start | bytes 786436
  58.7 12.7 %collective-permute-start.4 = (bf16[64,2048]{1,0:T(8,128)(2,1)S(1)}, bf16[64,2048]{1,0:T(8,128)(2,1)S(1)}, u32[]{:S(2)}, u32[]{:S(2)}) collective-permute-start(bf16[64,2048]{1,0:T(8,128)(2,1)S(1)} %collective-permute-done.3.refs_8_), channel_id=1, source_target_pairs={{0,2},{2,4},{4,6},{6,7},{7,5},{5,3},{3,1},{1,0},{8,10},{10,12},{12... | collective-permute-start | bytes 786440 | tf_op jit(solution)/shard_map/ppermute | solution.py:126
  64.1 13.0 %collective-permute-start.9 = (bf16[64,2048]{1,0:T(8,128)(2,1)S(1)}, bf16[64,2048]{1,0:T(8,128)(2,1)S(1)}, u32[]{:S(2)}, u32[]{:S(2)}) collective-permute-start(bf16[64,2048]{1,0:T(8,128)(2,1)S(1)} %collective-permute-done.8.refs_9_), channel_id=1, source_target_pairs={{0,2},{2,4},{4,6},{6,7},{7,5},{5,3},{3,1},{1,0},{8,10},{10,12},{12... | collective-permute-start | bytes 786440 | tf_op jit(solution)/shard_map/ppermute | solution.py:126
  71.4 11.9 %collective-permute-start.10 = (bf16[64,2048]{1,0:T(8,128)(2,1)S(1)}, bf16[64,2048]{1,0:T(8,128)(2,1)S(1)}, u32[]{:S(2)}, u32[]{:S(2)}) collective-permute-start(bf16[64,2048]{1,0:T(8,128)(2,1)S(1)} %collective-permute-done.4.refs_10_), channel_id=1, source_target_pairs={{0,2},{2,4},{4,6},{6,7},{7,5},{5,3},{3,1},{1,0},{8,10},{10,12},{12... | collective-permute-start | bytes 786440 | tf_op jit(solution)/shard_map/ppermute | solution.py:126
  77.0 12.9 %collective-permute-start.11 = (bf16[64,2048]{1,0:T(8,128)(2,1)S(1)}, bf16[64,2048]{1,0:T(8,128)(2,1)}, u32[]{:S(2)}, u32[]{:S(2)}) collective-permute-start(bf16[64,2048]{1,0:T(8,128)(2,1)S(1)} %collective-permute-done.9.refs_11_), channel_id=1, source_target_pairs={{0,2},{2,4},{4,6},{6,7},{7,5},{5,3},{3,1},{1,0},{8,10},{10,12},{12... | collective-permute-start | bytes 786440 | tf_op jit(solution)/shard_map/ppermute | solution.py:126
  83.3 11.8 %collective-permute-start.12 = (bf16[64,2048]{1,0:T(8,128)(2,1)S(1)}, bf16[64,2048]{1,0:T(8,128)(2,1)}, u32[]{:S(2)}, u32[]{:S(2)}) collective-permute-start(bf16[64,2048]{1,0:T(8,128)(2,1)S(1)} %collective-permute-done.10.refs_12_), channel_id=1, source_target_pairs={{0,2},{2,4},{4,6},{6,7},{7,5},{5,3},{3,1},{1,0},{8,10},{10,12},{12... | collective-permute-start | bytes 786440 | tf_op jit(solution)/shard_map/ppermute | solution.py:126
  89.9 10.7 %collective-permute-start.13 = (bf16[64,2048]{1,0:T(8,128)(2,1)}, bf16[64,2048]{1,0:T(8,128)(2,1)}, u32[]{:S(2)}, u32[]{:S(2)}) collective-permute-start(bf16[64,2048]{1,0:T(8,128)(2,1)} %collective-permute-done.11.refs_13_), channel_id=1, source_target_pairs={{0,2},{2,4},{4,6},{6,7},{7,5},{5,3},{3,1},{1,0},{8,10},{10,12},{12... | collective-permute-start | bytes 786440 | tf_op jit(solution)/shard_map/ppermute | solution.py:126
  100.6 2.2 %copy-start = (bf16[2048,1024]{1,0:T(8,128)(2,1)S(1)}, bf16[2048,1024]{1,0:T(8,128)(2,1)}, u32[]{:S(2)}) copy-start(bf16[2048,1024]{1,0:T(8,128)(2,1)} %all-gather.2.cloned.1.call-done.columns) | copy-start | bytes 12582916
  102.8 14.2 %copy-start.1 = (bf16[2048,1024]{1,0:T(8,128)(2,1)S(1)}, bf16[2048,1024]{1,0:T(8,128)(2,1)}, u32[]{:S(2)}) copy-start(bf16[2048,1024]{1,0:T(8,128)(2,1)} %all-gather.2.cloned.1.call-done.columns) | copy-start | bytes 12582916
  106.9 14.1 %collective-permute-start.16 = (bf16[128,1024]{1,0:T(8,128)(2,1)S(1)}, bf16[128,1024]{1,0:T(8,128)(2,1)S(1)}, u32[]{:S(2)}, u32[]{:S(2)}) collective-permute-start(bf16[128,1024]{1,0:T(8,128)(2,1)S(1)} %get-tuple-element.43), channel_id=1, source_target_pairs={{0,192},{64,0},{128,64},{192,128},{1,193},{65,1},{129,65},{193,129... | collective-permute-start | bytes 786440 | tf_op jit(solution)/shard_map/ppermute | solution.py:146
  111.5 9.8 %collective-permute-start.15 = (bf16[128,1024]{1,0:T(8,128)(2,1)S(1)}, bf16[128,1024]{1,0:T(8,128)(2,1)S(1)}, u32[]{:S(2)}, u32[]{:S(2)}) collective-permute-start(bf16[128,1024]{1,0:T(8,128)(2,1)S(1)} %get-tuple-element.42), channel_id=1, source_target_pairs={{0,128},{64,192},{128,0},{192,64},{1,129},{65,193},{129,1},{193,65... | collective-permute-start | bytes 786440 | tf_op jit(solution)/shard_map/ppermute | solution.py:146
  114.2 9.9 %collective-permute-start.14 = (bf16[128,1024]{1,0:T(8,128)(2,1)S(1)}, bf16[128,1024]{1,0:T(8,128)(2,1)S(1)}, u32[]{:S(2)}, u32[]{:S(2)}) collective-permute-start(bf16[128,1024]{1,0:T(8,128)(2,1)S(1)} %get-tuple-element.41), channel_id=1, source_target_pairs={{0,64},{64,128},{128,192},{192,0},{1,65},{65,129},{129,193},{193,1... | collective-permute-start | bytes 786440 | tf_op jit(solution)/shard_map/ppermute | solution.py:146
  124.3 28.0 %collective-permute-start.20 = (bf16[128,1024]{1,0:T(8,128)(2,1)S(1)}, bf16[128,1024]{1,0:T(8,128)(2,1)S(1)}, u32[]{:S(2)}, u32[]{:S(2)}) collective-permute-start(bf16[128,1024]{1,0:T(8,128)(2,1)S(1)} %add_convert_fusion), channel_id=1, source_target_pairs={{0,256},{256,0},{1,257},{257,1},{2,258},{258,2},{3,259},{259,3},{4... | collective-permute-start | bytes 786440 | tf_op jit(solution)/shard_map/ppermute | solution.py:159
  137.3 15.0 %collective-permute-start.19 = (bf16[128,1024]{1,0:T(8,128)(2,1)S(1)}, bf16[128,1024]{1,0:T(8,128)(2,1)S(1)}, u32[]{:S(2)}, u32[]{:S(2)}) collective-permute-start(bf16[128,1024]{1,0:T(8,128)(2,1)S(1)} %get-tuple-element.49), channel_id=1, source_target_pairs={{0,192},{64,0},{128,64},{192,128},{1,193},{65,1},{129,65},{193,129... | collective-permute-start | bytes 786440 | tf_op jit(solution)/shard_map/ppermute | solution.py:146
  139.8 12.5 %collective-permute-start.18 = (bf16[128,1024]{1,0:T(8,128)(2,1)S(1)}, bf16[128,1024]{1,0:T(8,128)(2,1)S(1)}, u32[]{:S(2)}, u32[]{:S(2)}) collective-permute-start(bf16[128,1024]{1,0:T(8,128)(2,1)S(1)} %get-tuple-element.48), channel_id=1, source_target_pairs={{0,128},{64,192},{128,0},{192,64},{1,129},{65,193},{129,1},{193,65... | collective-permute-start | bytes 786440 | tf_op jit(solution)/shard_map/ppermute | solution.py:146
  142.5 9.9 %collective-permute-start.17 = (bf16[128,1024]{1,0:T(8,128)(2,1)S(1)}, bf16[128,1024]{1,0:T(8,128)(2,1)S(1)}, u32[]{:S(2)}, u32[]{:S(2)}) collective-permute-start(bf16[128,1024]{1,0:T(8,128)(2,1)S(1)} %get-tuple-element.47), channel_id=1, source_target_pairs={{0,64},{64,128},{128,192},{192,0},{1,65},{65,129},{129,193},{193,1... | collective-permute-start | bytes 786440 | tf_op jit(solution)/shard_map/ppermute | solution.py:146
Sparse Core Ops, SparseCore 0:
  9.5 46.1 all-gather.1

commit v8 on v7

--- a/solution.py
+++ b/solution.py
@@ -112,6 +112,39 @@
     )(slots, factor, columns, *pieces)
 
 
+def arrival(row, at, n):
+    return (at - row + n) % n
+
+
+def early_slots(n_x, n_z):
+    my_x, at = lax.axis_index("x"), place(lax.axis_index("zl"), n_z)
+    turns = jnp.arange(n_z, dtype=jnp.int32)
+    origin = (at - turns + n_z) % n_z
+    row = jnp.where(origin < n_z // 2, 2 * origin, 2 * n_z - 1 - 2 * origin)
+    slot = (row % n_x - my_x + n_x) % n_x
+    early = turns < arrival(place((row + n_x) % n_z, n_z), at, n_z)
+    stays = arrival(place(my_x, n_z), at, n_z) < arrival(place(my_x + n_x, n_z), at, n_z)
+    return (
+        jnp.where(early, slot, n_x),
+        jnp.where(early, n_x, slot),
+        stays == (lax.axis_index("zh") == 0),
+    )
+
+
+def swaps(n_x, n_z):
+    order = circle(n_z)
+    early, late = [], []
+    for x in range(n_x):
+        for col in range(n_z):
+            at = order.index(col)
+            turns = [arrival(order.index(half * n_x + x), at, n_z) for half in range(2)]
+            first = 0 if turns[0] < turns[1] else 1
+            ends = [(half * n_x + x) * n_z + col for half in range(2)]
+            early.append((ends[1 - first], ends[first]))
+            late.append((ends[first], ends[1 - first]))
+    return early, late
+
+
 def body(pair_elements, valence_of, conduction_of, valence_depth, conduction_height):
     n_pair, n_g = pair_elements.shape
     n_x, n_z = lax.axis_size("x"), lax.axis_size("zl")
@@ -122,42 +155,45 @@
     parts = 2
     chunks = turned(pair_elements, parts)
     pieces = list(chunks)
+    early_turns = n_z - 2
     for turn in range(1, n_z):
+        if turn == early_turns + 1:
+            early, *early_sent = product(
+                early_slots(n_x, n_z)[0], factor, columns, pieces[: early_turns * parts], parts, n_x
+            )
+            chunks[0], early, *early_sent = lax.optimization_barrier(
+                (chunks[0], early, *early_sent)
+            )
         chunks = [lax.ppermute(chunk, "zl", step) for chunk in chunks]
         pieces += chunks
-        if turn == n_z // 2 - 1:
+        if turn == n_z // 2 - 2:
             valence_of, conduction_of, _ = lax.optimization_barrier(
                 (valence_of, conduction_of, chunks[0])
             )
             pair_gap = lookup(valence_of, valence_depth)
             pair_gap = pair_gap + lookup(conduction_of, conduction_height)
             factor = (-4.0 / pair_gap)[None, :]
-        if turn == n_z - 3:
+        if turn == n_z - 4:
             chunks[0], factor = lax.optimization_barrier((chunks[0], factor))
 
-    my_half, my_x = lax.axis_index("zh"), lax.axis_index("x")
-    turns = jnp.arange(n_z, dtype=jnp.int32)
-    origin = lax.rem(place(lax.axis_index("zl"), n_z) - turns + n_z, n_z)
-    col = jnp.where(origin < n_z // 2, 2 * origin, 2 * n_z - 1 - 2 * origin)
-    slot = lax.rem(col % n_x - my_x + n_x, n_x)
-    stays = col // n_x == my_half
-
-    def summed_over_x(own, others):
+    def summed_over_x(own, others, *beside):
         got = [lax.ppermute(one, "x", shift(n_x, s)) for s, one in enumerate(others, 1)]
+        got, beside = lax.optimization_barrier((got, beside))
         for one in got:
             own = own + one.astype(jnp.float32)
-        return own
-
-    given, *given_sent = product(
-        jnp.where(stays, n_x, slot), factor, columns, pieces, parts, n_x
-    )
-    last = jnp.where(stays, slot, n_x)
-    last, given, *given_sent = lax.optimization_barrier((last, given, *given_sent))
-    kept, *kept_sent = product(last, factor, columns, pieces, parts, n_x)
-    given = summed_over_x(given, given_sent).astype(jnp.bfloat16)
-    given, *kept_sent = lax.optimization_barrier((given, *kept_sent))
-    got = lax.ppermute(given, "zh", shift(2, 1)).astype(jnp.float32)
-    total = summed_over_x(kept, kept_sent) + got
+        return own, *beside
+
+    axes = ("zh", "x", "zl")
+    first_sends, then_sends = swaps(n_x, n_z)
+    late_slots, early_stays = early_slots(n_x, n_z)[1:]
+    early, = summed_over_x(early, early_sent)
+    early_narrow, late_slots = lax.optimization_barrier((early.astype(jnp.bfloat16), late_slots))
+    got_early = lax.ppermute(early_narrow, axes, first_sends)
+    late, *late_sent = product(late_slots, factor, columns, pieces, parts, n_x)
+    late, got_early = summed_over_x(late, late_sent, got_early)
+    got_late = lax.ppermute(late.astype(jnp.bfloat16), axes, then_sends)
+    kept = jnp.where(early_stays, early, late)
+    total = kept + got_early.astype(jnp.float32) + got_late.astype(jnp.float32)
     return total.reshape(1, n_g, -1, n_g)
 
 

time: 161 us -> 179 us (1.11)
  the two profiles are of different devices: /device:TPU:120 before, /device:TPU:462 now
where the time goes in v8:
time: 179 us; the launch traced here: 178 us
  waiting for transfers between devices  88 us (49%)
  starting transfers between devices  58.6 us (33%)
  between operations  14 us (8%)
  Pallas kernels  9.68 us (5%)
  local copies, waits for them, and re-layouts  4.7 us (3%)
  other arithmetic  2.49 us (1%)
    ppermute x14, waiting for transfers between devices, body(): chunks = [lax.ppermute(chunk, 'zl', step) for chunk in chunks]  58.6 us
    ppermute x14, starting transfers between devices, body(): chunks = [lax.ppermute(chunk, 'zl', step) for chunk in chunks]  37 us
    ppermute x1, waiting for transfers between devices, body(): got_late = lax.ppermute(late.astype(jnp.bfloat16), axes, then_sends)  22.6 us
    ppermute x6, starting transfers between devices, summed_over_x(): lax.ppermute(one, 'x', shift(n_x, s))  19 us
    pallas_call x2, Pallas kernels, product(): pl.pallas_call(functools.partial(product_kernel, n_turns, parts), out_sha...  7.66 us
    ppermute x6, waiting for transfers between devices, summed_over_x(): lax.ppermute(one, 'x', shift(n_x, s))  6.13 us
  transfers between devices with their start and end apart: 23, of which 15 were waited for; matrix products, arithmetic and copies ran while one was open for 2% of the time, Pallas kernels for 5%

profile of v8, /device:TPU:462, one launch (start us, length us, event | category | flops | bytes accessed | tf_op | source)
XLA Modules:
  0.0 178.3 jit_solution(5868985991636002460)
XLA Ops:
  7.3 2.0 %shard_map.55 = (bf16[64,2048]{1,0:T(8,128)(2,1)}, bf16[64,2048]{1,0:T(8,128)(2,1)}) custom-call(bf16[2048,128]{1,0:T(8,128)(2,1)} %elements.1), custom_call_target="tpu_custom_call" | custom-call | tf_op jit(solution)/shard_map/pallas_call | solution.py:59
  9.3 2.9 %collective-permute-start = (bf16[64,2048]{1,0:T(8,128)(2,1)}, bf16[64,2048]{1,0:T(8,128)(2,1)S(1)}, u32[]{:S(2)}, u32[]{:S(2)}) collective-permute-start(bf16[64,2048]{1,0:T(8,128)(2,1)} %get-tuple-element.33.refs_0_), channel_id=1, source_target_pairs={{0,2},{2,4},{4,6},{6,7},{7,5},{5,3},{3,1},{1,0},{8,10},{10,12},{12... | collective-permute-start | bytes 786440 | tf_op jit(solution)/shard_map/ppermute | solution.py:167
  12.2 3.4 %collective-permute-start.6 = (bf16[64,2048]{1,0:T(8,128)(2,1)}, bf16[64,2048]{1,0:T(8,128)(2,1)S(1)}, u32[]{:S(2)}, u32[]{:S(2)}) collective-permute-start(bf16[64,2048]{1,0:T(8,128)(2,1)} %get-tuple-element.38.refs_1_), channel_id=1, source_target_pairs={{0,2},{2,4},{4,6},{6,7},{7,5},{5,3},{3,1},{1,0},{8,10},{10,12},{12... | collective-permute-start | bytes 786440 | tf_op jit(solution)/shard_map/ppermute | solution.py:167
  17.1 4.3 %collective-permute-done.refs_2_ = bf16[64,2048]{1,0:T(8,128)(2,1)S(1)} collective-permute-done((bf16[64,2048]{1,0:T(8,128)(2,1)}, bf16[64,2048]{1,0:T(8,128)(2,1)S(1)}, u32[]{:S(2)}, u32[]{:S(2)}) %collective-permute-start) | collective-permute-done | bytes 262176 | tf_op jit(solution)/shard_map/ppermute | solution.py:167
  21.5 2.0 %collective-permute-start.1 = (bf16[64,2048]{1,0:T(8,128)(2,1)S(1)}, bf16[64,2048]{1,0:T(8,128)(2,1)S(1)}, u32[]{:S(2)}, u32[]{:S(2)}) collective-permute-start(bf16[64,2048]{1,0:T(8,128)(2,1)S(1)} %collective-permute-done.refs_2_), channel_id=1, source_target_pairs={{0,2},{2,4},{4,6},{6,7},{7,5},{5,3},{3,1},{1,0},{8,10},{10,12},{12... | collective-permute-start | bytes 786440 | tf_op jit(solution)/shard_map/ppermute | solution.py:167
  23.5 3.6 %collective-permute-done.6.refs_3_ = bf16[64,2048]{1,0:T(8,128)(2,1)S(1)} collective-permute-done((bf16[64,2048]{1,0:T(8,128)(2,1)}, bf16[64,2048]{1,0:T(8,128)(2,1)S(1)}, u32[]{:S(2)}, u32[]{:S(2)}) %collective-permute-start.6) | collective-permute-done | bytes 262176 | tf_op jit(solution)/shard_map/ppermute | solution.py:167
  27.1 2.0 %collective-permute-start.7 = (bf16[64,2048]{1,0:T(8,128)(2,1)S(1)}, bf16[64,2048]{1,0:T(8,128)(2,1)S(1)}, u32[]{:S(2)}, u32[]{:S(2)}) collective-permute-start(bf16[64,2048]{1,0:T(8,128)(2,1)S(1)} %collective-permute-done.6.refs_3_), channel_id=1, source_target_pairs={{0,2},{2,4},{4,6},{6,7},{7,5},{5,3},{3,1},{1,0},{8,10},{10,12},{12... | collective-permute-start | bytes 786440 | tf_op jit(solution)/shard_map/ppermute | solution.py:167
  29.1 3.6 %collective-permute-done.1.refs_4_ = bf16[64,2048]{1,0:T(8,128)(2,1)S(1)} collective-permute-done((bf16[64,2048]{1,0:T(8,128)(2,1)S(1)}, bf16[64,2048]{1,0:T(8,128)(2,1)S(1)}, u32[]{:S(2)}, u32[]{:S(2)}) %collective-permute-start.1) | collective-permute-done | bytes 262176 | tf_op jit(solution)/shard_map/ppermute | solution.py:167
  32.7 2.0 %collective-permute-start.2 = (bf16[64,2048]{1,0:T(8,128)(2,1)S(1)}, bf16[64,2048]{1,0:T(8,128)(2,1)S(1)}, u32[]{:S(2)}, u32[]{:S(2)}) collective-permute-start(bf16[64,2048]{1,0:T(8,128)(2,1)S(1)} %collective-permute-done.1.refs_4_), channel_id=1, source_target_pairs={{0,2},{2,4},{4,6},{6,7},{7,5},{5,3},{3,1},{1,0},{8,10},{10,12},{12... | collective-permute-start | bytes 786440 | tf_op jit(solution)/shard_map/ppermute | solution.py:167
  35.5 3.6 %collective-permute-done.7.refs_5_ = bf16[64,2048]{1,0:T(8,128)(2,1)S(1)} collective-permute-done((bf16[64,2048]{1,0:T(8,128)(2,1)S(1)}, bf16[64,2048]{1,0:T(8,128)(2,1)S(1)}, u32[]{:S(2)}, u32[]{:S(2)}) %collective-permute-start.7) | collective-permute-done | bytes 262176 | tf_op jit(solution)/shard_map/ppermute | solution.py:167
  41.5 2.7 %collective-permute-done.2.refs_6_ = bf16[64,2048]{1,0:T(8,128)(2,1)S(1)} collective-permute-done((bf16[64,2048]{1,0:T(8,128)(2,1)S(1)}, bf16[64,2048]{1,0:T(8,128)(2,1)S(1)}, u32[]{:S(2)}, u32[]{:S(2)}) %collective-permute-start.2) | collective-permute-done | bytes 262176 | tf_op jit(solution)/shard_map/ppermute | solution.py:167
  46.7 3.8 %collective-permute-done.8.refs_7_ = bf16[64,2048]{1,0:T(8,128)(2,1)S(1)} collective-permute-done((bf16[64,2048]{1,0:T(8,128)(2,1)S(1)}, bf16[64,2048]{1,0:T(8,128)(2,1)S(1)}, u32[]{:S(2)}, u32[]{:S(2)}) %collective-permute-start.8) | collective-permute-done | bytes 262176 | tf_op jit(solution)/shard_map/ppermute | solution.py:167
  52.4 3.9 %collective-permute-done.3.refs_8_ = bf16[64,2048]{1,0:T(8,128)(2,1)S(1)} collective-permute-done((bf16[64,2048]{1,0:T(8,128)(2,1)S(1)}, bf16[64,2048]{1,0:T(8,128)(2,1)S(1)}, u32[]{:S(2)}, u32[]{:S(2)}) %collective-permute-start.3) | collective-permute-done | bytes 262176 | tf_op jit(solution)/shard_map/ppermute | solution.py:167
  58.2 4.3 %collective-permute-done.9.refs_9_ = bf16[64,2048]{1,0:T(8,128)(2,1)S(1)} collective-permute-done((bf16[64,2048]{1,0:T(8,128)(2,1)S(1)}, bf16[64,2048]{1,0:T(8,128)(2,1)S(1)}, u32[]{:S(2)}, u32[]{:S(2)}) %collective-permute-start.9) | collective-permute-done | bytes 262176 | tf_op jit(solution)/shard_map/ppermute | solution.py:167
  62.5 1.9 %collective-permute-start.10 = (bf16[64,2048]{1,0:T(8,128)(2,1)S(1)}, bf16[64,2048]{1,0:T(8,128)(2,1)}, u32[]{:S(2)}, u32[]{:S(2)}) collective-permute-start(bf16[64,2048]{1,0:T(8,128)(2,1)S(1)} %collective-permute-done.9.refs_9_), channel_id=1, source_target_pairs={{0,2},{2,4},{4,6},{6,7},{7,5},{5,3},{3,1},{1,0},{8,10},{10,12},{12... | collective-permute-start | bytes 786440 | tf_op jit(solution)/shard_map/ppermute | solution.py:167
  64.4 4.5 %collective-permute-done.4.refs_10_ = bf16[64,2048]{1,0:T(8,128)(2,1)S(1)} collective-permute-done((bf16[64,2048]{1,0:T(8,128)(2,1)S(1)}, bf16[64,2048]{1,0:T(8,128)(2,1)S(1)}, u32[]{:S(2)}, u32[]{:S(2)}) %collective-permute-start.4) | collective-permute-done | bytes 262176 | tf_op jit(solution)/shard_map/ppermute | solution.py:167
  70.9 4.8 %collective-permute-done.10.refs_11_ = bf16[64,2048]{1,0:T(8,128)(2,1)} collective-permute-done((bf16[64,2048]{1,0:T(8,128)(2,1)S(1)}, bf16[64,2048]{1,0:T(8,128)(2,1)}, u32[]{:S(2)}, u32[]{:S(2)}) %collective-permute-start.10) | collective-permute-done | bytes 262176 | tf_op jit(solution)/shard_map/ppermute | solution.py:167
  77.7 2.2 %copy-done = bf16[2048,1024]{1,0:T(8,128)(2,1)S(1)} copy-done((bf16[2048,1024]{1,0:T(8,128)(2,1)S(1)}, bf16[2048,1024]{1,0:T(8,128)(2,1)}, u32[]{:S(2)}) %copy-start) | copy-done | bytes 4194328
  79.9 3.8 %shard_map.56 = (f32[128,1024]{1,0:T(8,128)S(1)}, bf16[128,1024]{1,0:T(8,128)(2,1)S(1)}, bf16[128,1024]{1,0:T(8,128)(2,1)S(1)}, bf16[128,1024]{1,0:T(8,128)(2,1)S(1)}) custom-call(s32[8]{0:T(128)S(1)} %broadcast_select_fusion.slots, f32[1,2048]{1,0:T(1,128)S(1)} %bitcast.5, bf16[2048,1024]{1,0:T(8,128)(2,1)S(1)} %copy-done, bf16[64,2048]{1,0:T(8,128)(2,1)S(1)} %copy-done.2, ...), custom_call_target="tpu_custom_call" | custom-call | flops 2147483648 | bytes 8388608 | tf_op jit(solution)/shard_map/pallas_call | solution.py:100
  83.8 2.5 %collective-permute-start.11 = (bf16[128,1024]{1,0:T(8,128)(2,1)S(1)}, bf16[128,1024]{1,0:T(8,128)(2,1)S(1)}, u32[]{:S(2)}, u32[]{:S(2)}) collective-permute-start(bf16[128,1024]{1,0:T(8,128)(2,1)S(1)} %get-tuple-element.44), channel_id=1, source_target_pairs={{0,64},{64,128},{128,192},{192,0},{1,65},{65,129},{129,193},{193,1... | collective-permute-start | bytes 786440 | tf_op jit(solution)/shard_map/ppermute | solution.py:180
  86.3 4.3 %collective-permute-start.12 = (bf16[128,1024]{1,0:T(8,128)(2,1)S(1)}, bf16[128,1024]{1,0:T(8,128)(2,1)S(1)}, u32[]{:S(2)}, u32[]{:S(2)}) collective-permute-start(bf16[128,1024]{1,0:T(8,128)(2,1)S(1)} %get-tuple-element.45), channel_id=1, source_target_pairs={{0,128},{64,192},{128,0},{192,64},{1,129},{65,193},{129,1},{193,65... | collective-permute-start | bytes 786440 | tf_op jit(solution)/shard_map/ppermute | solution.py:180
  90.6 1.9 %collective-permute-start.13 = (bf16[128,1024]{1,0:T(8,128)(2,1)S(1)}, bf16[128,1024]{1,0:T(8,128)(2,1)S(1)}, u32[]{:S(2)}, u32[]{:S(2)}) collective-permute-start(bf16[128,1024]{1,0:T(8,128)(2,1)S(1)} %get-tuple-element.46), channel_id=1, source_target_pairs={{0,192},{64,0},{128,64},{192,128},{1,193},{65,1},{129,65},{193,129... | collective-permute-start | bytes 786440 | tf_op jit(solution)/shard_map/ppermute | solution.py:180
  92.6 4.9 %collective-permute-start.16 = (bf16[64,2048]{1,0:T(8,128)(2,1)}, bf16[64,2048]{1,0:T(8,128)(2,1)S(1)}, u32[]{:S(2)}, u32[]{:S(2)}) collective-permute-start(bf16[64,2048]{1,0:T(8,128)(2,1)} %collective-permute-done.14.refs_13_), channel_id=1, source_target_pairs={{0,2},{2,4},{4,6},{6,7},{7,5},{5,3},{3,1},{1,0},{8,10},{10,12},{12... | collective-permute-start | bytes 786440 | tf_op jit(solution)/shard_map/ppermute | solution.py:167
  97.5 6.5 %collective-permute-start.15 = (bf16[64,2048]{1,0:T(8,128)(2,1)}, bf16[64,2048]{1,0:T(8,128)(2,1)S(1)}, u32[]{:S(2)}, u32[]{:S(2)}) collective-permute-start(bf16[64,2048]{1,0:T(8,128)(2,1)} %collective-permute-done.5.refs_12_), channel_id=1, source_target_pairs={{0,2},{2,4},{4,6},{6,7},{7,5},{5,3},{3,1},{1,0},{8,10},{10,12},{12... | collective-permute-start | bytes 786440 | tf_op jit(solution)/shard_map/ppermute | solution.py:167
  105.5 10.4 %collective-permute-done.16.refs_15_ = bf16[64,2048]{1,0:T(8,128)(2,1)S(1)} collective-permute-done((bf16[64,2048]{1,0:T(8,128)(2,1)}, bf16[64,2048]{1,0:T(8,128)(2,1)S(1)}, u32[]{:S(2)}, u32[]{:S(2)}) %collective-permute-start.16) | collective-permute-done | bytes 262176 | tf_op jit(solution)/shard_map/ppermute | solution.py:167
  115.9 9.0 %collective-permute-done.15.refs_14_ = bf16[64,2048]{1,0:T(8,128)(2,1)S(1)} collective-permute-done((bf16[64,2048]{1,0:T(8,128)(2,1)}, bf16[64,2048]{1,0:T(8,128)(2,1)S(1)}, u32[]{:S(2)}, u32[]{:S(2)}) %collective-permute-start.15) | collective-permute-done | bytes 262176 | tf_op jit(solution)/shard_map/ppermute | solution.py:167
  124.9 3.8 %shard_map.57 = (f32[128,1024]{1,0:T(8,128)S(1)}, bf16[128,1024]{1,0:T(8,128)(2,1)S(1)}, bf16[128,1024]{1,0:T(8,128)(2,1)S(1)}, bf16[128,1024]{1,0:T(8,128)(2,1)S(1)}) custom-call(s32[8]{0:T(128)S(1)} %broadcast_select_fusion.1.slots, f32[1,2048]{1,0:T(1,128)S(1)} %bitcast.6, bf16[2048,1024]{1,0:T(8,128)(2,1)S(1)} %copy-done.1, ...), custom_call_target="tpu_custom_call" | custom-call | flops 2147483648 | bytes 8388608 | tf_op jit(solution)/shard_map/pallas_call | solution.py:100
  128.7 2.1 %collective-permute-start.17 = (bf16[128,1024]{1,0:T(8,128)(2,1)S(1)}, bf16[128,1024]{1,0:T(8,128)(2,1)S(1)}, u32[]{:S(2)}, u32[]{:S(2)}) collective-permute-start(bf16[128,1024]{1,0:T(8,128)(2,1)S(1)} %get-tuple-element.53), channel_id=1, source_target_pairs={{0,64},{64,128},{128,192},{192,0},{1,65},{65,129},{129,193},{193,1... | collective-permute-start | bytes 786440 | tf_op jit(solution)/shard_map/ppermute | solution.py:180
  130.8 4.9 %collective-permute-start.18 = (bf16[128,1024]{1,0:T(8,128)(2,1)S(1)}, bf16[128,1024]{1,0:T(8,128)(2,1)S(1)}, u32[]{:S(2)}, u32[]{:S(2)}) collective-permute-start(bf16[128,1024]{1,0:T(8,128)(2,1)S(1)} %get-tuple-element.54), channel_id=1, source_target_pairs={{0,128},{64,192},{128,0},{192,64},{1,129},{65,193},{129,1},{193,65... | collective-permute-start | bytes 786440 | tf_op jit(solution)/shard_map/ppermute | solution.py:180
  135.7 3.3 %collective-permute-start.19 = (bf16[128,1024]{1,0:T(8,128)(2,1)S(1)}, bf16[128,1024]{1,0:T(8,128)(2,1)S(1)}, u32[]{:S(2)}, u32[]{:S(2)}) collective-permute-start(bf16[128,1024]{1,0:T(8,128)(2,1)S(1)} %get-tuple-element.55), channel_id=1, source_target_pairs={{0,192},{64,0},{128,64},{192,128},{1,193},{65,1},{129,65},{193,129... | collective-permute-start | bytes 786440 | tf_op jit(solution)/shard_map/ppermute | solution.py:180
  140.6 4.6 %collective-permute-done.19 = bf16[128,1024]{1,0:T(8,128)(2,1)S(1)} collective-permute-done((bf16[128,1024]{1,0:T(8,128)(2,1)S(1)}, bf16[128,1024]{1,0:T(8,128)(2,1)S(1)}, u32[]{:S(2)}, u32[]{:S(2)}) %collective-permute-start.19) | collective-permute-done | bytes 262176 | tf_op jit(solution)/shard_map/ppermute | solution.py:180
  146.7 22.6 %collective-permute-done.21 = bf16[128,1024]{1,0:T(8,128)(2,1)S(1)} collective-permute-done((bf16[128,1024]{1,0:T(8,128)(2,1)S(1)}, bf16[128,1024]{1,0:T(8,128)(2,1)S(1)}, u32[]{:S(2)}, u32[]{:S(2)}) %collective-permute-start.21) | collective-permute-done | bytes 262176 | tf_op jit(solution)/shard_map/ppermute | solution.py:194
  (64 shorter events, 22.3 us)
Async XLA Ops:
  6.5 71.1 %all-gather.2.cloned.1.call-start = ((), (), s32[]{:S(2)}) async-start(), calls=%async_computation | async-start | bytes 4718592 | tf_op jit(solution)/shard_map/all_gather | solution.py:151
  9.3 12.2 %collective-permute-start = (bf16[64,2048]{1,0:T(8,128)(2,1)}, bf16[64,2048]{1,0:T(8,128)(2,1)S(1)}, u32[]{:S(2)}, u32[]{:S(2)}) collective-permute-start(bf16[64,2048]{1,0:T(8,128)(2,1)} %get-tuple-element.33.refs_0_), channel_id=1, source_target_pairs={{0,2},{2,4},{4,6},{6,7},{7,5},{5,3},{3,1},{1,0},{8,10},{10,12},{12... | collective-permute-start | bytes 786440 | tf_op jit(solution)/shard_map/ppermute | solution.py:167
  12.2 14.9 %collective-permute-start.6 = (bf16[64,2048]{1,0:T(8,128)(2,1)}, bf16[64,2048]{1,0:T(8,128)(2,1)S(1)}, u32[]{:S(2)}, u32[]{:S(2)}) collective-permute-start(bf16[64,2048]{1,0:T(8,128)(2,1)} %get-tuple-element.38.refs_1_), channel_id=1, source_target_pairs={{0,2},{2,4},{4,6},{6,7},{7,5},{5,3},{3,1},{1,0},{8,10},{10,12},{12... | collective-permute-start | bytes 786440 | tf_op jit(solution)/shard_map/ppermute | solution.py:167
  21.5 11.3 %collective-permute-start.1 = (bf16[64,2048]{1,0:T(8,128)(2,1)S(1)}, bf16[64,2048]{1,0:T(8,128)(2,1)S(1)}, u32[]{:S(2)}, u32[]{:S(2)}) collective-permute-start(bf16[64,2048]{1,0:T(8,128)(2,1)S(1)} %collective-permute-done.refs_2_), channel_id=1, source_target_pairs={{0,2},{2,4},{4,6},{6,7},{7,5},{5,3},{3,1},{1,0},{8,10},{10,12},{12... | collective-permute-start | bytes 786440 | tf_op jit(solution)/shard_map/ppermute | solution.py:167
  27.1 12.0 %collective-permute-start.7 = (bf16[64,2048]{1,0:T(8,128)(2,1)S(1)}, bf16[64,2048]{1,0:T(8,128)(2,1)S(1)}, u32[]{:S(2)}, u32[]{:S(2)}) collective-permute-start(bf16[64,2048]{1,0:T(8,128)(2,1)S(1)} %collective-permute-done.6.refs_3_), channel_id=1, source_target_pairs={{0,2},{2,4},{4,6},{6,7},{7,5},{5,3},{3,1},{1,0},{8,10},{10,12},{12... | collective-permute-start | bytes 786440 | tf_op jit(solution)/shard_map/ppermute | solution.py:167
  32.7 11.5 %collective-permute-start.2 = (bf16[64,2048]{1,0:T(8,128)(2,1)S(1)}, bf16[64,2048]{1,0:T(8,128)(2,1)S(1)}, u32[]{:S(2)}, u32[]{:S(2)}) collective-permute-start(bf16[64,2048]{1,0:T(8,128)(2,1)S(1)} %collective-permute-done.1.refs_4_), channel_id=1, source_target_pairs={{0,2},{2,4},{4,6},{6,7},{7,5},{5,3},{3,1},{1,0},{8,10},{10,12},{12... | collective-permute-start | bytes 786440 | tf_op jit(solution)/shard_map/ppermute | solution.py:167
  39.1 11.4 %collective-permute-start.8 = (bf16[64,2048]{1,0:T(8,128)(2,1)S(1)}, bf16[64,2048]{1,0:T(8,128)(2,1)S(1)}, u32[]{:S(2)}, u32[]{:S(2)}) collective-permute-start(bf16[64,2048]{1,0:T(8,128)(2,1)S(1)} %collective-permute-done.7.refs_5_), channel_id=1, source_target_pairs={{0,2},{2,4},{4,6},{6,7},{7,5},{5,3},{3,1},{1,0},{8,10},{10,12},{12... | collective-permute-start | bytes 786440 | tf_op jit(solution)/shard_map/ppermute | solution.py:167
  41.0 36.7 %copy-start.2 = (bf16[64,2048]{1,0:T(8,128)(2,1)S(1)}, bf16[64,2048]{1,0:T(8,128)(2,1)}, u32[]{:S(2)}) copy-start(bf16[64,2048]{1,0:T(8,128)(2,1)} %get-tuple-element.33.refs_0_) | copy-start | bytes 786436
  41.0 36.7 %copy-start.3 = (bf16[64,2048]{1,0:T(8,128)(2,1)S(1)}, bf16[64,2048]{1,0:T(8,128)(2,1)}, u32[]{:S(2)}) copy-start(bf16[64,2048]{1,0:T(8,128)(2,1)} %get-tuple-element.38.refs_1_) | copy-start | bytes 786436
  44.3 12.0 %collective-permute-start.3 = (bf16[64,2048]{1,0:T(8,128)(2,1)S(1)}, bf16[64,2048]{1,0:T(8,128)(2,1)S(1)}, u32[]{:S(2)}, u32[]{:S(2)}) collective-permute-start(bf16[64,2048]{1,0:T(8,128)(2,1)S(1)} %collective-permute-done.2.refs_6_), channel_id=1, source_target_pairs={{0,2},{2,4},{4,6},{6,7},{7,5},{5,3},{3,1},{1,0},{8,10},{10,12},{12... | collective-permute-start | bytes 786440 | tf_op jit(solution)/shard_map/ppermute | solution.py:167
  50.5 12.0 %collective-permute-start.9 = (bf16[64,2048]{1,0:T(8,128)(2,1)S(1)}, bf16[64,2048]{1,0:T(8,128)(2,1)S(1)}, u32[]{:S(2)}, u32[]{:S(2)}) collective-permute-start(bf16[64,2048]{1,0:T(8,128)(2,1)S(1)} %collective-permute-done.8.refs_7_), channel_id=1, source_target_pairs={{0,2},{2,4},{4,6},{6,7},{7,5},{5,3},{3,1},{1,0},{8,10},{10,12},{12... | collective-permute-start | bytes 786440 | tf_op jit(solution)/shard_map/ppermute | solution.py:167
  56.3 12.7 %collective-permute-start.4 = (bf16[64,2048]{1,0:T(8,128)(2,1)S(1)}, bf16[64,2048]{1,0:T(8,128)(2,1)S(1)}, u32[]{:S(2)}, u32[]{:S(2)}) collective-permute-start(bf16[64,2048]{1,0:T(8,128)(2,1)S(1)} %collective-permute-done.3.refs_8_), channel_id=1, source_target_pairs={{0,2},{2,4},{4,6},{6,7},{7,5},{5,3},{3,1},{1,0},{8,10},{10,12},{12... | collective-permute-start | bytes 786440 | tf_op jit(solution)/shard_map/ppermute | solution.py:167
  62.5 21.2 %copy-start.4 = (bf16[64,2048]{1,0:T(8,128)(2,1)}, bf16[64,2048]{1,0:T(8,128)(2,1)S(1)}, u32[]{:S(2)}) copy-start(bf16[64,2048]{1,0:T(8,128)(2,1)S(1)} %collective-permute-done.9.refs_9_) | copy-start | bytes 786436
  62.5 13.3 %collective-permute-start.10 = (bf16[64,2048]{1,0:T(8,128)(2,1)S(1)}, bf16[64,2048]{1,0:T(8,128)(2,1)}, u32[]{:S(2)}, u32[]{:S(2)}) collective-permute-start(bf16[64,2048]{1,0:T(8,128)(2,1)S(1)} %collective-permute-done.9.refs_9_), channel_id=1, source_target_pairs={{0,2},{2,4},{4,6},{6,7},{7,5},{5,3},{3,1},{1,0},{8,10},{10,12},{12... | collective-permute-start | bytes 786440 | tf_op jit(solution)/shard_map/ppermute | solution.py:167
  68.9 14.8 %collective-permute-start.5 = (bf16[64,2048]{1,0:T(8,128)(2,1)S(1)}, bf16[64,2048]{1,0:T(8,128)(2,1)}, u32[]{:S(2)}, u32[]{:S(2)}) collective-permute-start(bf16[64,2048]{1,0:T(8,128)(2,1)S(1)} %collective-permute-done.4.refs_10_), channel_id=1, source_target_pairs={{0,2},{2,4},{4,6},{6,7},{7,5},{5,3},{3,1},{1,0},{8,10},{10,12},{12... | collective-permute-start | bytes 786440 | tf_op jit(solution)/shard_map/ppermute | solution.py:167
  75.7 16.9 %collective-permute-start.14 = (bf16[64,2048]{1,0:T(8,128)(2,1)}, bf16[64,2048]{1,0:T(8,128)(2,1)}, u32[]{:S(2)}, u32[]{:S(2)}) collective-permute-start(bf16[64,2048]{1,0:T(8,128)(2,1)} %collective-permute-done.10.refs_11_), channel_id=1, source_target_pairs={{0,2},{2,4},{4,6},{6,7},{7,5},{5,3},{3,1},{1,0},{8,10},{10,12},{12... | collective-permute-start | bytes 786440 | tf_op jit(solution)/shard_map/ppermute | solution.py:167
  79.9 45.0 %copy-start.1 = (bf16[2048,1024]{1,0:T(8,128)(2,1)S(1)}, bf16[2048,1024]{1,0:T(8,128)(2,1)}, u32[]{:S(2)}) copy-start(bf16[2048,1024]{1,0:T(8,128)(2,1)} %all-gather.2.cloned.1.call-done.columns) | copy-start | bytes 12582916
  83.7 41.1 %copy-start.5 = (bf16[64,2048]{1,0:T(8,128)(2,1)S(1)}, bf16[64,2048]{1,0:T(8,128)(2,1)}, u32[]{:S(2)}) copy-start(bf16[64,2048]{1,0:T(8,128)(2,1)} %copy-done.4) | copy-start | bytes 786436
  83.8 41.1 %copy-start.7 = (bf16[64,2048]{1,0:T(8,128)(2,1)S(1)}, bf16[64,2048]{1,0:T(8,128)(2,1)}, u32[]{:S(2)}) copy-start(bf16[64,2048]{1,0:T(8,128)(2,1)} %copy-done.6) | copy-start | bytes 786436
  83.8 20.2 %collective-permute-start.11 = (bf16[128,1024]{1,0:T(8,128)(2,1)S(1)}, bf16[128,1024]{1,0:T(8,128)(2,1)S(1)}, u32[]{:S(2)}, u32[]{:S(2)}) collective-permute-start(bf16[128,1024]{1,0:T(8,128)(2,1)S(1)} %get-tuple-element.44), channel_id=1, source_target_pairs={{0,64},{64,128},{128,192},{192,0},{1,65},{65,129},{129,193},{193,1... | collective-permute-start | bytes 786440 | tf_op jit(solution)/shard_map/ppermute | solution.py:180
  86.3 17.7 %collective-permute-start.12 = (bf16[128,1024]{1,0:T(8,128)(2,1)S(1)}, bf16[128,1024]{1,0:T(8,128)(2,1)S(1)}, u32[]{:S(2)}, u32[]{:S(2)}) collective-permute-start(bf16[128,1024]{1,0:T(8,128)(2,1)S(1)} %get-tuple-element.45), channel_id=1, source_target_pairs={{0,128},{64,192},{128,0},{192,64},{1,129},{65,193},{129,1},{193,65... | collective-permute-start | bytes 786440 | tf_op jit(solution)/shard_map/ppermute | solution.py:180
  90.6 13.4 %collective-permute-start.13 = (bf16[128,1024]{1,0:T(8,128)(2,1)S(1)}, bf16[128,1024]{1,0:T(8,128)(2,1)S(1)}, u32[]{:S(2)}, u32[]{:S(2)}) collective-permute-start(bf16[128,1024]{1,0:T(8,128)(2,1)S(1)} %get-tuple-element.46), channel_id=1, source_target_pairs={{0,192},{64,0},{128,64},{192,128},{1,193},{65,1},{129,65},{193,129... | collective-permute-start | bytes 786440 | tf_op jit(solution)/shard_map/ppermute | solution.py:180
  92.6 23.2 %collective-permute-start.16 = (bf16[64,2048]{1,0:T(8,128)(2,1)}, bf16[64,2048]{1,0:T(8,128)(2,1)S(1)}, u32[]{:S(2)}, u32[]{:S(2)}) collective-permute-start(bf16[64,2048]{1,0:T(8,128)(2,1)} %collective-permute-done.14.refs_13_), channel_id=1, source_target_pairs={{0,2},{2,4},{4,6},{6,7},{7,5},{5,3},{3,1},{1,0},{8,10},{10,12},{12... | collective-permute-start | bytes 786440 | tf_op jit(solution)/shard_map/ppermute | solution.py:167
  97.5 27.4 %collective-permute-start.15 = (bf16[64,2048]{1,0:T(8,128)(2,1)}, bf16[64,2048]{1,0:T(8,128)(2,1)S(1)}, u32[]{:S(2)}, u32[]{:S(2)}) collective-permute-start(bf16[64,2048]{1,0:T(8,128)(2,1)} %collective-permute-done.5.refs_12_), channel_id=1, source_target_pairs={{0,2},{2,4},{4,6},{6,7},{7,5},{5,3},{3,1},{1,0},{8,10},{10,12},{12... | collective-permute-start | bytes 786440 | tf_op jit(solution)/shard_map/ppermute | solution.py:167
  104.2 34.9 %collective-permute-start.20 = (bf16[128,1024]{1,0:T(8,128)(2,1)S(1)}, bf16[128,1024]{1,0:T(8,128)(2,1)S(1)}, u32[]{:S(2)}, u32[]{:S(2)}) collective-permute-start(bf16[128,1024]{1,0:T(8,128)(2,1)S(1)} %fusion.4), channel_id=1, source_target_pairs={{256,0},{1,257},{258,2},{3,259},{4,260},{5,261},{6,262},{7,263},{3... | collective-permute-start | bytes 786440 | tf_op jit(solution)/shard_map/ppermute | solution.py:191
  128.7 40.5 %copy-start.9 = (bf16[128,1024]{1,0:T(8,128)(2,1)S(1)}, bf16[128,1024]{1,0:T(8,128)(2,1)}, u32[]{:S(2)}) copy-start(bf16[128,1024]{1,0:T(8,128)(2,1)} %copy-done.8) | copy-start | bytes 786436
  128.7 40.5 %copy-start.11 = (bf16[128,1024]{1,0:T(8,128)(2,1)S(1)}, bf16[128,1024]{1,0:T(8,128)(2,1)}, u32[]{:S(2)}) copy-start(bf16[128,1024]{1,0:T(8,128)(2,1)} %copy-done.10) | copy-start | bytes 786436
  128.7 40.5 %copy-start.13 = (bf16[128,1024]{1,0:T(8,128)(2,1)S(1)}, bf16[128,1024]{1,0:T(8,128)(2,1)}, u32[]{:S(2)}) copy-start(bf16[128,1024]{1,0:T(8,128)(2,1)} %copy-done.12) | copy-start | bytes 786436
  128.7 10.3 %collective-permute-start.17 = (bf16[128,1024]{1,0:T(8,128)(2,1)S(1)}, bf16[128,1024]{1,0:T(8,128)(2,1)S(1)}, u32[]{:S(2)}, u32[]{:S(2)}) collective-permute-start(bf16[128,1024]{1,0:T(8,128)(2,1)S(1)} %get-tuple-element.53), channel_id=1, source_target_pairs={{0,64},{64,128},{128,192},{192,0},{1,65},{65,129},{129,193},{193,1... | collective-permute-start | bytes 786440 | tf_op jit(solution)/shard_map/ppermute | solution.py:180
  130.8 9.8 %collective-permute-start.18 = (bf16[128,1024]{1,0:T(8,128)(2,1)S(1)}, bf16[128,1024]{1,0:T(8,128)(2,1)S(1)}, u32[]{:S(2)}, u32[]{:S(2)}) collective-permute-start(bf16[128,1024]{1,0:T(8,128)(2,1)S(1)} %get-tuple-element.54), channel_id=1, source_target_pairs={{0,128},{64,192},{128,0},{192,64},{1,129},{65,193},{129,1},{193,65... | collective-permute-start | bytes 786440 | tf_op jit(solution)/shard_map/ppermute | solution.py:180
  135.7 9.5 %collective-permute-start.19 = (bf16[128,1024]{1,0:T(8,128)(2,1)S(1)}, bf16[128,1024]{1,0:T(8,128)(2,1)S(1)}, u32[]{:S(2)}, u32[]{:S(2)}) collective-permute-start(bf16[128,1024]{1,0:T(8,128)(2,1)S(1)} %get-tuple-element.55), channel_id=1, source_target_pairs={{0,192},{64,0},{128,64},{192,128},{1,193},{65,1},{129,65},{193,129... | collective-permute-start | bytes 786440 | tf_op jit(solution)/shard_map/ppermute | solution.py:180
  145.3 23.9 %collective-permute-start.21 = (bf16[128,1024]{1,0:T(8,128)(2,1)S(1)}, bf16[128,1024]{1,0:T(8,128)(2,1)S(1)}, u32[]{:S(2)}, u32[]{:S(2)}) collective-permute-start(bf16[128,1024]{1,0:T(8,128)(2,1)S(1)} %fusion.5), channel_id=1, source_target_pairs={{0,256},{257,1},{2,258},{259,3},{260,4},{261,5},{262,6},{263,7},{6... | collective-permute-start | bytes 786440 | tf_op jit(solution)/shard_map/ppermute | solution.py:194
  (6 other events, 58.7 us)
Sparse Core Ops, SparseCore 0:
  9.5 42.6 all-gather.1

commit v9 on v7

--- a/solution.py
+++ b/solution.py
@@ -24,10 +24,10 @@
     return jnp.where(col % 2 == 0, col // 2, (2 * n - 1 - col) // 2)
 
 
-def cuts(rows, parts):
-    tiles = rows // 16
-    sizes = [16 * (tiles // parts + (i < tiles % parts)) for i in range(parts)]
-    return [(sum(sizes[:i]), sum(sizes[: i + 1])) for i in range(parts)]
+def cuts(lanes, parts):
+    tiles = lanes // 128
+    ends = [128 * (tiles * i // parts) for i in range(parts + 1)]
+    return list(zip(ends, ends[1:]))
 
 
 def lookup(indices, table):
@@ -47,11 +47,8 @@
 
 
 def turned_kernel(elements, *chunks):
-    turned = elements[...].astype(jnp.float32).T.astype(jnp.bfloat16)
-    first = 0
-    for chunk in chunks:
-        chunk[...] = turned[first : first + chunk.shape[0]]
-        first += chunk.shape[0]
+    for chunk, (a, b) in zip(chunks, cuts(elements.shape[0], len(chunks))):
+        chunk[...] = elements[a:b, :].astype(jnp.float32).T.astype(jnp.bfloat16)
 
 
 def turned(elements, parts):
@@ -59,7 +56,7 @@
     return pl.pallas_call(
         turned_kernel,
         out_shape=[
-            jax.ShapeDtypeStruct((b - a, n_pair), elements.dtype) for a, b in cuts(n_g, parts)
+            jax.ShapeDtypeStruct((n_g, b - a), elements.dtype) for a, b in cuts(n_pair, parts)
         ],
         in_specs=[WHOLE],
         out_specs=[WHOLE] * parts,
@@ -75,14 +72,11 @@
 
         @pl.when(slot < 1 + len(others))
         def _():
-            base = slot * n_g
-            offset = 0
-            for piece in pieces[turn * parts : (turn + 1) * parts]:
-                size = piece.shape[0]
-                at = pl.multiple_of(base + offset, 16)
-                value = piece[...].astype(jnp.float32) * factor[...]
-                rows[pl.ds(at, size), :] = value.astype(jnp.bfloat16)
-                offset += size
+            at = pl.multiple_of(slot * n_g, 128)
+            ends = cuts(rows.shape[1], parts)
+            for piece, (a, b) in zip(pieces[turn * parts : (turn + 1) * parts], ends):
+                value = piece[...].astype(jnp.float32) * factor[:, a:b]
+                rows[pl.ds(at, n_g), a:b] = value.astype(jnp.bfloat16)
 
     for i in range(0, 1 + len(others), 2):
         both = jnp.dot(
@@ -95,7 +89,7 @@
 def product(slots, factor, columns, pieces, parts, n_slots):
     n_pair, width = columns.shape
     n_turns = len(pieces) // parts
-    n_g = sum(piece.shape[0] for piece in pieces[:parts])
+    n_g = pieces[0].shape[0]
     kinds = [jnp.float32] + [jnp.bfloat16] * (n_slots - 1)
     return pl.pallas_call(
         functools.partial(product_kernel, n_turns, parts),
@@ -119,21 +113,21 @@
 
     order = circle(n_z)
     step = [(order[i], order[(i + 1) % n_z]) for i in range(n_z)]
-    parts = 2
+    parts = 3
     chunks = turned(pair_elements, parts)
     pieces = list(chunks)
     for turn in range(1, n_z):
+        if turn == n_z - 2:
+            chunks[0], factor = lax.optimization_barrier((chunks[0], factor))
         chunks = [lax.ppermute(chunk, "zl", step) for chunk in chunks]
         pieces += chunks
-        if turn == n_z // 2 - 1:
+        if turn == n_z // 2 - 2:
             valence_of, conduction_of, _ = lax.optimization_barrier(
                 (valence_of, conduction_of, chunks[0])
             )
             pair_gap = lookup(valence_of, valence_depth)
             pair_gap = pair_gap + lookup(conduction_of, conduction_height)
             factor = (-4.0 / pair_gap)[None, :]
-        if turn == n_z - 3:
-            chunks[0], factor = lax.optimization_barrier((chunks[0], factor))
 
     my_half, my_x = lax.axis_index("zh"), lax.axis_index("x")
     turns = jnp.arange(n_z, dtype=jnp.int32)

time: 161 us -> 163 us (1.012)
  the two profiles are of different devices: /device:TPU:120 before, /device:TPU:72 now
where the time goes in v9:
time: 163 us; the launch traced here: 162 us
  starting transfers between devices  104 us (64%)
  waiting for transfers between devices  27 us (17%)
  between operations  13.9 us (9%)
  Pallas kernels  10.1 us (6%)
  local copies, waits for them, and re-layouts  4.65 us (3%)
    ppermute x21, starting transfers between devices, body(): chunks = [lax.ppermute(chunk, 'zl', step) for chunk in chunks]  76.5 us
    ppermute x6, starting transfers between devices, summed_over_x(): lax.ppermute(one, 'x', shift(n_x, s))  18.5 us
    ppermute x1, waiting for transfers between devices, body(): got = lax.ppermute(given, 'zh', shift(2, 1)).astype(jnp.float32)  12.9 us
    ppermute x21, waiting for transfers between devices, body(): chunks = [lax.ppermute(chunk, 'zl', step) for chunk in chunks]  9.34 us
    ppermute x1, starting transfers between devices, body(): got = lax.ppermute(given, 'zh', shift(2, 1)).astype(jnp.float32)  8.84 us
    pallas_call x2, Pallas kernels, product(): pl.pallas_call(functools.partial(product_kernel, n_turns, parts), out_sha...  8.09 us
    ppermute x6, waiting for transfers between devices, summed_over_x(): lax.ppermute(one, 'x', shift(n_x, s))  4.11 us
  transfers between devices with their start and end apart: 29, of which 10 were waited for; matrix products, arithmetic and copies ran while one was open for 2% of the time, Pallas kernels for 4%

profile of v9, /device:TPU:72, one launch (start us, length us, event | category | flops | bytes accessed | tf_op | source)
XLA Modules:
  0.0 161.5 jit_solution(15771044623819539593)
XLA Ops:
  9.2 6.4 %collective-permute-start.6 = (bf16[128,768]{1,0:T(8,128)(2,1)}, bf16[128,768]{1,0:T(8,128)(2,1)S(1)}, u32[]{:S(2)}, u32[]{:S(2)}) collective-permute-start(bf16[128,768]{1,0:T(8,128)(2,1)} %get-tuple-element.34.refs_2_), channel_id=1, source_target_pairs={{0,2},{2,4},{4,6},{6,7},{7,5},{5,3},{3,1},{1,0},{8,10},{10,12},{12... | collective-permute-start | bytes 589832 | tf_op jit(solution)/shard_map/ppermute | solution.py:122
  15.6 5.2 %collective-permute-start = (bf16[128,640]{1,0:T(8,128)(2,1)}, bf16[128,640]{1,0:T(8,128)(2,1)S(1)}, u32[]{:S(2)}, u32[]{:S(2)}) collective-permute-start(bf16[128,640]{1,0:T(8,128)(2,1)} %get-tuple-element.29.refs_0_), channel_id=1, source_target_pairs={{0,2},{2,4},{4,6},{6,7},{7,5},{5,3},{3,1},{1,0},{8,10},{10,12},{12... | collective-permute-start | bytes 491528 | tf_op jit(solution)/shard_map/ppermute | solution.py:122
  20.8 3.8 %collective-permute-start.5 = (bf16[128,640]{1,0:T(8,128)(2,1)}, bf16[128,640]{1,0:T(8,128)(2,1)S(1)}, u32[]{:S(2)}, u32[]{:S(2)}) collective-permute-start(bf16[128,640]{1,0:T(8,128)(2,1)} %get-tuple-element.33.refs_1_), channel_id=1, source_target_pairs={{0,2},{2,4},{4,6},{6,7},{7,5},{5,3},{3,1},{1,0},{8,10},{10,12},{12... | collective-permute-start | bytes 491528 | tf_op jit(solution)/shard_map/ppermute | solution.py:122
  28.1 2.9 %collective-permute-start.1 = (bf16[128,640]{1,0:T(8,128)(2,1)S(1)}, bf16[128,640]{1,0:T(8,128)(2,1)S(1)}, u32[]{:S(2)}, u32[]{:S(2)}) collective-permute-start(bf16[128,640]{1,0:T(8,128)(2,1)S(1)} %collective-permute-done.refs_3_), channel_id=1, source_target_pairs={{0,2},{2,4},{4,6},{6,7},{7,5},{5,3},{3,1},{1,0},{8,10},{10,12},{12... | collective-permute-start | bytes 491528 | tf_op jit(solution)/shard_map/ppermute | solution.py:122
  31.1 3.7 %collective-permute-start.7 = (bf16[128,640]{1,0:T(8,128)(2,1)S(1)}, bf16[128,640]{1,0:T(8,128)(2,1)S(1)}, u32[]{:S(2)}, u32[]{:S(2)}) collective-permute-start(bf16[128,640]{1,0:T(8,128)(2,1)S(1)} %collective-permute-done.5.refs_4_), channel_id=1, source_target_pairs={{0,2},{2,4},{4,6},{6,7},{7,5},{5,3},{3,1},{1,0},{8,10},{10,12},{12... | collective-permute-start | bytes 491528 | tf_op jit(solution)/shard_map/ppermute | solution.py:122
  36.8 3.1 %collective-permute-start.10 = (bf16[128,768]{1,0:T(8,128)(2,1)S(1)}, bf16[128,768]{1,0:T(8,128)(2,1)S(1)}, u32[]{:S(2)}, u32[]{:S(2)}) collective-permute-start(bf16[128,768]{1,0:T(8,128)(2,1)S(1)} %collective-permute-done.8.refs_8_), channel_id=1, source_target_pairs={{0,2},{2,4},{4,6},{6,7},{7,5},{5,3},{3,1},{1,0},{8,10},{10,12},{12... | collective-permute-start | bytes 589832 | tf_op jit(solution)/shard_map/ppermute | solution.py:122
  40.3 3.1 %collective-permute-start.2 = (bf16[128,640]{1,0:T(8,128)(2,1)S(1)}, bf16[128,640]{1,0:T(8,128)(2,1)S(1)}, u32[]{:S(2)}, u32[]{:S(2)}) collective-permute-start(bf16[128,640]{1,0:T(8,128)(2,1)S(1)} %collective-permute-done.1.refs_6_), channel_id=1, source_target_pairs={{0,2},{2,4},{4,6},{6,7},{7,5},{5,3},{3,1},{1,0},{8,10},{10,12},{12... | collective-permute-start | bytes 491528 | tf_op jit(solution)/shard_map/ppermute | solution.py:122
  43.8 3.1 %collective-permute-start.9 = (bf16[128,640]{1,0:T(8,128)(2,1)S(1)}, bf16[128,640]{1,0:T(8,128)(2,1)S(1)}, u32[]{:S(2)}, u32[]{:S(2)}) collective-permute-start(bf16[128,640]{1,0:T(8,128)(2,1)S(1)} %collective-permute-done.7.refs_7_), channel_id=1, source_target_pairs={{0,2},{2,4},{4,6},{6,7},{7,5},{5,3},{3,1},{1,0},{8,10},{10,12},{12... | collective-permute-start | bytes 491528 | tf_op jit(solution)/shard_map/ppermute | solution.py:122
  48.1 3.7 %collective-permute-start.12 = (bf16[128,768]{1,0:T(8,128)(2,1)S(1)}, bf16[128,768]{1,0:T(8,128)(2,1)S(1)}, u32[]{:S(2)}, u32[]{:S(2)}) collective-permute-start(bf16[128,768]{1,0:T(8,128)(2,1)S(1)} %collective-permute-done.10.refs_11_), channel_id=1, source_target_pairs={{0,2},{2,4},{4,6},{6,7},{7,5},{5,3},{3,1},{1,0},{8,10},{10,12},{12... | collective-permute-start | bytes 589832 | tf_op jit(solution)/shard_map/ppermute | solution.py:122
  52.5 2.8 %collective-permute-start.3 = (bf16[128,640]{1,0:T(8,128)(2,1)S(1)}, bf16[128,640]{1,0:T(8,128)(2,1)S(1)}, u32[]{:S(2)}, u32[]{:S(2)}) collective-permute-start(bf16[128,640]{1,0:T(8,128)(2,1)S(1)} %collective-permute-done.2.refs_9_), channel_id=1, source_target_pairs={{0,2},{2,4},{4,6},{6,7},{7,5},{5,3},{3,1},{1,0},{8,10},{10,12},{12... | collective-permute-start | bytes 491528 | tf_op jit(solution)/shard_map/ppermute | solution.py:122
  55.3 3.5 %collective-permute-start.11 = (bf16[128,640]{1,0:T(8,128)(2,1)S(1)}, bf16[128,640]{1,0:T(8,128)(2,1)S(1)}, u32[]{:S(2)}, u32[]{:S(2)}) collective-permute-start(bf16[128,640]{1,0:T(8,128)(2,1)S(1)} %collective-permute-done.9.refs_10_), channel_id=1, source_target_pairs={{0,2},{2,4},{4,6},{6,7},{7,5},{5,3},{3,1},{1,0},{8,10},{10,12},{12... | collective-permute-start | bytes 491528 | tf_op jit(solution)/shard_map/ppermute | solution.py:122
  59.3 4.2 %collective-permute-start.14 = (bf16[128,768]{1,0:T(8,128)(2,1)S(1)}, bf16[128,768]{1,0:T(8,128)(2,1)S(1)}, u32[]{:S(2)}, u32[]{:S(2)}) collective-permute-start(bf16[128,768]{1,0:T(8,128)(2,1)S(1)} %collective-permute-done.12.refs_14_), channel_id=1, source_target_pairs={{0,2},{2,4},{4,6},{6,7},{7,5},{5,3},{3,1},{1,0},{8,10},{10,12},{12... | collective-permute-start | bytes 589832 | tf_op jit(solution)/shard_map/ppermute | solution.py:122
  64.6 2.6 %collective-permute-start.4 = (bf16[128,640]{1,0:T(8,128)(2,1)S(1)}, bf16[128,640]{1,0:T(8,128)(2,1)S(1)}, u32[]{:S(2)}, u32[]{:S(2)}) collective-permute-start(bf16[128,640]{1,0:T(8,128)(2,1)S(1)} %collective-permute-done.3.refs_12_), channel_id=1, source_target_pairs={{0,2},{2,4},{4,6},{6,7},{7,5},{5,3},{3,1},{1,0},{8,10},{10,12},{12... | collective-permute-start | bytes 491528 | tf_op jit(solution)/shard_map/ppermute | solution.py:122
  67.2 3.3 %collective-permute-start.13 = (bf16[128,640]{1,0:T(8,128)(2,1)S(1)}, bf16[128,640]{1,0:T(8,128)(2,1)S(1)}, u32[]{:S(2)}, u32[]{:S(2)}) collective-permute-start(bf16[128,640]{1,0:T(8,128)(2,1)S(1)} %collective-permute-done.11.refs_13_), channel_id=1, source_target_pairs={{0,2},{2,4},{4,6},{6,7},{7,5},{5,3},{3,1},{1,0},{8,10},{10,12},{12... | collective-permute-start | bytes 491528 | tf_op jit(solution)/shard_map/ppermute | solution.py:122
  70.5 4.7 %collective-permute-start.17 = (bf16[128,768]{1,0:T(8,128)(2,1)S(1)}, bf16[128,768]{1,0:T(8,128)(2,1)S(1)}, u32[]{:S(2)}, u32[]{:S(2)}) collective-permute-start(bf16[128,768]{1,0:T(8,128)(2,1)S(1)} %collective-permute-done.14.refs_17_), channel_id=1, source_target_pairs={{0,2},{2,4},{4,6},{6,7},{7,5},{5,3},{3,1},{1,0},{8,10},{10,12},{12... | collective-permute-start | bytes 589832 | tf_op jit(solution)/shard_map/ppermute | solution.py:122
  75.2 3.5 %collective-permute-start.15 = (bf16[128,640]{1,0:T(8,128)(2,1)S(1)}, bf16[128,640]{1,0:T(8,128)(2,1)}, u32[]{:S(2)}, u32[]{:S(2)}) collective-permute-start(bf16[128,640]{1,0:T(8,128)(2,1)S(1)} %collective-permute-done.4.refs_15_), channel_id=1, source_target_pairs={{0,2},{2,4},{4,6},{6,7},{7,5},{5,3},{3,1},{1,0},{8,10},{10,12},{12... | collective-permute-start | bytes 491528 | tf_op jit(solution)/shard_map/ppermute | solution.py:122
  78.7 3.5 %collective-permute-start.16 = (bf16[128,640]{1,0:T(8,128)(2,1)S(1)}, bf16[128,640]{1,0:T(8,128)(2,1)}, u32[]{:S(2)}, u32[]{:S(2)}) collective-permute-start(bf16[128,640]{1,0:T(8,128)(2,1)S(1)} %collective-permute-done.13.refs_16_), channel_id=1, source_target_pairs={{0,2},{2,4},{4,6},{6,7},{7,5},{5,3},{3,1},{1,0},{8,10},{10,12},{12... | collective-permute-start | bytes 491528 | tf_op jit(solution)/shard_map/ppermute | solution.py:122
  82.3 4.8 %collective-permute-start.20 = (bf16[128,768]{1,0:T(8,128)(2,1)S(1)}, bf16[128,768]{1,0:T(8,128)(2,1)S(1)}, u32[]{:S(2)}, u32[]{:S(2)}) collective-permute-start(bf16[128,768]{1,0:T(8,128)(2,1)S(1)} %collective-permute-done.17.refs_20_), channel_id=1, source_target_pairs={{0,2},{2,4},{4,6},{6,7},{7,5},{5,3},{3,1},{1,0},{8,10},{10,12},{12... | collective-permute-start | bytes 589832 | tf_op jit(solution)/shard_map/ppermute | solution.py:122
  87.1 3.3 %collective-permute-start.18 = (bf16[128,640]{1,0:T(8,128)(2,1)}, bf16[128,640]{1,0:T(8,128)(2,1)}, u32[]{:S(2)}, u32[]{:S(2)}) collective-permute-start(bf16[128,640]{1,0:T(8,128)(2,1)} %collective-permute-done.15.refs_18_), channel_id=1, source_target_pairs={{0,2},{2,4},{4,6},{6,7},{7,5},{5,3},{3,1},{1,0},{8,10},{10,12},{12... | collective-permute-start | bytes 491528 | tf_op jit(solution)/shard_map/ppermute | solution.py:122
  90.3 3.5 %collective-permute-start.19 = (bf16[128,640]{1,0:T(8,128)(2,1)}, bf16[128,640]{1,0:T(8,128)(2,1)}, u32[]{:S(2)}, u32[]{:S(2)}) collective-permute-start(bf16[128,640]{1,0:T(8,128)(2,1)} %collective-permute-done.16.refs_19_), channel_id=1, source_target_pairs={{0,2},{2,4},{4,6},{6,7},{7,5},{5,3},{3,1},{1,0},{8,10},{10,12},{12... | collective-permute-start | bytes 491528 | tf_op jit(solution)/shard_map/ppermute | solution.py:122
  96.3 2.4 %collective-permute-done.19.refs_22_ = bf16[128,640]{1,0:T(8,128)(2,1)} collective-permute-done((bf16[128,640]{1,0:T(8,128)(2,1)}, bf16[128,640]{1,0:T(8,128)(2,1)}, u32[]{:S(2)}, u32[]{:S(2)}) %collective-permute-start.19) | collective-permute-done | bytes 163872 | tf_op jit(solution)/shard_map/ppermute | solution.py:122
  101.0 4.1 %shard_map.56 = (f32[128,1024]{1,0:T(8,128)S(1)}, bf16[128,1024]{1,0:T(8,128)(2,1)S(1)}, bf16[128,1024]{1,0:T(8,128)(2,1)S(1)}, bf16[128,1024]{1,0:T(8,128)(2,1)S(1)}) custom-call(s32[8]{0:T(128)S(1)} %get-tuple-element.63.slots, f32[1,2048]{1,0:T(1,128)S(1)} %bitcast.5, bf16[2048,1024]{1,0:T(8,128)(2,1)S(1)} %copy-done, bf16[128,640]{1,0:T(8,128)(2,1)S(1)} %copy-done.3, ...), custom_call_target="tpu_custom_call" | custom-call | flops 2147483648 | bytes 8388608 | tf_op jit(solution)/shard_map/pallas_call | solution.py:94
  105.1 4.7 %collective-permute-start.23 = (bf16[128,1024]{1,0:T(8,128)(2,1)S(1)}, bf16[128,1024]{1,0:T(8,128)(2,1)S(1)}, u32[]{:S(2)}, u32[]{:S(2)}) collective-permute-start(bf16[128,1024]{1,0:T(8,128)(2,1)S(1)} %get-tuple-element.45), channel_id=1, source_target_pairs={{0,192},{64,0},{128,64},{192,128},{1,193},{65,1},{129,65},{193,129... | collective-permute-start | bytes 786440 | tf_op jit(solution)/shard_map/ppermute | solution.py:140
  109.8 2.7 %collective-permute-start.22 = (bf16[128,1024]{1,0:T(8,128)(2,1)S(1)}, bf16[128,1024]{1,0:T(8,128)(2,1)S(1)}, u32[]{:S(2)}, u32[]{:S(2)}) collective-permute-start(bf16[128,1024]{1,0:T(8,128)(2,1)S(1)} %get-tuple-element.44), channel_id=1, source_target_pairs={{0,128},{64,192},{128,0},{192,64},{1,129},{65,193},{129,1},{193,65... | collective-permute-start | bytes 786440 | tf_op jit(solution)/shard_map/ppermute | solution.py:140
  112.5 2.8 %collective-permute-start.21 = (bf16[128,1024]{1,0:T(8,128)(2,1)S(1)}, bf16[128,1024]{1,0:T(8,128)(2,1)S(1)}, u32[]{:S(2)}, u32[]{:S(2)}) collective-permute-start(bf16[128,1024]{1,0:T(8,128)(2,1)S(1)} %get-tuple-element.43), channel_id=1, source_target_pairs={{0,64},{64,128},{128,192},{192,0},{1,65},{65,129},{129,193},{193,1... | collective-permute-start | bytes 786440 | tf_op jit(solution)/shard_map/ppermute | solution.py:140
  115.3 4.0 %shard_map.57 = (f32[128,1024]{1,0:T(8,128)S(1)}, bf16[128,1024]{1,0:T(8,128)(2,1)S(1)}, bf16[128,1024]{1,0:T(8,128)(2,1)S(1)}, bf16[128,1024]{1,0:T(8,128)(2,1)S(1)}) custom-call(s32[8]{0:T(128)S(1)} %get-tuple-element.40.slots, f32[1,2048]{1,0:T(1,128)S(1)} %bitcast.6, bf16[2048,1024]{1,0:T(8,128)(2,1)S(1)} %copy-done.1, bf16[128,640]{1,0:T(8,128)(2,1)S(1)} %copy-done.3, ...), custom_call_target="tpu_custom_call" | custom-call | flops 2147483648 | bytes 8388608 | tf_op jit(solution)/shard_map/pallas_call | solution.py:94
  120.7 2.7 %collective-permute-done.21 = bf16[128,1024]{1,0:T(8,128)(2,1)S(1)} collective-permute-done((bf16[128,1024]{1,0:T(8,128)(2,1)S(1)}, bf16[128,1024]{1,0:T(8,128)(2,1)S(1)}, u32[]{:S(2)}, u32[]{:S(2)}) %collective-permute-start.21) | collective-permute-done | bytes 262176 | tf_op jit(solution)/shard_map/ppermute | solution.py:140
  123.6 8.8 %collective-permute-start.27 = (bf16[128,1024]{1,0:T(8,128)(2,1)S(1)}, bf16[128,1024]{1,0:T(8,128)(2,1)S(1)}, u32[]{:S(2)}, u32[]{:S(2)}) collective-permute-start(bf16[128,1024]{1,0:T(8,128)(2,1)S(1)} %add_convert_fusion), channel_id=1, source_target_pairs={{0,256},{256,0},{1,257},{257,1},{2,258},{258,2},{3,259},{259,3},{4... | collective-permute-start | bytes 786440 | tf_op jit(solution)/shard_map/ppermute | solution.py:153
  132.4 2.5 %collective-permute-start.26 = (bf16[128,1024]{1,0:T(8,128)(2,1)S(1)}, bf16[128,1024]{1,0:T(8,128)(2,1)S(1)}, u32[]{:S(2)}, u32[]{:S(2)}) collective-permute-start(bf16[128,1024]{1,0:T(8,128)(2,1)S(1)} %get-tuple-element.51), channel_id=1, source_target_pairs={{0,192},{64,0},{128,64},{192,128},{1,193},{65,1},{129,65},{193,129... | collective-permute-start | bytes 786440 | tf_op jit(solution)/shard_map/ppermute | solution.py:140
  134.9 2.7 %collective-permute-start.25 = (bf16[128,1024]{1,0:T(8,128)(2,1)S(1)}, bf16[128,1024]{1,0:T(8,128)(2,1)S(1)}, u32[]{:S(2)}, u32[]{:S(2)}) collective-permute-start(bf16[128,1024]{1,0:T(8,128)(2,1)S(1)} %get-tuple-element.50), channel_id=1, source_target_pairs={{0,128},{64,192},{128,0},{192,64},{1,129},{65,193},{129,1},{193,65... | collective-permute-start | bytes 786440 | tf_op jit(solution)/shard_map/ppermute | solution.py:140
  137.6 3.1 %collective-permute-start.24 = (bf16[128,1024]{1,0:T(8,128)(2,1)S(1)}, bf16[128,1024]{1,0:T(8,128)(2,1)S(1)}, u32[]{:S(2)}, u32[]{:S(2)}) collective-permute-start(bf16[128,1024]{1,0:T(8,128)(2,1)S(1)} %get-tuple-element.49), channel_id=1, source_target_pairs={{0,64},{64,128},{128,192},{192,0},{1,65},{65,129},{129,193},{193,1... | collective-permute-start | bytes 786440 | tf_op jit(solution)/shard_map/ppermute | solution.py:140
  140.7 12.9 %collective-permute-done.27 = bf16[128,1024]{1,0:T(8,128)(2,1)S(1)} collective-permute-done((bf16[128,1024]{1,0:T(8,128)(2,1)S(1)}, bf16[128,1024]{1,0:T(8,128)(2,1)S(1)}, u32[]{:S(2)}, u32[]{:S(2)}) %collective-permute-start.27) | collective-permute-done | bytes 262176 | tf_op jit(solution)/shard_map/ppermute | solution.py:153
  (54 shorter events, 19.6 us)
Async XLA Ops:
  6.5 92.2 %all-gather.2.cloned.1.call-start = ((), (), s32[]{:S(2)}) async-start(), calls=%async_computation | async-start | bytes 4718592 | tf_op jit(solution)/shard_map/all_gather | solution.py:112
  9.2 17.0 %collective-permute-start.6 = (bf16[128,768]{1,0:T(8,128)(2,1)}, bf16[128,768]{1,0:T(8,128)(2,1)S(1)}, u32[]{:S(2)}, u32[]{:S(2)}) collective-permute-start(bf16[128,768]{1,0:T(8,128)(2,1)} %get-tuple-element.34.refs_2_), channel_id=1, source_target_pairs={{0,2},{2,4},{4,6},{6,7},{7,5},{5,3},{3,1},{1,0},{8,10},{10,12},{12... | collective-permute-start | bytes 589832 | tf_op jit(solution)/shard_map/ppermute | solution.py:122
  15.6 12.5 %collective-permute-start = (bf16[128,640]{1,0:T(8,128)(2,1)}, bf16[128,640]{1,0:T(8,128)(2,1)S(1)}, u32[]{:S(2)}, u32[]{:S(2)}) collective-permute-start(bf16[128,640]{1,0:T(8,128)(2,1)} %get-tuple-element.29.refs_0_), channel_id=1, source_target_pairs={{0,2},{2,4},{4,6},{6,7},{7,5},{5,3},{3,1},{1,0},{8,10},{10,12},{12... | collective-permute-start | bytes 491528 | tf_op jit(solution)/shard_map/ppermute | solution.py:122
  20.8 10.3 %collective-permute-start.5 = (bf16[128,640]{1,0:T(8,128)(2,1)}, bf16[128,640]{1,0:T(8,128)(2,1)S(1)}, u32[]{:S(2)}, u32[]{:S(2)}) collective-permute-start(bf16[128,640]{1,0:T(8,128)(2,1)} %get-tuple-element.33.refs_1_), channel_id=1, source_target_pairs={{0,2},{2,4},{4,6},{6,7},{7,5},{5,3},{3,1},{1,0},{8,10},{10,12},{12... | collective-permute-start | bytes 491528 | tf_op jit(solution)/shard_map/ppermute | solution.py:122
  26.2 10.6 %collective-permute-start.8 = (bf16[128,768]{1,0:T(8,128)(2,1)S(1)}, bf16[128,768]{1,0:T(8,128)(2,1)S(1)}, u32[]{:S(2)}, u32[]{:S(2)}) collective-permute-start(bf16[128,768]{1,0:T(8,128)(2,1)S(1)} %collective-permute-done.6.refs_5_), channel_id=1, source_target_pairs={{0,2},{2,4},{4,6},{6,7},{7,5},{5,3},{3,1},{1,0},{8,10},{10,12},{12... | collective-permute-start | bytes 589832 | tf_op jit(solution)/shard_map/ppermute | solution.py:122
  28.1 12.2 %collective-permute-start.1 = (bf16[128,640]{1,0:T(8,128)(2,1)S(1)}, bf16[128,640]{1,0:T(8,128)(2,1)S(1)}, u32[]{:S(2)}, u32[]{:S(2)}) collective-permute-start(bf16[128,640]{1,0:T(8,128)(2,1)S(1)} %collective-permute-done.refs_3_), channel_id=1, source_target_pairs={{0,2},{2,4},{4,6},{6,7},{7,5},{5,3},{3,1},{1,0},{8,10},{10,12},{12... | collective-permute-start | bytes 491528 | tf_op jit(solution)/shard_map/ppermute | solution.py:122
  31.1 12.8 %collective-permute-start.7 = (bf16[128,640]{1,0:T(8,128)(2,1)S(1)}, bf16[128,640]{1,0:T(8,128)(2,1)S(1)}, u32[]{:S(2)}, u32[]{:S(2)}) collective-permute-start(bf16[128,640]{1,0:T(8,128)(2,1)S(1)} %collective-permute-done.5.refs_4_), channel_id=1, source_target_pairs={{0,2},{2,4},{4,6},{6,7},{7,5},{5,3},{3,1},{1,0},{8,10},{10,12},{12... | collective-permute-start | bytes 491528 | tf_op jit(solution)/shard_map/ppermute | solution.py:122
  36.8 11.2 %collective-permute-start.10 = (bf16[128,768]{1,0:T(8,128)(2,1)S(1)}, bf16[128,768]{1,0:T(8,128)(2,1)S(1)}, u32[]{:S(2)}, u32[]{:S(2)}) collective-permute-start(bf16[128,768]{1,0:T(8,128)(2,1)S(1)} %collective-permute-done.8.refs_8_), channel_id=1, source_target_pairs={{0,2},{2,4},{4,6},{6,7},{7,5},{5,3},{3,1},{1,0},{8,10},{10,12},{12... | collective-permute-start | bytes 589832 | tf_op jit(solution)/shard_map/ppermute | solution.py:122
  40.3 12.2 %collective-permute-start.2 = (bf16[128,640]{1,0:T(8,128)(2,1)S(1)}, bf16[128,640]{1,0:T(8,128)(2,1)S(1)}, u32[]{:S(2)}, u32[]{:S(2)}) collective-permute-start(bf16[128,640]{1,0:T(8,128)(2,1)S(1)} %collective-permute-done.1.refs_6_), channel_id=1, source_target_pairs={{0,2},{2,4},{4,6},{6,7},{7,5},{5,3},{3,1},{1,0},{8,10},{10,12},{12... | collective-permute-start | bytes 491528 | tf_op jit(solution)/shard_map/ppermute | solution.py:122
  43.8 11.5 %collective-permute-start.9 = (bf16[128,640]{1,0:T(8,128)(2,1)S(1)}, bf16[128,640]{1,0:T(8,128)(2,1)S(1)}, u32[]{:S(2)}, u32[]{:S(2)}) collective-permute-start(bf16[128,640]{1,0:T(8,128)(2,1)S(1)} %collective-permute-done.7.refs_7_), channel_id=1, source_target_pairs={{0,2},{2,4},{4,6},{6,7},{7,5},{5,3},{3,1},{1,0},{8,10},{10,12},{12... | collective-permute-start | bytes 491528 | tf_op jit(solution)/shard_map/ppermute | solution.py:122
  48.1 11.2 %collective-permute-start.12 = (bf16[128,768]{1,0:T(8,128)(2,1)S(1)}, bf16[128,768]{1,0:T(8,128)(2,1)S(1)}, u32[]{:S(2)}, u32[]{:S(2)}) collective-permute-start(bf16[128,768]{1,0:T(8,128)(2,1)S(1)} %collective-permute-done.10.refs_11_), channel_id=1, source_target_pairs={{0,2},{2,4},{4,6},{6,7},{7,5},{5,3},{3,1},{1,0},{8,10},{10,12},{12... | collective-permute-start | bytes 589832 | tf_op jit(solution)/shard_map/ppermute | solution.py:122
  52.5 12.0 %collective-permute-start.3 = (bf16[128,640]{1,0:T(8,128)(2,1)S(1)}, bf16[128,640]{1,0:T(8,128)(2,1)S(1)}, u32[]{:S(2)}, u32[]{:S(2)}) collective-permute-start(bf16[128,640]{1,0:T(8,128)(2,1)S(1)} %collective-permute-done.2.refs_9_), channel_id=1, source_target_pairs={{0,2},{2,4},{4,6},{6,7},{7,5},{5,3},{3,1},{1,0},{8,10},{10,12},{12... | collective-permute-start | bytes 491528 | tf_op jit(solution)/shard_map/ppermute | solution.py:122
  55.3 11.9 %collective-permute-start.11 = (bf16[128,640]{1,0:T(8,128)(2,1)S(1)}, bf16[128,640]{1,0:T(8,128)(2,1)S(1)}, u32[]{:S(2)}, u32[]{:S(2)}) collective-permute-start(bf16[128,640]{1,0:T(8,128)(2,1)S(1)} %collective-permute-done.9.refs_10_), channel_id=1, source_target_pairs={{0,2},{2,4},{4,6},{6,7},{7,5},{5,3},{3,1},{1,0},{8,10},{10,12},{12... | collective-permute-start | bytes 491528 | tf_op jit(solution)/shard_map/ppermute | solution.py:122
  59.3 11.2 %collective-permute-start.14 = (bf16[128,768]{1,0:T(8,128)(2,1)S(1)}, bf16[128,768]{1,0:T(8,128)(2,1)S(1)}, u32[]{:S(2)}, u32[]{:S(2)}) collective-permute-start(bf16[128,768]{1,0:T(8,128)(2,1)S(1)} %collective-permute-done.12.refs_14_), channel_id=1, source_target_pairs={{0,2},{2,4},{4,6},{6,7},{7,5},{5,3},{3,1},{1,0},{8,10},{10,12},{12... | collective-permute-start | bytes 589832 | tf_op jit(solution)/shard_map/ppermute | solution.py:122
  63.5 35.2 %copy-start.2 = (bf16[128,768]{1,0:T(8,128)(2,1)S(1)}, bf16[128,768]{1,0:T(8,128)(2,1)}, u32[]{:S(2)}) copy-start(bf16[128,768]{1,0:T(8,128)(2,1)} %get-tuple-element.34.refs_2_) | copy-start | bytes 589828
  63.6 35.2 %copy-start.3 = (bf16[128,640]{1,0:T(8,128)(2,1)S(1)}, bf16[128,640]{1,0:T(8,128)(2,1)}, u32[]{:S(2)}) copy-start(bf16[128,640]{1,0:T(8,128)(2,1)} %get-tuple-element.29.refs_0_) | copy-start | bytes 491524
  63.6 35.2 %copy-start.4 = (bf16[128,640]{1,0:T(8,128)(2,1)S(1)}, bf16[128,640]{1,0:T(8,128)(2,1)}, u32[]{:S(2)}) copy-start(bf16[128,640]{1,0:T(8,128)(2,1)} %get-tuple-element.33.refs_1_) | copy-start | bytes 491524
  64.6 10.7 %collective-permute-start.4 = (bf16[128,640]{1,0:T(8,128)(2,1)S(1)}, bf16[128,640]{1,0:T(8,128)(2,1)S(1)}, u32[]{:S(2)}, u32[]{:S(2)}) collective-permute-start(bf16[128,640]{1,0:T(8,128)(2,1)S(1)} %collective-permute-done.3.refs_12_), channel_id=1, source_target_pairs={{0,2},{2,4},{4,6},{6,7},{7,5},{5,3},{3,1},{1,0},{8,10},{10,12},{12... | collective-permute-start | bytes 491528 | tf_op jit(solution)/shard_map/ppermute | solution.py:122
  67.2 11.5 %collective-permute-start.13 = (bf16[128,640]{1,0:T(8,128)(2,1)S(1)}, bf16[128,640]{1,0:T(8,128)(2,1)S(1)}, u32[]{:S(2)}, u32[]{:S(2)}) collective-permute-start(bf16[128,640]{1,0:T(8,128)(2,1)S(1)} %collective-permute-done.11.refs_13_), channel_id=1, source_target_pairs={{0,2},{2,4},{4,6},{6,7},{7,5},{5,3},{3,1},{1,0},{8,10},{10,12},{12... | collective-permute-start | bytes 491528 | tf_op jit(solution)/shard_map/ppermute | solution.py:122
  70.5 11.7 %collective-permute-start.17 = (bf16[128,768]{1,0:T(8,128)(2,1)S(1)}, bf16[128,768]{1,0:T(8,128)(2,1)S(1)}, u32[]{:S(2)}, u32[]{:S(2)}) collective-permute-start(bf16[128,768]{1,0:T(8,128)(2,1)S(1)} %collective-permute-done.14.refs_17_), channel_id=1, source_target_pairs={{0,2},{2,4},{4,6},{6,7},{7,5},{5,3},{3,1},{1,0},{8,10},{10,12},{12... | collective-permute-start | bytes 589832 | tf_op jit(solution)/shard_map/ppermute | solution.py:122
  75.2 11.8 %collective-permute-start.15 = (bf16[128,640]{1,0:T(8,128)(2,1)S(1)}, bf16[128,640]{1,0:T(8,128)(2,1)}, u32[]{:S(2)}, u32[]{:S(2)}) collective-permute-start(bf16[128,640]{1,0:T(8,128)(2,1)S(1)} %collective-permute-done.4.refs_15_), channel_id=1, source_target_pairs={{0,2},{2,4},{4,6},{6,7},{7,5},{5,3},{3,1},{1,0},{8,10},{10,12},{12... | collective-permute-start | bytes 491528 | tf_op jit(solution)/shard_map/ppermute | solution.py:122
  78.7 11.6 %collective-permute-start.16 = (bf16[128,640]{1,0:T(8,128)(2,1)S(1)}, bf16[128,640]{1,0:T(8,128)(2,1)}, u32[]{:S(2)}, u32[]{:S(2)}) collective-permute-start(bf16[128,640]{1,0:T(8,128)(2,1)S(1)} %collective-permute-done.13.refs_16_), channel_id=1, source_target_pairs={{0,2},{2,4},{4,6},{6,7},{7,5},{5,3},{3,1},{1,0},{8,10},{10,12},{12... | collective-permute-start | bytes 491528 | tf_op jit(solution)/shard_map/ppermute | solution.py:122
  82.3 16.5 %collective-permute-start.20 = (bf16[128,768]{1,0:T(8,128)(2,1)S(1)}, bf16[128,768]{1,0:T(8,128)(2,1)S(1)}, u32[]{:S(2)}, u32[]{:S(2)}) collective-permute-start(bf16[128,768]{1,0:T(8,128)(2,1)S(1)} %collective-permute-done.17.refs_20_), channel_id=1, source_target_pairs={{0,2},{2,4},{4,6},{6,7},{7,5},{5,3},{3,1},{1,0},{8,10},{10,12},{12... | collective-permute-start | bytes 589832 | tf_op jit(solution)/shard_map/ppermute | solution.py:122
  87.1 9.3 %collective-permute-start.18 = (bf16[128,640]{1,0:T(8,128)(2,1)}, bf16[128,640]{1,0:T(8,128)(2,1)}, u32[]{:S(2)}, u32[]{:S(2)}) collective-permute-start(bf16[128,640]{1,0:T(8,128)(2,1)} %collective-permute-done.15.refs_18_), channel_id=1, source_target_pairs={{0,2},{2,4},{4,6},{6,7},{7,5},{5,3},{3,1},{1,0},{8,10},{10,12},{12... | collective-permute-start | bytes 491528 | tf_op jit(solution)/shard_map/ppermute | solution.py:122
  90.3 8.4 %collective-permute-start.19 = (bf16[128,640]{1,0:T(8,128)(2,1)}, bf16[128,640]{1,0:T(8,128)(2,1)}, u32[]{:S(2)}, u32[]{:S(2)}) collective-permute-start(bf16[128,640]{1,0:T(8,128)(2,1)} %collective-permute-done.16.refs_19_), channel_id=1, source_target_pairs={{0,2},{2,4},{4,6},{6,7},{7,5},{5,3},{3,1},{1,0},{8,10},{10,12},{12... | collective-permute-start | bytes 491528 | tf_op jit(solution)/shard_map/ppermute | solution.py:122
  105.1 14.2 %collective-permute-start.23 = (bf16[128,1024]{1,0:T(8,128)(2,1)S(1)}, bf16[128,1024]{1,0:T(8,128)(2,1)S(1)}, u32[]{:S(2)}, u32[]{:S(2)}) collective-permute-start(bf16[128,1024]{1,0:T(8,128)(2,1)S(1)} %get-tuple-element.45), channel_id=1, source_target_pairs={{0,192},{64,0},{128,64},{192,128},{1,193},{65,1},{129,65},{193,129... | collective-permute-start | bytes 786440 | tf_op jit(solution)/shard_map/ppermute | solution.py:140
  109.8 10.9 %collective-permute-start.22 = (bf16[128,1024]{1,0:T(8,128)(2,1)S(1)}, bf16[128,1024]{1,0:T(8,128)(2,1)S(1)}, u32[]{:S(2)}, u32[]{:S(2)}) collective-permute-start(bf16[128,1024]{1,0:T(8,128)(2,1)S(1)} %get-tuple-element.44), channel_id=1, source_target_pairs={{0,128},{64,192},{128,0},{192,64},{1,129},{65,193},{129,1},{193,65... | collective-permute-start | bytes 786440 | tf_op jit(solution)/shard_map/ppermute | solution.py:140
  112.5 10.9 %collective-permute-start.21 = (bf16[128,1024]{1,0:T(8,128)(2,1)S(1)}, bf16[128,1024]{1,0:T(8,128)(2,1)S(1)}, u32[]{:S(2)}, u32[]{:S(2)}) collective-permute-start(bf16[128,1024]{1,0:T(8,128)(2,1)S(1)} %get-tuple-element.43), channel_id=1, source_target_pairs={{0,64},{64,128},{128,192},{192,0},{1,65},{65,129},{129,193},{193,1... | collective-permute-start | bytes 786440 | tf_op jit(solution)/shard_map/ppermute | solution.py:140
  123.6 30.0 %collective-permute-start.27 = (bf16[128,1024]{1,0:T(8,128)(2,1)S(1)}, bf16[128,1024]{1,0:T(8,128)(2,1)S(1)}, u32[]{:S(2)}, u32[]{:S(2)}) collective-permute-start(bf16[128,1024]{1,0:T(8,128)(2,1)S(1)} %add_convert_fusion), channel_id=1, source_target_pairs={{0,256},{256,0},{1,257},{257,1},{2,258},{258,2},{3,259},{259,3},{4... | collective-permute-start | bytes 786440 | tf_op jit(solution)/shard_map/ppermute | solution.py:153
  132.4 21.2 %collective-permute-start.26 = (bf16[128,1024]{1,0:T(8,128)(2,1)S(1)}, bf16[128,1024]{1,0:T(8,128)(2,1)S(1)}, u32[]{:S(2)}, u32[]{:S(2)}) collective-permute-start(bf16[128,1024]{1,0:T(8,128)(2,1)S(1)} %get-tuple-element.51), channel_id=1, source_target_pairs={{0,192},{64,0},{128,64},{192,128},{1,193},{65,1},{129,65},{193,129... | collective-permute-start | bytes 786440 | tf_op jit(solution)/shard_map/ppermute | solution.py:140
  134.9 18.7 %collective-permute-start.25 = (bf16[128,1024]{1,0:T(8,128)(2,1)S(1)}, bf16[128,1024]{1,0:T(8,128)(2,1)S(1)}, u32[]{:S(2)}, u32[]{:S(2)}) collective-permute-start(bf16[128,1024]{1,0:T(8,128)(2,1)S(1)} %get-tuple-element.50), channel_id=1, source_target_pairs={{0,128},{64,192},{128,0},{192,64},{1,129},{65,193},{129,1},{193,65... | collective-permute-start | bytes 786440 | tf_op jit(solution)/shard_map/ppermute | solution.py:140
  137.6 16.0 %collective-permute-start.24 = (bf16[128,1024]{1,0:T(8,128)(2,1)S(1)}, bf16[128,1024]{1,0:T(8,128)(2,1)S(1)}, u32[]{:S(2)}, u32[]{:S(2)}) collective-permute-start(bf16[128,1024]{1,0:T(8,128)(2,1)S(1)} %get-tuple-element.49), channel_id=1, source_target_pairs={{0,64},{64,128},{128,192},{192,0},{1,65},{65,129},{129,193},{193,1... | collective-permute-start | bytes 786440 | tf_op jit(solution)/shard_map/ppermute | solution.py:140
  (2 other events, 16.5 us)
Sparse Core Ops, SparseCore 0:
  9.5 47.0 all-gather.1

commit v10 on v9

--- a/solution.py
+++ b/solution.py
@@ -63,10 +63,13 @@
     )(elements)
 
 
-def product_kernel(n_turns, parts, slots, factor, columns, *refs):
-    pieces = refs[: n_turns * parts]
-    own, *others, rows = refs[n_turns * parts :]
+def product_kernel(n_rows, n_turns, parts, slots, order, factor, *refs):
+    near, pieces = refs[:n_rows], refs[n_rows : n_rows + n_turns * parts]
+    own, *others, rows, columns = refs[n_rows + n_turns * parts :]
     n_g = own.shape[0]
+    for i, piece in enumerate(near):
+        at = pl.multiple_of(order[i] * n_g, 128)
+        columns[:, pl.ds(at, n_g)] = piece[...]
     for turn in range(n_turns):
         slot = slots[turn]
 
@@ -86,41 +89,58 @@
             out[...] = value.astype(out.dtype)
 
 
-def product(slots, factor, columns, pieces, parts, n_slots):
-    n_pair, width = columns.shape
+def product(slots, order, factor, near, pieces, parts, n_slots):
+    n_pair, n_g = near[0].shape
+    width = n_g * len(near)
     n_turns = len(pieces) // parts
-    n_g = pieces[0].shape[0]
     kinds = [jnp.float32] + [jnp.bfloat16] * (n_slots - 1)
     return pl.pallas_call(
-        functools.partial(product_kernel, n_turns, parts),
+        functools.partial(product_kernel, len(near), n_turns, parts),
         out_shape=[jax.ShapeDtypeStruct((n_g, width), kind) for kind in kinds],
-        in_specs=[pl.BlockSpec(memory_space=pltpu.SMEM)] + [WHOLE] * (2 + len(pieces)),
+        in_specs=[pl.BlockSpec(memory_space=pltpu.SMEM)] * 2
+        + [WHOLE] * (1 + len(near) + len(pieces)),
         out_specs=[WHOLE] * n_slots,
-        scratch_shapes=[pltpu.VMEM((n_slots * n_g, n_pair), jnp.bfloat16)],
+        scratch_shapes=[
+            pltpu.VMEM((n_slots * n_g, n_pair), jnp.bfloat16),
+            pltpu.VMEM((n_pair, width), jnp.bfloat16),
+        ],
         compiler_params=pltpu.CompilerParams(vmem_limit_bytes=40 * 1024 * 1024),
         cost_estimate=pl.CostEstimate(
             flops=2 * n_slots * n_g * n_pair * width,
             bytes_accessed=8 * 1024 * 1024,
             transcendentals=0,
         ),
-    )(slots, factor, columns, *pieces)
+    )(slots, order, factor, *near, *pieces)
 
 
 def body(pair_elements, valence_of, conduction_of, valence_depth, conduction_height):
     n_pair, n_g = pair_elements.shape
     n_x, n_z = lax.axis_size("x"), lax.axis_size("zl")
-    columns = lax.all_gather(pair_elements, ("y", "core"), axis=1, tiled=True)
+    n_row = lax.axis_size("y") * lax.axis_size("core")
+    near = [pair_elements]
+
+    def fetch(count, after):
+        source, _ = lax.optimization_barrier((pair_elements, after))
+        for s in range(len(near), min(len(near) + count, n_row)):
+            near.append(lax.ppermute(source, ("y", "core"), shift(n_row, -s)))
 
     order = circle(n_z)
     step = [(order[i], order[(i + 1) % n_z]) for i in range(n_z)]
     parts = 3
     chunks = turned(pair_elements, parts)
     pieces = list(chunks)
+    fetch(2, chunks[0])
     for turn in range(1, n_z):
+        if turn >= n_z // 2:
+            first = 1 + 2 * (turn - n_z // 2)
+            chunks[0], *near[first : first + 2] = lax.optimization_barrier(
+                (chunks[0], *near[first : first + 2])
+            )
         if turn == n_z - 2:
             chunks[0], factor = lax.optimization_barrier((chunks[0], factor))
         chunks = [lax.ppermute(chunk, "zl", step) for chunk in chunks]
         pieces += chunks
+        fetch(2, chunks[0])
         if turn == n_z // 2 - 2:
             valence_of, conduction_of, _ = lax.optimization_barrier(
                 (valence_of, conduction_of, chunks[0])
@@ -129,6 +149,8 @@
             pair_gap = pair_gap + lookup(conduction_of, conduction_height)
             factor = (-4.0 / pair_gap)[None, :]
 
+    my_row = lax.axis_index("y") * lax.axis_size("core") + lax.axis_index("core")
+    places = lax.rem(my_row + jnp.arange(n_row, dtype=jnp.int32), n_row)
     my_half, my_x = lax.axis_index("zh"), lax.axis_index("x")
     turns = jnp.arange(n_z, dtype=jnp.int32)
     origin = lax.rem(place(lax.axis_index("zl"), n_z) - turns + n_z, n_z)
@@ -143,11 +165,11 @@
         return own
 
     given, *given_sent = product(
-        jnp.where(stays, n_x, slot), factor, columns, pieces, parts, n_x
+        jnp.where(stays, n_x, slot), places, factor, near, pieces, parts, n_x
     )
     last = jnp.where(stays, slot, n_x)
     last, given, *given_sent = lax.optimization_barrier((last, given, *given_sent))
-    kept, *kept_sent = product(last, factor, columns, pieces, parts, n_x)
+    kept, *kept_sent = product(last, places, factor, near, pieces, parts, n_x)
     given = summed_over_x(given, given_sent).astype(jnp.bfloat16)
     given, *kept_sent = lax.optimization_barrier((given, *kept_sent))
     got = lax.ppermute(given, "zh", shift(2, 1)).astype(jnp.float32)

time: 163 us -> 194 us (1.19)
  the two profiles are of different devices: /device:TPU:72 before, /device:TPU:120 now
where the time goes in v10:
time: 194 us; the launch traced here: 192 us
  starting transfers between devices  103 us (53%)
  waiting for transfers between devices  55.3 us (29%)
  local copies, waits for them, and re-layouts  18 us (9%)
  Pallas kernels  13.6 us (7%)
    ppermute x21, starting transfers between devices, body(): chunks = [lax.ppermute(chunk, 'zl', step) for chunk in chunks]  61.7 us
    ppermute x21, waiting for transfers between devices, body(): chunks = [lax.ppermute(chunk, 'zl', step) for chunk in chunks]  32.9 us
    ppermute x6, starting transfers between devices, summed_over_x(): lax.ppermute(one, 'x', shift(n_x, s))  18.1 us
    ppermute x1, waiting for transfers between devices, body(): got = lax.ppermute(given, 'zh', shift(2, 1)).astype(jnp.float32)  17.3 us
    unnamed x69, local copies, waits for them, and re-layouts  17.1 us
    ppermute x7, starting transfers between devices, fetch(): near.append(lax.ppermute(source, ('y', 'core'), shift(n_row, -s)))  14.1 us
    pallas_call x2, Pallas kernels, product(): pl.pallas_call(functools.partial(product_kernel, len(near), n_turns, part...  11.5 us
    ppermute x1, starting transfers between devices, body(): got = lax.ppermute(given, 'zh', shift(2, 1)).astype(jnp.float32)  9.1 us
  transfers between devices with their start and end apart: 35, of which 16 were waited for; matrix products, arithmetic and copies ran while one was open for 1% of the time, Pallas kernels for 3%

profile of v10, /device:TPU:120, one launch (start us, length us, event | category | flops | bytes accessed | tf_op | source)
XLA Modules:
  0.0 192.0 jit_solution(7658039225067850937)
XLA Ops:
  5.9 4.9 %collective-permute-start.14 = (bf16[128,768]{1,0:T(8,128)(2,1)}, bf16[128,768]{1,0:T(8,128)(2,1)S(1)}, u32[]{:S(2)}, u32[]{:S(2)}) collective-permute-start(bf16[128,768]{1,0:T(8,128)(2,1)} %get-tuple-element.64.refs_10_), channel_id=1, source_target_pairs={{0,2},{2,4},{4,6},{6,7},{7,5},{5,3},{3,1},{1,0},{8,10},{10,12},{12... | collective-permute-start | bytes 589832 | tf_op jit(solution)/shard_map/ppermute | solution.py:141
  10.8 2.8 %collective-permute-done.refs_11_ = bf16[128,640]{1,0:T(8,128)(2,1)S(1)} collective-permute-done((bf16[128,640]{1,0:T(8,128)(2,1)}, bf16[128,640]{1,0:T(8,128)(2,1)S(1)}, u32[]{:S(2)}, u32[]{:S(2)}) %collective-permute-start) | collective-permute-done | bytes 163872 | tf_op jit(solution)/shard_map/ppermute | solution.py:141
  13.7 3.6 %collective-permute-start.1 = (bf16[128,640]{1,0:T(8,128)(2,1)S(1)}, bf16[128,640]{1,0:T(8,128)(2,1)S(1)}, u32[]{:S(2)}, u32[]{:S(2)}) collective-permute-start(bf16[128,640]{1,0:T(8,128)(2,1)S(1)} %collective-permute-done.refs_11_), channel_id=1, source_target_pairs={{0,2},{2,4},{4,6},{6,7},{7,5},{5,3},{3,1},{1,0},{8,10},{10,12},{12... | collective-permute-start | bytes 491528 | tf_op jit(solution)/shard_map/ppermute | solution.py:141
  17.3 5.2 %collective-permute-start.15 = (bf16[128,640]{1,0:T(8,128)(2,1)S(1)}, bf16[128,640]{1,0:T(8,128)(2,1)}, u32[]{:S(2)}, u32[]{:S(2)}) collective-permute-start(bf16[128,640]{1,0:T(8,128)(2,1)S(1)} %collective-permute-done.13.refs_12_), channel_id=1, source_target_pairs={{0,2},{2,4},{4,6},{6,7},{7,5},{5,3},{3,1},{1,0},{8,10},{10,12},{12... | collective-permute-start | bytes 491528 | tf_op jit(solution)/shard_map/ppermute | solution.py:141
  23.1 2.6 %collective-permute-start.4 = (bf16[2048,128]{1,0:T(8,128)(2,1)S(1)}, bf16[2048,128]{1,0:T(8,128)(2,1)S(1)}, u32[]{:S(2)}, u32[]{:S(2)}) collective-permute-start(bf16[2048,128]{1,0:T(8,128)(2,1)S(1)} %copy-done), channel_id=1, source_target_pairs={{0,48},{8,56},{16,0},{24,8},{32,16},{40,24},{48,32},{56,40},{1,49}... | collective-permute-start | bytes 1572872 | tf_op jit(solution)/shard_map/ppermute | solution.py:125
  26.6 3.8 %collective-permute-start.16 = (bf16[128,768]{1,0:T(8,128)(2,1)S(1)}, bf16[128,768]{1,0:T(8,128)(2,1)S(1)}, u32[]{:S(2)}, u32[]{:S(2)}) collective-permute-start(bf16[128,768]{1,0:T(8,128)(2,1)S(1)} %collective-permute-done.14.refs_13_), channel_id=1, source_target_pairs={{0,2},{2,4},{4,6},{6,7},{7,5},{5,3},{3,1},{1,0},{8,10},{10,12},{12... | collective-permute-start | bytes 589832 | tf_op jit(solution)/shard_map/ppermute | solution.py:141
  33.1 4.0 %collective-permute-start.17 = (bf16[128,640]{1,0:T(8,128)(2,1)}, bf16[128,640]{1,0:T(8,128)(2,1)S(1)}, u32[]{:S(2)}, u32[]{:S(2)}) collective-permute-start(bf16[128,640]{1,0:T(8,128)(2,1)} %collective-permute-done.15.refs_15_), channel_id=1, source_target_pairs={{0,2},{2,4},{4,6},{6,7},{7,5},{5,3},{3,1},{1,0},{8,10},{10,12},{12... | collective-permute-start | bytes 491528 | tf_op jit(solution)/shard_map/ppermute | solution.py:141
  41.8 3.6 %collective-permute-start.7 = (bf16[2048,128]{1,0:T(8,128)(2,1)S(1)}, bf16[2048,128]{1,0:T(8,128)(2,1)S(1)}, u32[]{:S(2)}, u32[]{:S(2)}) collective-permute-start(bf16[2048,128]{1,0:T(8,128)(2,1)S(1)} %copy-done), channel_id=1, source_target_pairs={{0,32},{8,40},{16,48},{24,56},{32,0},{40,8},{48,16},{56,24},{1,33}... | collective-permute-start | bytes 1572872 | tf_op jit(solution)/shard_map/ppermute | solution.py:125
  45.4 2.6 %collective-permute-start.18 = (bf16[128,768]{1,0:T(8,128)(2,1)S(1)}, bf16[128,768]{1,0:T(8,128)(2,1)S(1)}, u32[]{:S(2)}, u32[]{:S(2)}) collective-permute-start(bf16[128,768]{1,0:T(8,128)(2,1)S(1)} %collective-permute-done.16.refs_16_), channel_id=1, source_target_pairs={{0,2},{2,4},{4,6},{6,7},{7,5},{5,3},{3,1},{1,0},{8,10},{10,12},{12... | collective-permute-start | bytes 589832 | tf_op jit(solution)/shard_map/ppermute | solution.py:141
  51.6 3.1 %collective-permute-start.5 = (bf16[128,640]{1,0:T(8,128)(2,1)S(1)}, bf16[128,640]{1,0:T(8,128)(2,1)S(1)}, u32[]{:S(2)}, u32[]{:S(2)}) collective-permute-start(bf16[128,640]{1,0:T(8,128)(2,1)S(1)} %collective-permute-done.2.refs_17_), channel_id=1, source_target_pairs={{0,2},{2,4},{4,6},{6,7},{7,5},{5,3},{3,1},{1,0},{8,10},{10,12},{12... | collective-permute-start | bytes 491528 | tf_op jit(solution)/shard_map/ppermute | solution.py:141
  57.1 3.6 %collective-permute-start.20 = (bf16[128,768]{1,0:T(8,128)(2,1)S(1)}, bf16[128,768]{1,0:T(8,128)(2,1)S(1)}, u32[]{:S(2)}, u32[]{:S(2)}) collective-permute-start(bf16[128,768]{1,0:T(8,128)(2,1)S(1)} %collective-permute-done.18.refs_19_), channel_id=1, source_target_pairs={{0,2},{2,4},{4,6},{6,7},{7,5},{5,3},{3,1},{1,0},{8,10},{10,12},{12... | collective-permute-start | bytes 589832 | tf_op jit(solution)/shard_map/ppermute | solution.py:141
  64.2 3.4 %collective-permute-start.10 = (bf16[2048,128]{1,0:T(8,128)(2,1)S(1)}, bf16[2048,128]{1,0:T(8,128)(2,1)S(1)}, u32[]{:S(2)}, u32[]{:S(2)}) collective-permute-start(bf16[2048,128]{1,0:T(8,128)(2,1)S(1)} %copy-done), channel_id=1, source_target_pairs={{0,16},{8,24},{16,32},{24,40},{32,48},{40,56},{48,0},{56,8},{1,17}... | collective-permute-start | bytes 1572872 | tf_op jit(solution)/shard_map/ppermute | solution.py:125
  69.6 3.8 %collective-permute-start.22 = (bf16[128,768]{1,0:T(8,128)(2,1)S(1)}, bf16[128,768]{1,0:T(8,128)(2,1)}, u32[]{:S(2)}, u32[]{:S(2)}) collective-permute-start(bf16[128,768]{1,0:T(8,128)(2,1)S(1)} %collective-permute-done.20.refs_22_), channel_id=1, source_target_pairs={{0,2},{2,4},{4,6},{6,7},{7,5},{5,3},{3,1},{1,0},{8,10},{10,12},{12... | collective-permute-start | bytes 589832 | tf_op jit(solution)/shard_map/ppermute | solution.py:141
  74.7 3.0 %collective-permute-done.21.refs_24_ = bf16[128,640]{1,0:T(8,128)(2,1)} collective-permute-done((bf16[128,640]{1,0:T(8,128)(2,1)S(1)}, bf16[128,640]{1,0:T(8,128)(2,1)}, u32[]{:S(2)}, u32[]{:S(2)}) %collective-permute-start.21) | collective-permute-done | bytes 163872 | tf_op jit(solution)/shard_map/ppermute | solution.py:141
  79.6 2.3 %collective-permute-done.22.refs_25_ = bf16[128,768]{1,0:T(8,128)(2,1)} collective-permute-done((bf16[128,768]{1,0:T(8,128)(2,1)S(1)}, bf16[128,768]{1,0:T(8,128)(2,1)}, u32[]{:S(2)}, u32[]{:S(2)}) %collective-permute-start.22) | collective-permute-done | bytes 196640 | tf_op jit(solution)/shard_map/ppermute | solution.py:141
  83.9 3.8 %collective-permute-done.8.refs_23_ = bf16[128,640]{1,0:T(8,128)(2,1)} collective-permute-done((bf16[128,640]{1,0:T(8,128)(2,1)S(1)}, bf16[128,640]{1,0:T(8,128)(2,1)}, u32[]{:S(2)}, u32[]{:S(2)}) %collective-permute-start.8) | collective-permute-done | bytes 163872 | tf_op jit(solution)/shard_map/ppermute | solution.py:141
  90.4 3.2 %collective-permute-start.11 = (bf16[128,640]{1,0:T(8,128)(2,1)}, bf16[128,640]{1,0:T(8,128)(2,1)}, u32[]{:S(2)}, u32[]{:S(2)}) collective-permute-start(bf16[128,640]{1,0:T(8,128)(2,1)} %collective-permute-done.8.refs_23_), channel_id=1, source_target_pairs={{0,2},{2,4},{4,6},{6,7},{7,5},{5,3},{3,1},{1,0},{8,10},{10,12},{12... | collective-permute-start | bytes 491528 | tf_op jit(solution)/shard_map/ppermute | solution.py:141
  93.6 5.4 %collective-permute-done.23.refs_27_ = bf16[128,640]{1,0:T(8,128)(2,1)} collective-permute-done((bf16[128,640]{1,0:T(8,128)(2,1)}, bf16[128,640]{1,0:T(8,128)(2,1)}, u32[]{:S(2)}, u32[]{:S(2)}) %collective-permute-start.23) | collective-permute-done | bytes 163872 | tf_op jit(solution)/shard_map/ppermute | solution.py:141
  104.4 4.5 %collective-permute-start.27 = (bf16[128,768]{1,0:T(8,128)(2,1)}, bf16[128,768]{1,0:T(8,128)(2,1)}, u32[]{:S(2)}, u32[]{:S(2)}) collective-permute-start(bf16[128,768]{1,0:T(8,128)(2,1)} %collective-permute-done.24.refs_28_), channel_id=1, source_target_pairs={{0,2},{2,4},{4,6},{6,7},{7,5},{5,3},{3,1},{1,0},{8,10},{10,12},{12... | collective-permute-start | bytes 589832 | tf_op jit(solution)/shard_map/ppermute | solution.py:141
  109.7 4.1 %collective-permute-done.25.refs_29_ = bf16[128,640]{1,0:T(8,128)(2,1)} collective-permute-done((bf16[128,640]{1,0:T(8,128)(2,1)}, bf16[128,640]{1,0:T(8,128)(2,1)}, u32[]{:S(2)}, u32[]{:S(2)}) %collective-permute-start.25) | collective-permute-done | bytes 163872 | tf_op jit(solution)/shard_map/ppermute | solution.py:141
  113.9 3.5 %collective-permute-done.27.refs_31_ = bf16[128,768]{1,0:T(8,128)(2,1)} collective-permute-done((bf16[128,768]{1,0:T(8,128)(2,1)}, bf16[128,768]{1,0:T(8,128)(2,1)}, u32[]{:S(2)}, u32[]{:S(2)}) %collective-permute-start.27) | collective-permute-done | bytes 196640 | tf_op jit(solution)/shard_map/ppermute | solution.py:141
  129.5 5.8 %shard_map.56 = (f32[128,1024]{1,0:T(8,128)S(1)}, bf16[128,1024]{1,0:T(8,128)(2,1)S(1)}, bf16[128,1024]{1,0:T(8,128)(2,1)S(1)}, bf16[128,1024]{1,0:T(8,128)(2,1)S(1)}) custom-call(s32[8]{0:T(128)S(1)} %get-tuple-element.93.slots, s32[8]{0:T(128)S(1)} %compare_select_fusion.order, f32[1,2048]{1,0:T(1,128)S(1)} %bitcast.5, bf16[2048,128]{1,0:T(8,128)(2,1)S(1)} %copy-done, ...), custom_call_target="tpu_custom_call" | custom-call | flops 2147483648 | bytes 8388608 | tf_op jit(solution)/shard_map/pallas_call | solution.py:97
  135.3 4.7 %collective-permute-start.30 = (bf16[128,1024]{1,0:T(8,128)(2,1)S(1)}, bf16[128,1024]{1,0:T(8,128)(2,1)S(1)}, u32[]{:S(2)}, u32[]{:S(2)}) collective-permute-start(bf16[128,1024]{1,0:T(8,128)(2,1)S(1)} %get-tuple-element.75), channel_id=1, source_target_pairs={{0,192},{64,0},{128,64},{192,128},{1,193},{65,1},{129,65},{193,129... | collective-permute-start | bytes 786440 | tf_op jit(solution)/shard_map/ppermute | solution.py:162
  140.0 2.7 %collective-permute-start.29 = (bf16[128,1024]{1,0:T(8,128)(2,1)S(1)}, bf16[128,1024]{1,0:T(8,128)(2,1)S(1)}, u32[]{:S(2)}, u32[]{:S(2)}) collective-permute-start(bf16[128,1024]{1,0:T(8,128)(2,1)S(1)} %get-tuple-element.74), channel_id=1, source_target_pairs={{0,128},{64,192},{128,0},{192,64},{1,129},{65,193},{129,1},{193,65... | collective-permute-start | bytes 786440 | tf_op jit(solution)/shard_map/ppermute | solution.py:162
  142.7 2.8 %collective-permute-start.28 = (bf16[128,1024]{1,0:T(8,128)(2,1)S(1)}, bf16[128,1024]{1,0:T(8,128)(2,1)S(1)}, u32[]{:S(2)}, u32[]{:S(2)}) collective-permute-start(bf16[128,1024]{1,0:T(8,128)(2,1)S(1)} %get-tuple-element.73), channel_id=1, source_target_pairs={{0,64},{64,128},{128,192},{192,0},{1,65},{65,129},{129,193},{193,1... | collective-permute-start | bytes 786440 | tf_op jit(solution)/shard_map/ppermute | solution.py:162
  145.5 5.7 %shard_map.57 = (f32[128,1024]{1,0:T(8,128)S(1)}, bf16[128,1024]{1,0:T(8,128)(2,1)S(1)}, bf16[128,1024]{1,0:T(8,128)(2,1)S(1)}, bf16[128,1024]{1,0:T(8,128)(2,1)S(1)}) custom-call(s32[8]{0:T(128)S(1)} %get-tuple-element.70.slots, s32[8]{0:T(128)S(1)} %compare_select_fusion.order, f32[1,2048]{1,0:T(1,128)S(1)} %bitcast.6, bf16[2048,128]{1,0:T(8,128)(2,1)S(1)} %copy-done, ...), custom_call_target="tpu_custom_call" | custom-call | flops 2147483648 | bytes 8388608 | tf_op jit(solution)/shard_map/pallas_call | solution.py:97
  152.6 3.7 %collective-permute-done.28 = bf16[128,1024]{1,0:T(8,128)(2,1)S(1)} collective-permute-done((bf16[128,1024]{1,0:T(8,128)(2,1)S(1)}, bf16[128,1024]{1,0:T(8,128)(2,1)S(1)}, u32[]{:S(2)}, u32[]{:S(2)}) %collective-permute-start.28) | collective-permute-done | bytes 262176 | tf_op jit(solution)/shard_map/ppermute | solution.py:162
  156.5 9.1 %collective-permute-start.34 = (bf16[128,1024]{1,0:T(8,128)(2,1)S(1)}, bf16[128,1024]{1,0:T(8,128)(2,1)S(1)}, u32[]{:S(2)}, u32[]{:S(2)}) collective-permute-start(bf16[128,1024]{1,0:T(8,128)(2,1)S(1)} %add_convert_fusion), channel_id=1, source_target_pairs={{0,256},{256,0},{1,257},{257,1},{2,258},{258,2},{3,259},{259,3},{4... | collective-permute-start | bytes 786440 | tf_op jit(solution)/shard_map/ppermute | solution.py:175
  165.6 2.5 %collective-permute-start.33 = (bf16[128,1024]{1,0:T(8,128)(2,1)S(1)}, bf16[128,1024]{1,0:T(8,128)(2,1)S(1)}, u32[]{:S(2)}, u32[]{:S(2)}) collective-permute-start(bf16[128,1024]{1,0:T(8,128)(2,1)S(1)} %get-tuple-element.81), channel_id=1, source_target_pairs={{0,192},{64,0},{128,64},{192,128},{1,193},{65,1},{129,65},{193,129... | collective-permute-start | bytes 786440 | tf_op jit(solution)/shard_map/ppermute | solution.py:162
  168.1 2.7 %collective-permute-start.32 = (bf16[128,1024]{1,0:T(8,128)(2,1)S(1)}, bf16[128,1024]{1,0:T(8,128)(2,1)S(1)}, u32[]{:S(2)}, u32[]{:S(2)}) collective-permute-start(bf16[128,1024]{1,0:T(8,128)(2,1)S(1)} %get-tuple-element.80), channel_id=1, source_target_pairs={{0,128},{64,192},{128,0},{192,64},{1,129},{65,193},{129,1},{193,65... | collective-permute-start | bytes 786440 | tf_op jit(solution)/shard_map/ppermute | solution.py:162
  170.8 2.8 %collective-permute-start.31 = (bf16[128,1024]{1,0:T(8,128)(2,1)S(1)}, bf16[128,1024]{1,0:T(8,128)(2,1)S(1)}, u32[]{:S(2)}, u32[]{:S(2)}) collective-permute-start(bf16[128,1024]{1,0:T(8,128)(2,1)S(1)} %get-tuple-element.79), channel_id=1, source_target_pairs={{0,64},{64,128},{128,192},{192,0},{1,65},{65,129},{129,193},{193,1... | collective-permute-start | bytes 786440 | tf_op jit(solution)/shard_map/ppermute | solution.py:162
  173.6 17.3 %collective-permute-done.34 = bf16[128,1024]{1,0:T(8,128)(2,1)S(1)} collective-permute-done((bf16[128,1024]{1,0:T(8,128)(2,1)S(1)}, bf16[128,1024]{1,0:T(8,128)(2,1)S(1)}, u32[]{:S(2)}, u32[]{:S(2)}) %collective-permute-start.34) | collective-permute-done | bytes 262176 | tf_op jit(solution)/shard_map/ppermute | solution.py:175
  (124 shorter events, 54.6 us)
Async XLA Ops:
  2.1 11.6 %collective-permute-start = (bf16[128,640]{1,0:T(8,128)(2,1)}, bf16[128,640]{1,0:T(8,128)(2,1)S(1)}, u32[]{:S(2)}, u32[]{:S(2)}) collective-permute-start(bf16[128,640]{1,0:T(8,128)(2,1)} %get-tuple-element.44.refs_8_), channel_id=1, source_target_pairs={{0,2},{2,4},{4,6},{6,7},{7,5},{5,3},{3,1},{1,0},{8,10},{10,12},{12... | collective-permute-start | bytes 491528 | tf_op jit(solution)/shard_map/ppermute | solution.py:141
  4.0 13.3 %collective-permute-start.13 = (bf16[128,640]{1,0:T(8,128)(2,1)}, bf16[128,640]{1,0:T(8,128)(2,1)S(1)}, u32[]{:S(2)}, u32[]{:S(2)}) collective-permute-start(bf16[128,640]{1,0:T(8,128)(2,1)} %get-tuple-element.63.refs_9_), channel_id=1, source_target_pairs={{0,2},{2,4},{4,6},{6,7},{7,5},{5,3},{3,1},{1,0},{8,10},{10,12},{12... | collective-permute-start | bytes 491528 | tf_op jit(solution)/shard_map/ppermute | solution.py:141
  5.9 20.7 %collective-permute-start.14 = (bf16[128,768]{1,0:T(8,128)(2,1)}, bf16[128,768]{1,0:T(8,128)(2,1)S(1)}, u32[]{:S(2)}, u32[]{:S(2)}) collective-permute-start(bf16[128,768]{1,0:T(8,128)(2,1)} %get-tuple-element.64.refs_10_), channel_id=1, source_target_pairs={{0,2},{2,4},{4,6},{6,7},{7,5},{5,3},{3,1},{1,0},{8,10},{10,12},{12... | collective-permute-start | bytes 589832 | tf_op jit(solution)/shard_map/ppermute | solution.py:141
  13.7 16.8 %collective-permute-start.1 = (bf16[128,640]{1,0:T(8,128)(2,1)S(1)}, bf16[128,640]{1,0:T(8,128)(2,1)S(1)}, u32[]{:S(2)}, u32[]{:S(2)}) collective-permute-start(bf16[128,640]{1,0:T(8,128)(2,1)S(1)} %collective-permute-done.refs_11_), channel_id=1, source_target_pairs={{0,2},{2,4},{4,6},{6,7},{7,5},{5,3},{3,1},{1,0},{8,10},{10,12},{12... | collective-permute-start | bytes 491528 | tf_op jit(solution)/shard_map/ppermute | solution.py:141
  17.3 15.8 %collective-permute-start.15 = (bf16[128,640]{1,0:T(8,128)(2,1)S(1)}, bf16[128,640]{1,0:T(8,128)(2,1)}, u32[]{:S(2)}, u32[]{:S(2)}) collective-permute-start(bf16[128,640]{1,0:T(8,128)(2,1)S(1)} %collective-permute-done.13.refs_12_), channel_id=1, source_target_pairs={{0,2},{2,4},{4,6},{6,7},{7,5},{5,3},{3,1},{1,0},{8,10},{10,12},{12... | collective-permute-start | bytes 491528 | tf_op jit(solution)/shard_map/ppermute | solution.py:141
  23.1 25.6 %collective-permute-start.3 = (bf16[2048,128]{1,0:T(8,128)(2,1)S(1)}, bf16[2048,128]{1,0:T(8,128)(2,1)S(1)}, u32[]{:S(2)}, u32[]{:S(2)}) collective-permute-start(bf16[2048,128]{1,0:T(8,128)(2,1)S(1)} %copy-done), channel_id=1, source_target_pairs={{0,56},{8,0},{16,8},{24,16},{32,24},{40,32},{48,40},{56,48},{1,57}... | collective-permute-start | bytes 1572872 | tf_op jit(solution)/shard_map/ppermute | solution.py:125
  23.1 28.5 %collective-permute-start.4 = (bf16[2048,128]{1,0:T(8,128)(2,1)S(1)}, bf16[2048,128]{1,0:T(8,128)(2,1)S(1)}, u32[]{:S(2)}, u32[]{:S(2)}) collective-permute-start(bf16[2048,128]{1,0:T(8,128)(2,1)S(1)} %copy-done), channel_id=1, source_target_pairs={{0,48},{8,56},{16,0},{24,8},{32,16},{40,24},{48,32},{56,40},{1,49}... | collective-permute-start | bytes 1572872 | tf_op jit(solution)/shard_map/ppermute | solution.py:125
  26.6 11.6 %collective-permute-start.16 = (bf16[128,768]{1,0:T(8,128)(2,1)S(1)}, bf16[128,768]{1,0:T(8,128)(2,1)S(1)}, u32[]{:S(2)}, u32[]{:S(2)}) collective-permute-start(bf16[128,768]{1,0:T(8,128)(2,1)S(1)} %collective-permute-done.14.refs_13_), channel_id=1, source_target_pairs={{0,2},{2,4},{4,6},{6,7},{7,5},{5,3},{3,1},{1,0},{8,10},{10,12},{12... | collective-permute-start | bytes 589832 | tf_op jit(solution)/shard_map/ppermute | solution.py:141
  30.5 11.3 %collective-permute-start.2 = (bf16[128,640]{1,0:T(8,128)(2,1)S(1)}, bf16[128,640]{1,0:T(8,128)(2,1)S(1)}, u32[]{:S(2)}, u32[]{:S(2)}) collective-permute-start(bf16[128,640]{1,0:T(8,128)(2,1)S(1)} %collective-permute-done.1.refs_14_), channel_id=1, source_target_pairs={{0,2},{2,4},{4,6},{6,7},{7,5},{5,3},{3,1},{1,0},{8,10},{10,12},{12... | collective-permute-start | bytes 491528 | tf_op jit(solution)/shard_map/ppermute | solution.py:141
  33.1 12.3 %collective-permute-start.17 = (bf16[128,640]{1,0:T(8,128)(2,1)}, bf16[128,640]{1,0:T(8,128)(2,1)S(1)}, u32[]{:S(2)}, u32[]{:S(2)}) collective-permute-start(bf16[128,640]{1,0:T(8,128)(2,1)} %collective-permute-done.15.refs_15_), channel_id=1, source_target_pairs={{0,2},{2,4},{4,6},{6,7},{7,5},{5,3},{3,1},{1,0},{8,10},{10,12},{12... | collective-permute-start | bytes 491528 | tf_op jit(solution)/shard_map/ppermute | solution.py:141
  38.2 29.3 %collective-permute-start.6 = (bf16[2048,128]{1,0:T(8,128)(2,1)S(1)}, bf16[2048,128]{1,0:T(8,128)(2,1)S(1)}, u32[]{:S(2)}, u32[]{:S(2)}) collective-permute-start(bf16[2048,128]{1,0:T(8,128)(2,1)S(1)} %copy-done), channel_id=1, source_target_pairs={{0,40},{8,48},{16,56},{24,0},{32,8},{40,16},{48,24},{56,32},{1,41}... | collective-permute-start | bytes 1572872 | tf_op jit(solution)/shard_map/ppermute | solution.py:125
  41.8 32.2 %collective-permute-start.7 = (bf16[2048,128]{1,0:T(8,128)(2,1)S(1)}, bf16[2048,128]{1,0:T(8,128)(2,1)S(1)}, u32[]{:S(2)}, u32[]{:S(2)}) collective-permute-start(bf16[2048,128]{1,0:T(8,128)(2,1)S(1)} %copy-done), channel_id=1, source_target_pairs={{0,32},{8,40},{16,48},{24,56},{32,0},{40,8},{48,16},{56,24},{1,33}... | collective-permute-start | bytes 1572872 | tf_op jit(solution)/shard_map/ppermute | solution.py:125
  45.4 11.7 %collective-permute-start.18 = (bf16[128,768]{1,0:T(8,128)(2,1)S(1)}, bf16[128,768]{1,0:T(8,128)(2,1)S(1)}, u32[]{:S(2)}, u32[]{:S(2)}) collective-permute-start(bf16[128,768]{1,0:T(8,128)(2,1)S(1)} %collective-permute-done.16.refs_16_), channel_id=1, source_target_pairs={{0,2},{2,4},{4,6},{6,7},{7,5},{5,3},{3,1},{1,0},{8,10},{10,12},{12... | collective-permute-start | bytes 589832 | tf_op jit(solution)/shard_map/ppermute | solution.py:141
  48.7 12.1 %collective-permute-start.19 = (bf16[128,640]{1,0:T(8,128)(2,1)S(1)}, bf16[128,640]{1,0:T(8,128)(2,1)S(1)}, u32[]{:S(2)}, u32[]{:S(2)}) collective-permute-start(bf16[128,640]{1,0:T(8,128)(2,1)S(1)} %collective-permute-done.17.refs_18_), channel_id=1, source_target_pairs={{0,2},{2,4},{4,6},{6,7},{7,5},{5,3},{3,1},{1,0},{8,10},{10,12},{12... | collective-permute-start | bytes 491528 | tf_op jit(solution)/shard_map/ppermute | solution.py:141
  51.6 12.5 %collective-permute-start.5 = (bf16[128,640]{1,0:T(8,128)(2,1)S(1)}, bf16[128,640]{1,0:T(8,128)(2,1)S(1)}, u32[]{:S(2)}, u32[]{:S(2)}) collective-permute-start(bf16[128,640]{1,0:T(8,128)(2,1)S(1)} %collective-permute-done.2.refs_17_), channel_id=1, source_target_pairs={{0,2},{2,4},{4,6},{6,7},{7,5},{5,3},{3,1},{1,0},{8,10},{10,12},{12... | collective-permute-start | bytes 491528 | tf_op jit(solution)/shard_map/ppermute | solution.py:141
  57.1 12.4 %collective-permute-start.20 = (bf16[128,768]{1,0:T(8,128)(2,1)S(1)}, bf16[128,768]{1,0:T(8,128)(2,1)S(1)}, u32[]{:S(2)}, u32[]{:S(2)}) collective-permute-start(bf16[128,768]{1,0:T(8,128)(2,1)S(1)} %collective-permute-done.18.refs_19_), channel_id=1, source_target_pairs={{0,2},{2,4},{4,6},{6,7},{7,5},{5,3},{3,1},{1,0},{8,10},{10,12},{12... | collective-permute-start | bytes 589832 | tf_op jit(solution)/shard_map/ppermute | solution.py:141
  60.8 28.8 %collective-permute-start.9 = (bf16[2048,128]{1,0:T(8,128)(2,1)S(1)}, bf16[2048,128]{1,0:T(8,128)(2,1)S(1)}, u32[]{:S(2)}, u32[]{:S(2)}) collective-permute-start(bf16[2048,128]{1,0:T(8,128)(2,1)S(1)} %copy-done), channel_id=1, source_target_pairs={{0,24},{8,32},{16,40},{24,48},{32,56},{40,0},{48,8},{56,16},{1,25}... | collective-permute-start | bytes 1572872 | tf_op jit(solution)/shard_map/ppermute | solution.py:125
  64.2 25.5 %collective-permute-start.10 = (bf16[2048,128]{1,0:T(8,128)(2,1)S(1)}, bf16[2048,128]{1,0:T(8,128)(2,1)S(1)}, u32[]{:S(2)}, u32[]{:S(2)}) collective-permute-start(bf16[2048,128]{1,0:T(8,128)(2,1)S(1)} %copy-done), channel_id=1, source_target_pairs={{0,16},{8,24},{16,32},{24,40},{32,48},{40,56},{48,0},{56,8},{1,17}... | collective-permute-start | bytes 1572872 | tf_op jit(solution)/shard_map/ppermute | solution.py:125
  69.6 12.4 %collective-permute-start.22 = (bf16[128,768]{1,0:T(8,128)(2,1)S(1)}, bf16[128,768]{1,0:T(8,128)(2,1)}, u32[]{:S(2)}, u32[]{:S(2)}) collective-permute-start(bf16[128,768]{1,0:T(8,128)(2,1)S(1)} %collective-permute-done.20.refs_22_), channel_id=1, source_target_pairs={{0,2},{2,4},{4,6},{6,7},{7,5},{5,3},{3,1},{1,0},{8,10},{10,12},{12... | collective-permute-start | bytes 589832 | tf_op jit(solution)/shard_map/ppermute | solution.py:141
  73.9 28.6 %collective-permute-start.12 = (bf16[2048,128]{1,0:T(8,128)(2,1)S(1)}, bf16[2048,128]{1,0:T(8,128)(2,1)}, u32[]{:S(2)}, u32[]{:S(2)}) collective-permute-start(bf16[2048,128]{1,0:T(8,128)(2,1)S(1)} %copy-done), channel_id=1, source_target_pairs={{0,8},{8,16},{16,24},{24,32},{32,40},{40,48},{48,56},{56,0},{1,9},... | collective-permute-start | bytes 1572872 | tf_op jit(solution)/shard_map/ppermute | solution.py:125
  81.9 22.5 %collective-permute-start.24 = (bf16[128,768]{1,0:T(8,128)(2,1)}, bf16[128,768]{1,0:T(8,128)(2,1)}, u32[]{:S(2)}, u32[]{:S(2)}) collective-permute-start(bf16[128,768]{1,0:T(8,128)(2,1)} %collective-permute-done.22.refs_25_), channel_id=1, source_target_pairs={{0,2},{2,4},{4,6},{6,7},{7,5},{5,3},{3,1},{1,0},{8,10},{10,12},{12... | collective-permute-start | bytes 589832 | tf_op jit(solution)/shard_map/ppermute | solution.py:141
  87.7 11.3 %collective-permute-start.23 = (bf16[128,640]{1,0:T(8,128)(2,1)}, bf16[128,640]{1,0:T(8,128)(2,1)}, u32[]{:S(2)}, u32[]{:S(2)}) collective-permute-start(bf16[128,640]{1,0:T(8,128)(2,1)} %collective-permute-done.21.refs_24_), channel_id=1, source_target_pairs={{0,2},{2,4},{4,6},{6,7},{7,5},{5,3},{3,1},{1,0},{8,10},{10,12},{12... | collective-permute-start | bytes 491528 | tf_op jit(solution)/shard_map/ppermute | solution.py:141
  90.4 12.1 %collective-permute-start.11 = (bf16[128,640]{1,0:T(8,128)(2,1)}, bf16[128,640]{1,0:T(8,128)(2,1)}, u32[]{:S(2)}, u32[]{:S(2)}) collective-permute-start(bf16[128,640]{1,0:T(8,128)(2,1)} %collective-permute-done.8.refs_23_), channel_id=1, source_target_pairs={{0,2},{2,4},{4,6},{6,7},{7,5},{5,3},{3,1},{1,0},{8,10},{10,12},{12... | collective-permute-start | bytes 491528 | tf_op jit(solution)/shard_map/ppermute | solution.py:141
  102.5 11.4 %collective-permute-start.25 = (bf16[128,640]{1,0:T(8,128)(2,1)}, bf16[128,640]{1,0:T(8,128)(2,1)}, u32[]{:S(2)}, u32[]{:S(2)}) collective-permute-start(bf16[128,640]{1,0:T(8,128)(2,1)} %collective-permute-done.11.refs_26_), channel_id=1, source_target_pairs={{0,2},{2,4},{4,6},{6,7},{7,5},{5,3},{3,1},{1,0},{8,10},{10,12},{12... | collective-permute-start | bytes 491528 | tf_op jit(solution)/shard_map/ppermute | solution.py:141
  104.4 12.9 %collective-permute-start.27 = (bf16[128,768]{1,0:T(8,128)(2,1)}, bf16[128,768]{1,0:T(8,128)(2,1)}, u32[]{:S(2)}, u32[]{:S(2)}) collective-permute-start(bf16[128,768]{1,0:T(8,128)(2,1)} %collective-permute-done.24.refs_28_), channel_id=1, source_target_pairs={{0,2},{2,4},{4,6},{6,7},{7,5},{5,3},{3,1},{1,0},{8,10},{10,12},{12... | collective-permute-start | bytes 589832 | tf_op jit(solution)/shard_map/ppermute | solution.py:141
  135.3 16.0 %collective-permute-start.30 = (bf16[128,1024]{1,0:T(8,128)(2,1)S(1)}, bf16[128,1024]{1,0:T(8,128)(2,1)S(1)}, u32[]{:S(2)}, u32[]{:S(2)}) collective-permute-start(bf16[128,1024]{1,0:T(8,128)(2,1)S(1)} %get-tuple-element.75), channel_id=1, source_target_pairs={{0,192},{64,0},{128,64},{192,128},{1,193},{65,1},{129,65},{193,129... | collective-permute-start | bytes 786440 | tf_op jit(solution)/shard_map/ppermute | solution.py:162
  140.0 12.7 %collective-permute-start.29 = (bf16[128,1024]{1,0:T(8,128)(2,1)S(1)}, bf16[128,1024]{1,0:T(8,128)(2,1)S(1)}, u32[]{:S(2)}, u32[]{:S(2)}) collective-permute-start(bf16[128,1024]{1,0:T(8,128)(2,1)S(1)} %get-tuple-element.74), channel_id=1, source_target_pairs={{0,128},{64,192},{128,0},{192,64},{1,129},{65,193},{129,1},{193,65... | collective-permute-start | bytes 786440 | tf_op jit(solution)/shard_map/ppermute | solution.py:162
  142.7 13.6 %collective-permute-start.28 = (bf16[128,1024]{1,0:T(8,128)(2,1)S(1)}, bf16[128,1024]{1,0:T(8,128)(2,1)S(1)}, u32[]{:S(2)}, u32[]{:S(2)}) collective-permute-start(bf16[128,1024]{1,0:T(8,128)(2,1)S(1)} %get-tuple-element.73), channel_id=1, source_target_pairs={{0,64},{64,128},{128,192},{192,0},{1,65},{65,129},{129,193},{193,1... | collective-permute-start | bytes 786440 | tf_op jit(solution)/shard_map/ppermute | solution.py:162
  156.5 34.4 %collective-permute-start.34 = (bf16[128,1024]{1,0:T(8,128)(2,1)S(1)}, bf16[128,1024]{1,0:T(8,128)(2,1)S(1)}, u32[]{:S(2)}, u32[]{:S(2)}) collective-permute-start(bf16[128,1024]{1,0:T(8,128)(2,1)S(1)} %add_convert_fusion), channel_id=1, source_target_pairs={{0,256},{256,0},{1,257},{257,1},{2,258},{258,2},{3,259},{259,3},{4... | collective-permute-start | bytes 786440 | tf_op jit(solution)/shard_map/ppermute | solution.py:175
  165.6 25.3 %collective-permute-start.33 = (bf16[128,1024]{1,0:T(8,128)(2,1)S(1)}, bf16[128,1024]{1,0:T(8,128)(2,1)S(1)}, u32[]{:S(2)}, u32[]{:S(2)}) collective-permute-start(bf16[128,1024]{1,0:T(8,128)(2,1)S(1)} %get-tuple-element.81), channel_id=1, source_target_pairs={{0,192},{64,0},{128,64},{192,128},{1,193},{65,1},{129,65},{193,129... | collective-permute-start | bytes 786440 | tf_op jit(solution)/shard_map/ppermute | solution.py:162
  168.1 22.8 %collective-permute-start.32 = (bf16[128,1024]{1,0:T(8,128)(2,1)S(1)}, bf16[128,1024]{1,0:T(8,128)(2,1)S(1)}, u32[]{:S(2)}, u32[]{:S(2)}) collective-permute-start(bf16[128,1024]{1,0:T(8,128)(2,1)S(1)} %get-tuple-element.80), channel_id=1, source_target_pairs={{0,128},{64,192},{128,0},{192,64},{1,129},{65,193},{129,1},{193,65... | collective-permute-start | bytes 786440 | tf_op jit(solution)/shard_map/ppermute | solution.py:162
  170.8 20.1 %collective-permute-start.31 = (bf16[128,1024]{1,0:T(8,128)(2,1)S(1)}, bf16[128,1024]{1,0:T(8,128)(2,1)S(1)}, u32[]{:S(2)}, u32[]{:S(2)}) collective-permute-start(bf16[128,1024]{1,0:T(8,128)(2,1)S(1)} %get-tuple-element.79), channel_id=1, source_target_pairs={{0,64},{64,128},{128,192},{192,0},{1,65},{65,129},{129,193},{193,1... | collective-permute-start | bytes 786440 | tf_op jit(solution)/shard_map/ppermute | solution.py:162
  (37 other events, 436.4 us)

commit v11 on v9

--- a/solution.py
+++ b/solution.py
@@ -63,6 +63,25 @@
     )(elements)
 
 
+def ordered_kernel(n_g, order, *refs):
+    *near, columns = refs
+    for i, pair in enumerate(near):
+        for core in range(2):
+            at = pl.multiple_of(order[2 * i + core] * n_g, 128)
+            columns[:, pl.ds(at, n_g)] = pair[:, core * n_g : (core + 1) * n_g]
+
+
+def ordered(order, near):
+    n_pair, width = near[0].shape
+    return pl.pallas_call(
+        functools.partial(ordered_kernel, width // 2),
+        out_shape=jax.ShapeDtypeStruct((n_pair, width * len(near)), near[0].dtype),
+        in_specs=[pl.BlockSpec(memory_space=pltpu.SMEM)] + [WHOLE] * len(near),
+        out_specs=WHOLE,
+        compiler_params=pltpu.CompilerParams(vmem_limit_bytes=24 * 1024 * 1024),
+    )(order, *near)
+
+
 def product_kernel(n_turns, parts, slots, factor, columns, *refs):
     pieces = refs[: n_turns * parts]
     own, *others, rows = refs[n_turns * parts :]
@@ -97,7 +116,7 @@
         in_specs=[pl.BlockSpec(memory_space=pltpu.SMEM)] + [WHOLE] * (2 + len(pieces)),
         out_specs=[WHOLE] * n_slots,
         scratch_shapes=[pltpu.VMEM((n_slots * n_g, n_pair), jnp.bfloat16)],
-        compiler_params=pltpu.CompilerParams(vmem_limit_bytes=40 * 1024 * 1024),
+        compiler_params=pltpu.CompilerParams(vmem_limit_bytes=24 * 1024 * 1024),
         cost_estimate=pl.CostEstimate(
             flops=2 * n_slots * n_g * n_pair * width,
             bytes_accessed=8 * 1024 * 1024,
@@ -109,14 +128,24 @@
 def body(pair_elements, valence_of, conduction_of, valence_depth, conduction_height):
     n_pair, n_g = pair_elements.shape
     n_x, n_z = lax.axis_size("x"), lax.axis_size("zl")
-    columns = lax.all_gather(pair_elements, ("y", "core"), axis=1, tiled=True)
+    n_y = lax.axis_size("y")
 
     order = circle(n_z)
     step = [(order[i], order[(i + 1) % n_z]) for i in range(n_z)]
-    parts = 3
+    parts = 2
     chunks = turned(pair_elements, parts)
     pieces = list(chunks)
+    both = jnp.concatenate(
+        [pair_elements, lax.ppermute(pair_elements, "core", shift(2, 1))], axis=1
+    )
+    near = [both] + [lax.ppermute(both, "y", shift(n_y, -s)) for s in range(1, n_y)]
+    pair = jnp.arange(2 * n_y, dtype=jnp.int32)
+    places = 2 * lax.rem(lax.axis_index("y") + pair // 2, n_y)
+    places = places + lax.rem(lax.axis_index("core") + pair % 2, 2)
     for turn in range(1, n_z):
+        if turn == 6:
+            columns = ordered(places, near)
+            chunks[0], columns = lax.optimization_barrier((chunks[0], columns))
         if turn == n_z - 2:
             chunks[0], factor = lax.optimization_barrier((chunks[0], factor))
         chunks = [lax.ppermute(chunk, "zl", step) for chunk in chunks]

time: 163 us -> 179 us (1.098)
  the two profiles are of different devices: /device:TPU:72 before, /device:TPU:65 now
where the time goes in v11:
time: 179 us; the launch traced here: 178 us
  starting transfers between devices  102 us (57%)
  waiting for transfers between devices  47.7 us (27%)
  local copies, waits for them, and re-layouts  13.6 us (8%)
  Pallas kernels  12.6 us (7%)
    ppermute x14, starting transfers between devices, body(): chunks = [lax.ppermute(chunk, 'zl', step) for chunk in chunks]  63 us
    ppermute x14, waiting for transfers between devices, body(): chunks = [lax.ppermute(chunk, 'zl', step) for chunk in chunks]  18.7 us
    ppermute x1, waiting for transfers between devices, body(): got = lax.ppermute(given, 'zh', shift(2, 1)).astype(jnp.float32)  17.1 us
    ppermute x6, starting transfers between devices, summed_over_x(): lax.ppermute(one, 'x', shift(n_x, s))  16.5 us
    unnamed x38, local copies, waits for them, and re-layouts  12.6 us
    ppermute x1, starting transfers between devices, body(): got = lax.ppermute(given, 'zh', shift(2, 1)).astype(jnp.float32)  10.3 us
    ppermute x3, starting transfers between devices, body(): lax.ppermute(both, 'y', shift(n_y, -s))  9.5 us
    pallas_call x2, Pallas kernels, product(): pl.pallas_call(functools.partial(product_kernel, n_turns, parts), out_sha...  8.23 us
  transfers between devices with their start and end apart: 25, of which 13 were waited for; matrix products, arithmetic and copies ran while one was open for 2% of the time, Pallas kernels for 5%

profile of v11, /device:TPU:65, one launch (start us, length us, event | category | flops | bytes accessed | tf_op | source)
XLA Modules:
  0.0 177.9 jit_solution(12797094473763170731)
XLA Ops:
  0.0 2.7 %collective-permute-start.5 = (bf16[2048,128]{1,0:T(8,128)(2,1)}, bf16[2048,128]{1,0:T(8,128)(2,1)S(1)}, u32[]{:S(2)}, u32[]{:S(2)}) collective-permute-start(bf16[2048,128]{1,0:T(8,128)(2,1)} %elements.1), channel_id=1, source_target_pairs={{0,8},{8,0},{1,9},{9,1},{2,10},{10,2},{3,11},{11,3},{4,12},{12,4},... | collective-permute-start | bytes 1572872 | tf_op jit(solution)/shard_map/ppermute | solution.py:139
  4.7 6.1 %collective-permute-start = (bf16[128,1024]{1,0:T(8,128)(2,1)}, bf16[128,1024]{1,0:T(8,128)(2,1)S(1)}, u32[]{:S(2)}, u32[]{:S(2)}) collective-permute-start(bf16[128,1024]{1,0:T(8,128)(2,1)} %get-tuple-element.30.refs_0_), channel_id=1, source_target_pairs={{0,2},{2,4},{4,6},{6,7},{7,5},{5,3},{3,1},{1,0},{8,10},{10,12},{12... | collective-permute-start | bytes 786440 | tf_op jit(solution)/shard_map/ppermute | solution.py:151
  10.8 4.9 %collective-permute-start.9 = (bf16[128,1024]{1,0:T(8,128)(2,1)}, bf16[128,1024]{1,0:T(8,128)(2,1)}, u32[]{:S(2)}, u32[]{:S(2)}) collective-permute-start(bf16[128,1024]{1,0:T(8,128)(2,1)} %get-tuple-element.36.refs_1_), channel_id=1, source_target_pairs={{0,2},{2,4},{4,6},{6,7},{7,5},{5,3},{3,1},{1,0},{8,10},{10,12},{12... | collective-permute-start | bytes 786440 | tf_op jit(solution)/shard_map/ppermute | solution.py:151
  18.2 4.7 %collective-permute-start.1 = (bf16[128,1024]{1,0:T(8,128)(2,1)S(1)}, bf16[128,1024]{1,0:T(8,128)(2,1)}, u32[]{:S(2)}, u32[]{:S(2)}) collective-permute-start(bf16[128,1024]{1,0:T(8,128)(2,1)S(1)} %collective-permute-done.refs_2_), channel_id=1, source_target_pairs={{0,2},{2,4},{4,6},{6,7},{7,5},{5,3},{3,1},{1,0},{8,10},{10,12},{12... | collective-permute-start | bytes 786440 | tf_op jit(solution)/shard_map/ppermute | solution.py:151
  23.9 4.7 %collective-permute-start.10 = (bf16[128,1024]{1,0:T(8,128)(2,1)}, bf16[128,1024]{1,0:T(8,128)(2,1)}, u32[]{:S(2)}, u32[]{:S(2)}) collective-permute-start(bf16[128,1024]{1,0:T(8,128)(2,1)} %collective-permute-done.9.refs_3_), channel_id=1, source_target_pairs={{0,2},{2,4},{4,6},{6,7},{7,5},{5,3},{3,1},{1,0},{8,10},{10,12},{12... | collective-permute-start | bytes 786440 | tf_op jit(solution)/shard_map/ppermute | solution.py:151
  28.8 4.6 %collective-permute-start.6 = (bf16[2048,256]{1,0:T(8,128)(2,1)S(1)}, bf16[2048,256]{1,0:T(8,128)(2,1)S(1)}, u32[]{:S(2)}, u32[]{:S(2)}) collective-permute-start(bf16[2048,256]{1,0:T(8,128)(2,1)S(1)} %constant_dynamic-update-slice_fusion.refs_0_), channel_id=1, source_target_pairs={{0,48},{16,0},{32,16},{48,32},{1,49},{17,1},{33,17},{49,33},{2,50}... | collective-permute-start | bytes 3145736 | tf_op jit(solution)/shard_map/ppermute | solution.py:141
  33.5 2.3 %collective-permute-start.7 = (bf16[2048,256]{1,0:T(8,128)(2,1)S(1)}, bf16[2048,256]{1,0:T(8,128)(2,1)S(1)}, u32[]{:S(2)}, u32[]{:S(2)}) collective-permute-start(bf16[2048,256]{1,0:T(8,128)(2,1)S(1)} %constant_dynamic-update-slice_fusion.refs_0_), channel_id=1, source_target_pairs={{0,32},{16,48},{32,0},{48,16},{1,33},{17,49},{33,1},{49,17},{2,34}... | collective-permute-start | bytes 3145736 | tf_op jit(solution)/shard_map/ppermute | solution.py:141
  35.7 2.6 %collective-permute-start.8 = (bf16[2048,256]{1,0:T(8,128)(2,1)S(1)}, bf16[2048,256]{1,0:T(8,128)(2,1)}, u32[]{:S(2)}, u32[]{:S(2)}) collective-permute-start(bf16[2048,256]{1,0:T(8,128)(2,1)S(1)} %constant_dynamic-update-slice_fusion.refs_0_), channel_id=1, source_target_pairs={{0,16},{16,32},{32,48},{48,0},{1,17},{17,33},{33,49},{49,1},{2,18}... | collective-permute-start | bytes 3145736 | tf_op jit(solution)/shard_map/ppermute | solution.py:141
  38.4 3.7 %collective-permute-start.2 = (bf16[128,1024]{1,0:T(8,128)(2,1)}, bf16[128,1024]{1,0:T(8,128)(2,1)}, u32[]{:S(2)}, u32[]{:S(2)}) collective-permute-start(bf16[128,1024]{1,0:T(8,128)(2,1)} %collective-permute-done.1.refs_4_), channel_id=1, source_target_pairs={{0,2},{2,4},{4,6},{6,7},{7,5},{5,3},{3,1},{1,0},{8,10},{10,12},{12... | collective-permute-start | bytes 786440 | tf_op jit(solution)/shard_map/ppermute | solution.py:151
  42.1 2.6 %collective-permute-start.11 = (bf16[128,1024]{1,0:T(8,128)(2,1)}, bf16[128,1024]{1,0:T(8,128)(2,1)}, u32[]{:S(2)}, u32[]{:S(2)}) collective-permute-start(bf16[128,1024]{1,0:T(8,128)(2,1)} %collective-permute-done.10.refs_5_), channel_id=1, source_target_pairs={{0,2},{2,4},{4,6},{6,7},{7,5},{5,3},{3,1},{1,0},{8,10},{10,12},{12... | collective-permute-start | bytes 786440 | tf_op jit(solution)/shard_map/ppermute | solution.py:151
  44.8 2.5 %collective-permute-done.2.refs_6_ = bf16[128,1024]{1,0:T(8,128)(2,1)} collective-permute-done((bf16[128,1024]{1,0:T(8,128)(2,1)}, bf16[128,1024]{1,0:T(8,128)(2,1)}, u32[]{:S(2)}, u32[]{:S(2)}) %collective-permute-start.2) | collective-permute-done | bytes 262176 | tf_op jit(solution)/shard_map/ppermute | solution.py:151
  47.3 4.4 %collective-permute-start.3 = (bf16[128,1024]{1,0:T(8,128)(2,1)}, bf16[128,1024]{1,0:T(8,128)(2,1)S(1)}, u32[]{:S(2)}, u32[]{:S(2)}) collective-permute-start(bf16[128,1024]{1,0:T(8,128)(2,1)} %collective-permute-done.2.refs_6_), channel_id=1, source_target_pairs={{0,2},{2,4},{4,6},{6,7},{7,5},{5,3},{3,1},{1,0},{8,10},{10,12},{12... | collective-permute-start | bytes 786440 | tf_op jit(solution)/shard_map/ppermute | solution.py:151
  53.5 3.9 %collective-permute-start.12 = (bf16[128,1024]{1,0:T(8,128)(2,1)}, bf16[128,1024]{1,0:T(8,128)(2,1)S(1)}, u32[]{:S(2)}, u32[]{:S(2)}) collective-permute-start(bf16[128,1024]{1,0:T(8,128)(2,1)} %collective-permute-done.11.refs_7_), channel_id=1, source_target_pairs={{0,2},{2,4},{4,6},{6,7},{7,5},{5,3},{3,1},{1,0},{8,10},{10,12},{12... | collective-permute-start | bytes 786440 | tf_op jit(solution)/shard_map/ppermute | solution.py:151
  58.1 4.9 %collective-permute-start.4 = (bf16[128,1024]{1,0:T(8,128)(2,1)S(1)}, bf16[128,1024]{1,0:T(8,128)(2,1)S(1)}, u32[]{:S(2)}, u32[]{:S(2)}) collective-permute-start(bf16[128,1024]{1,0:T(8,128)(2,1)S(1)} %collective-permute-done.3.refs_8_), channel_id=1, source_target_pairs={{0,2},{2,4},{4,6},{6,7},{7,5},{5,3},{3,1},{1,0},{8,10},{10,12},{12... | collective-permute-start | bytes 786440 | tf_op jit(solution)/shard_map/ppermute | solution.py:151
  63.9 5.2 %collective-permute-start.13 = (bf16[128,1024]{1,0:T(8,128)(2,1)S(1)}, bf16[128,1024]{1,0:T(8,128)(2,1)S(1)}, u32[]{:S(2)}, u32[]{:S(2)}) collective-permute-start(bf16[128,1024]{1,0:T(8,128)(2,1)S(1)} %collective-permute-done.12.refs_9_), channel_id=1, source_target_pairs={{0,2},{2,4},{4,6},{6,7},{7,5},{5,3},{3,1},{1,0},{8,10},{10,12},{12... | collective-permute-start | bytes 786440 | tf_op jit(solution)/shard_map/ppermute | solution.py:151
  69.6 4.5 %collective-permute-done.13.refs_11_ = bf16[128,1024]{1,0:T(8,128)(2,1)S(1)} collective-permute-done((bf16[128,1024]{1,0:T(8,128)(2,1)S(1)}, bf16[128,1024]{1,0:T(8,128)(2,1)S(1)}, u32[]{:S(2)}, u32[]{:S(2)}) %collective-permute-start.13) | collective-permute-done | bytes 262176 | tf_op jit(solution)/shard_map/ppermute | solution.py:151
  74.2 5.3 %collective-permute-start.15 = (bf16[128,1024]{1,0:T(8,128)(2,1)S(1)}, bf16[128,1024]{1,0:T(8,128)(2,1)}, u32[]{:S(2)}, u32[]{:S(2)}) collective-permute-start(bf16[128,1024]{1,0:T(8,128)(2,1)S(1)} %collective-permute-done.13.refs_11_), channel_id=1, source_target_pairs={{0,2},{2,4},{4,6},{6,7},{7,5},{5,3},{3,1},{1,0},{8,10},{10,12},{12... | collective-permute-start | bytes 786440 | tf_op jit(solution)/shard_map/ppermute | solution.py:151
  79.5 5.0 %collective-permute-done.8.refs_3_ = bf16[2048,256]{1,0:T(8,128)(2,1)} collective-permute-done((bf16[2048,256]{1,0:T(8,128)(2,1)S(1)}, bf16[2048,256]{1,0:T(8,128)(2,1)}, u32[]{:S(2)}, u32[]{:S(2)}) %collective-permute-start.8) | collective-permute-done | bytes 1048608 | tf_op jit(solution)/shard_map/ppermute | solution.py:141
  84.5 2.4 %shard_map.56.columns = bf16[2048,1024]{1,0:T(8,128)(2,1)S(1)} custom-call(s32[8]{0:T(128)S(1)} %fusion.28.order, bf16[2048,256]{1,0:T(8,128)(2,1)S(1)} %constant_dynamic-update-slice_fusion.refs_0_, bf16[2048,256]{1,0:T(8,128)(2,1)S(1)} %collective-permute-done.6.refs_1_, bf16[2048,256]{1,0:T(8,128)(2,1)S(1)} %collective-permute-done.7.refs_2_, ...), custom_call_target="tpu_custom_call" | custom-call | tf_op jit(solution)/shard_map/pallas_call | solution.py:76
  89.0 3.7 %collective-permute-start.14 = (bf16[128,1024]{1,0:T(8,128)(2,1)S(1)}, bf16[128,1024]{1,0:T(8,128)(2,1)S(1)}, u32[]{:S(2)}, u32[]{:S(2)}) collective-permute-start(bf16[128,1024]{1,0:T(8,128)(2,1)S(1)} %collective-permute-done.4.refs_10_), channel_id=1, source_target_pairs={{0,2},{2,4},{4,6},{6,7},{7,5},{5,3},{3,1},{1,0},{8,10},{10,12},{12... | collective-permute-start | bytes 786440 | tf_op jit(solution)/shard_map/ppermute | solution.py:151
  93.4 2.6 %collective-permute-start.17 = (bf16[128,1024]{1,0:T(8,128)(2,1)}, bf16[128,1024]{1,0:T(8,128)(2,1)S(1)}, u32[]{:S(2)}, u32[]{:S(2)}) collective-permute-start(bf16[128,1024]{1,0:T(8,128)(2,1)} %collective-permute-done.15.refs_13_), channel_id=1, source_target_pairs={{0,2},{2,4},{4,6},{6,7},{7,5},{5,3},{3,1},{1,0},{8,10},{10,12},{12... | collective-permute-start | bytes 786440 | tf_op jit(solution)/shard_map/ppermute | solution.py:151
  97.6 6.2 %collective-permute-start.16 = (bf16[128,1024]{1,0:T(8,128)(2,1)S(1)}, bf16[128,1024]{1,0:T(8,128)(2,1)S(1)}, u32[]{:S(2)}, u32[]{:S(2)}) collective-permute-start(bf16[128,1024]{1,0:T(8,128)(2,1)S(1)} %collective-permute-done.14.refs_12_), channel_id=1, source_target_pairs={{0,2},{2,4},{4,6},{6,7},{7,5},{5,3},{3,1},{1,0},{8,10},{10,12},{12... | collective-permute-start | bytes 786440 | tf_op jit(solution)/shard_map/ppermute | solution.py:151
  104.7 4.8 %collective-permute-done.16.refs_14_ = bf16[128,1024]{1,0:T(8,128)(2,1)S(1)} collective-permute-done((bf16[128,1024]{1,0:T(8,128)(2,1)S(1)}, bf16[128,1024]{1,0:T(8,128)(2,1)S(1)}, u32[]{:S(2)}, u32[]{:S(2)}) %collective-permute-start.16) | collective-permute-done | bytes 262176 | tf_op jit(solution)/shard_map/ppermute | solution.py:151
  117.5 4.1 %shard_map.57 = (f32[128,1024]{1,0:T(8,128)S(1)}, bf16[128,1024]{1,0:T(8,128)(2,1)S(1)}, bf16[128,1024]{1,0:T(8,128)(2,1)S(1)}, bf16[128,1024]{1,0:T(8,128)(2,1)S(1)}) custom-call(s32[8]{0:T(128)S(1)} %get-tuple-element.65.slots, f32[1,2048]{1,0:T(1,128)S(1)} %bitcast.5, bf16[2048,1024]{1,0:T(8,128)(2,1)S(1)} %copy-done.1, bf16[128,1024]{1,0:T(8,128)(2,1)S(1)} %copy-done.2, ...), custom_call_target="tpu_custom_call" | custom-call | flops 2147483648 | bytes 8388608 | tf_op jit(solution)/shard_map/pallas_call | solution.py:113
  121.6 4.4 %collective-permute-start.20 = (bf16[128,1024]{1,0:T(8,128)(2,1)S(1)}, bf16[128,1024]{1,0:T(8,128)(2,1)S(1)}, u32[]{:S(2)}, u32[]{:S(2)}) collective-permute-start(bf16[128,1024]{1,0:T(8,128)(2,1)S(1)} %get-tuple-element.47), channel_id=1, source_target_pairs={{0,192},{64,0},{128,64},{192,128},{1,193},{65,1},{129,65},{193,129... | collective-permute-start | bytes 786440 | tf_op jit(solution)/shard_map/ppermute | solution.py:169
  126.0 2.4 %collective-permute-start.19 = (bf16[128,1024]{1,0:T(8,128)(2,1)S(1)}, bf16[128,1024]{1,0:T(8,128)(2,1)S(1)}, u32[]{:S(2)}, u32[]{:S(2)}) collective-permute-start(bf16[128,1024]{1,0:T(8,128)(2,1)S(1)} %get-tuple-element.46), channel_id=1, source_target_pairs={{0,128},{64,192},{128,0},{192,64},{1,129},{65,193},{129,1},{193,65... | collective-permute-start | bytes 786440 | tf_op jit(solution)/shard_map/ppermute | solution.py:169
  128.4 2.5 %collective-permute-start.18 = (bf16[128,1024]{1,0:T(8,128)(2,1)S(1)}, bf16[128,1024]{1,0:T(8,128)(2,1)S(1)}, u32[]{:S(2)}, u32[]{:S(2)}) collective-permute-start(bf16[128,1024]{1,0:T(8,128)(2,1)S(1)} %get-tuple-element.45), channel_id=1, source_target_pairs={{0,64},{64,128},{128,192},{192,0},{1,65},{65,129},{129,193},{193,1... | collective-permute-start | bytes 786440 | tf_op jit(solution)/shard_map/ppermute | solution.py:169
  130.9 4.1 %shard_map.58 = (f32[128,1024]{1,0:T(8,128)S(1)}, bf16[128,1024]{1,0:T(8,128)(2,1)S(1)}, bf16[128,1024]{1,0:T(8,128)(2,1)S(1)}, bf16[128,1024]{1,0:T(8,128)(2,1)S(1)}) custom-call(s32[8]{0:T(128)S(1)} %get-tuple-element.42.slots, f32[1,2048]{1,0:T(1,128)S(1)} %bitcast.6, bf16[2048,1024]{1,0:T(8,128)(2,1)S(1)} %copy-done.1, bf16[128,1024]{1,0:T(8,128)(2,1)S(1)} %copy-done.2, ...), custom_call_target="tpu_custom_call" | custom-call | flops 2147483648 | bytes 8388608 | tf_op jit(solution)/shard_map/pallas_call | solution.py:113
  135.1 6.9 %collective-permute-done.18 = bf16[128,1024]{1,0:T(8,128)(2,1)S(1)} collective-permute-done((bf16[128,1024]{1,0:T(8,128)(2,1)S(1)}, bf16[128,1024]{1,0:T(8,128)(2,1)S(1)}, u32[]{:S(2)}, u32[]{:S(2)}) %collective-permute-start.18) | collective-permute-done | bytes 262176 | tf_op jit(solution)/shard_map/ppermute | solution.py:169
  142.1 10.3 %collective-permute-start.24 = (bf16[128,1024]{1,0:T(8,128)(2,1)S(1)}, bf16[128,1024]{1,0:T(8,128)(2,1)S(1)}, u32[]{:S(2)}, u32[]{:S(2)}) collective-permute-start(bf16[128,1024]{1,0:T(8,128)(2,1)S(1)} %add_convert_fusion), channel_id=1, source_target_pairs={{0,256},{256,0},{1,257},{257,1},{2,258},{258,2},{3,259},{259,3},{4... | collective-permute-start | bytes 786440 | tf_op jit(solution)/shard_map/ppermute | solution.py:182
  156.6 3.1 %collective-permute-start.21 = (bf16[128,1024]{1,0:T(8,128)(2,1)S(1)}, bf16[128,1024]{1,0:T(8,128)(2,1)S(1)}, u32[]{:S(2)}, u32[]{:S(2)}) collective-permute-start(bf16[128,1024]{1,0:T(8,128)(2,1)S(1)} %get-tuple-element.51), channel_id=1, source_target_pairs={{0,64},{64,128},{128,192},{192,0},{1,65},{65,129},{129,193},{193,1... | collective-permute-start | bytes 786440 | tf_op jit(solution)/shard_map/ppermute | solution.py:169
  159.7 17.1 %collective-permute-done.24 = bf16[128,1024]{1,0:T(8,128)(2,1)S(1)} collective-permute-done((bf16[128,1024]{1,0:T(8,128)(2,1)S(1)}, bf16[128,1024]{1,0:T(8,128)(2,1)S(1)}, u32[]{:S(2)}, u32[]{:S(2)}) %collective-permute-start.24) | collective-permute-done | bytes 262176 | tf_op jit(solution)/shard_map/ppermute | solution.py:182
  (75 shorter events, 27.9 us)
Async XLA Ops:
  0.0 44.7 %copy-start.15 = (f32[4096]{0:T(1024)S(1)}, f32[4096]{0:T(1024)}, u32[]{:S(2)}) copy-start(f32[4096]{0:T(1024)} %param.9) | copy-start | bytes 49156
  0.0 57.5 %copy-start.17 = (s32[2048]{0:T(1024)S(1)}, s32[2048]{0:T(1024)}, u32[]{:S(2)}) copy-start(s32[2048]{0:T(1024)} %param.6) | copy-start | bytes 24580
  0.0 57.5 %copy-start.16 = (s32[2048]{0:T(1024)S(1)}, s32[2048]{0:T(1024)}, u32[]{:S(2)}) copy-start(s32[2048]{0:T(1024)} %param.7) | copy-start | bytes 24580
  0.0 28.7 %collective-permute-start.5 = (bf16[2048,128]{1,0:T(8,128)(2,1)}, bf16[2048,128]{1,0:T(8,128)(2,1)S(1)}, u32[]{:S(2)}, u32[]{:S(2)}) collective-permute-start(bf16[2048,128]{1,0:T(8,128)(2,1)} %elements.1), channel_id=1, source_target_pairs={{0,8},{8,0},{1,9},{9,1},{2,10},{10,2},{3,11},{11,3},{4,12},{12,4},... | collective-permute-start | bytes 1572872 | tf_op jit(solution)/shard_map/ppermute | solution.py:139
  4.7 13.5 %collective-permute-start = (bf16[128,1024]{1,0:T(8,128)(2,1)}, bf16[128,1024]{1,0:T(8,128)(2,1)S(1)}, u32[]{:S(2)}, u32[]{:S(2)}) collective-permute-start(bf16[128,1024]{1,0:T(8,128)(2,1)} %get-tuple-element.30.refs_0_), channel_id=1, source_target_pairs={{0,2},{2,4},{4,6},{6,7},{7,5},{5,3},{3,1},{1,0},{8,10},{10,12},{12... | collective-permute-start | bytes 786440 | tf_op jit(solution)/shard_map/ppermute | solution.py:151
  10.8 13.1 %collective-permute-start.9 = (bf16[128,1024]{1,0:T(8,128)(2,1)}, bf16[128,1024]{1,0:T(8,128)(2,1)}, u32[]{:S(2)}, u32[]{:S(2)}) collective-permute-start(bf16[128,1024]{1,0:T(8,128)(2,1)} %get-tuple-element.36.refs_1_), channel_id=1, source_target_pairs={{0,2},{2,4},{4,6},{6,7},{7,5},{5,3},{3,1},{1,0},{8,10},{10,12},{12... | collective-permute-start | bytes 786440 | tf_op jit(solution)/shard_map/ppermute | solution.py:151
  18.2 51.4 %copy-start.4 = (bf16[128,1024]{1,0:T(8,128)(2,1)}, bf16[128,1024]{1,0:T(8,128)(2,1)S(1)}, u32[]{:S(2)}) copy-start(bf16[128,1024]{1,0:T(8,128)(2,1)S(1)} %collective-permute-done.refs_2_) | copy-start | bytes 786436
  18.2 20.1 %collective-permute-start.1 = (bf16[128,1024]{1,0:T(8,128)(2,1)S(1)}, bf16[128,1024]{1,0:T(8,128)(2,1)}, u32[]{:S(2)}, u32[]{:S(2)}) collective-permute-start(bf16[128,1024]{1,0:T(8,128)(2,1)S(1)} %collective-permute-done.refs_2_), channel_id=1, source_target_pairs={{0,2},{2,4},{4,6},{6,7},{7,5},{5,3},{3,1},{1,0},{8,10},{10,12},{12... | collective-permute-start | bytes 786440 | tf_op jit(solution)/shard_map/ppermute | solution.py:151
  23.9 18.1 %collective-permute-start.10 = (bf16[128,1024]{1,0:T(8,128)(2,1)}, bf16[128,1024]{1,0:T(8,128)(2,1)}, u32[]{:S(2)}, u32[]{:S(2)}) collective-permute-start(bf16[128,1024]{1,0:T(8,128)(2,1)} %collective-permute-done.9.refs_3_), channel_id=1, source_target_pairs={{0,2},{2,4},{4,6},{6,7},{7,5},{5,3},{3,1},{1,0},{8,10},{10,12},{12... | collective-permute-start | bytes 786440 | tf_op jit(solution)/shard_map/ppermute | solution.py:151
  28.8 50.6 %collective-permute-start.6 = (bf16[2048,256]{1,0:T(8,128)(2,1)S(1)}, bf16[2048,256]{1,0:T(8,128)(2,1)S(1)}, u32[]{:S(2)}, u32[]{:S(2)}) collective-permute-start(bf16[2048,256]{1,0:T(8,128)(2,1)S(1)} %constant_dynamic-update-slice_fusion.refs_0_), channel_id=1, source_target_pairs={{0,48},{16,0},{32,16},{48,32},{1,49},{17,1},{33,17},{49,33},{2,50}... | collective-permute-start | bytes 3145736 | tf_op jit(solution)/shard_map/ppermute | solution.py:141
  33.5 46.0 %collective-permute-start.7 = (bf16[2048,256]{1,0:T(8,128)(2,1)S(1)}, bf16[2048,256]{1,0:T(8,128)(2,1)S(1)}, u32[]{:S(2)}, u32[]{:S(2)}) collective-permute-start(bf16[2048,256]{1,0:T(8,128)(2,1)S(1)} %constant_dynamic-update-slice_fusion.refs_0_), channel_id=1, source_target_pairs={{0,32},{16,48},{32,0},{48,16},{1,33},{17,49},{33,1},{49,17},{2,34}... | collective-permute-start | bytes 3145736 | tf_op jit(solution)/shard_map/ppermute | solution.py:141
  35.7 48.8 %collective-permute-start.8 = (bf16[2048,256]{1,0:T(8,128)(2,1)S(1)}, bf16[2048,256]{1,0:T(8,128)(2,1)}, u32[]{:S(2)}, u32[]{:S(2)}) collective-permute-start(bf16[2048,256]{1,0:T(8,128)(2,1)S(1)} %constant_dynamic-update-slice_fusion.refs_0_), channel_id=1, source_target_pairs={{0,16},{16,32},{32,48},{48,0},{1,17},{17,33},{33,49},{49,1},{2,18}... | collective-permute-start | bytes 3145736 | tf_op jit(solution)/shard_map/ppermute | solution.py:141
  38.4 9.0 %collective-permute-start.2 = (bf16[128,1024]{1,0:T(8,128)(2,1)}, bf16[128,1024]{1,0:T(8,128)(2,1)}, u32[]{:S(2)}, u32[]{:S(2)}) collective-permute-start(bf16[128,1024]{1,0:T(8,128)(2,1)} %collective-permute-done.1.refs_4_), channel_id=1, source_target_pairs={{0,2},{2,4},{4,6},{6,7},{7,5},{5,3},{3,1},{1,0},{8,10},{10,12},{12... | collective-permute-start | bytes 786440 | tf_op jit(solution)/shard_map/ppermute | solution.py:151
  42.1 11.5 %collective-permute-start.11 = (bf16[128,1024]{1,0:T(8,128)(2,1)}, bf16[128,1024]{1,0:T(8,128)(2,1)}, u32[]{:S(2)}, u32[]{:S(2)}) collective-permute-start(bf16[128,1024]{1,0:T(8,128)(2,1)} %collective-permute-done.10.refs_5_), channel_id=1, source_target_pairs={{0,2},{2,4},{4,6},{6,7},{7,5},{5,3},{3,1},{1,0},{8,10},{10,12},{12... | collective-permute-start | bytes 786440 | tf_op jit(solution)/shard_map/ppermute | solution.py:151
  47.3 10.8 %collective-permute-start.3 = (bf16[128,1024]{1,0:T(8,128)(2,1)}, bf16[128,1024]{1,0:T(8,128)(2,1)S(1)}, u32[]{:S(2)}, u32[]{:S(2)}) collective-permute-start(bf16[128,1024]{1,0:T(8,128)(2,1)} %collective-permute-done.2.refs_6_), channel_id=1, source_target_pairs={{0,2},{2,4},{4,6},{6,7},{7,5},{5,3},{3,1},{1,0},{8,10},{10,12},{12... | collective-permute-start | bytes 786440 | tf_op jit(solution)/shard_map/ppermute | solution.py:151
  53.5 10.4 %collective-permute-start.12 = (bf16[128,1024]{1,0:T(8,128)(2,1)}, bf16[128,1024]{1,0:T(8,128)(2,1)S(1)}, u32[]{:S(2)}, u32[]{:S(2)}) collective-permute-start(bf16[128,1024]{1,0:T(8,128)(2,1)} %collective-permute-done.11.refs_7_), channel_id=1, source_target_pairs={{0,2},{2,4},{4,6},{6,7},{7,5},{5,3},{3,1},{1,0},{8,10},{10,12},{12... | collective-permute-start | bytes 786440 | tf_op jit(solution)/shard_map/ppermute | solution.py:151
  58.1 28.9 %copy-start.6 = (bf16[128,1024]{1,0:T(8,128)(2,1)}, bf16[128,1024]{1,0:T(8,128)(2,1)S(1)}, u32[]{:S(2)}) copy-start(bf16[128,1024]{1,0:T(8,128)(2,1)S(1)} %collective-permute-done.3.refs_8_) | copy-start | bytes 786436
  58.1 30.8 %collective-permute-start.4 = (bf16[128,1024]{1,0:T(8,128)(2,1)S(1)}, bf16[128,1024]{1,0:T(8,128)(2,1)S(1)}, u32[]{:S(2)}, u32[]{:S(2)}) collective-permute-start(bf16[128,1024]{1,0:T(8,128)(2,1)S(1)} %collective-permute-done.3.refs_8_), channel_id=1, source_target_pairs={{0,2},{2,4},{4,6},{6,7},{7,5},{5,3},{3,1},{1,0},{8,10},{10,12},{12... | collective-permute-start | bytes 786440 | tf_op jit(solution)/shard_map/ppermute | solution.py:151
  63.9 15.5 %copy-start.9 = (bf16[128,1024]{1,0:T(8,128)(2,1)}, bf16[128,1024]{1,0:T(8,128)(2,1)S(1)}, u32[]{:S(2)}) copy-start(bf16[128,1024]{1,0:T(8,128)(2,1)S(1)} %collective-permute-done.12.refs_9_) | copy-start | bytes 786436
  63.9 10.2 %collective-permute-start.13 = (bf16[128,1024]{1,0:T(8,128)(2,1)S(1)}, bf16[128,1024]{1,0:T(8,128)(2,1)S(1)}, u32[]{:S(2)}, u32[]{:S(2)}) collective-permute-start(bf16[128,1024]{1,0:T(8,128)(2,1)S(1)} %collective-permute-done.12.refs_9_), channel_id=1, source_target_pairs={{0,2},{2,4},{4,6},{6,7},{7,5},{5,3},{3,1},{1,0},{8,10},{10,12},{12... | collective-permute-start | bytes 786440 | tf_op jit(solution)/shard_map/ppermute | solution.py:151
  69.6 39.9 %copy-start.2 = (bf16[128,1024]{1,0:T(8,128)(2,1)S(1)}, bf16[128,1024]{1,0:T(8,128)(2,1)}, u32[]{:S(2)}) copy-start(bf16[128,1024]{1,0:T(8,128)(2,1)} %get-tuple-element.30.refs_0_) | copy-start | bytes 786436
  74.2 19.2 %collective-permute-start.15 = (bf16[128,1024]{1,0:T(8,128)(2,1)S(1)}, bf16[128,1024]{1,0:T(8,128)(2,1)}, u32[]{:S(2)}, u32[]{:S(2)}) collective-permute-start(bf16[128,1024]{1,0:T(8,128)(2,1)S(1)} %collective-permute-done.13.refs_11_), channel_id=1, source_target_pairs={{0,2},{2,4},{4,6},{6,7},{7,5},{5,3},{3,1},{1,0},{8,10},{10,12},{12... | collective-permute-start | bytes 786440 | tf_op jit(solution)/shard_map/ppermute | solution.py:151
  89.0 8.7 %collective-permute-start.14 = (bf16[128,1024]{1,0:T(8,128)(2,1)S(1)}, bf16[128,1024]{1,0:T(8,128)(2,1)S(1)}, u32[]{:S(2)}, u32[]{:S(2)}) collective-permute-start(bf16[128,1024]{1,0:T(8,128)(2,1)S(1)} %collective-permute-done.4.refs_10_), channel_id=1, source_target_pairs={{0,2},{2,4},{4,6},{6,7},{7,5},{5,3},{3,1},{1,0},{8,10},{10,12},{12... | collective-permute-start | bytes 786440 | tf_op jit(solution)/shard_map/ppermute | solution.py:151
  93.4 11.4 %collective-permute-start.17 = (bf16[128,1024]{1,0:T(8,128)(2,1)}, bf16[128,1024]{1,0:T(8,128)(2,1)S(1)}, u32[]{:S(2)}, u32[]{:S(2)}) collective-permute-start(bf16[128,1024]{1,0:T(8,128)(2,1)} %collective-permute-done.15.refs_13_), channel_id=1, source_target_pairs={{0,2},{2,4},{4,6},{6,7},{7,5},{5,3},{3,1},{1,0},{8,10},{10,12},{12... | collective-permute-start | bytes 786440 | tf_op jit(solution)/shard_map/ppermute | solution.py:151
  97.6 11.9 %collective-permute-start.16 = (bf16[128,1024]{1,0:T(8,128)(2,1)S(1)}, bf16[128,1024]{1,0:T(8,128)(2,1)S(1)}, u32[]{:S(2)}, u32[]{:S(2)}) collective-permute-start(bf16[128,1024]{1,0:T(8,128)(2,1)S(1)} %collective-permute-done.14.refs_12_), channel_id=1, source_target_pairs={{0,2},{2,4},{4,6},{6,7},{7,5},{5,3},{3,1},{1,0},{8,10},{10,12},{12... | collective-permute-start | bytes 786440 | tf_op jit(solution)/shard_map/ppermute | solution.py:151
  121.6 13.5 %collective-permute-start.20 = (bf16[128,1024]{1,0:T(8,128)(2,1)S(1)}, bf16[128,1024]{1,0:T(8,128)(2,1)S(1)}, u32[]{:S(2)}, u32[]{:S(2)}) collective-permute-start(bf16[128,1024]{1,0:T(8,128)(2,1)S(1)} %get-tuple-element.47), channel_id=1, source_target_pairs={{0,192},{64,0},{128,64},{192,128},{1,193},{65,1},{129,65},{193,129... | collective-permute-start | bytes 786440 | tf_op jit(solution)/shard_map/ppermute | solution.py:169
  126.0 9.1 %collective-permute-start.19 = (bf16[128,1024]{1,0:T(8,128)(2,1)S(1)}, bf16[128,1024]{1,0:T(8,128)(2,1)S(1)}, u32[]{:S(2)}, u32[]{:S(2)}) collective-permute-start(bf16[128,1024]{1,0:T(8,128)(2,1)S(1)} %get-tuple-element.46), channel_id=1, source_target_pairs={{0,128},{64,192},{128,0},{192,64},{1,129},{65,193},{129,1},{193,65... | collective-permute-start | bytes 786440 | tf_op jit(solution)/shard_map/ppermute | solution.py:169
  128.4 13.5 %collective-permute-start.18 = (bf16[128,1024]{1,0:T(8,128)(2,1)S(1)}, bf16[128,1024]{1,0:T(8,128)(2,1)S(1)}, u32[]{:S(2)}, u32[]{:S(2)}) collective-permute-start(bf16[128,1024]{1,0:T(8,128)(2,1)S(1)} %get-tuple-element.45), channel_id=1, source_target_pairs={{0,64},{64,128},{128,192},{192,0},{1,65},{65,129},{129,193},{193,1... | collective-permute-start | bytes 786440 | tf_op jit(solution)/shard_map/ppermute | solution.py:169
  142.1 34.7 %collective-permute-start.24 = (bf16[128,1024]{1,0:T(8,128)(2,1)S(1)}, bf16[128,1024]{1,0:T(8,128)(2,1)S(1)}, u32[]{:S(2)}, u32[]{:S(2)}) collective-permute-start(bf16[128,1024]{1,0:T(8,128)(2,1)S(1)} %add_convert_fusion), channel_id=1, source_target_pairs={{0,256},{256,0},{1,257},{257,1},{2,258},{258,2},{3,259},{259,3},{4... | collective-permute-start | bytes 786440 | tf_op jit(solution)/shard_map/ppermute | solution.py:182
  152.5 24.3 %collective-permute-start.23 = (bf16[128,1024]{1,0:T(8,128)(2,1)S(1)}, bf16[128,1024]{1,0:T(8,128)(2,1)S(1)}, u32[]{:S(2)}, u32[]{:S(2)}) collective-permute-start(bf16[128,1024]{1,0:T(8,128)(2,1)S(1)} %get-tuple-element.53), channel_id=1, source_target_pairs={{0,192},{64,0},{128,64},{192,128},{1,193},{65,1},{129,65},{193,129... | collective-permute-start | bytes 786440 | tf_op jit(solution)/shard_map/ppermute | solution.py:169
  154.4 22.4 %collective-permute-start.22 = (bf16[128,1024]{1,0:T(8,128)(2,1)S(1)}, bf16[128,1024]{1,0:T(8,128)(2,1)S(1)}, u32[]{:S(2)}, u32[]{:S(2)}) collective-permute-start(bf16[128,1024]{1,0:T(8,128)(2,1)S(1)} %get-tuple-element.52), channel_id=1, source_target_pairs={{0,128},{64,192},{128,0},{192,64},{1,129},{65,193},{129,1},{193,65... | collective-permute-start | bytes 786440 | tf_op jit(solution)/shard_map/ppermute | solution.py:169
  156.6 20.2 %collective-permute-start.21 = (bf16[128,1024]{1,0:T(8,128)(2,1)S(1)}, bf16[128,1024]{1,0:T(8,128)(2,1)S(1)}, u32[]{:S(2)}, u32[]{:S(2)}) collective-permute-start(bf16[128,1024]{1,0:T(8,128)(2,1)S(1)} %get-tuple-element.51), channel_id=1, source_target_pairs={{0,64},{64,128},{128,192},{192,0},{1,65},{65,129},{129,193},{193,1... | collective-permute-start | bytes 786440 | tf_op jit(solution)/shard_map/ppermute | solution.py:169
  (11 other events, 36.9 us)

commit v12 on v7

--- a/solution.py
+++ b/solution.py
@@ -143,7 +143,8 @@
     stays = col // n_x == my_half
 
     def summed_over_x(own, others):
-        got = [lax.ppermute(one, "x", shift(n_x, s)) for s, one in enumerate(others, 1)]
+        apart = sorted(range(1, n_x), key=lambda s: min(s, n_x - s))
+        got = [lax.ppermute(others[s - 1], "x", shift(n_x, s)) for s in apart]
         for one in got:
             own = own + one.astype(jnp.float32)
         return own

time: 161 us -> 163 us (1.012)
  transfers between devices with their start and end apart: 22 -> 22, of which waited for: 18 -> 16; matrix products, arithmetic and copies ran while one was open for 2% -> 2% of each run, Pallas kernels for 4% -> 4%
where the time goes in v12:
time: 163 us; the launch traced here: 162 us
  waiting for transfers between devices  72.7 us (45%)
  starting transfers between devices  58.6 us (36%)
  between operations  13.7 us (8%)
  Pallas kernels  9.98 us (6%)
  local copies, waits for them, and re-layouts  4.66 us (3%)
    ppermute x14, waiting for transfers between devices, body(): chunks = [lax.ppermute(chunk, 'zl', step) for chunk in chunks]  61.1 us
    ppermute x14, starting transfers between devices, body(): chunks = [lax.ppermute(chunk, 'zl', step) for chunk in chunks]  26.7 us
    ppermute x6, starting transfers between devices, summed_over_x(): got = [lax.ppermute(others[s - 1], 'x', shift(n_x, s)) for s in apart]  18.9 us
    ppermute x1, starting transfers between devices, body(): got = lax.ppermute(given, 'zh', shift(2, 1)).astype(jnp.float32)  13 us
    ppermute x1, waiting for transfers between devices, body(): got = lax.ppermute(given, 'zh', shift(2, 1)).astype(jnp.float32)  8.21 us
    pallas_call x2, Pallas kernels, product(): pl.pallas_call(functools.partial(product_kernel, n_turns, parts), out_sha...  7.94 us
  transfers between devices with their start and end apart: 22, of which 16 were waited for; matrix products, arithmetic and copies ran while one was open for 2% of the time, Pallas kernels for 4%

profile of v12, /device:TPU:120, one launch (start us, length us, event | category | flops | bytes accessed | tf_op | source)
XLA Modules:
  0.0 161.7 jit_solution(1422291898385674270)
XLA Ops:
  7.3 2.0 %shard_map.55 = (bf16[64,2048]{1,0:T(8,128)(2,1)}, bf16[64,2048]{1,0:T(8,128)(2,1)}) custom-call(bf16[2048,128]{1,0:T(8,128)(2,1)} %elements.1), custom_call_target="tpu_custom_call" | custom-call | tf_op jit(solution)/shard_map/pallas_call | solution.py:59
  11.2 1.9 %collective-permute-start.5 = (bf16[64,2048]{1,0:T(8,128)(2,1)}, bf16[64,2048]{1,0:T(8,128)(2,1)S(1)}, u32[]{:S(2)}, u32[]{:S(2)}) collective-permute-start(bf16[64,2048]{1,0:T(8,128)(2,1)} %get-tuple-element.32.refs_1_), channel_id=1, source_target_pairs={{0,2},{2,4},{4,6},{6,7},{7,5},{5,3},{3,1},{1,0},{8,10},{10,12},{12... | collective-permute-start | bytes 786440 | tf_op jit(solution)/shard_map/ppermute | solution.py:126
  13.1 9.9 %collective-permute-done.refs_2_ = bf16[64,2048]{1,0:T(8,128)(2,1)S(1)} collective-permute-done((bf16[64,2048]{1,0:T(8,128)(2,1)}, bf16[64,2048]{1,0:T(8,128)(2,1)S(1)}, u32[]{:S(2)}, u32[]{:S(2)}) %collective-permute-start) | collective-permute-done | bytes 262176 | tf_op jit(solution)/shard_map/ppermute | solution.py:126
  23.0 1.9 %collective-permute-start.1 = (bf16[64,2048]{1,0:T(8,128)(2,1)S(1)}, bf16[64,2048]{1,0:T(8,128)(2,1)S(1)}, u32[]{:S(2)}, u32[]{:S(2)}) collective-permute-start(bf16[64,2048]{1,0:T(8,128)(2,1)S(1)} %collective-permute-done.refs_2_), channel_id=1, source_target_pairs={{0,2},{2,4},{4,6},{6,7},{7,5},{5,3},{3,1},{1,0},{8,10},{10,12},{12... | collective-permute-start | bytes 786440 | tf_op jit(solution)/shard_map/ppermute | solution.py:126
  24.9 2.9 %collective-permute-done.5.refs_3_ = bf16[64,2048]{1,0:T(8,128)(2,1)S(1)} collective-permute-done((bf16[64,2048]{1,0:T(8,128)(2,1)}, bf16[64,2048]{1,0:T(8,128)(2,1)S(1)}, u32[]{:S(2)}, u32[]{:S(2)}) %collective-permute-start.5) | collective-permute-done | bytes 262176 | tf_op jit(solution)/shard_map/ppermute | solution.py:126
  30.5 3.2 %collective-permute-done.1.refs_4_ = bf16[64,2048]{1,0:T(8,128)(2,1)S(1)} collective-permute-done((bf16[64,2048]{1,0:T(8,128)(2,1)S(1)}, bf16[64,2048]{1,0:T(8,128)(2,1)S(1)}, u32[]{:S(2)}, u32[]{:S(2)}) %collective-permute-start.1) | collective-permute-done | bytes 262176 | tf_op jit(solution)/shard_map/ppermute | solution.py:126
  35.6 5.0 %collective-permute-done.6.refs_5_ = bf16[64,2048]{1,0:T(8,128)(2,1)S(1)} collective-permute-done((bf16[64,2048]{1,0:T(8,128)(2,1)S(1)}, bf16[64,2048]{1,0:T(8,128)(2,1)S(1)}, u32[]{:S(2)}, u32[]{:S(2)}) %collective-permute-start.6) | collective-permute-done | bytes 262176 | tf_op jit(solution)/shard_map/ppermute | solution.py:126
  43.3 2.2 %collective-permute-done.2.refs_6_ = bf16[64,2048]{1,0:T(8,128)(2,1)S(1)} collective-permute-done((bf16[64,2048]{1,0:T(8,128)(2,1)S(1)}, bf16[64,2048]{1,0:T(8,128)(2,1)S(1)}, u32[]{:S(2)}, u32[]{:S(2)}) %collective-permute-start.2) | collective-permute-done | bytes 262176 | tf_op jit(solution)/shard_map/ppermute | solution.py:126
  47.4 4.8 %collective-permute-done.7.refs_7_ = bf16[64,2048]{1,0:T(8,128)(2,1)S(1)} collective-permute-done((bf16[64,2048]{1,0:T(8,128)(2,1)S(1)}, bf16[64,2048]{1,0:T(8,128)(2,1)S(1)}, u32[]{:S(2)}, u32[]{:S(2)}) %collective-permute-start.7) | collective-permute-done | bytes 262176 | tf_op jit(solution)/shard_map/ppermute | solution.py:126
  55.4 3.4 %collective-permute-done.3.refs_8_ = bf16[64,2048]{1,0:T(8,128)(2,1)S(1)} collective-permute-done((bf16[64,2048]{1,0:T(8,128)(2,1)S(1)}, bf16[64,2048]{1,0:T(8,128)(2,1)S(1)}, u32[]{:S(2)}, u32[]{:S(2)}) %collective-permute-start.3) | collective-permute-done | bytes 262176 | tf_op jit(solution)/shard_map/ppermute | solution.py:126
  60.6 3.4 %collective-permute-done.8.refs_9_ = bf16[64,2048]{1,0:T(8,128)(2,1)S(1)} collective-permute-done((bf16[64,2048]{1,0:T(8,128)(2,1)S(1)}, bf16[64,2048]{1,0:T(8,128)(2,1)S(1)}, u32[]{:S(2)}, u32[]{:S(2)}) %collective-permute-start.8) | collective-permute-done | bytes 262176 | tf_op jit(solution)/shard_map/ppermute | solution.py:126
  66.5 4.9 %collective-permute-done.4.refs_10_ = bf16[64,2048]{1,0:T(8,128)(2,1)S(1)} collective-permute-done((bf16[64,2048]{1,0:T(8,128)(2,1)S(1)}, bf16[64,2048]{1,0:T(8,128)(2,1)S(1)}, u32[]{:S(2)}, u32[]{:S(2)}) %collective-permute-start.4) | collective-permute-done | bytes 262176 | tf_op jit(solution)/shard_map/ppermute | solution.py:126
  73.3 3.7 %collective-permute-done.9.refs_11_ = bf16[64,2048]{1,0:T(8,128)(2,1)S(1)} collective-permute-done((bf16[64,2048]{1,0:T(8,128)(2,1)S(1)}, bf16[64,2048]{1,0:T(8,128)(2,1)S(1)}, u32[]{:S(2)}, u32[]{:S(2)}) %collective-permute-start.9) | collective-permute-done | bytes 262176 | tf_op jit(solution)/shard_map/ppermute | solution.py:126
  77.0 1.9 %collective-permute-start.11 = (bf16[64,2048]{1,0:T(8,128)(2,1)S(1)}, bf16[64,2048]{1,0:T(8,128)(2,1)}, u32[]{:S(2)}, u32[]{:S(2)}) collective-permute-start(bf16[64,2048]{1,0:T(8,128)(2,1)S(1)} %collective-permute-done.9.refs_11_), channel_id=1, source_target_pairs={{0,2},{2,4},{4,6},{6,7},{7,5},{5,3},{3,1},{1,0},{8,10},{10,12},{12... | collective-permute-start | bytes 786440 | tf_op jit(solution)/shard_map/ppermute | solution.py:126
  79.0 4.3 %collective-permute-done.10.refs_12_ = bf16[64,2048]{1,0:T(8,128)(2,1)S(1)} collective-permute-done((bf16[64,2048]{1,0:T(8,128)(2,1)S(1)}, bf16[64,2048]{1,0:T(8,128)(2,1)S(1)}, u32[]{:S(2)}, u32[]{:S(2)}) %collective-permute-start.10) | collective-permute-done | bytes 262176 | tf_op jit(solution)/shard_map/ppermute | solution.py:126
  83.3 1.9 %collective-permute-start.12 = (bf16[64,2048]{1,0:T(8,128)(2,1)S(1)}, bf16[64,2048]{1,0:T(8,128)(2,1)}, u32[]{:S(2)}, u32[]{:S(2)}) collective-permute-start(bf16[64,2048]{1,0:T(8,128)(2,1)S(1)} %collective-permute-done.10.refs_12_), channel_id=1, source_target_pairs={{0,2},{2,4},{4,6},{6,7},{7,5},{5,3},{3,1},{1,0},{8,10},{10,12},{12... | collective-permute-start | bytes 786440 | tf_op jit(solution)/shard_map/ppermute | solution.py:126
  85.2 4.7 %collective-permute-done.11.refs_13_ = bf16[64,2048]{1,0:T(8,128)(2,1)} collective-permute-done((bf16[64,2048]{1,0:T(8,128)(2,1)S(1)}, bf16[64,2048]{1,0:T(8,128)(2,1)}, u32[]{:S(2)}, u32[]{:S(2)}) %collective-permute-start.11) | collective-permute-done | bytes 262176 | tf_op jit(solution)/shard_map/ppermute | solution.py:126
  89.9 1.9 %collective-permute-start.13 = (bf16[64,2048]{1,0:T(8,128)(2,1)}, bf16[64,2048]{1,0:T(8,128)(2,1)}, u32[]{:S(2)}, u32[]{:S(2)}) collective-permute-start(bf16[64,2048]{1,0:T(8,128)(2,1)} %collective-permute-done.11.refs_13_), channel_id=1, source_target_pairs={{0,2},{2,4},{4,6},{6,7},{7,5},{5,3},{3,1},{1,0},{8,10},{10,12},{12... | collective-permute-start | bytes 786440 | tf_op jit(solution)/shard_map/ppermute | solution.py:126
  91.9 3.2 %collective-permute-done.12.refs_14_ = bf16[64,2048]{1,0:T(8,128)(2,1)} collective-permute-done((bf16[64,2048]{1,0:T(8,128)(2,1)S(1)}, bf16[64,2048]{1,0:T(8,128)(2,1)}, u32[]{:S(2)}, u32[]{:S(2)}) %collective-permute-start.12) | collective-permute-done | bytes 262176 | tf_op jit(solution)/shard_map/ppermute | solution.py:126
  95.1 5.5 %collective-permute-done.13.refs_15_ = bf16[64,2048]{1,0:T(8,128)(2,1)} collective-permute-done((bf16[64,2048]{1,0:T(8,128)(2,1)}, bf16[64,2048]{1,0:T(8,128)(2,1)}, u32[]{:S(2)}, u32[]{:S(2)}) %collective-permute-start.13) | collective-permute-done | bytes 262176 | tf_op jit(solution)/shard_map/ppermute | solution.py:126
  100.6 2.2 %copy-done = bf16[2048,1024]{1,0:T(8,128)(2,1)S(1)} copy-done((bf16[2048,1024]{1,0:T(8,128)(2,1)S(1)}, bf16[2048,1024]{1,0:T(8,128)(2,1)}, u32[]{:S(2)}) %copy-start) | copy-done | bytes 4194328
  102.8 4.0 %shard_map.56 = (f32[128,1024]{1,0:T(8,128)S(1)}, bf16[128,1024]{1,0:T(8,128)(2,1)S(1)}, bf16[128,1024]{1,0:T(8,128)(2,1)S(1)}, bf16[128,1024]{1,0:T(8,128)(2,1)S(1)}) custom-call(s32[8]{0:T(128)S(1)} %get-tuple-element.61.slots, f32[1,2048]{1,0:T(1,128)S(1)} %bitcast.5, bf16[2048,1024]{1,0:T(8,128)(2,1)S(1)} %copy-done, bf16[64,2048]{1,0:T(8,128)(2,1)S(1)} %copy-done.2, ...), custom_call_target="tpu_custom_call" | custom-call | flops 2147483648 | bytes 8388608 | tf_op jit(solution)/shard_map/pallas_call | solution.py:100
  106.9 4.9 %collective-permute-start.16 = (bf16[128,1024]{1,0:T(8,128)(2,1)S(1)}, bf16[128,1024]{1,0:T(8,128)(2,1)S(1)}, u32[]{:S(2)}, u32[]{:S(2)}) collective-permute-start(bf16[128,1024]{1,0:T(8,128)(2,1)S(1)} %get-tuple-element.43), channel_id=1, source_target_pairs={{0,128},{64,192},{128,0},{192,64},{1,129},{65,193},{129,1},{193,65... | collective-permute-start | bytes 786440 | tf_op jit(solution)/shard_map/ppermute | solution.py:147
  111.8 3.0 %collective-permute-start.15 = (bf16[128,1024]{1,0:T(8,128)(2,1)S(1)}, bf16[128,1024]{1,0:T(8,128)(2,1)S(1)}, u32[]{:S(2)}, u32[]{:S(2)}) collective-permute-start(bf16[128,1024]{1,0:T(8,128)(2,1)S(1)} %get-tuple-element.42), channel_id=1, source_target_pairs={{0,192},{64,0},{128,64},{192,128},{1,193},{65,1},{129,65},{193,129... | collective-permute-start | bytes 786440 | tf_op jit(solution)/shard_map/ppermute | solution.py:147
  114.8 2.8 %collective-permute-start.14 = (bf16[128,1024]{1,0:T(8,128)(2,1)S(1)}, bf16[128,1024]{1,0:T(8,128)(2,1)S(1)}, u32[]{:S(2)}, u32[]{:S(2)}) collective-permute-start(bf16[128,1024]{1,0:T(8,128)(2,1)S(1)} %get-tuple-element.41), channel_id=1, source_target_pairs={{0,64},{64,128},{128,192},{192,0},{1,65},{65,129},{129,193},{193,1... | collective-permute-start | bytes 786440 | tf_op jit(solution)/shard_map/ppermute | solution.py:147
  117.7 3.9 %shard_map.57 = (f32[128,1024]{1,0:T(8,128)S(1)}, bf16[128,1024]{1,0:T(8,128)(2,1)S(1)}, bf16[128,1024]{1,0:T(8,128)(2,1)S(1)}, bf16[128,1024]{1,0:T(8,128)(2,1)S(1)}) custom-call(s32[8]{0:T(128)S(1)} %get-tuple-element.38.slots, f32[1,2048]{1,0:T(1,128)S(1)} %bitcast.6, bf16[2048,1024]{1,0:T(8,128)(2,1)S(1)} %copy-done.1, bf16[64,2048]{1,0:T(8,128)(2,1)S(1)} %copy-done.2, ...), custom_call_target="tpu_custom_call" | custom-call | flops 2147483648 | bytes 8388608 | tf_op jit(solution)/shard_map/pallas_call | solution.py:100
  121.6 2.7 %collective-permute-done.14 = bf16[128,1024]{1,0:T(8,128)(2,1)S(1)} collective-permute-done((bf16[128,1024]{1,0:T(8,128)(2,1)S(1)}, bf16[128,1024]{1,0:T(8,128)(2,1)S(1)}, u32[]{:S(2)}, u32[]{:S(2)}) %collective-permute-start.14) | collective-permute-done | bytes 262176 | tf_op jit(solution)/shard_map/ppermute | solution.py:147
  124.5 13.0 %collective-permute-start.20 = (bf16[128,1024]{1,0:T(8,128)(2,1)S(1)}, bf16[128,1024]{1,0:T(8,128)(2,1)S(1)}, u32[]{:S(2)}, u32[]{:S(2)}) collective-permute-start(bf16[128,1024]{1,0:T(8,128)(2,1)S(1)} %add_convert_fusion), channel_id=1, source_target_pairs={{0,256},{256,0},{1,257},{257,1},{2,258},{258,2},{3,259},{259,3},{4... | collective-permute-start | bytes 786440 | tf_op jit(solution)/shard_map/ppermute | solution.py:160
  137.5 2.2 %collective-permute-start.19 = (bf16[128,1024]{1,0:T(8,128)(2,1)S(1)}, bf16[128,1024]{1,0:T(8,128)(2,1)S(1)}, u32[]{:S(2)}, u32[]{:S(2)}) collective-permute-start(bf16[128,1024]{1,0:T(8,128)(2,1)S(1)} %get-tuple-element.49), channel_id=1, source_target_pairs={{0,128},{64,192},{128,0},{192,64},{1,129},{65,193},{129,1},{193,65... | collective-permute-start | bytes 786440 | tf_op jit(solution)/shard_map/ppermute | solution.py:147
  139.7 3.9 %collective-permute-start.18 = (bf16[128,1024]{1,0:T(8,128)(2,1)S(1)}, bf16[128,1024]{1,0:T(8,128)(2,1)S(1)}, u32[]{:S(2)}, u32[]{:S(2)}) collective-permute-start(bf16[128,1024]{1,0:T(8,128)(2,1)S(1)} %get-tuple-element.48), channel_id=1, source_target_pairs={{0,192},{64,0},{128,64},{192,128},{1,193},{65,1},{129,65},{193,129... | collective-permute-start | bytes 786440 | tf_op jit(solution)/shard_map/ppermute | solution.py:147
  143.7 1.9 %collective-permute-start.17 = (bf16[128,1024]{1,0:T(8,128)(2,1)S(1)}, bf16[128,1024]{1,0:T(8,128)(2,1)S(1)}, u32[]{:S(2)}, u32[]{:S(2)}) collective-permute-start(bf16[128,1024]{1,0:T(8,128)(2,1)S(1)} %get-tuple-element.47), channel_id=1, source_target_pairs={{0,64},{64,128},{128,192},{192,0},{1,65},{65,129},{129,193},{193,1... | collective-permute-start | bytes 786440 | tf_op jit(solution)/shard_map/ppermute | solution.py:147
  145.6 8.2 %collective-permute-done.20 = bf16[128,1024]{1,0:T(8,128)(2,1)S(1)} collective-permute-done((bf16[128,1024]{1,0:T(8,128)(2,1)S(1)}, bf16[128,1024]{1,0:T(8,128)(2,1)S(1)}, u32[]{:S(2)}, u32[]{:S(2)}) %collective-permute-start.20) | collective-permute-done | bytes 262176 | tf_op jit(solution)/shard_map/ppermute | solution.py:160
  (38 shorter events, 22.5 us)
Async XLA Ops:
  6.5 94.1 %all-gather.2.cloned.1.call-start = ((), (), s32[]{:S(2)}) async-start(), calls=%async_computation | async-start | bytes 4718592 | tf_op jit(solution)/shard_map/all_gather | solution.py:118
  9.3 13.7 %collective-permute-start = (bf16[64,2048]{1,0:T(8,128)(2,1)}, bf16[64,2048]{1,0:T(8,128)(2,1)S(1)}, u32[]{:S(2)}, u32[]{:S(2)}) collective-permute-start(bf16[64,2048]{1,0:T(8,128)(2,1)} %get-tuple-element.28.refs_0_), channel_id=1, source_target_pairs={{0,2},{2,4},{4,6},{6,7},{7,5},{5,3},{3,1},{1,0},{8,10},{10,12},{12... | collective-permute-start | bytes 786440 | tf_op jit(solution)/shard_map/ppermute | solution.py:126
  11.2 16.6 %collective-permute-start.5 = (bf16[64,2048]{1,0:T(8,128)(2,1)}, bf16[64,2048]{1,0:T(8,128)(2,1)S(1)}, u32[]{:S(2)}, u32[]{:S(2)}) collective-permute-start(bf16[64,2048]{1,0:T(8,128)(2,1)} %get-tuple-element.32.refs_1_), channel_id=1, source_target_pairs={{0,2},{2,4},{4,6},{6,7},{7,5},{5,3},{3,1},{1,0},{8,10},{10,12},{12... | collective-permute-start | bytes 786440 | tf_op jit(solution)/shard_map/ppermute | solution.py:126
  23.0 10.7 %collective-permute-start.1 = (bf16[64,2048]{1,0:T(8,128)(2,1)S(1)}, bf16[64,2048]{1,0:T(8,128)(2,1)S(1)}, u32[]{:S(2)}, u32[]{:S(2)}) collective-permute-start(bf16[64,2048]{1,0:T(8,128)(2,1)S(1)} %collective-permute-done.refs_2_), channel_id=1, source_target_pairs={{0,2},{2,4},{4,6},{6,7},{7,5},{5,3},{3,1},{1,0},{8,10},{10,12},{12... | collective-permute-start | bytes 786440 | tf_op jit(solution)/shard_map/ppermute | solution.py:126
  27.8 12.8 %collective-permute-start.6 = (bf16[64,2048]{1,0:T(8,128)(2,1)S(1)}, bf16[64,2048]{1,0:T(8,128)(2,1)S(1)}, u32[]{:S(2)}, u32[]{:S(2)}) collective-permute-start(bf16[64,2048]{1,0:T(8,128)(2,1)S(1)} %collective-permute-done.5.refs_3_), channel_id=1, source_target_pairs={{0,2},{2,4},{4,6},{6,7},{7,5},{5,3},{3,1},{1,0},{8,10},{10,12},{12... | collective-permute-start | bytes 786440 | tf_op jit(solution)/shard_map/ppermute | solution.py:126
  33.7 11.8 %collective-permute-start.2 = (bf16[64,2048]{1,0:T(8,128)(2,1)S(1)}, bf16[64,2048]{1,0:T(8,128)(2,1)S(1)}, u32[]{:S(2)}, u32[]{:S(2)}) collective-permute-start(bf16[64,2048]{1,0:T(8,128)(2,1)S(1)} %collective-permute-done.1.refs_4_), channel_id=1, source_target_pairs={{0,2},{2,4},{4,6},{6,7},{7,5},{5,3},{3,1},{1,0},{8,10},{10,12},{12... | collective-permute-start | bytes 786440 | tf_op jit(solution)/shard_map/ppermute | solution.py:126
  40.6 11.6 %collective-permute-start.7 = (bf16[64,2048]{1,0:T(8,128)(2,1)S(1)}, bf16[64,2048]{1,0:T(8,128)(2,1)S(1)}, u32[]{:S(2)}, u32[]{:S(2)}) collective-permute-start(bf16[64,2048]{1,0:T(8,128)(2,1)S(1)} %collective-permute-done.6.refs_5_), channel_id=1, source_target_pairs={{0,2},{2,4},{4,6},{6,7},{7,5},{5,3},{3,1},{1,0},{8,10},{10,12},{12... | collective-permute-start | bytes 786440 | tf_op jit(solution)/shard_map/ppermute | solution.py:126
  45.5 13.2 %collective-permute-start.3 = (bf16[64,2048]{1,0:T(8,128)(2,1)S(1)}, bf16[64,2048]{1,0:T(8,128)(2,1)S(1)}, u32[]{:S(2)}, u32[]{:S(2)}) collective-permute-start(bf16[64,2048]{1,0:T(8,128)(2,1)S(1)} %collective-permute-done.2.refs_6_), channel_id=1, source_target_pairs={{0,2},{2,4},{4,6},{6,7},{7,5},{5,3},{3,1},{1,0},{8,10},{10,12},{12... | collective-permute-start | bytes 786440 | tf_op jit(solution)/shard_map/ppermute | solution.py:126
  52.2 11.8 %collective-permute-start.8 = (bf16[64,2048]{1,0:T(8,128)(2,1)S(1)}, bf16[64,2048]{1,0:T(8,128)(2,1)S(1)}, u32[]{:S(2)}, u32[]{:S(2)}) collective-permute-start(bf16[64,2048]{1,0:T(8,128)(2,1)S(1)} %collective-permute-done.7.refs_7_), channel_id=1, source_target_pairs={{0,2},{2,4},{4,6},{6,7},{7,5},{5,3},{3,1},{1,0},{8,10},{10,12},{12... | collective-permute-start | bytes 786440 | tf_op jit(solution)/shard_map/ppermute | solution.py:126
  54.9 45.7 %copy-start.2 = (bf16[64,2048]{1,0:T(8,128)(2,1)S(1)}, bf16[64,2048]{1,0:T(8,128)(2,1)}, u32[]{:S(2)}) copy-start(bf16[64,2048]{1,0:T(8,128)(2,1)} %get-tuple-element.28.refs_0_) | copy-start | bytes 786436
  54.9 45.7 %copy-start.3 = (bf16[64,2048]{1,0:T(8,128)(2,1)S(1)}, bf16[64,2048]{1,0:T(8,128)(2,1)}, u32[]{:S(2)}) copy-start(bf16[64,2048]{1,0:T(8,128)(2,1)} %get-tuple-element.32.refs_1_) | copy-start | bytes 786436
  58.7 12.7 %collective-permute-start.4 = (bf16[64,2048]{1,0:T(8,128)(2,1)S(1)}, bf16[64,2048]{1,0:T(8,128)(2,1)S(1)}, u32[]{:S(2)}, u32[]{:S(2)}) collective-permute-start(bf16[64,2048]{1,0:T(8,128)(2,1)S(1)} %collective-permute-done.3.refs_8_), channel_id=1, source_target_pairs={{0,2},{2,4},{4,6},{6,7},{7,5},{5,3},{3,1},{1,0},{8,10},{10,12},{12... | collective-permute-start | bytes 786440 | tf_op jit(solution)/shard_map/ppermute | solution.py:126
  64.1 13.0 %collective-permute-start.9 = (bf16[64,2048]{1,0:T(8,128)(2,1)S(1)}, bf16[64,2048]{1,0:T(8,128)(2,1)S(1)}, u32[]{:S(2)}, u32[]{:S(2)}) collective-permute-start(bf16[64,2048]{1,0:T(8,128)(2,1)S(1)} %collective-permute-done.8.refs_9_), channel_id=1, source_target_pairs={{0,2},{2,4},{4,6},{6,7},{7,5},{5,3},{3,1},{1,0},{8,10},{10,12},{12... | collective-permute-start | bytes 786440 | tf_op jit(solution)/shard_map/ppermute | solution.py:126
  71.4 11.9 %collective-permute-start.10 = (bf16[64,2048]{1,0:T(8,128)(2,1)S(1)}, bf16[64,2048]{1,0:T(8,128)(2,1)S(1)}, u32[]{:S(2)}, u32[]{:S(2)}) collective-permute-start(bf16[64,2048]{1,0:T(8,128)(2,1)S(1)} %collective-permute-done.4.refs_10_), channel_id=1, source_target_pairs={{0,2},{2,4},{4,6},{6,7},{7,5},{5,3},{3,1},{1,0},{8,10},{10,12},{12... | collective-permute-start | bytes 786440 | tf_op jit(solution)/shard_map/ppermute | solution.py:126
  77.0 12.9 %collective-permute-start.11 = (bf16[64,2048]{1,0:T(8,128)(2,1)S(1)}, bf16[64,2048]{1,0:T(8,128)(2,1)}, u32[]{:S(2)}, u32[]{:S(2)}) collective-permute-start(bf16[64,2048]{1,0:T(8,128)(2,1)S(1)} %collective-permute-done.9.refs_11_), channel_id=1, source_target_pairs={{0,2},{2,4},{4,6},{6,7},{7,5},{5,3},{3,1},{1,0},{8,10},{10,12},{12... | collective-permute-start | bytes 786440 | tf_op jit(solution)/shard_map/ppermute | solution.py:126
  83.3 11.8 %collective-permute-start.12 = (bf16[64,2048]{1,0:T(8,128)(2,1)S(1)}, bf16[64,2048]{1,0:T(8,128)(2,1)}, u32[]{:S(2)}, u32[]{:S(2)}) collective-permute-start(bf16[64,2048]{1,0:T(8,128)(2,1)S(1)} %collective-permute-done.10.refs_12_), channel_id=1, source_target_pairs={{0,2},{2,4},{4,6},{6,7},{7,5},{5,3},{3,1},{1,0},{8,10},{10,12},{12... | collective-permute-start | bytes 786440 | tf_op jit(solution)/shard_map/ppermute | solution.py:126
  89.9 10.7 %collective-permute-start.13 = (bf16[64,2048]{1,0:T(8,128)(2,1)}, bf16[64,2048]{1,0:T(8,128)(2,1)}, u32[]{:S(2)}, u32[]{:S(2)}) collective-permute-start(bf16[64,2048]{1,0:T(8,128)(2,1)} %collective-permute-done.11.refs_13_), channel_id=1, source_target_pairs={{0,2},{2,4},{4,6},{6,7},{7,5},{5,3},{3,1},{1,0},{8,10},{10,12},{12... | collective-permute-start | bytes 786440 | tf_op jit(solution)/shard_map/ppermute | solution.py:126
  100.6 2.2 %copy-start = (bf16[2048,1024]{1,0:T(8,128)(2,1)S(1)}, bf16[2048,1024]{1,0:T(8,128)(2,1)}, u32[]{:S(2)}) copy-start(bf16[2048,1024]{1,0:T(8,128)(2,1)} %all-gather.2.cloned.1.call-done.columns) | copy-start | bytes 12582916
  102.8 14.9 %copy-start.1 = (bf16[2048,1024]{1,0:T(8,128)(2,1)S(1)}, bf16[2048,1024]{1,0:T(8,128)(2,1)}, u32[]{:S(2)}) copy-start(bf16[2048,1024]{1,0:T(8,128)(2,1)} %all-gather.2.cloned.1.call-done.columns) | copy-start | bytes 12582916
  106.9 14.7 %collective-permute-start.16 = (bf16[128,1024]{1,0:T(8,128)(2,1)S(1)}, bf16[128,1024]{1,0:T(8,128)(2,1)S(1)}, u32[]{:S(2)}, u32[]{:S(2)}) collective-permute-start(bf16[128,1024]{1,0:T(8,128)(2,1)S(1)} %get-tuple-element.43), channel_id=1, source_target_pairs={{0,128},{64,192},{128,0},{192,64},{1,129},{65,193},{129,1},{193,65... | collective-permute-start | bytes 786440 | tf_op jit(solution)/shard_map/ppermute | solution.py:147
  111.8 9.8 %collective-permute-start.15 = (bf16[128,1024]{1,0:T(8,128)(2,1)S(1)}, bf16[128,1024]{1,0:T(8,128)(2,1)S(1)}, u32[]{:S(2)}, u32[]{:S(2)}) collective-permute-start(bf16[128,1024]{1,0:T(8,128)(2,1)S(1)} %get-tuple-element.42), channel_id=1, source_target_pairs={{0,192},{64,0},{128,64},{192,128},{1,193},{65,1},{129,65},{193,129... | collective-permute-start | bytes 786440 | tf_op jit(solution)/shard_map/ppermute | solution.py:147
  114.8 9.5 %collective-permute-start.14 = (bf16[128,1024]{1,0:T(8,128)(2,1)S(1)}, bf16[128,1024]{1,0:T(8,128)(2,1)S(1)}, u32[]{:S(2)}, u32[]{:S(2)}) collective-permute-start(bf16[128,1024]{1,0:T(8,128)(2,1)S(1)} %get-tuple-element.41), channel_id=1, source_target_pairs={{0,64},{64,128},{128,192},{192,0},{1,65},{65,129},{129,193},{193,1... | collective-permute-start | bytes 786440 | tf_op jit(solution)/shard_map/ppermute | solution.py:147
  124.5 29.3 %collective-permute-start.20 = (bf16[128,1024]{1,0:T(8,128)(2,1)S(1)}, bf16[128,1024]{1,0:T(8,128)(2,1)S(1)}, u32[]{:S(2)}, u32[]{:S(2)}) collective-permute-start(bf16[128,1024]{1,0:T(8,128)(2,1)S(1)} %add_convert_fusion), channel_id=1, source_target_pairs={{0,256},{256,0},{1,257},{257,1},{2,258},{258,2},{3,259},{259,3},{4... | collective-permute-start | bytes 786440 | tf_op jit(solution)/shard_map/ppermute | solution.py:160
  137.5 16.3 %collective-permute-start.19 = (bf16[128,1024]{1,0:T(8,128)(2,1)S(1)}, bf16[128,1024]{1,0:T(8,128)(2,1)S(1)}, u32[]{:S(2)}, u32[]{:S(2)}) collective-permute-start(bf16[128,1024]{1,0:T(8,128)(2,1)S(1)} %get-tuple-element.49), channel_id=1, source_target_pairs={{0,128},{64,192},{128,0},{192,64},{1,129},{65,193},{129,1},{193,65... | collective-permute-start | bytes 786440 | tf_op jit(solution)/shard_map/ppermute | solution.py:147
  139.7 14.1 %collective-permute-start.18 = (bf16[128,1024]{1,0:T(8,128)(2,1)S(1)}, bf16[128,1024]{1,0:T(8,128)(2,1)S(1)}, u32[]{:S(2)}, u32[]{:S(2)}) collective-permute-start(bf16[128,1024]{1,0:T(8,128)(2,1)S(1)} %get-tuple-element.48), channel_id=1, source_target_pairs={{0,192},{64,0},{128,64},{192,128},{1,193},{65,1},{129,65},{193,129... | collective-permute-start | bytes 786440 | tf_op jit(solution)/shard_map/ppermute | solution.py:147
  143.7 10.1 %collective-permute-start.17 = (bf16[128,1024]{1,0:T(8,128)(2,1)S(1)}, bf16[128,1024]{1,0:T(8,128)(2,1)S(1)}, u32[]{:S(2)}, u32[]{:S(2)}) collective-permute-start(bf16[128,1024]{1,0:T(8,128)(2,1)S(1)} %get-tuple-element.47), channel_id=1, source_target_pairs={{0,64},{64,128},{128,192},{192,0},{1,65},{65,129},{129,193},{193,1... | collective-permute-start | bytes 786440 | tf_op jit(solution)/shard_map/ppermute | solution.py:147
Sparse Core Ops, SparseCore 0:
  9.5 46.1 all-gather.1

commit v13 on v7

--- a/solution.py
+++ b/solution.py
@@ -46,24 +46,22 @@
     return jnp.sum(jnp.where(indices[None, :] % width == within, picked, 0.0), axis=0)
 
 
-def turned_kernel(elements, *chunks):
-    turned = elements[...].astype(jnp.float32).T.astype(jnp.bfloat16)
-    first = 0
-    for chunk in chunks:
-        chunk[...] = turned[first : first + chunk.shape[0]]
-        first += chunk.shape[0]
+def turned_kernel(first, elements, chunk):
+    value = elements[...].astype(jnp.float32).T
+    chunk[...] = value[first : first + chunk.shape[0]].astype(jnp.bfloat16)
 
 
 def turned(elements, parts):
     n_pair, n_g = elements.shape
-    return pl.pallas_call(
-        turned_kernel,
-        out_shape=[
-            jax.ShapeDtypeStruct((b - a, n_pair), elements.dtype) for a, b in cuts(n_g, parts)
-        ],
-        in_specs=[WHOLE],
-        out_specs=[WHOLE] * parts,
-    )(elements)
+    return [
+        pl.pallas_call(
+            functools.partial(turned_kernel, a),
+            out_shape=jax.ShapeDtypeStruct((b - a, n_pair), elements.dtype),
+            in_specs=[WHOLE],
+            out_specs=WHOLE,
+        )(elements)
+        for a, b in cuts(n_g, parts)
+    ]
 
 
 def product_kernel(n_turns, parts, slots, factor, columns, *refs):

time: 161 us -> 160 us (level)
  the two profiles are of different devices: /device:TPU:120 before, /device:TPU:112 now
where the time goes in v13:
time: 160 us; the launch traced here: 159 us
  waiting for transfers between devices  72 us (45%)
  starting transfers between devices  57.2 us (36%)
  between operations  13.8 us (9%)
  Pallas kernels  11.8 us (7%)
  local copies, waits for them, and re-layouts  3.25 us (2%)
    ppermute x14, waiting for transfers between devices, body(): chunks = [lax.ppermute(chunk, 'zl', step) for chunk in chunks]  61.2 us
    ppermute x14, starting transfers between devices, body(): chunks = [lax.ppermute(chunk, 'zl', step) for chunk in chunks]  26.7 us
    ppermute x6, starting transfers between devices, summed_over_x(): lax.ppermute(one, 'x', shift(n_x, s))  18.4 us
    ppermute x1, starting transfers between devices, body(): got = lax.ppermute(given, 'zh', shift(2, 1)).astype(jnp.float32)  12 us
    pallas_call x2, Pallas kernels, product(): pl.pallas_call(functools.partial(product_kernel, n_turns, parts), out_sha...  7.85 us
    ppermute x1, waiting for transfers between devices, body(): got = lax.ppermute(given, 'zh', shift(2, 1)).astype(jnp.float32)  6.99 us
    pallas_call x2, Pallas kernels, turned(): pl.pallas_call(functools.partial(turned_kernel, a), out_shape=jax.ShapeDt...  3.91 us
  transfers between devices with their start and end apart: 22, of which 17 were waited for; matrix products, arithmetic and copies ran while one was open for 1% of the time, Pallas kernels for 5%

profile of v13, /device:TPU:112, one launch (start us, length us, event | category | flops | bytes accessed | tf_op | source)
XLA Modules:
  0.0 159.4 jit_solution(16166429474655345560)
XLA Ops:
  7.3 1.9 %shard_map.55.refs_0_ = bf16[64,2048]{1,0:T(8,128)(2,1)} custom-call(bf16[2048,128]{1,0:T(8,128)(2,1)} %elements.3), custom_call_target="tpu_custom_call" | custom-call | tf_op jit(solution)/shard_map/pallas_call | solution.py:57
  11.1 2.0 %shard_map.56.refs_1_ = bf16[64,2048]{1,0:T(8,128)(2,1)} custom-call(bf16[2048,128]{1,0:T(8,128)(2,1)} %elements.3), custom_call_target="tpu_custom_call" | custom-call | tf_op jit(solution)/shard_map/pallas_call | solution.py:57
  15.0 7.9 %collective-permute-done.refs_2_ = bf16[64,2048]{1,0:T(8,128)(2,1)S(1)} collective-permute-done((bf16[64,2048]{1,0:T(8,128)(2,1)}, bf16[64,2048]{1,0:T(8,128)(2,1)S(1)}, u32[]{:S(2)}, u32[]{:S(2)}) %collective-permute-start) | collective-permute-done | bytes 262176 | tf_op jit(solution)/shard_map/ppermute | solution.py:124
  24.8 2.9 %collective-permute-done.5.refs_3_ = bf16[64,2048]{1,0:T(8,128)(2,1)S(1)} collective-permute-done((bf16[64,2048]{1,0:T(8,128)(2,1)}, bf16[64,2048]{1,0:T(8,128)(2,1)S(1)}, u32[]{:S(2)}, u32[]{:S(2)}) %collective-permute-start.5) | collective-permute-done | bytes 262176 | tf_op jit(solution)/shard_map/ppermute | solution.py:124
  27.7 1.9 %collective-permute-start.6 = (bf16[64,2048]{1,0:T(8,128)(2,1)S(1)}, bf16[64,2048]{1,0:T(8,128)(2,1)S(1)}, u32[]{:S(2)}, u32[]{:S(2)}) collective-permute-start(bf16[64,2048]{1,0:T(8,128)(2,1)S(1)} %collective-permute-done.5.refs_3_), channel_id=1, source_target_pairs={{0,2},{2,4},{4,6},{6,7},{7,5},{5,3},{3,1},{1,0},{8,10},{10,12},{12... | collective-permute-start | bytes 786440 | tf_op jit(solution)/shard_map/ppermute | solution.py:124
  29.7 3.8 %collective-permute-done.1.refs_4_ = bf16[64,2048]{1,0:T(8,128)(2,1)S(1)} collective-permute-done((bf16[64,2048]{1,0:T(8,128)(2,1)S(1)}, bf16[64,2048]{1,0:T(8,128)(2,1)S(1)}, u32[]{:S(2)}, u32[]{:S(2)}) %collective-permute-start.1) | collective-permute-done | bytes 262176 | tf_op jit(solution)/shard_map/ppermute | solution.py:124
  35.5 5.0 %collective-permute-done.6.refs_5_ = bf16[64,2048]{1,0:T(8,128)(2,1)S(1)} collective-permute-done((bf16[64,2048]{1,0:T(8,128)(2,1)S(1)}, bf16[64,2048]{1,0:T(8,128)(2,1)S(1)}, u32[]{:S(2)}, u32[]{:S(2)}) %collective-permute-start.6) | collective-permute-done | bytes 262176 | tf_op jit(solution)/shard_map/ppermute | solution.py:124
  42.5 2.9 %collective-permute-done.2.refs_6_ = bf16[64,2048]{1,0:T(8,128)(2,1)S(1)} collective-permute-done((bf16[64,2048]{1,0:T(8,128)(2,1)S(1)}, bf16[64,2048]{1,0:T(8,128)(2,1)S(1)}, u32[]{:S(2)}, u32[]{:S(2)}) %collective-permute-start.2) | collective-permute-done | bytes 262176 | tf_op jit(solution)/shard_map/ppermute | solution.py:124
  47.3 4.8 %collective-permute-done.7.refs_7_ = bf16[64,2048]{1,0:T(8,128)(2,1)S(1)} collective-permute-done((bf16[64,2048]{1,0:T(8,128)(2,1)S(1)}, bf16[64,2048]{1,0:T(8,128)(2,1)S(1)}, u32[]{:S(2)}, u32[]{:S(2)}) %collective-permute-start.7) | collective-permute-done | bytes 262176 | tf_op jit(solution)/shard_map/ppermute | solution.py:124
  54.6 4.0 %collective-permute-done.3.refs_8_ = bf16[64,2048]{1,0:T(8,128)(2,1)S(1)} collective-permute-done((bf16[64,2048]{1,0:T(8,128)(2,1)S(1)}, bf16[64,2048]{1,0:T(8,128)(2,1)S(1)}, u32[]{:S(2)}, u32[]{:S(2)}) %collective-permute-start.3) | collective-permute-done | bytes 262176 | tf_op jit(solution)/shard_map/ppermute | solution.py:124
  60.6 3.4 %collective-permute-done.8.refs_9_ = bf16[64,2048]{1,0:T(8,128)(2,1)S(1)} collective-permute-done((bf16[64,2048]{1,0:T(8,128)(2,1)S(1)}, bf16[64,2048]{1,0:T(8,128)(2,1)S(1)}, u32[]{:S(2)}, u32[]{:S(2)}) %collective-permute-start.8) | collective-permute-done | bytes 262176 | tf_op jit(solution)/shard_map/ppermute | solution.py:124
  66.4 4.9 %collective-permute-done.4.refs_10_ = bf16[64,2048]{1,0:T(8,128)(2,1)S(1)} collective-permute-done((bf16[64,2048]{1,0:T(8,128)(2,1)S(1)}, bf16[64,2048]{1,0:T(8,128)(2,1)S(1)}, u32[]{:S(2)}, u32[]{:S(2)}) %collective-permute-start.4) | collective-permute-done | bytes 262176 | tf_op jit(solution)/shard_map/ppermute | solution.py:124
  73.2 3.7 %collective-permute-done.9.refs_11_ = bf16[64,2048]{1,0:T(8,128)(2,1)S(1)} collective-permute-done((bf16[64,2048]{1,0:T(8,128)(2,1)S(1)}, bf16[64,2048]{1,0:T(8,128)(2,1)S(1)}, u32[]{:S(2)}, u32[]{:S(2)}) %collective-permute-start.9) | collective-permute-done | bytes 262176 | tf_op jit(solution)/shard_map/ppermute | solution.py:124
  77.0 1.9 %collective-permute-start.11 = (bf16[64,2048]{1,0:T(8,128)(2,1)S(1)}, bf16[64,2048]{1,0:T(8,128)(2,1)}, u32[]{:S(2)}, u32[]{:S(2)}) collective-permute-start(bf16[64,2048]{1,0:T(8,128)(2,1)S(1)} %collective-permute-done.9.refs_11_), channel_id=1, source_target_pairs={{0,2},{2,4},{4,6},{6,7},{7,5},{5,3},{3,1},{1,0},{8,10},{10,12},{12... | collective-permute-start | bytes 786440 | tf_op jit(solution)/shard_map/ppermute | solution.py:124
  78.9 4.3 %collective-permute-done.10.refs_12_ = bf16[64,2048]{1,0:T(8,128)(2,1)S(1)} collective-permute-done((bf16[64,2048]{1,0:T(8,128)(2,1)S(1)}, bf16[64,2048]{1,0:T(8,128)(2,1)S(1)}, u32[]{:S(2)}, u32[]{:S(2)}) %collective-permute-start.10) | collective-permute-done | bytes 262176 | tf_op jit(solution)/shard_map/ppermute | solution.py:124
  83.2 1.9 %collective-permute-start.12 = (bf16[64,2048]{1,0:T(8,128)(2,1)S(1)}, bf16[64,2048]{1,0:T(8,128)(2,1)}, u32[]{:S(2)}, u32[]{:S(2)}) collective-permute-start(bf16[64,2048]{1,0:T(8,128)(2,1)S(1)} %collective-permute-done.10.refs_12_), channel_id=1, source_target_pairs={{0,2},{2,4},{4,6},{6,7},{7,5},{5,3},{3,1},{1,0},{8,10},{10,12},{12... | collective-permute-start | bytes 786440 | tf_op jit(solution)/shard_map/ppermute | solution.py:124
  85.1 4.7 %collective-permute-done.11.refs_13_ = bf16[64,2048]{1,0:T(8,128)(2,1)} collective-permute-done((bf16[64,2048]{1,0:T(8,128)(2,1)S(1)}, bf16[64,2048]{1,0:T(8,128)(2,1)}, u32[]{:S(2)}, u32[]{:S(2)}) %collective-permute-start.11) | collective-permute-done | bytes 262176 | tf_op jit(solution)/shard_map/ppermute | solution.py:124
  89.8 1.9 %collective-permute-start.13 = (bf16[64,2048]{1,0:T(8,128)(2,1)}, bf16[64,2048]{1,0:T(8,128)(2,1)}, u32[]{:S(2)}, u32[]{:S(2)}) collective-permute-start(bf16[64,2048]{1,0:T(8,128)(2,1)} %collective-permute-done.11.refs_13_), channel_id=1, source_target_pairs={{0,2},{2,4},{4,6},{6,7},{7,5},{5,3},{3,1},{1,0},{8,10},{10,12},{12... | collective-permute-start | bytes 786440 | tf_op jit(solution)/shard_map/ppermute | solution.py:124
  91.8 3.2 %collective-permute-done.12.refs_14_ = bf16[64,2048]{1,0:T(8,128)(2,1)} collective-permute-done((bf16[64,2048]{1,0:T(8,128)(2,1)S(1)}, bf16[64,2048]{1,0:T(8,128)(2,1)}, u32[]{:S(2)}, u32[]{:S(2)}) %collective-permute-start.12) | collective-permute-done | bytes 262176 | tf_op jit(solution)/shard_map/ppermute | solution.py:124
  95.0 5.5 %collective-permute-done.13.refs_15_ = bf16[64,2048]{1,0:T(8,128)(2,1)} collective-permute-done((bf16[64,2048]{1,0:T(8,128)(2,1)}, bf16[64,2048]{1,0:T(8,128)(2,1)}, u32[]{:S(2)}, u32[]{:S(2)}) %collective-permute-start.13) | collective-permute-done | bytes 262176 | tf_op jit(solution)/shard_map/ppermute | solution.py:124
  100.5 2.2 %copy-done = bf16[2048,1024]{1,0:T(8,128)(2,1)S(1)} copy-done((bf16[2048,1024]{1,0:T(8,128)(2,1)S(1)}, bf16[2048,1024]{1,0:T(8,128)(2,1)}, u32[]{:S(2)}) %copy-start) | copy-done | bytes 4194328
  102.7 4.0 %shard_map.57 = (f32[128,1024]{1,0:T(8,128)S(1)}, bf16[128,1024]{1,0:T(8,128)(2,1)S(1)}, bf16[128,1024]{1,0:T(8,128)(2,1)S(1)}, bf16[128,1024]{1,0:T(8,128)(2,1)S(1)}) custom-call(s32[8]{0:T(128)S(1)} %get-tuple-element.57.slots, f32[1,2048]{1,0:T(1,128)S(1)} %bitcast.5, bf16[2048,1024]{1,0:T(8,128)(2,1)S(1)} %copy-done, bf16[64,2048]{1,0:T(8,128)(2,1)S(1)} %copy-done.2, ...), custom_call_target="tpu_custom_call" | custom-call | flops 2147483648 | bytes 8388608 | tf_op jit(solution)/shard_map/pallas_call | solution.py:98
  106.7 4.7 %collective-permute-start.16 = (bf16[128,1024]{1,0:T(8,128)(2,1)S(1)}, bf16[128,1024]{1,0:T(8,128)(2,1)S(1)}, u32[]{:S(2)}, u32[]{:S(2)}) collective-permute-start(bf16[128,1024]{1,0:T(8,128)(2,1)S(1)} %get-tuple-element.39), channel_id=1, source_target_pairs={{0,192},{64,0},{128,64},{192,128},{1,193},{65,1},{129,65},{193,129... | collective-permute-start | bytes 786440 | tf_op jit(solution)/shard_map/ppermute | solution.py:144
  111.4 2.7 %collective-permute-start.15 = (bf16[128,1024]{1,0:T(8,128)(2,1)S(1)}, bf16[128,1024]{1,0:T(8,128)(2,1)S(1)}, u32[]{:S(2)}, u32[]{:S(2)}) collective-permute-start(bf16[128,1024]{1,0:T(8,128)(2,1)S(1)} %get-tuple-element.38), channel_id=1, source_target_pairs={{0,128},{64,192},{128,0},{192,64},{1,129},{65,193},{129,1},{193,65... | collective-permute-start | bytes 786440 | tf_op jit(solution)/shard_map/ppermute | solution.py:144
  114.1 2.8 %collective-permute-start.14 = (bf16[128,1024]{1,0:T(8,128)(2,1)S(1)}, bf16[128,1024]{1,0:T(8,128)(2,1)S(1)}, u32[]{:S(2)}, u32[]{:S(2)}) collective-permute-start(bf16[128,1024]{1,0:T(8,128)(2,1)S(1)} %get-tuple-element.37), channel_id=1, source_target_pairs={{0,64},{64,128},{128,192},{192,0},{1,65},{65,129},{129,193},{193,1... | collective-permute-start | bytes 786440 | tf_op jit(solution)/shard_map/ppermute | solution.py:144
  116.9 3.9 %shard_map.58 = (f32[128,1024]{1,0:T(8,128)S(1)}, bf16[128,1024]{1,0:T(8,128)(2,1)S(1)}, bf16[128,1024]{1,0:T(8,128)(2,1)S(1)}, bf16[128,1024]{1,0:T(8,128)(2,1)S(1)}) custom-call(s32[8]{0:T(128)S(1)} %get-tuple-element.34.slots, f32[1,2048]{1,0:T(1,128)S(1)} %bitcast.6, bf16[2048,1024]{1,0:T(8,128)(2,1)S(1)} %copy-done.1, bf16[64,2048]{1,0:T(8,128)(2,1)S(1)} %copy-done.2, ...), custom_call_target="tpu_custom_call" | custom-call | flops 2147483648 | bytes 8388608 | tf_op jit(solution)/shard_map/pallas_call | solution.py:98
  121.2 2.8 %collective-permute-done.14 = bf16[128,1024]{1,0:T(8,128)(2,1)S(1)} collective-permute-done((bf16[128,1024]{1,0:T(8,128)(2,1)S(1)}, bf16[128,1024]{1,0:T(8,128)(2,1)S(1)}, u32[]{:S(2)}, u32[]{:S(2)}) %collective-permute-start.14) | collective-permute-done | bytes 262176 | tf_op jit(solution)/shard_map/ppermute | solution.py:144
  124.1 12.0 %collective-permute-start.20 = (bf16[128,1024]{1,0:T(8,128)(2,1)S(1)}, bf16[128,1024]{1,0:T(8,128)(2,1)S(1)}, u32[]{:S(2)}, u32[]{:S(2)}) collective-permute-start(bf16[128,1024]{1,0:T(8,128)(2,1)S(1)} %add_convert_fusion), channel_id=1, source_target_pairs={{0,256},{256,0},{1,257},{257,1},{2,258},{258,2},{3,259},{259,3},{4... | collective-permute-start | bytes 786440 | tf_op jit(solution)/shard_map/ppermute | solution.py:157
  136.1 2.5 %collective-permute-start.19 = (bf16[128,1024]{1,0:T(8,128)(2,1)S(1)}, bf16[128,1024]{1,0:T(8,128)(2,1)S(1)}, u32[]{:S(2)}, u32[]{:S(2)}) collective-permute-start(bf16[128,1024]{1,0:T(8,128)(2,1)S(1)} %get-tuple-element.45), channel_id=1, source_target_pairs={{0,192},{64,0},{128,64},{192,128},{1,193},{65,1},{129,65},{193,129... | collective-permute-start | bytes 786440 | tf_op jit(solution)/shard_map/ppermute | solution.py:144
  138.6 2.7 %collective-permute-start.18 = (bf16[128,1024]{1,0:T(8,128)(2,1)S(1)}, bf16[128,1024]{1,0:T(8,128)(2,1)S(1)}, u32[]{:S(2)}, u32[]{:S(2)}) collective-permute-start(bf16[128,1024]{1,0:T(8,128)(2,1)S(1)} %get-tuple-element.44), channel_id=1, source_target_pairs={{0,128},{64,192},{128,0},{192,64},{1,129},{65,193},{129,1},{193,65... | collective-permute-start | bytes 786440 | tf_op jit(solution)/shard_map/ppermute | solution.py:144
  141.3 3.1 %collective-permute-start.17 = (bf16[128,1024]{1,0:T(8,128)(2,1)S(1)}, bf16[128,1024]{1,0:T(8,128)(2,1)S(1)}, u32[]{:S(2)}, u32[]{:S(2)}) collective-permute-start(bf16[128,1024]{1,0:T(8,128)(2,1)S(1)} %get-tuple-element.43), channel_id=1, source_target_pairs={{0,64},{64,128},{128,192},{192,0},{1,65},{65,129},{129,193},{193,1... | collective-permute-start | bytes 786440 | tf_op jit(solution)/shard_map/ppermute | solution.py:144
  144.5 7.0 %collective-permute-done.20 = bf16[128,1024]{1,0:T(8,128)(2,1)S(1)} collective-permute-done((bf16[128,1024]{1,0:T(8,128)(2,1)S(1)}, bf16[128,1024]{1,0:T(8,128)(2,1)S(1)}, u32[]{:S(2)}, u32[]{:S(2)}) %collective-permute-start.20) | collective-permute-done | bytes 262176 | tf_op jit(solution)/shard_map/ppermute | solution.py:157
  (47 shorter events, 22.7 us)
Async XLA Ops:
  6.5 23.1 %copy-start.5 = (f32[2000]{0:T(1024)S(1)}, f32[2000]{0:T(1024)}, u32[]{:S(2)}) copy-start(f32[2000]{0:T(1024)} %param.8) | copy-start | bytes 24004
  6.5 35.9 %copy-start.4 = (f32[4096]{0:T(1024)S(1)}, f32[4096]{0:T(1024)}, u32[]{:S(2)}) copy-start(f32[4096]{0:T(1024)} %param.9) | copy-start | bytes 49156
  6.5 47.5 %copy-start.7 = (s32[2048]{0:T(1024)S(1)}, s32[2048]{0:T(1024)}, u32[]{:S(2)}) copy-start(s32[2048]{0:T(1024)} %param.6) | copy-start | bytes 24580
  6.5 47.5 %copy-start.6 = (s32[2048]{0:T(1024)S(1)}, s32[2048]{0:T(1024)}, u32[]{:S(2)}) copy-start(s32[2048]{0:T(1024)} %param.7) | copy-start | bytes 24580
  6.5 94.0 %all-gather.2.cloned.1.call-start = ((), (), s32[]{:S(2)}) async-start(), calls=%async_computation | async-start | bytes 4718592 | tf_op jit(solution)/shard_map/all_gather | solution.py:116
  9.2 13.7 %collective-permute-start = (bf16[64,2048]{1,0:T(8,128)(2,1)}, bf16[64,2048]{1,0:T(8,128)(2,1)S(1)}, u32[]{:S(2)}, u32[]{:S(2)}) collective-permute-start(bf16[64,2048]{1,0:T(8,128)(2,1)} %shard_map.55.refs_0_), channel_id=1, source_target_pairs={{0,2},{2,4},{4,6},{6,7},{7,5},{5,3},{3,1},{1,0},{8,10},{10,12},{12... | collective-permute-start | bytes 786440 | tf_op jit(solution)/shard_map/ppermute | solution.py:124
  13.1 14.6 %collective-permute-start.5 = (bf16[64,2048]{1,0:T(8,128)(2,1)}, bf16[64,2048]{1,0:T(8,128)(2,1)S(1)}, u32[]{:S(2)}, u32[]{:S(2)}) collective-permute-start(bf16[64,2048]{1,0:T(8,128)(2,1)} %shard_map.56.refs_1_), channel_id=1, source_target_pairs={{0,2},{2,4},{4,6},{6,7},{7,5},{5,3},{3,1},{1,0},{8,10},{10,12},{12... | collective-permute-start | bytes 786440 | tf_op jit(solution)/shard_map/ppermute | solution.py:124
  22.9 10.7 %collective-permute-start.1 = (bf16[64,2048]{1,0:T(8,128)(2,1)S(1)}, bf16[64,2048]{1,0:T(8,128)(2,1)S(1)}, u32[]{:S(2)}, u32[]{:S(2)}) collective-permute-start(bf16[64,2048]{1,0:T(8,128)(2,1)S(1)} %collective-permute-done.refs_2_), channel_id=1, source_target_pairs={{0,2},{2,4},{4,6},{6,7},{7,5},{5,3},{3,1},{1,0},{8,10},{10,12},{12... | collective-permute-start | bytes 786440 | tf_op jit(solution)/shard_map/ppermute | solution.py:124
  27.7 12.8 %collective-permute-start.6 = (bf16[64,2048]{1,0:T(8,128)(2,1)S(1)}, bf16[64,2048]{1,0:T(8,128)(2,1)S(1)}, u32[]{:S(2)}, u32[]{:S(2)}) collective-permute-start(bf16[64,2048]{1,0:T(8,128)(2,1)S(1)} %collective-permute-done.5.refs_3_), channel_id=1, source_target_pairs={{0,2},{2,4},{4,6},{6,7},{7,5},{5,3},{3,1},{1,0},{8,10},{10,12},{12... | collective-permute-start | bytes 786440 | tf_op jit(solution)/shard_map/ppermute | solution.py:124
  33.6 11.8 %collective-permute-start.2 = (bf16[64,2048]{1,0:T(8,128)(2,1)S(1)}, bf16[64,2048]{1,0:T(8,128)(2,1)S(1)}, u32[]{:S(2)}, u32[]{:S(2)}) collective-permute-start(bf16[64,2048]{1,0:T(8,128)(2,1)S(1)} %collective-permute-done.1.refs_4_), channel_id=1, source_target_pairs={{0,2},{2,4},{4,6},{6,7},{7,5},{5,3},{3,1},{1,0},{8,10},{10,12},{12... | collective-permute-start | bytes 786440 | tf_op jit(solution)/shard_map/ppermute | solution.py:124
  40.5 11.6 %collective-permute-start.7 = (bf16[64,2048]{1,0:T(8,128)(2,1)S(1)}, bf16[64,2048]{1,0:T(8,128)(2,1)S(1)}, u32[]{:S(2)}, u32[]{:S(2)}) collective-permute-start(bf16[64,2048]{1,0:T(8,128)(2,1)S(1)} %collective-permute-done.6.refs_5_), channel_id=1, source_target_pairs={{0,2},{2,4},{4,6},{6,7},{7,5},{5,3},{3,1},{1,0},{8,10},{10,12},{12... | collective-permute-start | bytes 786440 | tf_op jit(solution)/shard_map/ppermute | solution.py:124
  45.4 13.2 %collective-permute-start.3 = (bf16[64,2048]{1,0:T(8,128)(2,1)S(1)}, bf16[64,2048]{1,0:T(8,128)(2,1)S(1)}, u32[]{:S(2)}, u32[]{:S(2)}) collective-permute-start(bf16[64,2048]{1,0:T(8,128)(2,1)S(1)} %collective-permute-done.2.refs_6_), channel_id=1, source_target_pairs={{0,2},{2,4},{4,6},{6,7},{7,5},{5,3},{3,1},{1,0},{8,10},{10,12},{12... | collective-permute-start | bytes 786440 | tf_op jit(solution)/shard_map/ppermute | solution.py:124
  52.1 11.8 %collective-permute-start.8 = (bf16[64,2048]{1,0:T(8,128)(2,1)S(1)}, bf16[64,2048]{1,0:T(8,128)(2,1)S(1)}, u32[]{:S(2)}, u32[]{:S(2)}) collective-permute-start(bf16[64,2048]{1,0:T(8,128)(2,1)S(1)} %collective-permute-done.7.refs_7_), channel_id=1, source_target_pairs={{0,2},{2,4},{4,6},{6,7},{7,5},{5,3},{3,1},{1,0},{8,10},{10,12},{12... | collective-permute-start | bytes 786440 | tf_op jit(solution)/shard_map/ppermute | solution.py:124
  54.1 46.4 %copy-start.2 = (bf16[64,2048]{1,0:T(8,128)(2,1)S(1)}, bf16[64,2048]{1,0:T(8,128)(2,1)}, u32[]{:S(2)}) copy-start(bf16[64,2048]{1,0:T(8,128)(2,1)} %shard_map.55.refs_0_) | copy-start | bytes 786436
  54.1 46.4 %copy-start.3 = (bf16[64,2048]{1,0:T(8,128)(2,1)S(1)}, bf16[64,2048]{1,0:T(8,128)(2,1)}, u32[]{:S(2)}) copy-start(bf16[64,2048]{1,0:T(8,128)(2,1)} %shard_map.56.refs_1_) | copy-start | bytes 786436
  58.7 12.7 %collective-permute-start.4 = (bf16[64,2048]{1,0:T(8,128)(2,1)S(1)}, bf16[64,2048]{1,0:T(8,128)(2,1)S(1)}, u32[]{:S(2)}, u32[]{:S(2)}) collective-permute-start(bf16[64,2048]{1,0:T(8,128)(2,1)S(1)} %collective-permute-done.3.refs_8_), channel_id=1, source_target_pairs={{0,2},{2,4},{4,6},{6,7},{7,5},{5,3},{3,1},{1,0},{8,10},{10,12},{12... | collective-permute-start | bytes 786440 | tf_op jit(solution)/shard_map/ppermute | solution.py:124
  64.0 13.0 %collective-permute-start.9 = (bf16[64,2048]{1,0:T(8,128)(2,1)S(1)}, bf16[64,2048]{1,0:T(8,128)(2,1)S(1)}, u32[]{:S(2)}, u32[]{:S(2)}) collective-permute-start(bf16[64,2048]{1,0:T(8,128)(2,1)S(1)} %collective-permute-done.8.refs_9_), channel_id=1, source_target_pairs={{0,2},{2,4},{4,6},{6,7},{7,5},{5,3},{3,1},{1,0},{8,10},{10,12},{12... | collective-permute-start | bytes 786440 | tf_op jit(solution)/shard_map/ppermute | solution.py:124
  71.3 11.9 %collective-permute-start.10 = (bf16[64,2048]{1,0:T(8,128)(2,1)S(1)}, bf16[64,2048]{1,0:T(8,128)(2,1)S(1)}, u32[]{:S(2)}, u32[]{:S(2)}) collective-permute-start(bf16[64,2048]{1,0:T(8,128)(2,1)S(1)} %collective-permute-done.4.refs_10_), channel_id=1, source_target_pairs={{0,2},{2,4},{4,6},{6,7},{7,5},{5,3},{3,1},{1,0},{8,10},{10,12},{12... | collective-permute-start | bytes 786440 | tf_op jit(solution)/shard_map/ppermute | solution.py:124
  77.0 12.9 %collective-permute-start.11 = (bf16[64,2048]{1,0:T(8,128)(2,1)S(1)}, bf16[64,2048]{1,0:T(8,128)(2,1)}, u32[]{:S(2)}, u32[]{:S(2)}) collective-permute-start(bf16[64,2048]{1,0:T(8,128)(2,1)S(1)} %collective-permute-done.9.refs_11_), channel_id=1, source_target_pairs={{0,2},{2,4},{4,6},{6,7},{7,5},{5,3},{3,1},{1,0},{8,10},{10,12},{12... | collective-permute-start | bytes 786440 | tf_op jit(solution)/shard_map/ppermute | solution.py:124
  83.2 11.8 %collective-permute-start.12 = (bf16[64,2048]{1,0:T(8,128)(2,1)S(1)}, bf16[64,2048]{1,0:T(8,128)(2,1)}, u32[]{:S(2)}, u32[]{:S(2)}) collective-permute-start(bf16[64,2048]{1,0:T(8,128)(2,1)S(1)} %collective-permute-done.10.refs_12_), channel_id=1, source_target_pairs={{0,2},{2,4},{4,6},{6,7},{7,5},{5,3},{3,1},{1,0},{8,10},{10,12},{12... | collective-permute-start | bytes 786440 | tf_op jit(solution)/shard_map/ppermute | solution.py:124
  89.8 10.7 %collective-permute-start.13 = (bf16[64,2048]{1,0:T(8,128)(2,1)}, bf16[64,2048]{1,0:T(8,128)(2,1)}, u32[]{:S(2)}, u32[]{:S(2)}) collective-permute-start(bf16[64,2048]{1,0:T(8,128)(2,1)} %collective-permute-done.11.refs_13_), channel_id=1, source_target_pairs={{0,2},{2,4},{4,6},{6,7},{7,5},{5,3},{3,1},{1,0},{8,10},{10,12},{12... | collective-permute-start | bytes 786440 | tf_op jit(solution)/shard_map/ppermute | solution.py:124
  100.5 2.2 %copy-start = (bf16[2048,1024]{1,0:T(8,128)(2,1)S(1)}, bf16[2048,1024]{1,0:T(8,128)(2,1)}, u32[]{:S(2)}) copy-start(bf16[2048,1024]{1,0:T(8,128)(2,1)} %all-gather.2.cloned.1.call-done.columns) | copy-start | bytes 12582916
  102.7 14.2 %copy-start.1 = (bf16[2048,1024]{1,0:T(8,128)(2,1)S(1)}, bf16[2048,1024]{1,0:T(8,128)(2,1)}, u32[]{:S(2)}) copy-start(bf16[2048,1024]{1,0:T(8,128)(2,1)} %all-gather.2.cloned.1.call-done.columns) | copy-start | bytes 12582916
  106.7 14.1 %collective-permute-start.16 = (bf16[128,1024]{1,0:T(8,128)(2,1)S(1)}, bf16[128,1024]{1,0:T(8,128)(2,1)S(1)}, u32[]{:S(2)}, u32[]{:S(2)}) collective-permute-start(bf16[128,1024]{1,0:T(8,128)(2,1)S(1)} %get-tuple-element.39), channel_id=1, source_target_pairs={{0,192},{64,0},{128,64},{192,128},{1,193},{65,1},{129,65},{193,129... | collective-permute-start | bytes 786440 | tf_op jit(solution)/shard_map/ppermute | solution.py:144
  111.4 9.8 %collective-permute-start.15 = (bf16[128,1024]{1,0:T(8,128)(2,1)S(1)}, bf16[128,1024]{1,0:T(8,128)(2,1)S(1)}, u32[]{:S(2)}, u32[]{:S(2)}) collective-permute-start(bf16[128,1024]{1,0:T(8,128)(2,1)S(1)} %get-tuple-element.38), channel_id=1, source_target_pairs={{0,128},{64,192},{128,0},{192,64},{1,129},{65,193},{129,1},{193,65... | collective-permute-start | bytes 786440 | tf_op jit(solution)/shard_map/ppermute | solution.py:144
  114.1 9.9 %collective-permute-start.14 = (bf16[128,1024]{1,0:T(8,128)(2,1)S(1)}, bf16[128,1024]{1,0:T(8,128)(2,1)S(1)}, u32[]{:S(2)}, u32[]{:S(2)}) collective-permute-start(bf16[128,1024]{1,0:T(8,128)(2,1)S(1)} %get-tuple-element.37), channel_id=1, source_target_pairs={{0,64},{64,128},{128,192},{192,0},{1,65},{65,129},{129,193},{193,1... | collective-permute-start | bytes 786440 | tf_op jit(solution)/shard_map/ppermute | solution.py:144
  124.1 27.3 %collective-permute-start.20 = (bf16[128,1024]{1,0:T(8,128)(2,1)S(1)}, bf16[128,1024]{1,0:T(8,128)(2,1)S(1)}, u32[]{:S(2)}, u32[]{:S(2)}) collective-permute-start(bf16[128,1024]{1,0:T(8,128)(2,1)S(1)} %add_convert_fusion), channel_id=1, source_target_pairs={{0,256},{256,0},{1,257},{257,1},{2,258},{258,2},{3,259},{259,3},{4... | collective-permute-start | bytes 786440 | tf_op jit(solution)/shard_map/ppermute | solution.py:157
  136.1 15.3 %collective-permute-start.19 = (bf16[128,1024]{1,0:T(8,128)(2,1)S(1)}, bf16[128,1024]{1,0:T(8,128)(2,1)S(1)}, u32[]{:S(2)}, u32[]{:S(2)}) collective-permute-start(bf16[128,1024]{1,0:T(8,128)(2,1)S(1)} %get-tuple-element.45), channel_id=1, source_target_pairs={{0,192},{64,0},{128,64},{192,128},{1,193},{65,1},{129,65},{193,129... | collective-permute-start | bytes 786440 | tf_op jit(solution)/shard_map/ppermute | solution.py:144
  138.6 12.8 %collective-permute-start.18 = (bf16[128,1024]{1,0:T(8,128)(2,1)S(1)}, bf16[128,1024]{1,0:T(8,128)(2,1)S(1)}, u32[]{:S(2)}, u32[]{:S(2)}) collective-permute-start(bf16[128,1024]{1,0:T(8,128)(2,1)S(1)} %get-tuple-element.44), channel_id=1, source_target_pairs={{0,128},{64,192},{128,0},{192,64},{1,129},{65,193},{129,1},{193,65... | collective-permute-start | bytes 786440 | tf_op jit(solution)/shard_map/ppermute | solution.py:144
  141.3 10.1 %collective-permute-start.17 = (bf16[128,1024]{1,0:T(8,128)(2,1)S(1)}, bf16[128,1024]{1,0:T(8,128)(2,1)S(1)}, u32[]{:S(2)}, u32[]{:S(2)}) collective-permute-start(bf16[128,1024]{1,0:T(8,128)(2,1)S(1)} %get-tuple-element.43), channel_id=1, source_target_pairs={{0,64},{64,128},{128,192},{192,0},{1,65},{65,129},{129,193},{193,1... | collective-permute-start | bytes 786440 | tf_op jit(solution)/shard_map/ppermute | solution.py:144
Sparse Core Ops, SparseCore 0:
  9.5 46.6 all-gather.1
